TPU v7x, 32 devices: a whole 2x2x4 slice. The times are simulated.
32 devices in a mesh: ctx: 8 (over z, x), fsdp: 4 (over y, core).
Axes of the slice: x: 2, y: 2, z: 4, core: 2. Of those that a mesh axis runs over, the one named last changes fastest.
Arguments:
- tokens: bfloat16 [4, 2048, 768], P('fsdp', 'ctx'), may hold values from -6 to 6
- cotangent: bfloat16 [4, 2048, 768], P('fsdp', 'ctx'), may hold values from -6 to 6
- seq_lengths: int32 [4, 2], P('fsdp'), may hold values from 1024 to 1024, as said below
- block_order: int32 [4, 16], P('fsdp'), may hold values from 0 to 15, as said below
- routes: int32 [2, 4, 2048, 2], P(None, 'fsdp', 'ctx'), may hold values from 0 to 11, all different within a row; in each aligned block of 256 rows (0 to 255, 256 to 511, ..., all dimensions but the last counted through in order) at most 64 rows name the same one
- gains: bfloat16 [2, 2, 768], P(None, None, 'fsdp'), may hold values from 0.5 to 1.5
- qkv_weights: bfloat16 [2, 3, 768, 768], P(None, None, 'fsdp'), may hold values from -0.21875 to 0.21875
- out_weight: bfloat16 [2, 768, 768], P(None, 'fsdp'), may hold values from -3 to 3
- router: bfloat16 [2, 768, 16], P(None, 'fsdp'), may hold values from -0.125 to 0.125
- const_values: bfloat16 [2, 2, 768], P(None, None, 'fsdp'), may hold values from -6 to 6
- w_gate_up: bfloat16 [2, 8, 2, 768, 2048], P(None, None, None, None, 'fsdp'), may hold values from -0.21875 to 0.21875
- w_down: bfloat16 [2, 8, 2048, 768], P(None, None, 'fsdp'), may hold values from -0.125 to 0.125
Outputs:
- output: float32 [4, 2048, 768], P('fsdp', 'ctx')
- input_grad: float32 [4, 2048, 768], P('fsdp', 'ctx')
- grad_gains: float32 [2, 2, 768], P(None, None, 'fsdp')
- grad_qkv: float32 [2, 3, 768, 768], P(None, None, 'fsdp')
- grad_out: float32 [2, 768, 768], P(None, 'fsdp')
- grad_router: float32 [2, 768, 16], P(None, 'fsdp')
- grad_const: float32 [2, 2, 768], P(None, None, 'fsdp')
- grad_gate_up: float32 [2, 8, 2, 768, 2048], P(None, None, None, None, 'fsdp')
- grad_down: float32 [2, 8, 2048, 768], P(None, None, 'fsdp')
Inputs may be any that keep to these rules, and one draw needn't show every extreme that they name: `seq_lengths`: the first sequence of a pack holds 1024 to half the pack's tokens, the second the rest; in some pack the first holds exactly 1024. `block_order`: A pack is cut into blocks of 128 positions; entries 2c and 2c + 1 of a pack's row name the blocks that index c of ctx holds, in that order, the first from the pack's first half and the second from its second half; every block is named once. `routes`: each row names two different experts; among one device's 256 rows of a layer no expert is named more than 64 times, a bound that some block reaches.
All inputs are finite; a program needn't handle non-finite values.
Results may differ from a plain program's by a relative error of at most 0.035.
Values may be sent and summed in bfloat16 or wider, within the bound.
A program may use at most 384 MiB of HBM per device.

v0:
```python
import jax
import jax.numpy as jnp
from jax import lax
from jax.sharding import PartitionSpec as P

HEADS = 12
HEAD_DIM = 64
NF = 8
NC = 2
LAYERS = 2
NE = 12
MOST = 64


def from_behind(x, axis, by):
    devices = lax.axis_size(axis)
    return lax.ppermute(x, axis, [(i, (i + by) % devices) for i in range(devices)])


def layout_tables(lengths, order_row, tok_count):
    block_len = tok_count // 2
    pack_len = order_row.shape[0] * block_len
    pack_rows = jnp.arange(pack_len, dtype=jnp.int32)
    owner = pack_rows // tok_count
    which_half = pack_rows % tok_count // block_len
    block_ids = order_row[2 * owner + which_half]
    pack_pos = block_ids * block_len + pack_rows % block_len
    segment = (pack_pos >= lengths[0]).astype(jnp.int32)
    seq_pos = pack_pos - segment * lengths[0]
    return (pack_pos, segment, seq_pos)


def angle_tables(seq_pos, head_size):
    half_size = head_size // 2
    frequency = jnp.exp(-jnp.log(10000.0) * jnp.arange(half_size, dtype=jnp.float32) / half_size)
    angles = seq_pos.astype(jnp.float32)[:, None] * frequency[None, :]
    return (jnp.cos(angles)[:, None, :], jnp.sin(angles)[:, None, :])


def rotate_pairs(values, cosine_table, sine_table, direction):
    half_size = values.shape[-1] // 2
    first_half = values[..., :half_size]
    second_half = values[..., half_size:]
    return jnp.concatenate(
        [
            first_half * cosine_table - direction * second_half * sine_table,
            second_half * cosine_table + direction * first_half * sine_table,
        ],
        axis=-1,
    )


def rms_parts(values):
    inverse = lax.rsqrt(jnp.mean(values * values, axis=-1, keepdims=True) + 1e-06)
    return (values * inverse, inverse)


def rms_back(grad_normed, base_values, inverse):
    return inverse * (
        grad_normed - base_values * jnp.mean(grad_normed * base_values, axis=-1, keepdims=True)
    )


def expert_forward(inputs_low, gate_up_use, down_use):
    gate_up_out = jnp.einsum(
        "emd,ecdf->ecmf", inputs_low, gate_up_use, preferred_element_type=jnp.float32
    )
    hidden_low = (jax.nn.silu(gate_up_out[:, 0]) * gate_up_out[:, 1]).astype(jnp.bfloat16)
    partial_value = jnp.einsum(
        "emf,efd->emd", hidden_low, down_use, preferred_element_type=jnp.float32
    )
    return (gate_up_out, hidden_low, partial_value)


def expert_backward(inputs_low, gate_up_out, hidden_low, grad_part_low, gate_up_use, down_use):
    grad_down = jnp.einsum(
        "emf,emd->efd", hidden_low, grad_part_low, preferred_element_type=jnp.float32
    )
    grad_hidden = jnp.einsum(
        "emd,efd->emf", grad_part_low, down_use, preferred_element_type=jnp.float32
    )
    gate_out = gate_up_out[:, 0]
    sigmoid_gate = jax.nn.sigmoid(gate_out)
    grad_pair_low = jnp.stack(
        [
            grad_hidden
            * gate_up_out[:, 1]
            * sigmoid_gate
            * (1.0 + gate_out * (1.0 - sigmoid_gate)),
            grad_hidden * gate_out * sigmoid_gate,
        ],
        axis=1,
    ).astype(jnp.bfloat16)
    grad_gate_up = jnp.einsum(
        "emd,ecmf->ecdf", inputs_low, grad_pair_low, preferred_element_type=jnp.float32
    )
    grad_rows = jnp.einsum(
        "ecmf,ecdf->emd", grad_pair_low, gate_up_use, preferred_element_type=jnp.float32
    )
    return (grad_gate_up, grad_down, grad_rows)


def shards(
    tokens,
    cotangent,
    seq_lengths,
    block_order,
    routes,
    gains,
    qkv_weights,
    out_weight,
    router,
    const_values,
    w_gate_up,
    w_down,
):
    tok_count = tokens.shape[1]
    width = tokens.shape[2]
    ctx_size = lax.axis_size("ctx")
    own_index = lax.axis_index("ctx")
    score_scale = HEAD_DIM ** (-0.5)
    pack_pos, segment, seq_pos = layout_tables(seq_lengths[0], block_order[0], tok_count)
    own_start = own_index * tok_count
    query_pos = lax.dynamic_slice_in_dim(pack_pos, own_start, tok_count)
    query_seg = lax.dynamic_slice_in_dim(segment, own_start, tok_count)
    cosine_table, sine_table = angle_tables(
        lax.dynamic_slice_in_dim(seq_pos, own_start, tok_count), HEAD_DIM
    )
    head_shape = (tok_count, HEADS, HEAD_DIM)
    expert_ids = jnp.arange(NE, dtype=jnp.int32)
    slot_ids = jnp.arange(MOST, dtype=jnp.int32)
    row_ids = jnp.arange(tok_count, dtype=jnp.int32)

    def allowed_pairs(key_offset, key_count):
        key_pos = lax.dynamic_slice_in_dim(pack_pos, key_offset, key_count)
        key_seg = lax.dynamic_slice_in_dim(segment, key_offset, key_count)
        return (query_seg[:, None] == key_seg[None, :]) & (key_pos[None, :] <= query_pos[:, None])

    stream = tokens[0].astype(jnp.float32)
    previous = jnp.zeros((tok_count, NE), jnp.float32)
    saved = []
    for layer_index in range(LAYERS):
        gain_all, qkv_all, out_all, router_all, const_all = (
            lax.all_gather(gains[layer_index], "fsdp", axis=1, tiled=True),
            lax.all_gather(qkv_weights[layer_index], "fsdp", axis=1, tiled=True),
            lax.all_gather(out_weight[layer_index], "fsdp", axis=0, tiled=True),
            lax.all_gather(router[layer_index], "fsdp", axis=0, tiled=True),
            lax.all_gather(const_values[layer_index], "fsdp", axis=1, tiled=True),
        )
        gain_float = gain_all.astype(jnp.float32)
        base_one, inverse_one = rms_parts(stream)
        normed_low = (base_one * gain_float[0]).astype(jnp.bfloat16)
        projected = jnp.einsum(
            "td,cde->cte", normed_low, qkv_all, preferred_element_type=jnp.float32
        )
        queries_low = rotate_pairs(
            projected[0].reshape(head_shape), cosine_table, sine_table, 1.0
        ).astype(jnp.bfloat16)
        keys_low = rotate_pairs(
            projected[1].reshape(head_shape), cosine_table, sine_table, 1.0
        ).astype(jnp.bfloat16)
        values_low = projected[2].reshape(head_shape).astype(jnp.bfloat16)

        def fold_step(running, shard_piece, offset, queries_use=queries_low):
            keys_piece, values_piece = shard_piece
            allowed = allowed_pairs(offset, keys_piece.shape[0])[None]
            scores = (
                jnp.einsum(
                    "qhd,khd->hqk", queries_use, keys_piece, preferred_element_type=jnp.float32
                )
                * score_scale
            )
            scores = jnp.where(allowed, scores, -1e30)
            top_old, total_old, accumulated = running
            top_new = jnp.maximum(top_old, jnp.max(scores, axis=-1))
            weights = jnp.where(allowed, jnp.exp(scores - top_new[..., None]), 0.0)
            factor = jnp.exp(top_old - top_new)
            accumulated = jnp.einsum(
                "hqk,khd->hqd",
                weights.astype(jnp.bfloat16),
                values_piece,
                preferred_element_type=jnp.float32,
            )
            return (top_new, jnp.sum(weights, axis=-1), accumulated)

        starting = (
            jnp.full((HEADS, tok_count), -1e30, jnp.float32),
            jnp.zeros((HEADS, tok_count), jnp.float32),
            jnp.zeros((HEADS, tok_count, HEAD_DIM), jnp.float32),
        )
        top_value, total_sum, accumulated = fold_step(
            starting,
            (
                lax.all_gather(keys_low, "ctx", axis=0, tiled=True),
                lax.all_gather(values_low, "ctx", axis=0, tiled=True),
            ),
            jnp.int32(0),
        )
        log_total = top_value + jnp.log(total_sum)
        attended = jnp.transpose(accumulated / total_sum[..., None], (1, 0, 2))
        mixed_low = attended.reshape(tok_count, width).astype(jnp.bfloat16)
        hidden_state = stream + jnp.dot(mixed_low, out_all, preferred_element_type=jnp.float32)
        base_two, inverse_two = rms_parts(hidden_state)
        expert_in = base_two * gain_float[1]
        expert_low = expert_in.astype(jnp.bfloat16)
        raw_logits = jnp.dot(expert_low, router_all, preferred_element_type=jnp.float32)
        logits = raw_logits[:, :NE] + previous
        route_ids = routes[layer_index, 0]
        chosen = route_ids[:, :, None] == expert_ids[None, None, :]
        chosen_f = chosen.astype(jnp.float32)
        hit_count = jnp.sum(chosen.astype(jnp.int32), axis=1)
        slot_index = jnp.cumsum(hit_count, axis=0) - 1
        picked = jnp.sum(chosen_f * logits[:, None, :], axis=-1)
        gate_weights = jax.nn.softmax(picked, axis=-1)
        coeffs = jnp.sum(gate_weights[:, :, None] * chosen_f, axis=1)
        slot_table = jnp.zeros((NF, MOST), jnp.int32)
        for expert in range(NF):
            target = jnp.where(hit_count[:, expert] > 0, slot_index[:, expert], MOST)
            slot_table = slot_table.at[expert, target].set(row_ids, mode="drop")
        filled = (slot_ids[None, :] < jnp.sum(hit_count[:, :NF], axis=0)[:, None]).astype(
            jnp.float32
        )
        rows_low = expert_low[slot_table]
        inputs_low = lax.all_gather(rows_low, "fsdp", axis=1, tiled=True)
        gate_up_out, hidden_low, partial_value = expert_forward(
            inputs_low, w_gate_up[layer_index], w_down[layer_index]
        )
        result = lax.psum_scatter(
            partial_value.astype(jnp.bfloat16), "fsdp", scatter_dimension=1, tiled=True
        ).astype(jnp.float32)
        flat_index = jnp.arange(NF, dtype=jnp.int32)[None, :] * MOST + jnp.clip(
            slot_index[:, :NF], 0, MOST - 1
        )
        token_result = result.reshape(NF * MOST, width)[flat_index]
        expert_mix = (
            jnp.sum(coeffs[:, :NF, None] * token_result, axis=1)
            + coeffs[:, NF + 1 : NF + 2] * expert_in
        )
        mixings = []
        for const_index in range(NC):
            column = NE + 2 * const_index
            mixing = jax.nn.softmax(raw_logits[:, column : column + 2], axis=-1)
            mixings.append(mixing)
            expert_mix = expert_mix + coeffs[:, NF + 2 + const_index : NF + 3 + const_index] * (
                mixing[:, 0:1] * expert_in
                + mixing[:, 1:2] * const_all[const_index].astype(jnp.float32)[None, :]
            )
        saved.append(
            (
                gain_float,
                qkv_all,
                out_all,
                router_all,
                const_all,
                base_one,
                inverse_one,
                normed_low,
                queries_low,
                keys_low,
                values_low,
                log_total,
                attended,
                mixed_low,
                base_two,
                inverse_two,
                expert_in,
                expert_low,
                chosen_f,
                hit_count,
                gate_weights,
                coeffs,
                slot_table,
                filled,
                inputs_low,
                gate_up_out,
                hidden_low,
                flat_index,
                token_result,
                mixings,
            )
        )
        stream = hidden_state + expert_mix
        previous = logits
    grad_stream = cotangent[0].astype(jnp.float32)
    grad_previous = jnp.zeros((tok_count, NE), jnp.float32)
    layer_grads = [None] * LAYERS
    for layer_index in reversed(range(LAYERS)):
        (
            gain_float,
            qkv_all,
            out_all,
            router_all,
            const_all,
            base_one,
            inverse_one,
            normed_low,
            queries_low,
            keys_low,
            values_low,
            log_total,
            attended,
            mixed_low,
            base_two,
            inverse_two,
            expert_in,
            expert_low,
            chosen_f,
            hit_count,
            gate_weights,
            coeffs,
            slot_table,
            filled,
            inputs_low,
            gate_up_out,
            hidden_low,
            flat_index,
            token_result,
            mixings,
        ) = saved[layer_index]
        grad_mix = grad_stream
        dot_input = jnp.sum(grad_mix * expert_in, axis=-1, keepdims=True)
        coef_grads = [
            jnp.sum(grad_mix[:, None, :] * token_result, axis=-1),
            jnp.zeros((tok_count, 1), jnp.float32),
            dot_input,
        ]
        grad_in = grad_mix * coeffs[:, NF + 1 : NF + 2]
        const_cols = []
        const_grads = []
        for const_index in range(NC):
            mixing = mixings[const_index]
            const_row = const_all[const_index].astype(jnp.float32)[None, :]
            dot_const = jnp.sum(grad_mix * const_row, axis=-1, keepdims=True)
            share = coeffs[:, NF + 2 + const_index : NF + 3 + const_index]
            coef_grads.append(mixing[:, 0:1] * dot_input + mixing[:, 1:2] * dot_const)
            grad_in = grad_in + grad_mix * (share * mixing[:, 0:1])
            grad_mixing = share * jnp.concatenate([dot_input, dot_const], axis=1)
            const_cols.append(
                mixing * (grad_mixing - jnp.sum(mixing * grad_mixing, axis=-1, keepdims=True))
            )
            const_grads.append(jnp.sum(grad_mix * (share * mixing[:, 1:2]), axis=0))
        grad_coeffs = jnp.concatenate(coef_grads, axis=1)
        grad_gates = jnp.sum(chosen_f * grad_coeffs[:, None, :], axis=-1)
        grad_picked = gate_weights * (
            grad_gates - jnp.sum(gate_weights * grad_gates, axis=-1, keepdims=True)
        )
        grad_logits = jnp.sum(grad_picked[:, :, None] * chosen_f, axis=1) + grad_previous
        grad_previous = grad_logits
        grad_raw_low = jnp.concatenate([grad_logits] + const_cols, axis=1).astype(jnp.bfloat16)
        grad_router = jnp.einsum(
            "td,tc->dc", expert_low, grad_raw_low, preferred_element_type=jnp.float32
        )
        grad_in = grad_in + jnp.einsum(
            "tc,dc->td", grad_raw_low, router_all, preferred_element_type=jnp.float32
        )
        slot_weight = (
            jnp.take_along_axis(jnp.transpose(coeffs[:, :NF]), slot_table, axis=1) * filled
        )
        grad_result_low = (grad_mix[slot_table] * slot_weight[:, :, None]).astype(jnp.bfloat16)
        grad_part_low = lax.all_gather(grad_result_low, "fsdp", axis=1, tiled=True)
        grad_gate_up, grad_down, grad_rows = expert_backward(
            inputs_low,
            gate_up_out,
            hidden_low,
            grad_part_low,
            w_gate_up[layer_index],
            w_down[layer_index],
        )
        grad_rows = lax.psum_scatter(
            grad_rows.astype(jnp.bfloat16), "fsdp", scatter_dimension=1, tiled=True
        ).astype(jnp.float32)
        token_grads = grad_rows.reshape(NF * MOST, width)[flat_index]
        grad_in = grad_in + jnp.sum(
            jnp.where(hit_count[:, :NF, None] > 0, token_grads, 0.0), axis=1
        )
        grad_gain_two = jnp.sum(grad_in * base_two, axis=0)
        grad_hidden_state = grad_stream + rms_back(grad_in * gain_float[1], base_two, inverse_two)
        grad_out_low = grad_hidden_state.astype(jnp.bfloat16)
        grad_out_w = jnp.einsum(
            "td,te->de", mixed_low, grad_out_low, preferred_element_type=jnp.float32
        )
        grad_attended = (
            jnp.einsum("te,de->td", grad_out_low, out_all, preferred_element_type=jnp.float32)
            .astype(jnp.bfloat16)
            .reshape(head_shape)
        )
        delta = jnp.transpose(jnp.sum(grad_attended.astype(jnp.float32) * attended, axis=-1))

        def visit(
            turn_index,
            carried,
            queries_use=queries_low,
            grad_use=grad_attended,
            log_use=log_total,
            delta_use=delta,
        ):
            keys_piece, values_piece, key_grads, value_grads, query_grads = carried
            source = (own_index - turn_index) % ctx_size
            allowed = allowed_pairs(source * tok_count, tok_count)[None]
            scores = (
                jnp.einsum(
                    "qhd,khd->hqk", queries_use, keys_piece, preferred_element_type=jnp.float32
                )
                * score_scale
            )
            probs = jnp.where(
                allowed, jnp.exp(jnp.where(allowed, scores, -1e30) - log_use[..., None]), 0.0
            )
            value_grads = value_grads + jnp.einsum(
                "hqk,qhd->khd",
                probs.astype(jnp.bfloat16),
                grad_use,
                preferred_element_type=jnp.float32,
            )
            prob_grads = jnp.einsum(
                "qhd,khd->hqk", grad_use, values_piece, preferred_element_type=jnp.float32
            )
            score_grads = (probs * (prob_grads - delta_use[..., None])).astype(jnp.bfloat16)
            query_grads = query_grads + jnp.einsum(
                "hqk,khd->qhd", score_grads, keys_piece, preferred_element_type=jnp.float32
            )
            key_grads = key_grads + jnp.einsum(
                "hqk,qhd->khd", score_grads, queries_use, preferred_element_type=jnp.float32
            )
            keys_piece, values_piece = from_behind((keys_piece, values_piece), "ctx", 1)
            key_grads, value_grads = (
                from_behind(key_grads.astype(jnp.bfloat16), "ctx", 1).astype(key_grads.dtype),
                from_behind(value_grads.astype(jnp.bfloat16), "ctx", 1).astype(value_grads.dtype),
            )
            return (keys_piece, values_piece, key_grads, value_grads, query_grads)

        zero_heads = jnp.zeros(head_shape, jnp.float32)
        finished = lax.fori_loop(
            0, ctx_size, visit, (keys_low, values_low, zero_heads, zero_heads, zero_heads)
        )
        grad_query = (
            rotate_pairs(finished[4] * score_scale, cosine_table, sine_table, -1.0)
            .astype(jnp.bfloat16)
            .reshape(tok_count, width)
        )
        grad_key = (
            rotate_pairs(finished[2] * score_scale, cosine_table, sine_table, -1.0)
            .astype(jnp.bfloat16)
            .reshape(tok_count, width)
        )
        grad_value = finished[3].astype(jnp.bfloat16).reshape(tok_count, width)
        grad_proj_low = jnp.stack([grad_query, grad_key, grad_value], axis=0)
        grad_qkv = jnp.einsum(
            "td,cte->cde", normed_low, grad_proj_low, preferred_element_type=jnp.float32
        )
        grad_normed = jnp.einsum(
            "cte,cde->td", grad_proj_low, qkv_all, preferred_element_type=jnp.float32
        )
        grad_gain_one = jnp.sum(grad_normed * base_one, axis=0)
        grad_stream = grad_hidden_state + rms_back(
            grad_normed * gain_float[0], base_one, inverse_one
        )
        gains_shard, qkv_shard, out_shard, router_shard, const_shard = (
            lax.psum_scatter(
                jnp.stack([grad_gain_one, grad_gain_two]).astype(jnp.bfloat16),
                "fsdp",
                scatter_dimension=1,
                tiled=True,
            ).astype(jnp.float32),
            lax.psum_scatter(
                grad_qkv.astype(jnp.bfloat16), "fsdp", scatter_dimension=1, tiled=True
            ).astype(jnp.float32),
            lax.psum_scatter(
                grad_out_w.astype(jnp.bfloat16), "fsdp", scatter_dimension=0, tiled=True
            ).astype(jnp.float32),
            lax.psum_scatter(
                grad_router.astype(jnp.bfloat16), "fsdp", scatter_dimension=0, tiled=True
            ).astype(jnp.float32),
            lax.psum_scatter(
                jnp.stack(const_grads).astype(jnp.bfloat16), "fsdp", scatter_dimension=1, tiled=True
            ).astype(jnp.float32),
        )
        layer_grads[layer_index] = (
            lax.psum(gains_shard.astype(jnp.bfloat16), "ctx").astype(jnp.float32),
            lax.psum(qkv_shard.astype(jnp.bfloat16), "ctx").astype(jnp.float32),
            lax.psum(out_shard.astype(jnp.bfloat16), "ctx").astype(jnp.float32),
            lax.psum(router_shard.astype(jnp.bfloat16), "ctx").astype(jnp.float32),
            lax.psum(const_shard.astype(jnp.bfloat16), "ctx").astype(jnp.float32),
            lax.psum(grad_gate_up.astype(jnp.bfloat16), "ctx").astype(jnp.float32),
            lax.psum(grad_down.astype(jnp.bfloat16), "ctx").astype(jnp.float32),
        )
    stacked = [
        jnp.stack([layer_grads[layer_index][member_index] for layer_index in range(LAYERS)])
        for member_index in range(7)
    ]
    return (
        stream[None],
        grad_stream[None],
        stacked[0],
        stacked[1],
        stacked[2],
        stacked[3],
        stacked[4],
        stacked[5],
        stacked[6],
    )


def solution(mesh):
    placed = (
        P("fsdp", "ctx", None),
        P("fsdp", "ctx", None),
        P("fsdp", None),
        P("fsdp", None),
        P(None, "fsdp", "ctx", None),
        P(None, None, "fsdp"),
        P(None, None, "fsdp", None),
        P(None, "fsdp", None),
        P(None, "fsdp", None),
        P(None, None, "fsdp"),
        P(None, None, None, None, "fsdp"),
        P(None, None, "fsdp", None),
    )
    return jax.shard_map(
        shards,
        mesh=mesh,
        in_specs=placed,
        out_specs=(
            P("fsdp", "ctx", None),
            P("fsdp", "ctx", None),
            P(None, None, "fsdp"),
            P(None, None, "fsdp", None),
            P(None, "fsdp", None),
            P(None, "fsdp", None),
            P(None, None, "fsdp"),
            P(None, None, None, None, "fsdp"),
            P(None, None, "fsdp", None),
        ),
        check_vma=False,
    )
```

profile of v0, /device:TPU:0, one launch (start us, length us, event | category | flops | bytes accessed | tf_op | source)
XLA Modules:
  0.0 3065.2 jit_solution(11071840059687893451)
XLA Ops:
  61.0 11.2 scatter_fusion
  72.2 11.2 scatter_fusion.1
  83.4 11.2 scatter_fusion.2
  94.6 11.2 scatter_fusion.3
  105.8 11.2 scatter_fusion.4
  117.1 11.2 scatter_fusion.5
  128.3 11.2 scatter_fusion.6
  139.5 11.2 scatter_fusion.7
  152.1 13.3 fusion.38
  165.3 12.0 fusion.40
  183.3 13.9 fusion.234
  204.9 28.6 all-gather.41.cloned.1.call-done
  268.8 8.9 all-gather.5
  293.4 9.5 gather_fusion.1
  308.4 16.7 all-gather.43.cloned.1.call-done
  334.4 11.4 scatter_fusion.8
  345.9 11.2 scatter_fusion.9
  357.1 11.2 scatter_fusion.10
  368.3 11.2 scatter_fusion.11
  379.5 11.2 scatter_fusion.12
  390.7 11.2 scatter_fusion.13
  401.9 11.2 scatter_fusion.14
  413.1 11.2 scatter_fusion.15
  424.4 13.2 fusion.39
  437.6 12.0 fusion.42
  458.3 13.9 fusion.235
  497.0 17.4 slice_bitcast_fusion.1
  514.4 13.2 fusion.84
  527.6 12.0 all-gather.33.cloned.1.call-done
  556.4 10.4 bitcast_convert_fusion.1
  595.5 9.4 gather_fusion.3
  615.2 19.4 reduce-scatter.35.cloned.1.call-done
  635.9 9.4 gather_fusion.5
  660.1 352.0 %while.48 = (s32[]{:T(128)}, bf16[256,12,64]{0,2,1:T(8,128)(2,1)}, bf16[256,12,64]{0,2,1:T(8,128)(2,1)}, f32[256,12,64]{0,2,1:T(8,128)S(1)}, f32[256,12,64]{0,2,...) while((s32[]{:T(128)}, bf16[256,12,64]{0,2,1:T(8,128)(2,1)}, ...), condition=%wide.region_65.67_spmd.clone, body=%wide.region_64.66_spmd.clone.sunk | while | flops 514916352 | bytes 40841888 | solution.py:433
  811.6 10.3 collective-permute-done.2
  855.6 10.7 collective-permute-done.2
  899.1 10.7 collective-permute-done.2
  941.6 10.7 collective-permute-done.2
  983.3 10.7 collective-permute-done.2
  1027.8 26.0 all-gather.35.cloned.1.call-done
  1053.8 10.7 fusion.104
  1064.5 11.0 bitcast_convert_fusion
  1101.1 12.6 reduce-scatter.37.cloned.1.call-done
  1114.9 9.4 gather_fusion.7
  1133.8 344.3 %while.49 = (s32[]{:T(128)}, bf16[256,12,64]{0,2,1:T(8,128)(2,1)S(1)}, bf16[256,12,64]{0,2,1:T(8,128)(2,1)}, f32[256,12,64]{0,2,1:T(8,128)S(1)}, f32[256,12,64]{...) while((s32[]{:T(128)}, ...), condition=%wide.region_82.84_spmd.clone, body=%wide.region_81.83_spmd.clone.sunk | while | flops 514916352 | bytes 42414780 | solution.py:433
  1282.1 10.0 collective-permute-done.6
  1325.0 10.7 collective-permute-done.6
  1367.6 10.7 collective-permute-done.6
  1409.3 10.7 collective-permute-done.6
  1449.9 10.7 collective-permute-done.6
  1511.0 11.9 convert_bitcast_fusion
  1528.1 11.4 convert_bitcast_fusion.1
  1564.3 28.3 reduce-scatter.39.cloned.1.call-done
  1592.7 22.2 reduce-scatter.45.cloned.1.call-done
  1615.7 21.3 reduce-scatter.57.cloned.1.call-done
  1637.9 21.3 reduce-scatter.55.cloned.1.call-done
  1660.1 21.2 reduce-scatter.53.cloned.1.call-done
  1682.1 21.3 reduce-scatter.51.cloned.1.call-done
  1705.5 20.1 reduce-scatter.43.cloned.1.call-done
  1726.4 38.3 %all-reduce.16 = (bf16[1,2,192]{2,1,0:T(2,128)(2,1)S(1)}, bf16[1,2,192]{2,1,0:T(2,128)(2,1)S(1)}, bf16[1,192,16]{1,2,0:T(8,128)(2,1)S(1)}, bf16[1,192,16]{1,2,0:...) all-reduce(bf16[1,2,192]{2,1,0:T(2,128)(2,1)S(1)} %bitcast.623, ...), channel_id=1, replica_groups=mesh['ctx'=8,'fsdp'=4] {'ctx'}, use_global_device_ids=true, to_apply=%region_91.93 | all-reduce | flops 7680 | bytes 30720 | tf_op jit(solution)/shard_map/psum | solution.py:479
  1766.5 1190.1 %all-reduce.20.cloned.1.call-done = (bf16[1,3,192,768]{2,3,1,0:T(8,128)(2,1)}, bf16[1,3,192,768]{2,3,1,0:T(8,128)(2,1)}, bf16[1,192,768]{2,1,0:T(8,128)(2,1)}, b...) async-done(((bf16[1,3,192,768]{2,3,1,0:T(8,128)(2,1)}, ...) | async-done | bytes 40108048 | tf_op jit(solution)/shard_map/psum | solution.py:480
  2966.6 27.1 maximum_convert_fusion
  2993.7 48.9 %copy.318 = f32[2,8,2,768,512]{4,3,2,1,0:T(8,128)} copy(f32[2,8,2,768,512]{3,4,2,1,0:T(8,128)} %maximum_convert_fusion) | data formatting | bytes 100663296
  3043.7 14.3 maximum_convert_fusion.1
  (1276 shorter events, 959.2 us)
Async XLA Ops:
  7.2 36.5 %all-gather.37.cloned.1.call-start = ((), (), s32[]{:S(2)}) async-start(), calls=%async_computation.26 | async-start | bytes 4423680 | tf_op jit(solution)/shard_map/all_gather | solution.py:145
  10.1 142.0 %all-gather.25.cloned.1.call-start = ((), (), s32[]{:S(2)}) async-start(), calls=%async_computation.14 | async-start | bytes 3538944 | tf_op jit(solution)/shard_map/all_gather | solution.py:194
  55.8 127.5 %all-gather.27.cloned.1.call-start = ((), (), s32[]{:S(2)}) async-start(), calls=%async_computation.15 | async-start | bytes 3538944 | tf_op jit(solution)/shard_map/all_gather | solution.py:195
  56.9 143.2 %all-gather.39.cloned.1.call-start = ((), (), s32[]{:S(2)}) async-start(), calls=%async_computation.27 | async-start | bytes 1474560 | tf_op jit(solution)/shard_map/all_gather | solution.py:146
  58.8 174.7 %all-gather.41.cloned.1.call-start = ((), (), s32[]{:S(2)}) async-start(), calls=%async_computation.28 | async-start | bytes 3932160 | tf_op jit(solution)/shard_map/all_gather | solution.py:224
  204.9 87.3 %reduce-scatter.31.cloned.1.call-start = ((), (), s32[]{:S(2)}) async-start(), calls=%async_computation.16 | async-start | bytes 3932160 | tf_op jit(solution)/shard_map/reduce_scatter | solution.py:228
  251.9 73.3 %all-gather.43.cloned.1.call-start = ((), (), s32[]{:S(2)}) async-start(), calls=%async_computation.29 | async-start | bytes 4423680 | tf_op jit(solution)/shard_map/all_gather | solution.py:145
  252.6 171.8 %all-gather.29.cloned.1.call-start = ((), (), s32[]{:S(2)}) async-start(), calls=%async_computation.17 | async-start | bytes 3538944 | tf_op jit(solution)/shard_map/all_gather | solution.py:194
  331.6 126.8 %all-gather.31.cloned.1.call-start = ((), (), s32[]{:S(2)}) async-start(), calls=%async_computation.18 | async-start | bytes 3538944 | tf_op jit(solution)/shard_map/all_gather | solution.py:195
  333.7 142.4 %all-gather.45.cloned.1.call-start = ((), (), s32[]{:S(2)}) async-start(), calls=%async_computation.30 | async-start | bytes 1474560 | tf_op jit(solution)/shard_map/all_gather | solution.py:146
  334.3 180.1 %all-gather.47.cloned.1.call-start = ((), (), s32[]{:S(2)}) async-start(), calls=%async_computation.31 | async-start | bytes 3932160 | tf_op jit(solution)/shard_map/all_gather | solution.py:224
  480.9 58.7 %all-gather.33.cloned.1.call-start = ((), (), s32[]{:S(2)}) async-start(), calls=%async_computation.20 | async-start | bytes 3932160 | tf_op jit(solution)/shard_map/all_gather | solution.py:360
  497.0 97.3 %reduce-scatter.33.cloned.1.call-start = ((), (), s32[]{:S(2)}) async-start(), calls=%async_computation.19 | async-start | bytes 3932160 | tf_op jit(solution)/shard_map/reduce_scatter | solution.py:228
  556.2 78.5 %reduce-scatter.35.cloned.1.call-start = ((), (), s32[]{:S(2)}) async-start(), calls=%async_computation.21 | async-start | bytes 3932160 | tf_op jit(solution)/shard_map/reduce_scatter | solution.py:369
  566.9 486.9 %all-gather.35.cloned.1.call-start = ((), (), s32[]{:S(2)}) async-start(), calls=%async_computation.22 | async-start | bytes 3932160 | tf_op jit(solution)/shard_map/all_gather | solution.py:360
  673.7 26.3 collective-permute-start
  675.2 32.1 %collective-permute-start.1 = (bf16[256,12,64]{0,2,1:T(8,128)(2,1)S(1)}, bf16[256,12,64]{0,2,1:T(8,128)(2,1)}, u32[]{:S(2)}, u32[]{:S(2)}) collective-permute-start(bf16[256,12,64]{0,2,1:T(8,128)(2,1)S(1)} %copy.397), channel_id=1, source_target_pairs={{0,4},{4,8},{8,12},{12,16},{16,20},{20,24},{24,28},{28,0},{1,5},{5... | collective-permute-start | bytes 1179656 | tf_op jit(solution)/shard_map/while/body/eval_jaxpr/ppermute | solution.py:17
  718.0 20.8 collective-permute-start.3
  719.0 28.1 collective-permute-start
  719.6 33.9 %collective-permute-start.1 = (bf16[256,12,64]{0,2,1:T(8,128)(2,1)S(1)}, bf16[256,12,64]{0,2,1:T(8,128)(2,1)}, u32[]{:S(2)}, u32[]{:S(2)}) collective-permute-start(bf16[256,12,64]{0,2,1:T(8,128)(2,1)S(1)} %copy.397), channel_id=1, source_target_pairs={{0,4},{4,8},{8,12},{12,16},{16,20},{20,24},{24,28},{28,0},{1,5},{5... | collective-permute-start | bytes 1179656 | tf_op jit(solution)/shard_map/while/body/eval_jaxpr/ppermute | solution.py:17
  764.2 20.8 collective-permute-start.3
  764.2 29.2 collective-permute-start
  764.2 34.6 %collective-permute-start.1 = (bf16[256,12,64]{0,2,1:T(8,128)(2,1)S(1)}, bf16[256,12,64]{0,2,1:T(8,128)(2,1)}, u32[]{:S(2)}, u32[]{:S(2)}) collective-permute-start(bf16[256,12,64]{0,2,1:T(8,128)(2,1)S(1)} %copy.397), channel_id=1, source_target_pairs={{0,4},{4,8},{8,12},{12,16},{16,20},{20,24},{24,28},{28,0},{1,5},{5... | collective-permute-start | bytes 1179656 | tf_op jit(solution)/shard_map/while/body/eval_jaxpr/ppermute | solution.py:17
  809.5 20.8 collective-permute-start.3
  809.5 29.2 collective-permute-start
  809.5 33.7 %collective-permute-start.1 = (bf16[256,12,64]{0,2,1:T(8,128)(2,1)S(1)}, bf16[256,12,64]{0,2,1:T(8,128)(2,1)}, u32[]{:S(2)}, u32[]{:S(2)}) collective-permute-start(bf16[256,12,64]{0,2,1:T(8,128)(2,1)S(1)} %copy.397), channel_id=1, source_target_pairs={{0,4},{4,8},{8,12},{12,16},{16,20},{20,24},{24,28},{28,0},{1,5},{5... | collective-permute-start | bytes 1179656 | tf_op jit(solution)/shard_map/while/body/eval_jaxpr/ppermute | solution.py:17
  854.0 28.6 collective-permute-start
  854.0 32.8 %collective-permute-start.1 = (bf16[256,12,64]{0,2,1:T(8,128)(2,1)S(1)}, bf16[256,12,64]{0,2,1:T(8,128)(2,1)}, u32[]{:S(2)}, u32[]{:S(2)}) collective-permute-start(bf16[256,12,64]{0,2,1:T(8,128)(2,1)S(1)} %copy.397), channel_id=1, source_target_pairs={{0,4},{4,8},{8,12},{12,16},{16,20},{20,24},{24,28},{28,0},{1,5},{5... | collective-permute-start | bytes 1179656 | tf_op jit(solution)/shard_map/while/body/eval_jaxpr/ppermute | solution.py:17
  897.5 20.8 collective-permute-start.3
  897.5 27.6 collective-permute-start
  897.5 31.9 %collective-permute-start.1 = (bf16[256,12,64]{0,2,1:T(8,128)(2,1)S(1)}, bf16[256,12,64]{0,2,1:T(8,128)(2,1)}, u32[]{:S(2)}, u32[]{:S(2)}) collective-permute-start(bf16[256,12,64]{0,2,1:T(8,128)(2,1)S(1)} %copy.397), channel_id=1, source_target_pairs={{0,4},{4,8},{8,12},{12,16},{16,20},{20,24},{24,28},{28,0},{1,5},{5... | collective-permute-start | bytes 1179656 | tf_op jit(solution)/shard_map/while/body/eval_jaxpr/ppermute | solution.py:17
  940.0 26.7 collective-permute-start
  940.0 30.9 %collective-permute-start.1 = (bf16[256,12,64]{0,2,1:T(8,128)(2,1)S(1)}, bf16[256,12,64]{0,2,1:T(8,128)(2,1)}, u32[]{:S(2)}, u32[]{:S(2)}) collective-permute-start(bf16[256,12,64]{0,2,1:T(8,128)(2,1)S(1)} %copy.397), channel_id=1, source_target_pairs={{0,4},{4,8},{8,12},{12,16},{16,20},{20,24},{24,28},{28,0},{1,5},{5... | collective-permute-start | bytes 1179656 | tf_op jit(solution)/shard_map/while/body/eval_jaxpr/ppermute | solution.py:17
  981.7 20.8 collective-permute-start.3
  981.7 25.8 collective-permute-start
  981.7 30.0 collective-permute-start.1
  1027.8 85.9 %reduce-scatter.37.cloned.1.call-start = ((), (), s32[]{:S(2)}) async-start(), calls=%async_computation.23 | async-start | bytes 3932160 | tf_op jit(solution)/shard_map/reduce_scatter | solution.py:369
  1075.6 475.7 %reduce-scatter.49.cloned.1.call-start = ((), (), s32[]{:S(2)}) async-start(), calls=%async_computation.35 | async-start | bytes 4423680
  1101.1 454.5 %reduce-scatter.47.cloned.1.call-start = ((), (), s32[]{:S(2)}) async-start(), calls=%async_computation.34 | async-start | bytes 4423680
  1146.6 26.1 collective-permute-start.4
  1148.1 32.1 %collective-permute-start.5 = (bf16[256,12,64]{0,2,1:T(8,128)(2,1)}, bf16[256,12,64]{0,2,1:T(8,128)(2,1)}, u32[]{:S(2)}, u32[]{:S(2)}) collective-permute-start(bf16[256,12,64]{0,2,1:T(8,128)(2,1)} %copy-done.24), channel_id=1, source_target_pairs={{0,4},{4,8},{8,12},{12,16},{16,20},{20,24},{24,28},{28,0},{1,5},{5... | collective-permute-start | bytes 1179656 | tf_op jit(solution)/shard_map/while/body/eval_jaxpr/ppermute | solution.py:17
  1191.1 27.8 collective-permute-start.4
  1191.7 33.8 %collective-permute-start.5 = (bf16[256,12,64]{0,2,1:T(8,128)(2,1)}, bf16[256,12,64]{0,2,1:T(8,128)(2,1)}, u32[]{:S(2)}, u32[]{:S(2)}) collective-permute-start(bf16[256,12,64]{0,2,1:T(8,128)(2,1)} %copy-done.24), channel_id=1, source_target_pairs={{0,4},{4,8},{8,12},{12,16},{16,20},{20,24},{24,28},{28,0},{1,5},{5... | collective-permute-start | bytes 1179656 | tf_op jit(solution)/shard_map/while/body/eval_jaxpr/ppermute | solution.py:17
  1235.3 29.1 collective-permute-start.4
  1235.3 34.7 %collective-permute-start.5 = (bf16[256,12,64]{0,2,1:T(8,128)(2,1)}, bf16[256,12,64]{0,2,1:T(8,128)(2,1)}, u32[]{:S(2)}, u32[]{:S(2)}) collective-permute-start(bf16[256,12,64]{0,2,1:T(8,128)(2,1)} %copy-done.24), channel_id=1, source_target_pairs={{0,4},{4,8},{8,12},{12,16},{16,20},{20,24},{24,28},{28,0},{1,5},{5... | collective-permute-start | bytes 1179656 | tf_op jit(solution)/shard_map/while/body/eval_jaxpr/ppermute | solution.py:17
  1279.8 29.1 collective-permute-start.4
  1279.8 33.8 %collective-permute-start.5 = (bf16[256,12,64]{0,2,1:T(8,128)(2,1)}, bf16[256,12,64]{0,2,1:T(8,128)(2,1)}, u32[]{:S(2)}, u32[]{:S(2)}) collective-permute-start(bf16[256,12,64]{0,2,1:T(8,128)(2,1)} %copy-done.24), channel_id=1, source_target_pairs={{0,4},{4,8},{8,12},{12,16},{16,20},{20,24},{24,28},{28,0},{1,5},{5... | collective-permute-start | bytes 1179656 | tf_op jit(solution)/shard_map/while/body/eval_jaxpr/ppermute | solution.py:17
  1323.4 28.6 collective-permute-start.4
  1323.4 32.9 %collective-permute-start.5 = (bf16[256,12,64]{0,2,1:T(8,128)(2,1)}, bf16[256,12,64]{0,2,1:T(8,128)(2,1)}, u32[]{:S(2)}, u32[]{:S(2)}) collective-permute-start(bf16[256,12,64]{0,2,1:T(8,128)(2,1)} %copy-done.24), channel_id=1, source_target_pairs={{0,4},{4,8},{8,12},{12,16},{16,20},{20,24},{24,28},{28,0},{1,5},{5... | collective-permute-start | bytes 1179656 | tf_op jit(solution)/shard_map/while/body/eval_jaxpr/ppermute | solution.py:17
  1366.0 27.5 collective-permute-start.4
  1366.0 31.9 %collective-permute-start.5 = (bf16[256,12,64]{0,2,1:T(8,128)(2,1)}, bf16[256,12,64]{0,2,1:T(8,128)(2,1)}, u32[]{:S(2)}, u32[]{:S(2)}) collective-permute-start(bf16[256,12,64]{0,2,1:T(8,128)(2,1)} %copy-done.24), channel_id=1, source_target_pairs={{0,4},{4,8},{8,12},{12,16},{16,20},{20,24},{24,28},{28,0},{1,5},{5... | collective-permute-start | bytes 1179656 | tf_op jit(solution)/shard_map/while/body/eval_jaxpr/ppermute | solution.py:17
  1407.7 26.5 collective-permute-start.4
  1407.7 30.8 %collective-permute-start.5 = (bf16[256,12,64]{0,2,1:T(8,128)(2,1)}, bf16[256,12,64]{0,2,1:T(8,128)(2,1)}, u32[]{:S(2)}, u32[]{:S(2)}) collective-permute-start(bf16[256,12,64]{0,2,1:T(8,128)(2,1)} %copy-done.24), channel_id=1, source_target_pairs={{0,4},{4,8},{8,12},{12,16},{16,20},{20,24},{24,28},{28,0},{1,5},{5... | collective-permute-start | bytes 1179656 | tf_op jit(solution)/shard_map/while/body/eval_jaxpr/ppermute | solution.py:17
  1448.3 25.5 collective-permute-start.4
  1448.3 29.8 collective-permute-start.5
  1498.6 65.7 %reduce-scatter.41.cloned.1.call-start = ((), (), s32[]{:S(2)}) async-start(), calls=%async_computation.25 | async-start | bytes 1474560 | tf_op jit(solution)/shard_map/reduce_scatter | solution.py:468
  1501.3 91.3 %reduce-scatter.39.cloned.1.call-start = ((), (), s32[]{:S(2)}) async-start(), calls=%async_computation.24 | async-start | bytes 1474560 | tf_op jit(solution)/shard_map/reduce_scatter | solution.py:468
  1503.0 111.9 %reduce-scatter.45.cloned.1.call-start = ((), (), s32[]{:S(2)}) async-start(), calls=%async_computation.33 | async-start | bytes 245760
  1523.9 113.2 %reduce-scatter.57.cloned.1.call-start = ((), (), s32[]{:S(2)}) async-start(), calls=%async_computation.39 | async-start | bytes 245760
  1524.8 134.4 %reduce-scatter.55.cloned.1.call-start = ((), (), s32[]{:S(2)}) async-start(), calls=%async_computation.38 | async-start | bytes 245760
  1525.8 155.5 %reduce-scatter.53.cloned.1.call-start = ((), (), s32[]{:S(2)}) async-start(), calls=%async_computation.37 | async-start | bytes 245760
  1526.9 176.5 %reduce-scatter.51.cloned.1.call-start = ((), (), s32[]{:S(2)}) async-start(), calls=%async_computation.36 | async-start | bytes 245760
  1528.1 197.5 %reduce-scatter.43.cloned.1.call-start = ((), (), s32[]{:S(2)}) async-start(), calls=%async_computation.32 | async-start | bytes 245760
  1543.7 1412.9 %all-reduce.20.cloned.1.call-start = ((), (), s32[]{:S(2)}) async-start(), calls=%async_computation.40 | async-start | bytes 81395712 | tf_op jit(solution)/shard_map/psum | solution.py:480
  (322 other events, 4413.7 us)
Sparse Core Ops, SparseCore 0:
  10.2 33.4 all-gather.36
  55.9 63.0 all-gather.24
  121.1 62.1 all-gather.26
  185.3 14.7 all-gather.38
  205.0 28.5 all-gather.40
  252.0 40.0 reduce-scatter.30
  294.3 30.7 all-gather.42
  331.7 64.0 all-gather.28
  398.0 60.3 all-gather.30
  460.4 15.6 all-gather.44
  481.0 28.5 all-gather.46
  511.1 28.5 all-gather.32
  556.3 37.9 reduce-scatter.32
  596.6 37.9 reduce-scatter.34
  1027.9 25.8 all-gather.34
  1075.7 37.9 reduce-scatter.36
  1116.7 40.4 reduce-scatter.48
  1498.7 37.1 reduce-scatter.46
  1538.5 25.7 reduce-scatter.40
  1566.9 25.7 reduce-scatter.38
  1595.1 19.7 reduce-scatter.44
  1617.3 19.7 reduce-scatter.56
  1639.5 19.7 reduce-scatter.54
  1661.5 19.7 reduce-scatter.52
  1683.7 19.7 reduce-scatter.50
  1705.8 19.7 reduce-scatter.42
  1732.3 1224.2 all-reduce.19
where the time goes:
time: 3080 us; the launch traced here: 3070 us
  waiting for transfers between devices  1940 us (63%)
  local copies, waits for them, and re-layouts  467 us (15%)
  matrix products  320 us (10%)
  other arithmetic  213 us (7%)
  blocking collectives  81 us (3%)
    psum x1, waiting for transfers between devices, shards(): lax.psum(qkv_shard.astype(jnp.bfloat16), 'ctx').astype(jnp.float32)  1190 us
    ppermute x64, waiting for transfers between devices, from_behind(): lax.ppermute(x, axis, [(i, (i + by) % devices) for i in range(devices)])  432 us
    scatter x16, local copies, waits for them, and re-layouts, shards(): slot_table = slot_table.at[expert, target].set(row_ids, mode='drop')  179 us
    unnamed x35, waiting for transfers between devices  129 us
    unnamed x446, local copies, waits for them, and re-layouts  112 us
  transfers between devices with their start and end apart: 91, of which 86 were waited for; matrix products, arithmetic and copies ran while one was open for 22% of the time, Pallas kernels for 0%

commit v1 on v0

--- a/solution.py
+++ b/solution.py
@@ -1,6 +1,9 @@
 import jax
 import jax.numpy as jnp
+import numpy as np
 from jax import lax
+from jax.experimental import pallas as pl
+from jax.experimental.pallas import tpu as pltpu
 from jax.sharding import PartitionSpec as P
 
 HEADS = 12
@@ -10,6 +13,7 @@
 LAYERS = 2
 NE = 12
 MOST = 64
+GROUP_HEADS = 3
 
 
 def from_behind(x, axis, by):
@@ -501,6 +505,744 @@
     )
 
 
+MINLEN = 1024
+ROUT = 56
+RAW, COEF, SLOT, LOGI = 0, 16, 32, 40
+VMEM_MB = 60
+
+
+def nt(a, b):
+    return lax.dot_general(a, b, (((1,), (1,)), ((), ())), preferred_element_type=jnp.float32)
+
+
+def nn(a, b):
+    return lax.dot_general(a, b, (((1,), (0,)), ((), ())), preferred_element_type=jnp.float32)
+
+
+def tn(a, b):
+    return lax.dot_general(a, b, (((0,), (0,)), ((), ())), preferred_element_type=jnp.float32)
+
+
+def params_of(mb=VMEM_MB, **more):
+    return pltpu.CompilerParams(vmem_limit_bytes=mb * 2**20, **more)
+
+
+def block_call(fn, outs, args, name):
+    def kernel(*refs):
+        results = fn(*[ref[...] for ref in refs[: len(args)]])
+        for ref, value in zip(refs[len(args) :], results):
+            ref[...] = value
+
+    return pl.pallas_call(
+        kernel,
+        out_shape=outs,
+        in_specs=[pl.BlockSpec(memory_space=pltpu.VMEM)] * len(args),
+        out_specs=[pl.BlockSpec(memory_space=pltpu.VMEM)] * len(outs),
+        compiler_params=params_of(),
+        name=name,
+    )(*args)
+
+
+def shape_of(dims, kind):
+    return jax.ShapeDtypeStruct(dims, kind)
+
+
+def rms_factor(values):
+    return lax.rsqrt(jnp.mean(values * values, axis=-1, keepdims=True) + 1e-06)
+
+
+def to_rows(columns, count):
+    lane = lax.broadcasted_iota(jnp.int32, (columns[0].shape[0], 128), 1)
+    packed = jnp.zeros(lane.shape, jnp.float32)
+    for index, column in enumerate(columns):
+        packed = jnp.where(lane == index, column, packed)
+    return jnp.transpose(packed)[:count]
+
+
+def to_columns(rows):
+    count = rows[0].shape[1]
+    sub = lax.broadcasted_iota(jnp.int32, (128, count), 0)
+    packed = jnp.zeros(sub.shape, jnp.float32)
+    for index, row in enumerate(rows):
+        packed = jnp.where(sub == index, row, packed)
+    packed = jnp.transpose(packed)
+    return [packed[:, index : index + 1] for index in range(len(rows))]
+
+
+def swap_halves(values):
+    lanes = values.shape[1]
+    lane = lax.broadcasted_iota(jnp.int32, values.shape, 1)
+    ahead = pltpu.roll(values, lanes - 32, 1)
+    behind = pltpu.roll(values, 32, 1)
+    return jnp.where(lane % 64 < 32, ahead, behind)
+
+
+def spin(values, cosine, sine):
+    return values * cosine + swap_halves(values) * sine
+
+
+def attn_fwd_kernel(inv, n1, w, cosine, sine, qkv, o, lse, ob, rows):
+    blocks, blk, _ = n1.shape
+    lanes = o.shape[1]
+    seq = blocks * blk
+    step = 2 * blk
+    for b in range(blocks):
+        rows[b * blk : (b + 1) * blk, :] = n1[inv[b]]
+    for i in range(seq // step):
+        part = slice(i * step, (i + 1) * step)
+        y = nn(rows[part, :], w[...])
+        cos2 = jnp.concatenate([cosine[part, :]] * (lanes // 128), axis=1)
+        sin2 = jnp.concatenate([sine[part, :]] * (lanes // 128), axis=1)
+        q = spin(y[:, :lanes], cos2, sin2).astype(jnp.bfloat16)
+        qkv[part, :lanes] = q * jnp.asarray(HEAD_DIM**-0.5, jnp.bfloat16)
+        qkv[part, lanes : 2 * lanes] = spin(y[:, lanes : 2 * lanes], cos2, sin2).astype(jnp.bfloat16)
+        qkv[part, 2 * lanes :] = y[:, 2 * lanes :].astype(jnp.bfloat16)
+    lane = lax.broadcasted_iota(jnp.int32, (step, 128), 1)
+    for i in range(seq // step):
+        part = slice(i * step, (i + 1) * step)
+        span = (i + 1) * step
+        seen = lax.broadcasted_iota(jnp.int32, (step, span), 1) <= (
+            lax.broadcasted_iota(jnp.int32, (step, span), 0) + i * step
+        )
+        logs = jnp.zeros((step, 128), jnp.float32)
+        for head in range(GROUP_HEADS):
+            tile, side = head // 2, head % 2
+            at = tile * 128
+            mine = lane // 64 == side
+            q = jnp.where(mine, qkv[part, at : at + 128], jnp.asarray(0, jnp.bfloat16))
+            s = nt(q, qkv[:span, lanes + at : lanes + at + 128])
+            s = jnp.where(seen, s, -1e30)
+            top = jnp.max(s, axis=1, keepdims=True)
+            p = jnp.exp(s - top)
+            total = jnp.sum(p, axis=1, keepdims=True)
+            out = nn(p.astype(jnp.bfloat16), qkv[:span, 2 * lanes + at : 2 * lanes + at + 128]) / total
+            logs = jnp.where(lane == head, top + jnp.log(total), logs)
+            if side == 0:
+                kept = jnp.where(mine, out, 0.0)
+            else:
+                kept = jnp.where(mine, out, kept)
+            o[part, at : at + 128] = kept
+        lse[part, :] = logs
+    for b in range(blocks):
+        ob[inv[b]] = o[b * blk : (b + 1) * blk, :].astype(jnp.bfloat16)
+
+
+def attn_forward(inv, n1, w, cosine, sine):
+    blocks, blk, width = n1.shape
+    lanes = w.shape[1] // 3
+    seq = blocks * blk
+    vm = pl.BlockSpec(memory_space=pltpu.VMEM)
+    return pl.pallas_call(
+        attn_fwd_kernel,
+        out_shape=[
+            shape_of((seq, 3 * lanes), jnp.bfloat16),
+            shape_of((seq, lanes), jnp.float32),
+            shape_of((seq, 128), jnp.float32),
+            shape_of((blocks, blk, lanes), jnp.bfloat16),
+        ],
+        in_specs=[pl.BlockSpec(memory_space=pltpu.SMEM)] + [vm] * 4,
+        out_specs=[vm] * 4,
+        scratch_shapes=[pltpu.VMEM((seq, width), jnp.bfloat16)],
+        compiler_params=params_of(),
+        name="attn_fwd",
+    )(inv, n1, w, cosine, sine)
+
+
+def attn_bwd_kernel(inv, n1, w, cosine, sine, qkv, o, lse, go, gn, gw, rows, gos, grads, acc):
+    blocks, blk, width = n1.shape
+    lanes = o.shape[1]
+    seq = blocks * blk
+    step = 2 * blk
+    zero = jnp.asarray(0, jnp.bfloat16)
+    for b in range(blocks):
+        rows[b * blk : (b + 1) * blk, :] = n1[inv[b]]
+        gos[b * blk : (b + 1) * blk, :] = go[inv[b]]
+    acc[...] = jnp.zeros_like(acc)
+    lane = lax.broadcasted_iota(jnp.int32, (step, 128), 1)
+    for i in range(seq // step):
+        part = slice(i * step, (i + 1) * step)
+        span = (i + 1) * step
+        seen = lax.broadcasted_iota(jnp.int32, (step, span), 1) <= (
+            lax.broadcasted_iota(jnp.int32, (step, span), 0) + i * step
+        )
+        key_lane = lax.broadcasted_iota(jnp.int32, (span, 128), 1)
+        for head in range(GROUP_HEADS):
+            tile, side = head // 2, head % 2
+            at = tile * 128
+            mine = lane // 64 == side
+            q = jnp.where(mine, qkv[part, at : at + 128], zero)
+            g = jnp.where(mine, gos[part, at : at + 128], zero)
+            k = qkv[:span, lanes + at : lanes + at + 128]
+            v = qkv[:span, 2 * lanes + at : 2 * lanes + at + 128]
+            delta = jnp.sum(g.astype(jnp.float32) * o[part, at : at + 128], axis=1, keepdims=True)
+            s = nt(q, k)
+            p = jnp.where(seen, jnp.exp(jnp.where(seen, s, -1e30) - lse[part, head : head + 1]), 0.0)
+            ds = (p * (nt(g, v) - delta)).astype(jnp.bfloat16)
+            acc[:span, 2 * lanes + at : 2 * lanes + at + 128] += tn(p.astype(jnp.bfloat16), g)
+            acc[:span, lanes + at : lanes + at + 128] += tn(ds, q)
+            acc[part, at : at + 128] += nn(ds, jnp.where(key_lane // 64 == side, k, zero))
+    for i in range(seq // step):
+        part = slice(i * step, (i + 1) * step)
+        cos2 = jnp.concatenate([cosine[part, :]] * (lanes // 128), axis=1)
+        sin2 = jnp.concatenate([sine[part, :]] * (lanes // 128), axis=1)
+        grads[part, :lanes] = spin(acc[part, :lanes] * HEAD_DIM**-0.5, cos2, -sin2).astype(jnp.bfloat16)
+        grads[part, lanes : 2 * lanes] = spin(acc[part, lanes : 2 * lanes], cos2, -sin2).astype(jnp.bfloat16)
+        grads[part, 2 * lanes :] = acc[part, 2 * lanes :].astype(jnp.bfloat16)
+    for b in range(blocks):
+        gn[inv[b]] = nt(grads[b * blk : (b + 1) * blk, :], w[...]).astype(jnp.bfloat16)
+    for i in range(width // 256):
+        gw[i * 256 : (i + 1) * 256, :] = tn(rows[:, i * 256 : (i + 1) * 256], grads[...]).astype(jnp.bfloat16)
+
+
+def attn_backward(inv, n1, w, cosine, sine, qkv, o, lse, go):
+    blocks, blk, width = n1.shape
+    lanes = w.shape[1] // 3
+    seq = blocks * blk
+    vm = pl.BlockSpec(memory_space=pltpu.VMEM)
+    return pl.pallas_call(
+        attn_bwd_kernel,
+        out_shape=[
+            shape_of((blocks, blk, width), jnp.bfloat16),
+            shape_of((width, 3 * lanes), jnp.bfloat16),
+        ],
+        in_specs=[pl.BlockSpec(memory_space=pltpu.SMEM)] + [vm] * 8,
+        out_specs=[vm] * 2,
+        scratch_shapes=[
+            pltpu.VMEM((seq, width), jnp.bfloat16),
+            pltpu.VMEM((seq, lanes), jnp.bfloat16),
+            pltpu.VMEM((seq, 3 * lanes), jnp.bfloat16),
+            pltpu.VMEM((seq, 3 * lanes), jnp.float32),
+        ],
+        compiler_params=params_of(),
+        name="attn_bwd",
+    )(inv, n1, w, cosine, sine, qkv, o, lse, go)
+
+
+def routing(raw, before, routes):
+    count = raw.shape[1]
+    ids = lax.broadcasted_iota(jnp.int32, (16, count), 0)
+    logits = raw + before
+    first, second = ids == routes[0:1], ids == routes[1:2]
+    z0 = jnp.sum(jnp.where(first, logits, 0.0), axis=0, keepdims=True)
+    z1 = jnp.sum(jnp.where(second, logits, 0.0), axis=0, keepdims=True)
+    top = jnp.maximum(z0, z1)
+    e0, e1 = jnp.exp(z0 - top), jnp.exp(z1 - top)
+    total = e0 + e1
+    coef = jnp.where(first, e0 / total, 0.0) + jnp.where(second, e1 / total, 0.0)
+    hits = jnp.where(first | second, 1.0, 0.0)
+    upto = lax.broadcasted_iota(jnp.int32, (count, count), 0) <= lax.broadcasted_iota(jnp.int32, (count, count), 1)
+    place = nn(hits.astype(jnp.bfloat16), jnp.where(upto, 1.0, 0.0).astype(jnp.bfloat16)) - 1.0
+    slot = jnp.where(hits > 0, place, -1.0)
+    return jnp.concatenate([raw, coef, slot[:NF], logits], axis=0)
+
+
+def one_hot(slot):
+    count = slot.shape[1]
+    ids = lax.broadcasted_iota(jnp.int32, (NF, MOST, count), 1)
+    hit = ids == slot.astype(jnp.int32)[:, None, :]
+    return jnp.where(hit, 1.0, 0.0).reshape(NF * MOST, count)
+
+
+def slot_values(hot, rows):
+    count = rows.shape[1]
+    wide = jnp.broadcast_to(rows[:, None, :], (NF, MOST, count)).reshape(NF * MOST, count)
+    return jnp.sum(hot * wide, axis=1, keepdims=True)
+
+
+def ffn_fwd_kernel(ub, routes, before, router, wgu, wd, part, table, hot_s, x_s, y_s, coef_s):
+    e = pl.program_id(0)
+    packs = ub.shape[0]
+
+    @pl.when(e == 0)
+    def _():
+        for d in range(packs):
+            rows = routing(nt(router[...], ub[d]), before[d], routes[d])
+            table[d] = rows
+            hot = one_hot(rows[SLOT : SLOT + NF])
+            coef_s[d] = slot_values(hot, rows[COEF : COEF + NF])
+            hot_low = hot.astype(jnp.bfloat16)
+            hot_s[d] = hot_low
+            x = nn(hot_low, ub[d]).astype(jnp.bfloat16)
+            for n in range(NF):
+                x_s[n, d * MOST : (d + 1) * MOST, :] = x[n * MOST : (n + 1) * MOST]
+
+    x = x_s[e]
+    gate, up = nn(x, wgu[0, 0, 0]), nn(x, wgu[0, 0, 1])
+    hid = (gate * jax.nn.sigmoid(gate) * up).astype(jnp.bfloat16)
+    out = nn(hid, wd[0, 0])
+    at = pl.ds(pl.multiple_of(e * MOST, MOST), MOST)
+    for d in range(packs):
+        y_s[d, at, :] = (out[d * MOST : (d + 1) * MOST] * coef_s[d, at, :]).astype(jnp.bfloat16)
+
+    @pl.when(e == NF - 1)
+    def _():
+        for d in range(packs):
+            part[d] = tn(hot_s[d], y_s[d]).astype(jnp.bfloat16)
+
+
+def whole_spec(dims):
+    return pl.BlockSpec(dims, lambda *_: (0,) * len(dims))
+
+
+def ffn_forward(layer, ub, routes, before, router, wgu, wd):
+    packs, count, width = ub.shape
+    hidden = wd.shape[2]
+    return pl.pallas_call(
+        ffn_fwd_kernel,
+        grid=(NF,),
+        out_shape=[
+            shape_of((packs, count, width), jnp.bfloat16),
+            shape_of((packs, ROUT, count), jnp.float32),
+        ],
+        in_specs=[
+            whole_spec(ub.shape),
+            whole_spec(routes.shape),
+            whole_spec(before.shape),
+            whole_spec(router.shape),
+            pl.BlockSpec((1, 1, 2, width, hidden), lambda e: (layer, e, 0, 0, 0)),
+            pl.BlockSpec((1, 1, hidden, width), lambda e: (layer, e, 0, 0)),
+        ],
+        out_specs=[whole_spec((packs, count, width)), whole_spec((packs, ROUT, count))],
+        scratch_shapes=[
+            pltpu.VMEM((packs, NF * MOST, count), jnp.bfloat16),
+            pltpu.VMEM((NF, packs * MOST, width), jnp.bfloat16),
+            pltpu.VMEM((packs, NF * MOST, width), jnp.bfloat16),
+            pltpu.VMEM((packs, NF * MOST, 1), jnp.float32),
+        ],
+        compiler_params=params_of(),
+        name="ffn_fwd",
+    )(ub, routes, before, router, wgu, wd)
+
+
+def silu_parts(gate, up, ghid):
+    sig = jax.nn.sigmoid(gate)
+    act = gate * sig
+    dg = (ghid * up * sig * (1.0 + gate * (1.0 - sig))).astype(jnp.bfloat16)
+    du = (ghid * act).astype(jnp.bfloat16)
+    return act * up, dg, du
+
+
+def ffn_bwd_kernel(ub, gm, table, wgu, wd, part, gcoef, hot_s, x_s, g_s, y_s, coef_s, gc_s):
+    e = pl.program_id(0)
+    packs = ub.shape[0]
+
+    @pl.when(e == 0)
+    def _():
+        for d in range(packs):
+            hot = one_hot(table[d, SLOT : SLOT + NF, :])
+            coef_s[d] = slot_values(hot, table[d, COEF : COEF + NF, :])
+            hot_low = hot.astype(jnp.bfloat16)
+            hot_s[d] = hot_low
+            x = nn(hot_low, ub[d]).astype(jnp.bfloat16)
+            g = nn(hot_low, gm[d]).astype(jnp.bfloat16)
+            for n in range(NF):
+                x_s[n, d * MOST : (d + 1) * MOST, :] = x[n * MOST : (n + 1) * MOST]
+                g_s[n, d * MOST : (d + 1) * MOST, :] = g[n * MOST : (n + 1) * MOST]
+
+    x = x_s[e]
+    at = pl.ds(pl.multiple_of(e * MOST, MOST), MOST)
+    coef = jnp.concatenate([coef_s[d, at, :] for d in range(packs)], axis=0)
+    gate, up = nn(x, wgu[0, 0, 0]), nn(x, wgu[0, 0, 1])
+    ghid = nt(g_s[e], wd[0, 0])
+    hid, dg, du = silu_parts(gate, up, ghid * coef)
+    dots = jnp.sum(hid * ghid, axis=1, keepdims=True)
+    out = nt(dg, wgu[0, 0, 0]) + nt(du, wgu[0, 0, 1])
+    for d in range(packs):
+        y_s[d, at, :] = out[d * MOST : (d + 1) * MOST].astype(jnp.bfloat16)
+        gc_s[d, at, :] = dots[d * MOST : (d + 1) * MOST]
+
+    @pl.when(e == NF - 1)
+    def _():
+        for d in range(packs):
+            part[d] = tn(hot_s[d], y_s[d]).astype(jnp.bfloat16)
+            spread = hot_s[d].astype(jnp.float32) * gc_s[d]
+            gcoef[d] = jnp.sum(spread.reshape(NF, MOST, spread.shape[1]), axis=1)
+
+
+def ffn_backward(layer, ub, gm, table, wgu, wd):
+    packs, count, width = ub.shape
+    hidden = wd.shape[2]
+    return pl.pallas_call(
+        ffn_bwd_kernel,
+        grid=(NF,),
+        out_shape=[
+            shape_of((packs, count, width), jnp.bfloat16),
+            shape_of((packs, NF, count), jnp.float32),
+        ],
+        in_specs=[
+            whole_spec(ub.shape),
+            whole_spec(gm.shape),
+            whole_spec(table.shape),
+            pl.BlockSpec((1, 1, 2, width, hidden), lambda e: (layer, e, 0, 0, 0)),
+            pl.BlockSpec((1, 1, hidden, width), lambda e: (layer, e, 0, 0)),
+        ],
+        out_specs=[whole_spec((packs, count, width)), whole_spec((packs, NF, count))],
+        scratch_shapes=[
+            pltpu.VMEM((packs, NF * MOST, count), jnp.bfloat16),
+            pltpu.VMEM((NF, packs * MOST, width), jnp.bfloat16),
+            pltpu.VMEM((NF, packs * MOST, width), jnp.bfloat16),
+            pltpu.VMEM((packs, NF * MOST, width), jnp.bfloat16),
+            pltpu.VMEM((packs, NF * MOST, 1), jnp.float32),
+            pltpu.VMEM((packs, NF * MOST, 1), jnp.float32),
+        ],
+        compiler_params=params_of(),
+        name="ffn_bwd",
+    )(ub, gm, table, wgu, wd)
+
+
+def dispatch_kernel(small, u, gm, x, g):
+    rows = small[0]
+    hot = one_hot(rows[NF : 2 * NF])
+    coef = slot_values(hot, rows[:NF])
+    hot = hot.astype(jnp.bfloat16)
+    x[...] = nn(hot, u[0]).astype(jnp.bfloat16).reshape(x.shape)
+    g[...] = (nn(hot, gm[0]) * coef).astype(jnp.bfloat16).reshape(g.shape)
+
+
+def dispatch(small, u, gm):
+    devices, count, width = u.shape
+    grouped = pl.BlockSpec((NF, 1, MOST, width), lambda d: (0, d, 0, 0))
+    outs = shape_of((NF, devices, MOST, width), jnp.bfloat16)
+    return pl.pallas_call(
+        dispatch_kernel,
+        grid=(devices,),
+        out_shape=[outs, outs],
+        in_specs=[
+            pl.BlockSpec((1, 2 * NF, count), lambda d: (d, 0, 0)),
+            pl.BlockSpec((1, count, width), lambda d: (d, 0, 0)),
+            pl.BlockSpec((1, count, width), lambda d: (d, 0, 0)),
+        ],
+        out_specs=[grouped, grouped],
+        compiler_params=params_of(),
+        name="dispatch",
+    )(small, u, gm)
+
+
+def dw_kernel(*refs):
+    x, g, wgu, wd, dgu, dd, dg_s, du_s, hid_s = refs[:4] + refs[-5:]
+    rows = x.shape[1]
+    chunk = 256
+
+    def pieces(i, _):
+        part = pl.ds(pl.multiple_of(i * chunk, chunk), chunk)
+        xs = x[0, part, :]
+        hid, dg, du = silu_parts(nn(xs, wgu[0, 0, 0]), nn(xs, wgu[0, 0, 1]), nt(g[0, part, :], wd[0, 0]))
+        hid_s[part, :] = hid.astype(jnp.bfloat16)
+        dg_s[part, :] = dg
+        du_s[part, :] = du
+        return 0
+
+    lax.fori_loop(0, rows // chunk, pieces, 0)
+
+    def first(i, _):
+        part = pl.ds(pl.multiple_of(i * 256, 256), 256)
+        xs = x[0, :, part]
+        dgu[0, 0, 0, part, :] = tn(xs, dg_s[...])
+        dgu[0, 0, 1, part, :] = tn(xs, du_s[...])
+        return 0
+
+    lax.fori_loop(0, x.shape[2] // 256, first, 0)
+
+    def second(i, _):
+        part = pl.ds(pl.multiple_of(i * 256, 256), 256)
+        dd[0, 0, part, :] = tn(hid_s[:, part], g[0])
+        return 0
+
+    lax.fori_loop(0, hid_s.shape[1] // 256, second, 0)
+
+
+def weight_grads(layer, x, g, wgu, wd, earlier):
+    _, rows, width = x.shape
+    hidden = wd.shape[2]
+    gu_spec = pl.BlockSpec((1, 1, 2, width, hidden), lambda e: (layer, e, 0, 0, 0))
+    d_spec = pl.BlockSpec((1, 1, hidden, width), lambda e: (layer, e, 0, 0))
+    row_spec = pl.BlockSpec((1, rows, width), lambda e: (e, 0, 0))
+    kernel = dw_kernel
+    return pl.pallas_call(
+        kernel,
+        grid=(NF,),
+        out_shape=[shape_of(wgu.shape, jnp.float32), shape_of(wd.shape, jnp.float32)],
+        in_specs=[row_spec, row_spec, gu_spec, d_spec] + [pl.BlockSpec(memory_space=pl.ANY)] * len(earlier),
+        out_specs=[gu_spec, d_spec],
+        input_output_aliases={4 + i: i for i in range(len(earlier))},
+        scratch_shapes=[pltpu.VMEM((rows, hidden), jnp.bfloat16)] * 3,
+        compiler_params=params_of(),
+        name="weight_grads",
+    )(x, g, wgu, wd, *earlier)
+
+
+def norm_low(x, gain):
+    return ((x * rms_factor(x)) * gain).astype(jnp.bfloat16)
+
+
+def post_attention(ob, x, wo, gain):
+    groups = wo.shape[0]
+    inner = wo.shape[1]
+    blk = ob.shape[1]
+    halves = []
+    for h in range(2):
+        total = x[h * blk : (h + 1) * blk]
+        for g in range(groups):
+            total = total + nn(ob[h * groups + g][:, :inner], wo[g])
+        halves.append(total)
+    hst = jnp.concatenate(halves, axis=0)
+    return hst, norm_low(hst, gain)
+
+
+def mixing_rows(table):
+    raw, coef = table[RAW : RAW + 16], table[COEF : COEF + 16]
+    pairs = []
+    for c in range(NC):
+        r0, r1 = raw[NE + 2 * c : NE + 2 * c + 1], raw[NE + 2 * c + 1 : NE + 2 * c + 2]
+        top = jnp.maximum(r0, r1)
+        e0, e1 = jnp.exp(r0 - top), jnp.exp(r1 - top)
+        pairs.append((e0 / (e0 + e1), e1 / (e0 + e1)))
+    shares = [coef[NF + 2 + c : NF + 3 + c] for c in range(NC)]
+    scale_u = coef[NF + 1 : NF + 2]
+    for c in range(NC):
+        scale_u = scale_u + shares[c] * pairs[c][0]
+    return pairs, shares, scale_u, [shares[c] * pairs[c][1] for c in range(NC)]
+
+
+def combine(hst, parts, table, gain, consts, next_gain):
+    _, _, scale_u, scale_c = mixing_rows(table)
+    columns = to_columns([scale_u] + scale_c)
+    u = (hst * rms_factor(hst)) * gain
+    moe = columns[0] * u
+    for f in range(parts.shape[0]):
+        moe = moe + parts[f].astype(jnp.float32)
+    for c in range(NC):
+        moe = moe + columns[1 + c] * consts[c : c + 1].astype(jnp.float32)
+    x = hst + moe
+    return x, norm_low(x, next_gain)
+
+
+def middle(gx, parts, gcoef, table, routes, gprev, hst, ub, gain, consts, router, wo, ob):
+    groups = wo.shape[0]
+    inner = wo.shape[1]
+    blk = ob.shape[1]
+    consts = consts.astype(jnp.float32)
+    pairs, shares, scale_u, scale_c = mixing_rows(table)
+    columns = to_columns([scale_u] + scale_c)
+    factor = rms_factor(hst)
+    base = hst * factor
+    u = base * gain
+    dots = [jnp.sum(gx * u, axis=1, keepdims=True)]
+    dots += [jnp.sum(gx * consts[c : c + 1], axis=1, keepdims=True) for c in range(NC)]
+    dots = to_rows(dots, 8)
+    dot_u = dots[0:1]
+    dot_c = [dots[1 + c : 2 + c] for c in range(NC)]
+    ids = lax.broadcasted_iota(jnp.int32, (16, gx.shape[0]), 0)
+    grads = jnp.concatenate([gcoef, jnp.zeros_like(gcoef)], axis=0)
+    grads = jnp.where(ids == NF + 1, dot_u, grads)
+    raw_rows = []
+    for c in range(NC):
+        a0, a1 = pairs[c]
+        grads = jnp.where(ids == NF + 2 + c, a0 * dot_u + a1 * dot_c[c], grads)
+        g0, g1 = shares[c] * dot_u, shares[c] * dot_c[c]
+        both = a0 * g0 + a1 * g1
+        raw_rows += [a0 * (g0 - both), a1 * (g1 - both)]
+    logits = table[LOGI : LOGI + 16]
+    first, second = ids == routes[0:1], ids == routes[1:2]
+
+    def pick(chosen, rows):
+        return jnp.sum(jnp.where(chosen, rows, 0.0), axis=0, keepdims=True)
+
+    z0, z1 = pick(first, logits), pick(second, logits)
+    top = jnp.maximum(z0, z1)
+    e0, e1 = jnp.exp(z0 - top), jnp.exp(z1 - top)
+    w0, w1 = e0 / (e0 + e1), e1 / (e0 + e1)
+    gg0, gg1 = pick(first, grads), pick(second, grads)
+    both = w0 * gg0 + w1 * gg1
+    glog = jnp.where(first, w0 * (gg0 - both), 0.0) + jnp.where(second, w1 * (gg1 - both), 0.0) + gprev
+    graw = glog
+    for index, row in enumerate(raw_rows):
+        graw = jnp.where(ids == NE + index, row, graw)
+    graw = graw.astype(jnp.bfloat16)
+    grad_router = nn(graw, ub)
+    gu = gx * columns[0] + tn(graw, router)
+    for f in range(parts.shape[0]):
+        gu = gu + parts[f].astype(jnp.float32)
+    small = [jnp.sum(gu * base, axis=0, keepdims=True)]
+    small += [jnp.sum(gx * columns[1 + c], axis=0, keepdims=True) for c in range(NC)]
+    gb = gu * gain
+    ghst = gx + factor * (gb - base * jnp.mean(gb * base, axis=-1, keepdims=True))
+    gy = ghst.astype(jnp.bfloat16)
+    lanes = ob.shape[2]
+    go, gwo = [None] * (2 * groups), []
+    for g in range(groups):
+        value = nt(gy, wo[g]).astype(jnp.bfloat16)
+        value = jnp.concatenate([value, jnp.zeros((value.shape[0], lanes - inner), jnp.bfloat16)], axis=1)
+        for h in range(2):
+            go[h * groups + g] = value[h * blk : (h + 1) * blk]
+        mixed = jnp.concatenate([ob[g], ob[groups + g]], axis=0)
+        gwo.append(tn(mixed, gy)[:inner].astype(jnp.bfloat16))
+    return ghst, jnp.stack(go), jnp.concatenate(gwo, axis=0), jnp.concatenate(small + [grad_router], axis=0), glog
+
+
+def finish(parts, ghst, x, gain):
+    groups = parts.shape[0] // 2
+    halves = []
+    for h in range(2):
+        total = parts[h * groups].astype(jnp.float32)
+        for g in range(1, groups):
+            total = total + parts[h * groups + g].astype(jnp.float32)
+        halves.append(total)
+    gn = jnp.concatenate(halves, axis=0)
+    factor = rms_factor(x)
+    base = x * factor
+    gb = gn * gain
+    gx = ghst + factor * (gb - base * jnp.mean(gb * base, axis=-1, keepdims=True))
+    return gx, gx.astype(jnp.bfloat16), jnp.sum(gn * base, axis=0, keepdims=True)
+
+
+def turn_tables(seq):
+    half = HEAD_DIM // 2
+    frequency = np.exp((-np.log(np.float32(10000.0)) * np.arange(half, dtype=np.float32) / np.float32(half)))
+    angles = np.arange(seq, dtype=np.float32)[:, None] * frequency.astype(np.float32)[None, :]
+    cosine, sine = np.cos(angles), np.sin(angles)
+    cosine = np.concatenate([cosine, cosine] * 2, axis=1).astype(np.float32)
+    sine = np.concatenate([-sine, sine] * 2, axis=1).astype(np.float32)
+    return jnp.asarray(cosine), jnp.asarray(sine)
+
+
+def by_heads(
+    tokens,
+    cotangent,
+    seq_lengths,
+    block_order,
+    routes,
+    gains,
+    qkv_weights,
+    out_weight,
+    router,
+    const_values,
+    w_gate_up,
+    w_down,
+):
+    count, width = tokens.shape[1], tokens.shape[2]
+    ctx_size, packs = lax.axis_size("ctx"), lax.axis_size("fsdp")
+    groups = ctx_size // 2
+    blk = count // 2
+    seq = blk * ctx_size
+    own, pack = lax.axis_index("ctx"), lax.axis_index("fsdp")
+    sequence, group = own // groups, own % groups
+    inner = GROUP_HEADS * HEAD_DIM
+    lanes = -(-inner // 128) * 128
+    shard = width // packs
+    f32, bf = jnp.float32, jnp.bfloat16
+
+    cosine, sine = turn_tables(seq)
+    order = lax.dynamic_index_in_dim(block_order[0].reshape(ctx_size, 2), sequence, 1, keepdims=False) - ctx_size * sequence
+    ids = jnp.arange(ctx_size, dtype=jnp.int32)
+    inv = jnp.sum(jnp.where(order[None, :] == ids[:, None], ids[None, :], 0), axis=1)
+
+    smalls = jnp.concatenate([gains, const_values, jnp.swapaxes(router, 1, 2)], axis=1)
+    smalls = lax.all_gather(smalls, "fsdp", axis=2, tiled=True)
+    qkv_cols = lax.dynamic_slice_in_dim(qkv_weights, group * inner, inner, axis=3)
+    qkv_cols = jnp.pad(qkv_cols, ((0, 0), (0, 0), (0, 0), (0, lanes - inner)))
+    qkv_cols = jnp.swapaxes(qkv_cols, 1, 2).reshape(LAYERS, shard, 3 * lanes)
+    w_attn = [lax.all_gather(qkv_cols[l], "fsdp", axis=0, tiled=True) for l in range(LAYERS)]
+    w_out = [lax.all_gather(out_weight[l], "fsdp", axis=0, tiled=False) for l in range(LAYERS)]
+    routes_t = jnp.swapaxes(routes[:, 0], 1, 2)
+    routes_f = lax.all_gather(routes_t, "fsdp", axis=1, tiled=False)
+
+    def gain_of(l, which):
+        return smalls[l, which : which + 1].astype(f32)
+
+    x = tokens[0].astype(f32)
+    gm_low = cotangent[0]
+    gm_all = [None, lax.all_gather(gm_low, ("ctx", "fsdp"), axis=0, tiled=False)]
+    before = jnp.zeros((packs, 16, count), f32)
+    (n1,) = block_call(lambda a, b: (norm_low(a, b),), [shape_of((count, width), bf)], (x, gain_of(0, 0)), "norm")
+    kept = []
+    for l in range(LAYERS):
+        consts, router_t = smalls[l, 2 : 2 + NC], smalls[l, 2 + NC :]
+        send = jnp.broadcast_to(n1.reshape(2, 1, blk, width), (2, groups, blk, width)).reshape(ctx_size, blk, width)
+        n1_all = lax.all_to_all(send, "ctx", 0, 0)
+        qkv, o, lse, ob = attn_forward(inv, n1_all, w_attn[l], cosine, sine)
+        ob = lax.all_to_all(ob, "ctx", 0, 0)
+        hst, ub = block_call(
+            post_attention,
+            [shape_of((count, width), f32), shape_of((count, width), bf)],
+            (ob, x, w_out[l], gain_of(l, 1)),
+            "post_attention",
+        )
+        ub_f = lax.all_gather(ub, "fsdp", axis=0, tiled=False)
+        ub_all = lax.all_gather(ub, ("ctx", "fsdp"), axis=0, tiled=False)
+        parts, table_f = ffn_forward(l, ub_f, routes_f[l], before, router_t, w_gate_up, w_down)
+        before = table_f[:, LOGI : LOGI + 16]
+        table = lax.dynamic_index_in_dim(table_f, pack, 0, keepdims=False)
+        small_all = lax.all_gather(
+            jnp.concatenate([table[COEF : COEF + NF], table[SLOT : SLOT + NF]], axis=0), ("ctx", "fsdp"), axis=0, tiled=False
+        )
+        parts = lax.all_to_all(parts, "fsdp", 0, 0)
+        x_next, n1 = block_call(
+            combine,
+            [shape_of((count, width), f32), shape_of((count, width), bf)],
+            (hst, parts, table, gain_of(l, 1), consts, gain_of(min(l + 1, LAYERS - 1), 0)),
+            "combine",
+        )
+        kept.append((x, n1_all, qkv, o, lse, ob, hst, ub, ub_f, ub_all, table_f, table, small_all, consts, router_t))
+        x = x_next
+    output = x
+    gx = cotangent[0].astype(f32)
+    gprev = jnp.zeros((16, count), f32)
+    small_grads, qkv_grads, out_grads = [None] * LAYERS, [None] * LAYERS, [None] * LAYERS
+    done = ()
+    for l in reversed(range(LAYERS)):
+        x, n1_all, qkv, o, lse, ob, hst, ub, ub_f, ub_all, table_f, table, small_all, consts, router_t = kept[l]
+        gm_f = lax.all_gather(gm_low, "fsdp", axis=0, tiled=False)
+        if gm_all[l] is None:
+            gm_all[l] = lax.all_gather(gm_low, ("ctx", "fsdp"), axis=0, tiled=False)
+        parts, gcoef = ffn_backward(l, ub_f, gm_f, table_f, w_gate_up, w_down)
+        parts = lax.all_to_all(parts, "fsdp", 0, 0)
+        gcoef = jnp.sum(lax.all_to_all(gcoef, "fsdp", 0, 0), axis=0)
+        ghst, go, gwo, small, gprev = block_call(
+            middle,
+            [
+                shape_of((count, width), f32),
+                shape_of((ctx_size, blk, lanes), bf),
+                shape_of((width, width), bf),
+                shape_of((1 + NC + 16, width), f32),
+                shape_of((16, count), f32),
+            ],
+            (gx, parts, gcoef, table, routes_t[l], gprev, hst, ub, gain_of(l, 1), consts, router_t, w_out[l], ob),
+            "middle",
+        )
+        out_grads[l] = lax.psum(lax.psum_scatter(gwo, "fsdp", scatter_dimension=0, tiled=True), "ctx")
+        go = lax.all_to_all(go, "ctx", 0, 0)
+        gn, gw = attn_backward(inv, n1_all, w_attn[l], cosine, sine, qkv, o, lse, go)
+        gw = lax.psum_scatter(gw, "fsdp", scatter_dimension=0, tiled=True)
+        gw = lax.all_gather(gw, "ctx", axis=0, tiled=False).reshape(2, groups, shard, 3, lanes)[..., :inner]
+        gw = jnp.sum(gw.astype(f32), axis=0)
+        qkv_grads[l] = jnp.transpose(gw, (2, 1, 0, 3)).reshape(3, shard, width)
+        gn = lax.all_to_all(gn, "ctx", 0, 0)
+        gx, gm_low, gain_grad = block_call(
+            finish,
+            [shape_of((count, width), f32), shape_of((count, width), bf), shape_of((1, width), f32)],
+            (gn, ghst, x, gain_of(l, 0)),
+            "finish",
+        )
+        small_grads[l] = jnp.concatenate([gain_grad, small], axis=0)
+        x_all, g_all = dispatch(small_all, ub_all, gm_all[l])
+        rows = x_all.shape[1] * x_all.shape[2]
+        done = weight_grads(l, x_all.reshape(NF, rows, width), g_all.reshape(NF, rows, width), w_gate_up, w_down, done)
+    small = lax.psum(jnp.stack(small_grads).astype(bf), ("ctx", "fsdp"))
+    small = lax.dynamic_slice_in_dim(small, pack * shard, shard, axis=2).astype(f32)
+    return (
+        output[None],
+        gx[None],
+        small[:, :2],
+        jnp.stack(qkv_grads),
+        jnp.stack(out_grads).astype(f32),
+        jnp.swapaxes(small[:, 2 + NC :], 1, 2),
+        small[:, 2 : 2 + NC],
+        done[0],
+        done[1],
+    )
+
+
 def solution(mesh):
     placed = (
         P("fsdp", "ctx", None),
@@ -516,8 +1258,17 @@
         P(None, None, None, None, "fsdp"),
         P(None, None, "fsdp", None),
     )
+    contexts, packs = mesh.shape["ctx"], mesh.shape["fsdp"]
+    blocks_of_heads = HEADS // GROUP_HEADS
+
+    def plan(*args):
+        tokens = args[0]
+        even = tokens.shape[1] * contexts == 2 * MINLEN
+        grouped = contexts == 2 * blocks_of_heads and packs == blocks_of_heads
+        return (by_heads if even and grouped else shards)(*args)
+
     return jax.shard_map(
-        shards,
+        plan,
         mesh=mesh,
         in_specs=placed,
         out_specs=(

time: 3080 us -> 1330 us (0.43)
  waiting for transfers between devices: 1940 us -> 439 us
  Pallas kernels: 0 us -> 451 us
  local copies, waits for them, and re-layouts: 467 us -> 52.9 us
  matrix products: 320 us -> 0 us
  blocking collectives: 81 us -> 294 us
  other arithmetic: 213 us -> 25.8 us
    psum x1, waiting for transfers between devices: 1190 us -> 0.01 us  [by_heads(): lax.psum(lax.psum_scatter(gwo, 'fsdp', scatter_dimension=0, tiled=True),...]
    pallas_call x0 -> x21, Pallas kernels: none -> 451 us  [the longest x2 217 us: weight_grads(): pl.pallas_call(kernel, grid=(NF,), out_shape=[shape_of(wgu.shape, jnp.flo...]
    ppermute x64 -> x0, waiting for transfers between devices: 432 us -> none  [from_behind(): lax.ppermute(x, axis, [(i, (i + by) % devices) for i in range(devices)])]
    dot_general x114 -> x0, matrix products: 320 us -> none  [the longest x16 43.7 us: visit(): jnp.einsum('hqk,qhd->khd', probs.astype(jnp.bfloat16), grad_use, preferre...]
    all_gather x12 -> x14, waiting for transfers between devices: 110 us -> 299 us  [the longest x2 97.4 us: by_heads(): ub_all = lax.all_gather(ub, ('ctx', 'fsdp'), axis=0, tiled=False)]
    scatter x16 -> x0, local copies, waits for them, and re-layouts: 179 us -> none  [shards(): slot_table = slot_table.at[expert, target].set(row_ids, mode='drop')]
    unnamed x35 -> x19, waiting for transfers between devices: 129 us -> 5.43 us
    all_to_all x0 -> x6, blocking collectives: none -> 118 us  [the longest x1 40.4 us: by_heads(): gn = lax.all_to_all(gn, 'ctx', 0, 0)]
  transfers between devices with their start and end apart: 91 -> 27, of which waited for: 86 -> 17; matrix products, arithmetic and copies ran while one was open for 22% -> 4% of each run, Pallas kernels for 0% -> 18%
where the time goes in v1:
time: 1330 us; the launch traced here: 1310 us
  Pallas kernels  451 us (34%)
  waiting for transfers between devices  439 us (33%)
  blocking collectives  294 us (22%)
  local copies, waits for them, and re-layouts  52.9 us (4%)
  starting transfers between devices  37.3 us (3%)
  other arithmetic  25.8 us (2%)
  between operations  14.8 us (1%)
    pallas_call x2, Pallas kernels, weight_grads(): pl.pallas_call(kernel, grid=(NF,), out_shape=[shape_of(wgu.shape, jnp.flo...  217 us
    all_gather x2, blocking collectives, by_heads(): lax.all_gather(jnp.concatenate([table[COEF:COEF + NF], table[SLOT:SLOT +...  124 us
    all_gather x2, waiting for transfers between devices, by_heads(): ub_all = lax.all_gather(ub, ('ctx', 'fsdp'), axis=0, tiled=False)  97.4 us
    pallas_call x2, Pallas kernels, dispatch(): pl.pallas_call(dispatch_kernel, grid=(devices,), out_shape=[outs, outs],...  79.2 us
    all_gather x1, waiting for transfers between devices, by_heads(): lax.all_gather(gm_low, ('ctx', 'fsdp'), axis=0, tiled=False)  73 us
    all_to_all x3, waiting for transfers between devices, by_heads(): parts = lax.all_to_all(parts, 'fsdp', 0, 0)  51.5 us
    all_gather x1, waiting for transfers between devices, by_heads(): gm_all[l] = lax.all_gather(gm_low, ('ctx', 'fsdp'), axis=0, tiled=False)  46.9 us
    all_to_all x1, blocking collectives, by_heads(): gn = lax.all_to_all(gn, 'ctx', 0, 0)  40.4 us
  transfers between devices with their start and end apart: 27, of which 17 were waited for; matrix products, arithmetic and copies ran while one was open for 4% of the time, Pallas kernels for 18%

profile of v1, /device:TPU:0, one launch (start us, length us, event | category | flops | bytes accessed | tf_op | source)
XLA Modules:
  0.0 1314.8 jit_solution(2842439021599160344)
XLA Ops:
  10.3 7.9 all_gather.81
  18.3 9.0 fusion
  33.1 5.8 all-to-all-start
  44.4 16.0 %all-gather.26.cloned.1.call-done.w = bf16[768,768]{1,0:T(8,128)(2,1)} async-done(((bf16[192,768]{1,0:T(8,128)(2,1)}), bf16[768,768]{1,0:T(8,128)(2,1)}) %all-gather.26.cloned.1.call-update) | async-done | bytes 1179664 | tf_op jit(solution)/shard_map/all_gather | solution.py:1145
  60.5 16.1 %all-to-all-done.n1 = bf16[8,128,768]{2,1,0:T(8,128)(2,1)} async-done(((bf16[8,128,768]{2,1,0:T(8,128)(2,1)}), bf16[8,128,768]{2,1,0:T(8,128)(2,1)}, u32[]{:S(2)}, u32[]{:S(2)}) %all-to-all-start) | async-done | bytes 1572896 | tf_op jit(solution)/shard_map/all_to_all | solution.py:1162
  76.6 9.2 attn_fwd.2
  85.8 3.8 all-to-all-start.1
  90.2 14.1 %all-to-all-done.1.refs_0_.refs_12_ = bf16[8,128,256]{2,1,0:T(8,128)(2,1)S(1)} async-done(((bf16[8,128,256]{2,1,0:T(8,128)(2,1)}), bf16[8,128,256]{2,1,0:T(8,128)(2,1)S(1)}, u32[]{:S(2)}, u32[]{:S(2)}) %all-to-all-start.1) | async-done | bytes 524320 | tf_op jit(solution)/shard_map/all_to_all | solution.py:1164
  105.0 3.3 post_attention.2
  108.4 5.2 all-gather.1
  116.0 10.9 all-gather.38.cloned.1.call-done
  127.5 16.2 %ffn_fwd.2 = (bf16[4,256,768]{2,1,0:T(8,128)(2,1)}, f32[4,56,256]{2,1,0:T(8,128)}) custom-call(bf16[4,256,768]{2,1,0:T(8,128)(2,1)} %bitcast.75, s32[4,2,256]{2,1,0:T(2,128)} %squeeze.57.routes, f32[4,16,256]{2,1,0:T(8,128)} %broadcast_in_dim.45.before, bf16[16,768]{1,0:T(8,128)(2,1)} %bitcast.92, bf16[2,8,2,768,512]{4,3,2,1,0:T(8,128)(2,1)} %refs_2_.3, ...), custom_call_target="tpu_custom_call" | custom-call | tf_op jit(solution)/shard_map/ffn_fwd/pallas_call | solution.py:790
  143.7 4.0 all-to-all-start.2
  151.6 16.1 %all-to-all-done.2.refs_1_ = bf16[4,256,768]{2,1,0:T(8,128)(2,1)S(1)} async-done(((bf16[4,256,768]{2,1,0:T(8,128)(2,1)}), bf16[4,256,768]{2,1,0:T(8,128)(2,1)S(1)}, u32[]{:S(2)}, u32[]{:S(2)}) %all-to-all-start.2) | async-done | bytes 1572896 | tf_op jit(solution)/shard_map/all_to_all | solution.py:1179
  168.8 3.3 combine.2
  174.4 5.7 all-to-all-start.3
  181.8 18.9 %all-gather.30.cloned.1.call-done.w = bf16[768,768]{1,0:T(8,128)(2,1)} async-done(((bf16[192,768]{1,0:T(8,128)(2,1)}), bf16[768,768]{1,0:T(8,128)(2,1)}) %all-gather.30.cloned.1.call-update) | async-done | bytes 1179664 | tf_op jit(solution)/shard_map/all_gather | solution.py:1145
  200.7 16.2 %all-to-all-done.3.n1 = bf16[8,128,768]{2,1,0:T(8,128)(2,1)S(1)} async-done(((bf16[8,128,768]{2,1,0:T(8,128)(2,1)}), bf16[8,128,768]{2,1,0:T(8,128)(2,1)S(1)}, u32[]{:S(2)}, u32[]{:S(2)}) %all-to-all-start.3) | async-done | bytes 1572896 | tf_op jit(solution)/shard_map/all_to_all | solution.py:1162
  218.0 9.2 attn_fwd.3
  227.2 3.6 all-to-all-start.4
  231.5 14.0 %all-to-all-done.4.refs_0_.refs_12_ = bf16[8,128,256]{2,1,0:T(8,128)(2,1)S(1)} async-done(((bf16[8,128,256]{2,1,0:T(8,128)(2,1)}), bf16[8,128,256]{2,1,0:T(8,128)(2,1)S(1)}, u32[]{:S(2)}, u32[]{:S(2)}) %all-to-all-start.4) | async-done | bytes 524320 | tf_op jit(solution)/shard_map/all_to_all | solution.py:1164
  246.3 3.3 post_attention.3
  253.3 14.3 %all-gather.40.cloned.1.call-done = bf16[1024,768]{1,0:T(8,128)(2,1)} async-done(((bf16[256,768]{1,0:T(8,128)(2,1)}), bf16[1024,768]{1,0:T(8,128)(2,1)}) %all-gather.40.cloned.1.call-update) | async-done | bytes 1572880 | tf_op jit(solution)/shard_map/all_gather | solution.py:1171
  267.6 16.5 %ffn_fwd.3 = (bf16[4,256,768]{2,1,0:T(8,128)(2,1)}, f32[4,56,256]{2,1,0:T(8,128)}) custom-call(bf16[4,256,768]{2,1,0:T(8,128)(2,1)} %bitcast.77, s32[4,2,256]{2,1,0:T(2,128)} %squeeze.62.routes, f32[4,16,256]{2,1,0:T(8,128)} %slice.111.before, bf16[16,768]{1,0:T(8,128)(2,1)} %bitcast.94, bf16[2,8,2,768,512]{4,3,2,1,0:T(8,128)(2,1)} %refs_2_.3, ...), custom_call_target="tpu_custom_call" | custom-call | tf_op jit(solution)/shard_map/ffn_fwd/pallas_call | solution.py:790
  284.1 4.7 all-gather.34.cloned.1.call-done.gm
  288.9 19.3 %ffn_bwd.2 = (bf16[4,256,768]{2,1,0:T(8,128)(2,1)}, f32[4,8,256]{2,1,0:T(8,128)}) custom-call(bf16[4,256,768]{2,1,0:T(8,128)(2,1)} %bitcast.78, bf16[4,256,768]{2,1,0:T(8,128)(2,1)} %all-gather.34.cloned.1.call-done.gm, f32[4,56,256]{2,1,0:T(8,128)} %get-tuple-element.69.table, bf16[2,8,2,768,512]{4,3,2,1,0:T(8,128)(2,1)} %refs_2_.3, ...), custom_call_target="tpu_custom_call" | custom-call | tf_op jit(solution)/shard_map/ffn_bwd/pallas_call | solution.py:865
  308.2 7.2 all_to_all.70
  315.3 3.7 all-to-all-start.6
  323.5 15.6 %all-to-all-done.6.refs_1_ = bf16[4,256,768]{2,1,0:T(8,128)(2,1)S(1)} async-done(((bf16[4,256,768]{2,1,0:T(8,128)(2,1)}), bf16[4,256,768]{2,1,0:T(8,128)(2,1)S(1)}, u32[]{:S(2)}, u32[]{:S(2)}) %all-to-all-start.6) | async-done | bytes 1572896 | tf_op jit(solution)/shard_map/all_to_all | solution.py:1199
  340.3 5.8 middle.2
  346.1 20.1 %all_to_all.71.go = bf16[8,128,256]{2,1,0:T(8,128)(2,1)} all-to-all(bf16[8,128,256]{2,1,0:T(8,128)(2,1)} %get-tuple-element.79), channel_id=1, replica_groups=mesh['ctx'=8,'fsdp'=4] {'ctx'}, dimensions={0} | all-to-all | bytes 1048576 | tf_op jit(solution)/shard_map/all_to_all | solution.py:1214
  366.2 15.5 %attn_bwd.2 = (bf16[8,128,768]{2,1,0:T(8,128)(2,1)}, bf16[768,768]{1,0:T(8,128)(2,1)}) custom-call(s32[8]{0:T(128)} %select_reduce_fusion.inv, bf16[8,128,768]{2,1,0:T(8,128)(2,1)} %copy-done.2, bf16[768,768]{1,0:T(8,128)(2,1)} %all-gather.30.cloned.1.call-done.w, f32[1024,128]{1,0:T(8,128)} %constant.62.clone.cosine, f32[1024,128]{1,0:T(8,128)} %constant.63.clone.sine, ...), custom_call_target="tpu_custom_call" | custom-call | tf_op jit(solution)/shard_map/attn_bwd/pallas_call | solution.py:702
  381.7 40.4 %all_to_all.72.refs_0_ = bf16[8,128,768]{2,1,0:T(8,128)(2,1)} all-to-all(bf16[8,128,768]{2,1,0:T(8,128)(2,1)} %get-tuple-element.80), channel_id=1, replica_groups=mesh['ctx'=8,'fsdp'=4] {'ctx'}, dimensions={0} | all-to-all | bytes 3145728 | tf_op jit(solution)/shard_map/all_to_all | solution.py:1220
  422.1 3.4 finish.2
  426.9 16.7 %all-gather.42.cloned.1.call-done = bf16[1024,768]{1,0:T(8,128)(2,1)} async-done(((bf16[256,768]{1,0:T(8,128)(2,1)}), bf16[1024,768]{1,0:T(8,128)(2,1)}) %all-gather.42.cloned.1.call-update) | async-done | bytes 1572880 | tf_op jit(solution)/shard_map/all_gather | solution.py:1195
  443.5 19.4 %ffn_bwd.3 = (bf16[4,256,768]{2,1,0:T(8,128)(2,1)}, f32[4,8,256]{2,1,0:T(8,128)}) custom-call(bf16[4,256,768]{2,1,0:T(8,128)(2,1)} %bitcast.76, bf16[4,256,768]{2,1,0:T(8,128)(2,1)} %bitcast.82, f32[4,56,256]{2,1,0:T(8,128)} %get-tuple-element.62.table, bf16[2,8,2,768,512]{4,3,2,1,0:T(8,128)(2,1)} %refs_2_.3, bf16[2,8,512,768]{3,2,1,0:T(8,128)(2,1)} %refs_3_.3), custom_call_target="tpu_custom_call" | custom-call | tf_op jit(solution)/shard_map/ffn_bwd/pallas_call | solution.py:865
  462.9 7.5 all_to_all.73
  470.4 3.6 all-to-all-start.10
  474.6 19.8 %all-to-all-done.10.refs_1_ = bf16[4,256,768]{2,1,0:T(8,128)(2,1)S(1)} async-done(((bf16[4,256,768]{2,1,0:T(8,128)(2,1)}), bf16[4,256,768]{2,1,0:T(8,128)(2,1)S(1)}, u32[]{:S(2)}, u32[]{:S(2)}) %all-to-all-start.10) | async-done | bytes 1572896 | tf_op jit(solution)/shard_map/all_to_all | solution.py:1199
  495.6 5.9 middle.3
  501.6 19.7 %all_to_all.74.go = bf16[8,128,256]{2,1,0:T(8,128)(2,1)} all-to-all(bf16[8,128,256]{2,1,0:T(8,128)(2,1)} %get-tuple-element.87), channel_id=1, replica_groups=mesh['ctx'=8,'fsdp'=4] {'ctx'}, dimensions={0} | all-to-all | bytes 1048576 | tf_op jit(solution)/shard_map/all_to_all | solution.py:1214
  521.2 15.4 %attn_bwd.3 = (bf16[8,128,768]{2,1,0:T(8,128)(2,1)}, bf16[768,768]{1,0:T(8,128)(2,1)}) custom-call(s32[8]{0:T(128)} %select_reduce_fusion.inv, bf16[8,128,768]{2,1,0:T(8,128)(2,1)} %all-to-all-done.n1, bf16[768,768]{1,0:T(8,128)(2,1)} %all-gather.26.cloned.1.call-done.w, f32[1024,128]{1,0:T(8,128)} %constant.62.clone.cosine, ...), custom_call_target="tpu_custom_call" | custom-call | tf_op jit(solution)/shard_map/attn_bwd/pallas_call | solution.py:702
  538.1 22.9 %reduce-scatter.5.cloned.1.call-done = bf16[192,768]{1,0:T(8,128)(2,1)} async-done(((bf16[768,768]{1,0:T(8,128)(2,1)}), bf16[192,768]{1,0:T(8,128)(2,1)}) %reduce-scatter.5.cloned.1.call-update) | async-done | bytes 294928 | tf_op jit(solution)/shard_map/reduce_scatter | solution.py:1216
  563.5 23.3 %all_to_all.75.refs_1_ = bf16[4,256,768]{2,1,0:T(8,128)(2,1)} all-to-all(bf16[4,256,768]{2,1,0:T(8,128)(2,1)S(1)} %copy-done.9), channel_id=1, replica_groups=mesh['ctx'=8,'fsdp'=4] {'fsdp'}, dimensions={0} | all-to-all | bytes 3145728 | tf_op jit(solution)/shard_map/all_to_all | solution.py:1179
  586.8 5.6 all-to-all-start.13
  593.1 80.8 %all-gather.6 = f32[512,256]{1,0:T(8,128)} all-gather(f32[16,256]{1,0:T(8,128)S(1)} %pad_maximum_fusion.3), channel_id=8, replica_groups=mesh['ctx'=8,'fsdp'=4] {'ctx','fsdp'}, dimensions={0}, use_global_device_ids=true | all-gather | bytes 540672 | tf_op jit(solution)/shard_map/all_gather | solution.py:1176
  674.6 42.9 %all-gather.9 = f32[512,256]{1,0:T(8,128)} all-gather(f32[16,256]{1,0:T(8,128)S(1)} %pad_maximum_fusion.4), channel_id=11, replica_groups=mesh['ctx'=8,'fsdp'=4] {'ctx','fsdp'}, dimensions={0}, use_global_device_ids=true | all-gather | bytes 540672 | tf_op jit(solution)/shard_map/all_gather | solution.py:1176
  717.6 3.3 combine.3
  720.9 4.6 reshape.125
  725.5 2.3 convert_reduce_fusion
  729.3 2.8 stack_reshape.7
  734.3 3.4 finish.3
  738.4 39.2 %psum.21 = bf16[2,20,768]{2,1,0:T(8,128)(2,1)S(1)} all-reduce(bf16[2,20,768]{2,1,0:T(8,128)(2,1)S(1)} %pad_maximum_fusion.2), channel_id=1, replica_groups=mesh['ctx'=8,'fsdp'=4] {'ctx','fsdp'}, use_global_device_ids=true, to_apply=%region_3.4 | all-reduce | flops 30720 | bytes 122880 | tf_op jit(solution)/shard_map/psum | solution.py:1231
  778.9 4.6 reshape.124
  783.5 2.3 convert_reduce_fusion.1
  787.4 2.8 stack_reshape.6
  790.1 4.2 pad_maximum_fusion
  794.3 73.0 %all-gather.36.cloned.1.call-done.gm = bf16[32,256,768]{2,1,0:T(8,128)(2,1)} async-done(((bf16[1,256,768]{2,1,0:T(8,128)(2,1)}), bf16[32,256,768]{2,1,0:T(8,128)(2,1)}) %all-gather.36.cloned.1.call-update) | async-done | bytes 12582928 | tf_op jit(solution)/shard_map/all_gather | solution.py:1155
  867.3 97.4 %all-gather.52.cloned.1.call-done = bf16[8192,768]{1,0:T(8,128)(2,1)} async-done(((bf16[256,768]{1,0:T(8,128)(2,1)}), bf16[8192,768]{1,0:T(8,128)(2,1)}) %all-gather.52.cloned.1.call-update) | async-done | bytes 12582928 | tf_op jit(solution)/shard_map/all_gather | solution.py:1172
  964.8 39.7 %dispatch.3 = (bf16[8,32,64,768]{3,2,1,0:T(8,128)(2,1)}, bf16[8,32,64,768]{3,2,1,0:T(8,128)(2,1)}) custom-call(f32[32,16,256]{2,1,0:T(8,128)} %bitcast.81, bf16[32,256,768]{2,1,0:T(8,128)(2,1)} %bitcast.72, bf16[32,256,768]{2,1,0:T(8,128)(2,1)} %all-gather.36.cloned.1.call-done.gm), custom_call_target="tpu_custom_call" | custom-call | tf_op jit(solution)/shard_map/dispatch/pallas_call | solution.py:906
  1004.4 108.4 %weight_grads.2 = (f32[2,8,2,768,512]{4,3,2,1,0:T(8,128)}, f32[2,8,512,768]{3,2,1,0:T(8,128)}) custom-call(bf16[8,2048,768]{2,1,0:T(8,128)(2,1)} %bitcast.68, bf16[8,2048,768]{2,1,0:T(8,128)(2,1)} %bitcast.69, bf16[2,8,2,768,512]{4,3,2,1,0:T(8,128)(2,1)} %refs_2_.3, bf16[2,8,512,768]{3,2,1,0:T(8,128)(2,1)} %refs_3_.3), custom_call_target="tpu_custom_call" | custom-call | tf_op jit(solution)/shard_map/weight_grads/pallas_call | solution.py:961
  1112.9 46.9 %all-gather.50.cloned.1.call-done = bf16[8192,768]{1,0:T(8,128)(2,1)} async-done(((bf16[256,768]{1,0:T(8,128)(2,1)}), bf16[8192,768]{1,0:T(8,128)(2,1)}) %all-gather.50.cloned.1.call-update) | async-done | bytes 12582928 | tf_op jit(solution)/shard_map/all_gather | solution.py:1197
  1159.8 39.5 %dispatch.2 = (bf16[8,32,64,768]{3,2,1,0:T(8,128)(2,1)}, bf16[8,32,64,768]{3,2,1,0:T(8,128)(2,1)}) custom-call(f32[32,16,256]{2,1,0:T(8,128)} %bitcast.80, bf16[32,256,768]{2,1,0:T(8,128)(2,1)} %bitcast.70, bf16[32,256,768]{2,1,0:T(8,128)(2,1)} %bitcast.71), custom_call_target="tpu_custom_call" | custom-call | tf_op jit(solution)/shard_map/dispatch/pallas_call | solution.py:906
  1199.3 108.6 %weight_grads.3 = (f32[2,8,2,768,512]{4,3,2,1,0:T(8,128)}, f32[2,8,512,768]{3,2,1,0:T(8,128)}) custom-call(bf16[8,2048,768]{2,1,0:T(8,128)(2,1)} %bitcast.66, bf16[8,2048,768]{2,1,0:T(8,128)(2,1)} %bitcast.67, bf16[2,8,2,768,512]{4,3,2,1,0:T(8,128)(2,1)} %refs_2_.3, bf16[2,8,512,768]{3,2,1,0:T(8,128)(2,1)} %refs_3_.3, ...), custom_call_target="tpu_custom_call", output_to_operand_aliasing={{0}: (4, {}), {1}: (5, {})} | custom-call | tf_op jit(solution)/shard_map/weight_grads/pallas_call | solution.py:961
  (144 shorter events, 55.3 us)
Async XLA Ops:
  7.2 31.8 %copy-start = (bf16[2,3,192,768]{3,2,1,0:T(8,128)(2,1)S(1)}, bf16[2,3,192,768]{3,2,1,0:T(8,128)(2,1)}, u32[]{:S(2)}) copy-start(bf16[2,3,192,768]{3,2,1,0:T(8,128)(2,1)} %param.19) | copy-start | bytes 5308420
  7.2 20.7 %copy-start.12 = (bf16[1,256,768]{2,1,0:T(8,128)(2,1)S(1)}, bf16[1,256,768]{2,1,0:T(8,128)(2,1)}, u32[]{:S(2)}) copy-start(bf16[1,256,768]{2,1,0:T(8,128)(2,1)} %param.14) | copy-start | bytes 1179652
  33.1 43.4 %all-to-all-start = ((bf16[8,128,768]{2,1,0:T(8,128)(2,1)}), bf16[8,128,768]{2,1,0:T(8,128)(2,1)}, u32[]{:S(2)}, u32[]{:S(2)}) async-start(bf16[8,128,768]{2,1,0:T(8,128)(2,1)} %bitcast.79), calls=%async_computation | async-start | bytes 3145728 | tf_op jit(solution)/shard_map/all_to_all | solution.py:1162
  38.9 21.6 %all-gather.26.cloned.1.call-start = ((), (), s32[]{:S(2)}) async-start(), calls=%async_computation.18 | async-start | bytes 1474560 | tf_op jit(solution)/shard_map/all_gather | solution.py:1145
  39.3 2.2 copy-start.11
  40.1 2.7 copy-start.17
  41.2 49.0 %all-gather.28.cloned.1.call-start = ((), (), s32[]{:S(2)}) async-start(), calls=%async_computation.19 | async-start | bytes 1474560 | tf_op jit(solution)/shard_map/all_gather | solution.py:1146
  85.8 22.5 %copy-start.15 = (s32[2,1,256,2]{2,3,1,0:T(2,128)S(1)}, s32[2,1,256,2]{2,3,1,0:T(2,128)}, u32[]{:S(2)}) copy-start(s32[2,1,256,2]{2,3,1,0:T(2,128)} %param.17) | copy-start | bytes 12292
  85.8 18.4 %all-to-all-start.1 = ((bf16[8,128,256]{2,1,0:T(8,128)(2,1)}), bf16[8,128,256]{2,1,0:T(8,128)(2,1)S(1)}, u32[]{:S(2)}, u32[]{:S(2)}) async-start(bf16[8,128,256]{2,1,0:T(8,128)(2,1)} %get-tuple-element.58), calls=%async_computation.1 | async-start | bytes 1048576 | tf_op jit(solution)/shard_map/all_to_all | solution.py:1164
  89.6 37.3 %all-gather.38.cloned.1.call-start = ((), (), s32[]{:S(2)}) async-start(), calls=%async_computation.28 | async-start | bytes 1966080 | tf_op jit(solution)/shard_map/all_gather | solution.py:1171
  104.2 0.8 copy-start.6
  143.7 24.0 %all-to-all-start.2 = ((bf16[4,256,768]{2,1,0:T(8,128)(2,1)}), bf16[4,256,768]{2,1,0:T(8,128)(2,1)S(1)}, u32[]{:S(2)}, u32[]{:S(2)}) async-start(bf16[4,256,768]{2,1,0:T(8,128)(2,1)} %get-tuple-element.61), calls=%async_computation.2 | async-start | bytes 3145728 | tf_op jit(solution)/shard_map/all_to_all | solution.py:1179
  167.7 1.1 copy-start.3
  174.4 5.7 copy-start.10
  174.4 42.5 %all-to-all-start.3 = ((bf16[8,128,768]{2,1,0:T(8,128)(2,1)}), bf16[8,128,768]{2,1,0:T(8,128)(2,1)S(1)}, u32[]{:S(2)}, u32[]{:S(2)}) async-start(bf16[8,128,768]{2,1,0:T(8,128)(2,1)} %bitcast.12), calls=%async_computation.3 | async-start | bytes 3145728 | tf_op jit(solution)/shard_map/all_to_all | solution.py:1162
  180.1 20.6 %all-gather.30.cloned.1.call-start = ((), (), s32[]{:S(2)}) async-start(), calls=%async_computation.20 | async-start | bytes 1474560 | tf_op jit(solution)/shard_map/all_gather | solution.py:1145
  181.2 50.4 %all-gather.32.cloned.1.call-start = ((), (), s32[]{:S(2)}) async-start(), calls=%async_computation.21 | async-start | bytes 1474560 | tf_op jit(solution)/shard_map/all_gather | solution.py:1146
  216.9 1.1 copy-start.2
  227.2 18.3 %all-to-all-start.4 = ((bf16[8,128,256]{2,1,0:T(8,128)(2,1)}), bf16[8,128,256]{2,1,0:T(8,128)(2,1)S(1)}, u32[]{:S(2)}, u32[]{:S(2)}) async-start(bf16[8,128,256]{2,1,0:T(8,128)(2,1)} %get-tuple-element.64), calls=%async_computation.4 | async-start | bytes 1048576 | tf_op jit(solution)/shard_map/all_to_all | solution.py:1164
  230.9 36.8 %all-gather.40.cloned.1.call-start = ((), (), s32[]{:S(2)}) async-start(), calls=%async_computation.29 | async-start | bytes 1966080 | tf_op jit(solution)/shard_map/all_gather | solution.py:1171
  245.5 0.8 copy-start.7
  249.6 39.3 %all-gather.34.cloned.1.call-start = ((), (), s32[]{:S(2)}) async-start(), calls=%async_computation.22 | async-start | bytes 1966080 | tf_op jit(solution)/shard_map/all_gather | solution.py:1195
  315.3 5.2 copy-start.8
  315.3 23.7 %all-to-all-start.6 = ((bf16[4,256,768]{2,1,0:T(8,128)(2,1)}), bf16[4,256,768]{2,1,0:T(8,128)(2,1)S(1)}, u32[]{:S(2)}, u32[]{:S(2)}) async-start(bf16[4,256,768]{2,1,0:T(8,128)(2,1)} %get-tuple-element.77), calls=%async_computation.6 | async-start | bytes 3145728 | tf_op jit(solution)/shard_map/all_to_all | solution.py:1199
  319.0 124.5 %all-gather.42.cloned.1.call-start = ((), (), s32[]{:S(2)}) async-start(), calls=%async_computation.30 | async-start | bytes 1966080 | tf_op jit(solution)/shard_map/all_gather | solution.py:1195
  339.1 1.2 copy-start.4
  425.5 111.2 %reduce-scatter.7.cloned.1.call-start = ((), (), s32[]{:S(2)}) async-start(), calls=%async_computation.24 | async-start | bytes 1474560 | tf_op jit(solution)/shard_map/reduce_scatter | solution.py:1216
  426.3 111.2 %reduce-scatter.11.cloned.1.call-start = ((), (), s32[]{:S(2)}) async-start(), calls=%async_computation.26 | async-start | bytes 1474560 | tf_op jit(solution)/shard_map/reduce_scatter | solution.py:1213
  470.4 24.0 %all-to-all-start.10 = ((bf16[4,256,768]{2,1,0:T(8,128)(2,1)}), bf16[4,256,768]{2,1,0:T(8,128)(2,1)S(1)}, u32[]{:S(2)}, u32[]{:S(2)}) async-start(bf16[4,256,768]{2,1,0:T(8,128)(2,1)} %get-tuple-element.84), calls=%async_computation.10 | async-start | bytes 3145728 | tf_op jit(solution)/shard_map/all_to_all | solution.py:1199
  474.0 63.5 %reduce-scatter.9.cloned.1.call-start = ((), (), s32[]{:S(2)}) async-start(), calls=%async_computation.25 | async-start | bytes 1474560 | tf_op jit(solution)/shard_map/reduce_scatter | solution.py:1213
  494.5 1.1 copy-start.5
  501.5 59.5 %reduce-scatter.5.cloned.1.call-start = ((), (), s32[]{:S(2)}) async-start(), calls=%async_computation.23 | async-start | bytes 1474560 | tf_op jit(solution)/shard_map/reduce_scatter | solution.py:1216
  536.7 26.8 %copy-start.9 = (bf16[4,256,768]{2,1,0:T(8,128)(2,1)S(1)}, bf16[4,256,768]{2,1,0:T(8,128)(2,1)}, u32[]{:S(2)}) copy-start(bf16[4,256,768]{2,1,0:T(8,128)(2,1)} %get-tuple-element.68) | copy-start | bytes 4718596
  536.7 184.2 %all-gather.46.cloned.1.call-start = ((), (), s32[]{:S(2)}) async-start(), calls=%async_computation.32 | async-start | bytes 2654208 | tf_op jit(solution)/shard_map/all_gather | solution.py:1217
  537.5 194.7 %all-reduce.4.cloned.1.call-start = ((), (), s32[]{:S(2)}) async-start(), calls=%async_computation.36 | async-start | bytes 1179648 | tf_op jit(solution)/shard_map/psum | solution.py:1213
  538.0 240.9 %all-gather.44.cloned.1.call-start = ((), (), s32[]{:S(2)}) async-start(), calls=%async_computation.31 | async-start | bytes 2654208 | tf_op jit(solution)/shard_map/all_gather | solution.py:1217
  561.0 306.3 %all-gather.36.cloned.1.call-start = ((), (), s32[]{:S(2)}) async-start(), calls=%async_computation.27 | async-start | bytes 12976128 | tf_op jit(solution)/shard_map/all_gather | solution.py:1155
  561.6 403.2 %all-gather.52.cloned.1.call-start = ((), (), s32[]{:S(2)}) async-start(), calls=%async_computation.35 | async-start | bytes 12976128 | tf_op jit(solution)/shard_map/all_gather | solution.py:1172
  562.2 550.7 %all-gather.48.cloned.1.call-start = ((), (), s32[]{:S(2)}) async-start(), calls=%async_computation.33 | async-start | bytes 12976128 | tf_op jit(solution)/shard_map/all_gather | solution.py:1172
  562.7 597.0 %all-gather.50.cloned.1.call-start = ((), (), s32[]{:S(2)}) async-start(), calls=%async_computation.34 | async-start | bytes 12976128 | tf_op jit(solution)/shard_map/all_gather | solution.py:1197
  586.8 130.8 %copy-start.13 = (f32[19,768]{1,0:T(8,128)S(1)}, f32[19,768]{1,0:T(8,128)}, u32[]{:S(2)}) copy-start(f32[19,768]{1,0:T(8,128)} %get-tuple-element.94) | copy-start | bytes 175108
  586.8 147.5 %all-to-all-start.13 = ((bf16[8,128,768]{2,1,0:T(8,128)(2,1)}), bf16[8,128,768]{2,1,0:T(8,128)(2,1)}, u32[]{:S(2)}, u32[]{:S(2)}) async-start(bf16[8,128,768]{2,1,0:T(8,128)(2,1)} %get-tuple-element.88), calls=%async_computation.13 | async-start | bytes 3145728 | tf_op jit(solution)/shard_map/all_to_all | solution.py:1220
  593.1 127.7 %copy-start.16 = (f32[1,768]{1,0:T(1,128)S(1)}, f32[1,768]{1,0:T(1,128)}, u32[]{:S(2)}) copy-start(f32[1,768]{1,0:T(1,128)} %get-tuple-element.93) | copy-start | bytes 9220
  593.1 127.8 %copy-start.14 = (f32[19,768]{1,0:T(8,128)S(1)}, f32[19,768]{1,0:T(8,128)}, u32[]{:S(2)}) copy-start(f32[19,768]{1,0:T(8,128)} %get-tuple-element.92) | copy-start | bytes 175108
  1199.3 108.6 %copy-start.1 = (bf16[2,3,192,768]{3,2,1,0:T(8,128)(2,1)S(1)}, bf16[2,3,192,768]{3,2,1,0:T(8,128)(2,1)}, u32[]{:S(2)}) copy-start(bf16[2,3,192,768]{3,2,1,0:T(8,128)(2,1)} %param.19) | copy-start | bytes 5308420
Sparse Core Ops, SparseCore 0:
  41.9 18.5 all-gather.25
  62.6 17.4 all-gather.27
  108.5 18.3 all-gather.37
  182.7 17.9 all-gather.29
  202.1 17.4 all-gather.31
  249.8 17.8 all-gather.39
  269.2 19.6 all-gather.33
  425.7 17.8 all-gather.41
  446.1 26.0 reduce-scatter.6
  475.3 25.9 reduce-scatter.10
  503.9 25.7 reduce-scatter.8
  536.8 24.1 reduce-scatter.4
  563.2 77.4 all-gather.45
  643.9 71.5 all-reduce.3
  717.7 51.6 all-gather.43
  772.5 94.7 all-gather.35
  870.5 94.2 all-gather.51
  967.9 94.2 all-gather.47
  1065.5 94.2 all-gather.49

commit v2 on v1

--- a/solution.py
+++ b/solution.py
@@ -527,22 +527,6 @@
     return pltpu.CompilerParams(vmem_limit_bytes=mb * 2**20, **more)
 
 
-def block_call(fn, outs, args, name):
-    def kernel(*refs):
-        results = fn(*[ref[...] for ref in refs[: len(args)]])
-        for ref, value in zip(refs[len(args) :], results):
-            ref[...] = value
-
-    return pl.pallas_call(
-        kernel,
-        out_shape=outs,
-        in_specs=[pl.BlockSpec(memory_space=pltpu.VMEM)] * len(args),
-        out_specs=[pl.BlockSpec(memory_space=pltpu.VMEM)] * len(outs),
-        compiler_params=params_of(),
-        name=name,
-    )(*args)
-
-
 def shape_of(dims, kind):
     return jax.ShapeDtypeStruct(dims, kind)
 
@@ -581,22 +565,106 @@
     return values * cosine + swap_halves(values) * sine
 
 
-def attn_fwd_kernel(inv, n1, w, cosine, sine, qkv, o, lse, ob, rows):
-    blocks, blk, _ = n1.shape
+def place():
+    own, pack = lax.axis_index("ctx"), lax.axis_index("fsdp")
+    return own // 2, own % 2, pack // 2, pack % 2
+
+
+def remote(src, dst, send, recv, ctx, fsdp):
+    return pltpu.make_async_remote_copy(
+        src_ref=src,
+        dst_ref=dst,
+        send_sem=send,
+        recv_sem=recv,
+        device_id=(ctx, fsdp),
+        device_id_type=pl.DeviceIdType.MESH,
+    )
+
+
+def greet_plane(contexts):
+    own = lax.axis_index("ctx")
+    _, _, y, k = place()
+    barrier = pltpu.get_barrier_semaphore()
+    for ctx in range(contexts):
+        for core in range(2):
+
+            @pl.when(jnp.logical_or(ctx != own, core != k))
+            def _():
+                pl.semaphore_signal(barrier, inc=1, device_id=(ctx, 2 * y + core), device_id_type=pl.DeviceIdType.MESH)
+
+    return barrier, 2 * contexts - 1
+
+
+def greet_packs():
+    own = lax.axis_index("ctx")
+    _, _, y, k = place()
+    barrier = pltpu.get_barrier_semaphore()
+    for fsdp in (2 * y + 1 - k, 2 * (1 - y) + k, 2 * (1 - y) + 1 - k):
+        pl.semaphore_signal(barrier, inc=1, device_id=(own, fsdp), device_id_type=pl.DeviceIdType.MESH)
+    return barrier, 3
+
+
+def attn_fwd_kernel(
+    order, inv, x, small, w, cosine, sine, wo,
+    n1s, qkv, o, lse, ob, hst, ub,
+    n1own, n1r, osort, osend, orecv,
+    n_send, n_recv, f_send, f_recv, o_send, o_recv,
+):
+    blocks, blk, _ = n1r.shape
     lanes = o.shape[1]
     seq = blocks * blk
     step = 2 * blk
+    own = lax.axis_index("ctx")
+    z, xx, y, k = place()
+    depth = blocks // 2
+    same = xx == k
+
+    barrier, others = greet_plane(blocks)
+    n1 = norm_low(x[...], small[0:1, :].astype(jnp.float32))
+    n1own[0] = n1[:blk]
+    n1own[1] = n1[blk:]
+    pl.semaphore_wait(barrier, others)
+
+    def n1_copy(zz):
+        return remote(n1own.at[zz // 2], n1r.at[own], n_send.at[zz], n_recv.at[z], 2 * zz + k, 2 * y + xx)
+
+    for zz in range(depth):
+        alone = jnp.logical_and(same, zz == z)
+
+        @pl.when(jnp.logical_not(alone))
+        def _():
+            n1_copy(zz).start()
+
+        @pl.when(alone)
+        def _():
+            n1r[own] = n1own[zz // 2]
+
+    def forward_copy(zz):
+        slot = n1r.at[2 * zz + k]
+        return remote(slot, slot, f_send.at[zz], f_recv.at[zz], own, 2 * y + 1 - k)
+
+    for zz in range(depth):
+
+        @pl.when(jnp.logical_not(jnp.logical_and(same, zz == z)))
+        def _():
+            remote(n1own.at[0], n1r.at[2 * zz + k], n_send.at[zz], n_recv.at[zz], 2 * zz + k, 2 * y + xx).wait_recv()
+
+        forward_copy(zz).start()
+    for zz in range(depth):
+        slot = n1r.at[2 * zz + 1 - k]
+        remote(slot, slot, f_send.at[zz], f_recv.at[zz], own, 2 * y + 1 - k).wait_recv()
+
     for b in range(blocks):
-        rows[b * blk : (b + 1) * blk, :] = n1[inv[b]]
+        n1s[b * blk : (b + 1) * blk, :] = n1r[inv[b]]
     for i in range(seq // step):
         part = slice(i * step, (i + 1) * step)
-        y = nn(rows[part, :], w[...])
+        out = nn(n1s[part, :], w[...])
         cos2 = jnp.concatenate([cosine[part, :]] * (lanes // 128), axis=1)
         sin2 = jnp.concatenate([sine[part, :]] * (lanes // 128), axis=1)
-        q = spin(y[:, :lanes], cos2, sin2).astype(jnp.bfloat16)
+        q = spin(out[:, :lanes], cos2, sin2).astype(jnp.bfloat16)
         qkv[part, :lanes] = q * jnp.asarray(HEAD_DIM**-0.5, jnp.bfloat16)
-        qkv[part, lanes : 2 * lanes] = spin(y[:, lanes : 2 * lanes], cos2, sin2).astype(jnp.bfloat16)
-        qkv[part, 2 * lanes :] = y[:, 2 * lanes :].astype(jnp.bfloat16)
+        qkv[part, lanes : 2 * lanes] = spin(out[:, lanes : 2 * lanes], cos2, sin2).astype(jnp.bfloat16)
+        qkv[part, 2 * lanes :] = out[:, 2 * lanes :].astype(jnp.bfloat16)
     lane = lax.broadcasted_iota(jnp.int32, (step, 128), 1)
     for i in range(seq // step):
         part = slice(i * step, (i + 1) * step)
@@ -623,41 +691,128 @@
                 kept = jnp.where(mine, out, kept)
             o[part, at : at + 128] = kept
         lse[part, :] = logs
-    for b in range(blocks):
-        ob[inv[b]] = o[b * blk : (b + 1) * blk, :].astype(jnp.bfloat16)
-
-
-def attn_forward(inv, n1, w, cosine, sine):
-    blocks, blk, width = n1.shape
+        osort[2 * i] = o[part, :][:blk].astype(jnp.bfloat16)
+        osort[2 * i + 1] = o[part, :][blk:].astype(jnp.bfloat16)
+
+    mine_at = 2 * z + k
+
+    def o_copy(ctx):
+        return remote(osend.at[ctx], orecv.at[mine_at], o_send.at[ctx], o_recv.at[mine_at], ctx, 2 * y + xx)
+
+    for ctx in range(blocks):
+        alone = jnp.logical_and(same, ctx == own)
+        osend[ctx] = osort[order[ctx]]
+
+        @pl.when(jnp.logical_not(alone))
+        def _():
+            o_copy(ctx).start()
+
+        @pl.when(alone)
+        def _():
+            orecv[mine_at] = osend[ctx]
+
+    for src in range(blocks):
+
+        @pl.when(jnp.logical_not(jnp.logical_and(same, src == mine_at)))
+        def _():
+            remote(osend.at[0], orecv.at[src], o_send.at[0], o_recv.at[src], 2 * (src // 2) + k, 2 * y + src % 2).wait_recv()
+
+    ob[...] = orecv[...]
+    total, low = post_attention(orecv[...], x[...], wo[...], small[1:2, :].astype(jnp.float32))
+    hst[...] = total
+    ub[...] = low
+    for zz in range(depth):
+
+        @pl.when(jnp.logical_not(jnp.logical_and(same, zz == z)))
+        def _():
+            n1_copy(zz).wait_send()
+
+        forward_copy(zz).wait_send()
+    for ctx in range(blocks):
+
+        @pl.when(jnp.logical_not(jnp.logical_and(same, ctx == own)))
+        def _():
+            o_copy(ctx).wait_send()
+
+
+def attn_forward(order, inv, x, small, w, cosine, sine, wo, number):
+    count, width = x.shape
+    blocks, blk = order.shape[0], count // 2
     lanes = w.shape[1] // 3
     seq = blocks * blk
     vm = pl.BlockSpec(memory_space=pltpu.VMEM)
+    sm = pl.BlockSpec(memory_space=pltpu.SMEM)
+    bf = jnp.bfloat16
+    dma = pltpu.SemaphoreType.DMA
     return pl.pallas_call(
         attn_fwd_kernel,
         out_shape=[
-            shape_of((seq, 3 * lanes), jnp.bfloat16),
+            shape_of((seq, width), bf),
+            shape_of((seq, 3 * lanes), bf),
             shape_of((seq, lanes), jnp.float32),
             shape_of((seq, 128), jnp.float32),
-            shape_of((blocks, blk, lanes), jnp.bfloat16),
+            shape_of((blocks, blk, lanes), bf),
+            shape_of((count, width), jnp.float32),
+            shape_of((count, width), bf),
         ],
-        in_specs=[pl.BlockSpec(memory_space=pltpu.SMEM)] + [vm] * 4,
-        out_specs=[vm] * 4,
-        scratch_shapes=[pltpu.VMEM((seq, width), jnp.bfloat16)],
-        compiler_params=params_of(),
+        in_specs=[sm] * 2 + [vm] * 6,
+        out_specs=[vm] * 7,
+        scratch_shapes=[
+            pltpu.VMEM((2, blk, width), bf),
+            pltpu.VMEM((blocks, blk, width), bf),
+            pltpu.VMEM((blocks, blk, lanes), bf),
+            pltpu.VMEM((blocks, blk, lanes), bf),
+            pltpu.VMEM((blocks, blk, lanes), bf),
+        ]
+        + [dma((blocks // 2,))] * 4
+        + [dma((blocks,))] * 2,
+        compiler_params=params_of(collective_id=number, has_side_effects=True),
         name="attn_fwd",
-    )(inv, n1, w, cosine, sine)
-
-
-def attn_bwd_kernel(inv, n1, w, cosine, sine, qkv, o, lse, go, gn, gw, rows, gos, grads, acc):
-    blocks, blk, width = n1.shape
+    )(order, inv, x, small, w, cosine, sine, wo)
+
+
+def attn_bwd_kernel(
+    order, inv, n1s, w, cosine, sine, qkv, o, lse, go, ghst, x, small,
+    gx, gm, ggain, gw,
+    gor, gos, grads, acc, keep, sib_out, sib_in, gn_out, gnr,
+    o_send, o_recv, s_send, s_recv, g_send, g_recv,
+):
+    blocks, blk, width = grads.shape
     lanes = o.shape[1]
     seq = blocks * blk
     step = 2 * blk
     zero = jnp.asarray(0, jnp.bfloat16)
+    own = lax.axis_index("ctx")
+    z, xx, y, k = place()
+    depth = blocks // 2
+    same = xx == k
+
+    barrier, others = greet_plane(blocks)
+    acc[...] = jnp.zeros_like(acc)
+    pl.semaphore_wait(barrier, others)
+
+    def go_copy(unit):
+        return remote(go.at[unit], gor.at[own], o_send.at[unit], o_recv.at[own], 2 * (unit // 2) + k, 2 * y + unit % 2)
+
+    for unit in range(blocks):
+        alone = jnp.logical_and(same, unit == 2 * z + k)
+
+        @pl.when(jnp.logical_not(alone))
+        def _():
+            go_copy(unit).start()
+
+        @pl.when(alone)
+        def _():
+            gor[own] = go[unit]
+
+    for ctx in range(blocks):
+
+        @pl.when(jnp.logical_not(jnp.logical_and(same, ctx == own)))
+        def _():
+            remote(go.at[0], gor.at[ctx], o_send.at[0], o_recv.at[ctx], ctx, 2 * y + xx).wait_recv()
+
     for b in range(blocks):
-        rows[b * blk : (b + 1) * blk, :] = n1[inv[b]]
-        gos[b * blk : (b + 1) * blk, :] = go[inv[b]]
-    acc[...] = jnp.zeros_like(acc)
+        gos[b * blk : (b + 1) * blk, :] = gor[inv[b]]
     lane = lax.broadcasted_iota(jnp.int32, (step, 128), 1)
     for i in range(seq // step):
         part = slice(i * step, (i + 1) * step)
@@ -672,50 +827,121 @@
             mine = lane // 64 == side
             q = jnp.where(mine, qkv[part, at : at + 128], zero)
             g = jnp.where(mine, gos[part, at : at + 128], zero)
-            k = qkv[:span, lanes + at : lanes + at + 128]
-            v = qkv[:span, 2 * lanes + at : 2 * lanes + at + 128]
+            keys = qkv[:span, lanes + at : lanes + at + 128]
+            values = qkv[:span, 2 * lanes + at : 2 * lanes + at + 128]
             delta = jnp.sum(g.astype(jnp.float32) * o[part, at : at + 128], axis=1, keepdims=True)
-            s = nt(q, k)
+            s = nt(q, keys)
             p = jnp.where(seen, jnp.exp(jnp.where(seen, s, -1e30) - lse[part, head : head + 1]), 0.0)
-            ds = (p * (nt(g, v) - delta)).astype(jnp.bfloat16)
+            ds = (p * (nt(g, values) - delta)).astype(jnp.bfloat16)
             acc[:span, 2 * lanes + at : 2 * lanes + at + 128] += tn(p.astype(jnp.bfloat16), g)
             acc[:span, lanes + at : lanes + at + 128] += tn(ds, q)
-            acc[part, at : at + 128] += nn(ds, jnp.where(key_lane // 64 == side, k, zero))
-    for i in range(seq // step):
-        part = slice(i * step, (i + 1) * step)
+            acc[part, at : at + 128] += nn(ds, jnp.where(key_lane // 64 == side, keys, zero))
+    for b in range(blocks):
+        part = slice(b * blk, (b + 1) * blk)
         cos2 = jnp.concatenate([cosine[part, :]] * (lanes // 128), axis=1)
         sin2 = jnp.concatenate([sine[part, :]] * (lanes // 128), axis=1)
-        grads[part, :lanes] = spin(acc[part, :lanes] * HEAD_DIM**-0.5, cos2, -sin2).astype(jnp.bfloat16)
-        grads[part, lanes : 2 * lanes] = spin(acc[part, lanes : 2 * lanes], cos2, -sin2).astype(jnp.bfloat16)
-        grads[part, 2 * lanes :] = acc[part, 2 * lanes :].astype(jnp.bfloat16)
-    for b in range(blocks):
-        gn[inv[b]] = nt(grads[b * blk : (b + 1) * blk, :], w[...]).astype(jnp.bfloat16)
+        grads[b, :, :lanes] = spin(acc[part, :lanes] * HEAD_DIM**-0.5, cos2, -sin2).astype(jnp.bfloat16)
+        grads[b, :, lanes : 2 * lanes] = spin(acc[part, lanes : 2 * lanes], cos2, -sin2).astype(jnp.bfloat16)
+        grads[b, :, 2 * lanes :] = acc[part, 2 * lanes :].astype(jnp.bfloat16)
+
+    def sib_copy(zz):
+        return remote(sib_out.at[zz], sib_in.at[zz], s_send.at[zz], s_recv.at[zz], own, 2 * y + 1 - k)
+
+    def gn_copy(zz):
+        return remote(gn_out.at[zz], gnr.at[z], g_send.at[zz], g_recv.at[z], 2 * zz + k, 2 * y + xx)
+
+    for zz in range(depth):
+        sib_out[zz] = nt(grads[order[2 * zz + 1 - k]], w[...]).astype(jnp.bfloat16)
+        sib_copy(zz).start()
+    for zz in range(depth):
+        keep[zz] = nt(grads[order[2 * zz + k]], w[...])
+    for zz in range(depth):
+        sib_copy(zz).wait_recv()
+        alone = jnp.logical_and(same, zz == z)
+        gn_out[zz] = (keep[zz] + sib_in[zz].astype(jnp.float32)).astype(jnp.bfloat16)
+
+        @pl.when(jnp.logical_not(alone))
+        def _():
+            gn_copy(zz).start()
+
+        @pl.when(alone)
+        def _():
+            gnr[z] = gn_out[zz]
+
     for i in range(width // 256):
-        gw[i * 256 : (i + 1) * 256, :] = tn(rows[:, i * 256 : (i + 1) * 256], grads[...]).astype(jnp.bfloat16)
-
-
-def attn_backward(inv, n1, w, cosine, sine, qkv, o, lse, go):
-    blocks, blk, width = n1.shape
-    lanes = w.shape[1] // 3
-    seq = blocks * blk
+        part = slice(i * 256, (i + 1) * 256)
+        total = jnp.zeros((256, 3 * lanes), jnp.float32)
+        gw[part, :] = tn(n1s[:, part], grads[...].reshape(seq, 3 * lanes)).astype(jnp.bfloat16)
+    for zz in range(depth):
+
+        @pl.when(jnp.logical_not(jnp.logical_and(same, zz == z)))
+        def _():
+            remote(gn_out.at[0], gnr.at[zz], g_send.at[0], g_recv.at[zz], 2 * zz + k, 2 * y + xx).wait_recv()
+
+    halves = []
+    for h in range(2):
+        total = gnr[h * (depth // 2)].astype(jnp.float32)
+        for zz in range(1, depth // 2):
+            total = total + gnr[h * (depth // 2) + zz].astype(jnp.float32)
+        halves.append(total)
+    gn = jnp.concatenate(halves, axis=0)
+    values = x[...]
+    factor = rms_factor(values)
+    base = values * factor
+    gb = gn * small[0:1, :].astype(jnp.float32)
+    grad = ghst[...] + factor * (gb - base * jnp.mean(gb * base, axis=-1, keepdims=True))
+    gx[...] = grad
+    gm[...] = grad.astype(jnp.bfloat16)
+    ggain[...] = jnp.sum(gn * base, axis=0, keepdims=True)
+    for unit in range(blocks):
+
+        @pl.when(jnp.logical_not(jnp.logical_and(same, unit == 2 * z + k)))
+        def _():
+            go_copy(unit).wait_send()
+
+    for zz in range(depth):
+        sib_copy(zz).wait_send()
+
+        @pl.when(jnp.logical_not(jnp.logical_and(same, zz == z)))
+        def _():
+            gn_copy(zz).wait_send()
+
+
+def attn_backward(order, inv, n1s, w, cosine, sine, qkv, o, lse, go, ghst, x, small, number):
+    blocks, blk, lanes = go.shape
+    seq, width = n1s.shape
+    count = x.shape[0]
+    depth = blocks // 2
     vm = pl.BlockSpec(memory_space=pltpu.VMEM)
+    sm = pl.BlockSpec(memory_space=pltpu.SMEM)
+    bf = jnp.bfloat16
+    dma = pltpu.SemaphoreType.DMA
     return pl.pallas_call(
         attn_bwd_kernel,
         out_shape=[
-            shape_of((blocks, blk, width), jnp.bfloat16),
-            shape_of((width, 3 * lanes), jnp.bfloat16),
+            shape_of((count, width), jnp.float32),
+            shape_of((count, width), bf),
+            shape_of((1, width), jnp.float32),
+            shape_of((width, 3 * lanes), bf),
         ],
-        in_specs=[pl.BlockSpec(memory_space=pltpu.SMEM)] + [vm] * 8,
-        out_specs=[vm] * 2,
+        in_specs=[sm] * 2 + [vm] * 11,
+        out_specs=[vm] * 4,
         scratch_shapes=[
-            pltpu.VMEM((seq, width), jnp.bfloat16),
-            pltpu.VMEM((seq, lanes), jnp.bfloat16),
-            pltpu.VMEM((seq, 3 * lanes), jnp.bfloat16),
+            pltpu.VMEM((blocks, blk, lanes), bf),
+            pltpu.VMEM((seq, lanes), bf),
+            pltpu.VMEM((blocks, blk, 3 * lanes), bf),
             pltpu.VMEM((seq, 3 * lanes), jnp.float32),
-        ],
-        compiler_params=params_of(),
+            pltpu.VMEM((depth, blk, width), jnp.float32),
+            pltpu.VMEM((depth, blk, width), bf),
+            pltpu.VMEM((depth, blk, width), bf),
+            pltpu.VMEM((depth, blk, width), bf),
+            pltpu.VMEM((depth, blk, width), bf),
+        ]
+        + [dma((blocks,))] * 2
+        + [dma((depth,))] * 4,
+        compiler_params=params_of(collective_id=number, has_side_effects=True),
         name="attn_bwd",
-    )(inv, n1, w, cosine, sine, qkv, o, lse, go)
+    )(order, inv, n1s, w, cosine, sine, qkv, o, lse, go, ghst, x, small)
 
 
 def routing(raw, before, routes):
@@ -749,22 +975,81 @@
     return jnp.sum(hot * wide, axis=1, keepdims=True)
 
 
-def ffn_fwd_kernel(ub, routes, before, router, wgu, wd, part, table, hot_s, x_s, y_s, coef_s):
+def swap_rows(own, rows, send, recv, forward_send, forward_recv):
+    ctx = lax.axis_index("ctx")
+    _, _, y, k = place()
+    beside, across = 2 * y + 1 - k, 2 * (1 - y) + k
+    far = remote(own, rows.at[2], send.at[0], recv.at[0], ctx, across)
+    near = remote(own, rows.at[1], send.at[1], recv.at[1], ctx, beside)
+    onward = remote(rows.at[2], rows.at[3], forward_send, forward_recv, ctx, beside)
+    far.start()
+    near.start()
+    return near, far, onward
+
+
+def sum_rows(parts, beside_in, mid, across_in, send, recv):
+    ctx = lax.axis_index("ctx")
+    _, _, y, k = place()
+    beside, across = 2 * y + 1 - k, 2 * (1 - y) + k
+    first = remote(parts.at[3], beside_in.at[1], send.at[0], recv.at[0], ctx, beside)
+    second = remote(parts.at[1], beside_in.at[0], send.at[1], recv.at[1], ctx, beside)
+    third = remote(mid, across_in, send.at[2], recv.at[2], ctx, across)
+    return first, second, third
+
+
+def ffn_fwd_kernel(
+    ub, hst, small, routes, before, wgu, wd,
+    ubf, table, ext, x_next,
+    rows_s, hot_s, x_s, y_s, coef_s, parts, beside_in, mid, across_in,
+    a_send, a_recv, r_send, r_recv,
+):
     e = pl.program_id(0)
-    packs = ub.shape[0]
+    packs = ubf.shape[0]
+    count, width = ub.shape
+    router = small[2 + NC :, :]
+
+    def gathers():
+        return swap_rows(ub, rows_s, a_send, a_recv, a_send.at[2], a_recv.at[2])
+
+    def sums():
+        return sum_rows(parts, beside_in, mid, across_in, r_send, r_recv)
 
     @pl.when(e == 0)
     def _():
-        for d in range(packs):
-            rows = routing(nt(router[...], ub[d]), before[d], routes[d])
+        barrier, others = greet_packs()
+        rows_s[0] = ub[...]
+
+        def prepare(d):
+            rows = routing(nt(router, rows_s[d]), before[d], routes[d])
             table[d] = rows
             hot = one_hot(rows[SLOT : SLOT + NF])
             coef_s[d] = slot_values(hot, rows[COEF : COEF + NF])
             hot_low = hot.astype(jnp.bfloat16)
             hot_s[d] = hot_low
-            x = nn(hot_low, ub[d]).astype(jnp.bfloat16)
+            x = nn(hot_low, rows_s[d]).astype(jnp.bfloat16)
             for n in range(NF):
                 x_s[n, d * MOST : (d + 1) * MOST, :] = x[n * MOST : (n + 1) * MOST]
+
+        pl.semaphore_wait(barrier, others)
+        near, far, onward = gathers()
+        prepare(0)
+        near.wait_recv()
+        prepare(1)
+        far.wait_recv()
+        onward.start()
+        prepare(2)
+        onward.wait_recv()
+        prepare(3)
+        ubf[...] = rows_s[...]
+        ext[:count, :] = ub[...]
+        rows = table[0]
+        ext[count:, :] = jnp.zeros((16, width), jnp.bfloat16)
+        ext[count:, :count] = rows[COEF : COEF + 16].astype(jnp.bfloat16)
+        slots = jnp.concatenate([rows[SLOT : SLOT + NF], jnp.zeros((16 - NF, count), jnp.float32)], axis=0)
+        ext[count:, count : 2 * count] = slots.astype(jnp.bfloat16)
+        near.wait_send()
+        far.wait_send()
+        onward.wait_send()
 
     x = x_s[e]
     gate, up = nn(x, wgu[0, 0, 0]), nn(x, wgu[0, 0, 1])
@@ -776,42 +1061,78 @@
 
     @pl.when(e == NF - 1)
     def _():
-        for d in range(packs):
-            part[d] = tn(hot_s[d], y_s[d]).astype(jnp.bfloat16)
+        first, second, third = sums()
+        parts[3] = tn(hot_s[3], y_s[3]).astype(jnp.bfloat16)
+        first.start()
+        parts[1] = tn(hot_s[1], y_s[1]).astype(jnp.bfloat16)
+        second.start()
+        away = tn(hot_s[2], y_s[2])
+        first.wait_recv()
+        mid[...] = (away + beside_in[1].astype(jnp.float32)).astype(jnp.bfloat16)
+        third.start()
+        home = tn(hot_s[0], y_s[0])
+        _, _, scale_u, scale_c = mixing_rows(table[0])
+        columns = to_columns([scale_u] + scale_c)
+        values = hst[...]
+        moe = home + columns[0] * ((values * rms_factor(values)) * small[1:2, :].astype(jnp.float32))
+        for c in range(NC):
+            moe = moe + columns[1 + c] * small[2 + c : 3 + c, :].astype(jnp.float32)
+        second.wait_recv()
+        moe = moe + beside_in[0].astype(jnp.float32)
+        third.wait_recv()
+        x_next[...] = values + (moe + across_in[...].astype(jnp.float32))
+        first.wait_send()
+        second.wait_send()
+        third.wait_send()
 
 
 def whole_spec(dims):
     return pl.BlockSpec(dims, lambda *_: (0,) * len(dims))
 
 
-def ffn_forward(layer, ub, routes, before, router, wgu, wd):
-    packs, count, width = ub.shape
+def exchange_scratch(packs, count, width):
+    bf = jnp.bfloat16
+    return [
+        pltpu.VMEM((packs, count, width), bf),
+        pltpu.VMEM((2, count, width), bf),
+        pltpu.VMEM((count, width), bf),
+        pltpu.VMEM((count, width), bf),
+    ]
+
+
+def ffn_forward(layer, ub, hst, small, routes, before, wgu, wd, number):
+    count, width = ub.shape
+    packs = routes.shape[0]
     hidden = wd.shape[2]
+    bf = jnp.bfloat16
+    outs = [
+        shape_of((packs, count, width), bf),
+        shape_of((packs, ROUT, count), jnp.float32),
+        shape_of((count + 16, width), bf),
+        shape_of((count, width), jnp.float32),
+    ]
     return pl.pallas_call(
         ffn_fwd_kernel,
         grid=(NF,),
-        out_shape=[
-            shape_of((packs, count, width), jnp.bfloat16),
-            shape_of((packs, ROUT, count), jnp.float32),
-        ],
-        in_specs=[
-            whole_spec(ub.shape),
-            whole_spec(routes.shape),
-            whole_spec(before.shape),
-            whole_spec(router.shape),
+        out_shape=outs,
+        in_specs=[whole_spec(a.shape) for a in (ub, hst, small, routes, before)]
+        + [
             pl.BlockSpec((1, 1, 2, width, hidden), lambda e: (layer, e, 0, 0, 0)),
             pl.BlockSpec((1, 1, hidden, width), lambda e: (layer, e, 0, 0)),
         ],
-        out_specs=[whole_spec((packs, count, width)), whole_spec((packs, ROUT, count))],
+        out_specs=[whole_spec(a.shape) for a in outs],
         scratch_shapes=[
-            pltpu.VMEM((packs, NF * MOST, count), jnp.bfloat16),
-            pltpu.VMEM((NF, packs * MOST, width), jnp.bfloat16),
-            pltpu.VMEM((packs, NF * MOST, width), jnp.bfloat16),
+            pltpu.VMEM((packs, count, width), bf),
+            pltpu.VMEM((packs, NF * MOST, count), bf),
+            pltpu.VMEM((NF, packs * MOST, width), bf),
+            pltpu.VMEM((packs, NF * MOST, width), bf),
             pltpu.VMEM((packs, NF * MOST, 1), jnp.float32),
-        ],
-        compiler_params=params_of(),
+        ]
+        + exchange_scratch(packs, count, width)
+        + [pltpu.SemaphoreType.DMA((3,))] * 4,
+        compiler_params=params_of(collective_id=number, has_side_effects=True),
         name="ffn_fwd",
-    )(ub, routes, before, router, wgu, wd)
+    )(ub, hst, small, routes, before, wgu, wd)
 
 
 def silu_parts(gate, up, ghid):
@@ -822,22 +1143,58 @@
     return act * up, dg, du
 
 
-def ffn_bwd_kernel(ub, gm, table, wgu, wd, part, gcoef, hot_s, x_s, g_s, y_s, coef_s, gc_s):
+def ffn_bwd_kernel(
+    gm, gx, ubf, table, hst, small, routes, gprev, wo, ob, wgu, wd,
+    ghst, go, gwo, gsmall, glog,
+    rows_s, hot_s, x_s, g_s, y_s, coef_s, gc_s, gcoef, gcoef_in, parts, beside_in, mid, across_in,
+    a_send, a_recv, r_send, r_recv, c_send, c_recv,
+):
     e = pl.program_id(0)
-    packs = ub.shape[0]
+    packs = ubf.shape[0]
+    ctx = lax.axis_index("ctx")
+    _, _, y, k = place()
+    peers = [None, 2 * y + 1 - k, 2 * (1 - y) + k, 2 * (1 - y) + 1 - k]
+
+    def gathers():
+        return swap_rows(gm, rows_s, a_send, a_recv, a_send.at[2], a_recv.at[2])
+
+    def sums():
+        return sum_rows(parts, beside_in, mid, across_in, r_send, r_recv)
 
     @pl.when(e == 0)
     def _():
-        for d in range(packs):
+        barrier, others = greet_packs()
+        rows_s[0] = gm[...]
+
+        def prepare(d):
             hot = one_hot(table[d, SLOT : SLOT + NF, :])
             coef_s[d] = slot_values(hot, table[d, COEF : COEF + NF, :])
             hot_low = hot.astype(jnp.bfloat16)
             hot_s[d] = hot_low
-            x = nn(hot_low, ub[d]).astype(jnp.bfloat16)
-            g = nn(hot_low, gm[d]).astype(jnp.bfloat16)
+            x = nn(hot_low, ubf[d]).astype(jnp.bfloat16)
             for n in range(NF):
                 x_s[n, d * MOST : (d + 1) * MOST, :] = x[n * MOST : (n + 1) * MOST]
+
+        def spread(d):
+            g = nn(hot_s[d], rows_s[d]).astype(jnp.bfloat16)
+            for n in range(NF):
                 g_s[n, d * MOST : (d + 1) * MOST, :] = g[n * MOST : (n + 1) * MOST]
+
+        pl.semaphore_wait(barrier, others)
+        near, far, onward = gathers()
+        for d in range(packs):
+            prepare(d)
+        spread(0)
+        near.wait_recv()
+        far.wait_recv()
+        onward.start()
+        spread(1)
+        spread(2)
+        onward.wait_recv()
+        spread(3)
+        near.wait_send()
+        far.wait_send()
+        onward.wait_send()
 
     x = x_s[e]
     at = pl.ds(pl.multiple_of(e * MOST, MOST), MOST)
@@ -853,54 +1210,101 @@
 
     @pl.when(e == NF - 1)
     def _():
+        first, second, third = sums()
+
+        def coef_copy(d):
+            return remote(gcoef.at[d], gcoef_in.at[d - 1], c_send.at[d - 1], c_recv.at[d - 1], ctx, peers[d])
+
+        parts[3] = tn(hot_s[3], y_s[3]).astype(jnp.bfloat16)
+        first.start()
+        parts[1] = tn(hot_s[1], y_s[1]).astype(jnp.bfloat16)
+        second.start()
         for d in range(packs):
-            part[d] = tn(hot_s[d], y_s[d]).astype(jnp.bfloat16)
-            spread = hot_s[d].astype(jnp.float32) * gc_s[d]
-            gcoef[d] = jnp.sum(spread.reshape(NF, MOST, spread.shape[1]), axis=1)
-
-
-def ffn_backward(layer, ub, gm, table, wgu, wd):
-    packs, count, width = ub.shape
+            wide = hot_s[d].astype(jnp.float32) * gc_s[d]
+            gcoef[d] = jnp.sum(wide.reshape(NF, MOST, wide.shape[1]), axis=1)
+            if d > 0:
+                coef_copy(d).start()
+        away = tn(hot_s[2], y_s[2])
+        first.wait_recv()
+        mid[...] = (away + beside_in[1].astype(jnp.float32)).astype(jnp.bfloat16)
+        third.start()
+        home = tn(hot_s[0], y_s[0])
+        second.wait_recv()
+        home = home + beside_in[0].astype(jnp.float32)
+        total = gcoef[0]
+        for d in range(1, packs):
+            coef_copy(d).wait_recv()
+            total = total + gcoef_in[d - 1]
+        third.wait_recv()
+        home = home + across_in[...].astype(jnp.float32)
+        results = middle(
+            gx[...], home, total, table[0], routes[...], gprev[...], hst[...], ubf[0],
+            small[...], wo[...], ob[...],
+        )
+        for ref, value in zip((ghst, go, gwo, gsmall, glog), results):
+            ref[...] = value
+        first.wait_send()
+        second.wait_send()
+        third.wait_send()
+        for d in range(1, packs):
+            coef_copy(d).wait_send()
+
+
+def ffn_backward(layer, gm, gx, ubf, table, hst, small, routes, gprev, wo, ob, wgu, wd, number):
+    packs, count, width = ubf.shape
     hidden = wd.shape[2]
+    bf, f32 = jnp.bfloat16, jnp.float32
+    outs = [
+        shape_of((count, width), f32),
+        shape_of(ob.shape, bf),
+        shape_of((width, width), bf),
+        shape_of((1 + NC + 16, width), f32),
+        shape_of((16, count), f32),
+    ]
+    args = (gm, gx, ubf, table, hst, small, routes, gprev, wo, ob)
+    dma = pltpu.SemaphoreType.DMA
     return pl.pallas_call(
         ffn_bwd_kernel,
         grid=(NF,),
-        out_shape=[
-            shape_of((packs, count, width), jnp.bfloat16),
-            shape_of((packs, NF, count), jnp.float32),
-        ],
-        in_specs=[
-            whole_spec(ub.shape),
-            whole_spec(gm.shape),
-            whole_spec(table.shape),
+        out_shape=outs,
+        in_specs=[whole_spec(a.shape) for a in args]
+        + [
             pl.BlockSpec((1, 1, 2, width, hidden), lambda e: (layer, e, 0, 0, 0)),
             pl.BlockSpec((1, 1, hidden, width), lambda e: (layer, e, 0, 0)),
         ],
-        out_specs=[whole_spec((packs, count, width)), whole_spec((packs, NF, count))],
+        out_specs=[whole_spec(a.shape) for a in outs],
         scratch_shapes=[
-            pltpu.VMEM((packs, NF * MOST, count), jnp.bfloat16),
-            pltpu.VMEM((NF, packs * MOST, width), jnp.bfloat16),
-            pltpu.VMEM((NF, packs * MOST, width), jnp.bfloat16),
-            pltpu.VMEM((packs, NF * MOST, width), jnp.bfloat16),
-            pltpu.VMEM((packs, NF * MOST, 1), jnp.float32),
-            pltpu.VMEM((packs, NF * MOST, 1), jnp.float32),
-        ],
-        compiler_params=params_of(),
+            pltpu.VMEM((packs, count, width), bf),
+            pltpu.VMEM((packs, NF * MOST, count), bf),
+            pltpu.VMEM((NF, packs * MOST, width), bf),
+            pltpu.VMEM((NF, packs * MOST, width), bf),
+            pltpu.VMEM((packs, NF * MOST, width), bf),
+            pltpu.VMEM((packs, NF * MOST, 1), f32),
+            pltpu.VMEM((packs, NF * MOST, 1), f32),
+            pltpu.VMEM((packs, NF, count), f32),
+            pltpu.VMEM((packs - 1, NF, count), f32),
+        ]
+        + exchange_scratch(packs, count, width)
+        + [dma((3,))] * 6,
+        compiler_params=params_of(collective_id=number, has_side_effects=True),
         name="ffn_bwd",
-    )(ub, gm, table, wgu, wd)
-
-
-def dispatch_kernel(small, u, gm, x, g):
-    rows = small[0]
-    hot = one_hot(rows[NF : 2 * NF])
-    coef = slot_values(hot, rows[:NF])
-    hot = hot.astype(jnp.bfloat16)
-    x[...] = nn(hot, u[0]).astype(jnp.bfloat16).reshape(x.shape)
-    g[...] = (nn(hot, gm[0]) * coef).astype(jnp.bfloat16).reshape(g.shape)
-
-
-def dispatch(small, u, gm):
-    devices, count, width = u.shape
+    )(*args, wgu, wd)
+
+
+def dispatch_kernel(ext, gm, x, g):
+    count = gm.shape[1]
+    rows = ext[0, count:, :].astype(jnp.float32)
+    coef, slot = rows[:NF, :count], rows[:NF, count : 2 * count].astype(jnp.int32)
+    ids = lax.broadcasted_iota(jnp.int32, (NF, MOST, count), 1)
+    hit = ids == slot[:, None, :]
+    hot = jnp.where(hit, 1.0, 0.0).astype(jnp.bfloat16).reshape(NF * MOST, count)
+    weighted = jnp.where(hit, coef[:, None, :], 0.0).astype(jnp.bfloat16).reshape(NF * MOST, count)
+    x[...] = nn(hot, ext[0, :count, :]).astype(jnp.bfloat16).reshape(x.shape)
+    g[...] = nn(weighted, gm[0]).astype(jnp.bfloat16).reshape(g.shape)
+
+
+def dispatch(ext, gm):
+    devices, count, width = gm.shape
     grouped = pl.BlockSpec((NF, 1, MOST, width), lambda d: (0, d, 0, 0))
     outs = shape_of((NF, devices, MOST, width), jnp.bfloat16)
     return pl.pallas_call(
@@ -908,14 +1312,13 @@
         grid=(devices,),
         out_shape=[outs, outs],
         in_specs=[
-            pl.BlockSpec((1, 2 * NF, count), lambda d: (d, 0, 0)),
-            pl.BlockSpec((1, count, width), lambda d: (d, 0, 0)),
+            pl.BlockSpec((1,) + ext.shape[1:], lambda d: (d, 0, 0)),
             pl.BlockSpec((1, count, width), lambda d: (d, 0, 0)),
         ],
         out_specs=[grouped, grouped],
         compiler_params=params_of(),
         name="dispatch",
-    )(small, u, gm)
+    )(ext, gm)
 
 
 def dw_kernel(*refs):
@@ -1004,24 +1407,13 @@
     return pairs, shares, scale_u, [shares[c] * pairs[c][1] for c in range(NC)]
 
 
-def combine(hst, parts, table, gain, consts, next_gain):
-    _, _, scale_u, scale_c = mixing_rows(table)
-    columns = to_columns([scale_u] + scale_c)
-    u = (hst * rms_factor(hst)) * gain
-    moe = columns[0] * u
-    for f in range(parts.shape[0]):
-        moe = moe + parts[f].astype(jnp.float32)
-    for c in range(NC):
-        moe = moe + columns[1 + c] * consts[c : c + 1].astype(jnp.float32)
-    x = hst + moe
-    return x, norm_low(x, next_gain)
-
-
-def middle(gx, parts, gcoef, table, routes, gprev, hst, ub, gain, consts, router, wo, ob):
+def middle(gx, parts, gcoef, table, routes, gprev, hst, ub, small, wo, ob):
     groups = wo.shape[0]
     inner = wo.shape[1]
     blk = ob.shape[1]
-    consts = consts.astype(jnp.float32)
+    gain = small[1:2].astype(jnp.float32)
+    consts = small[2 : 2 + NC].astype(jnp.float32)
+    router = small[2 + NC :]
     pairs, shares, scale_u, scale_c = mixing_rows(table)
     columns = to_columns([scale_u] + scale_c)
     factor = rms_factor(hst)
@@ -1060,11 +1452,9 @@
         graw = jnp.where(ids == NE + index, row, graw)
     graw = graw.astype(jnp.bfloat16)
     grad_router = nn(graw, ub)
-    gu = gx * columns[0] + tn(graw, router)
-    for f in range(parts.shape[0]):
-        gu = gu + parts[f].astype(jnp.float32)
-    small = [jnp.sum(gu * base, axis=0, keepdims=True)]
-    small += [jnp.sum(gx * columns[1 + c], axis=0, keepdims=True) for c in range(NC)]
+    gu = gx * columns[0] + tn(graw, router) + parts
+    sums = [jnp.sum(gu * base, axis=0, keepdims=True)]
+    sums += [jnp.sum(gx * columns[1 + c], axis=0, keepdims=True) for c in range(NC)]
     gb = gu * gain
     ghst = gx + factor * (gb - base * jnp.mean(gb * base, axis=-1, keepdims=True))
     gy = ghst.astype(jnp.bfloat16)
@@ -1077,23 +1467,7 @@
             go[h * groups + g] = value[h * blk : (h + 1) * blk]
         mixed = jnp.concatenate([ob[g], ob[groups + g]], axis=0)
         gwo.append(tn(mixed, gy)[:inner].astype(jnp.bfloat16))
-    return ghst, jnp.stack(go), jnp.concatenate(gwo, axis=0), jnp.concatenate(small + [grad_router], axis=0), glog
-
-
-def finish(parts, ghst, x, gain):
-    groups = parts.shape[0] // 2
-    halves = []
-    for h in range(2):
-        total = parts[h * groups].astype(jnp.float32)
-        for g in range(1, groups):
-            total = total + parts[h * groups + g].astype(jnp.float32)
-        halves.append(total)
-    gn = jnp.concatenate(halves, axis=0)
-    factor = rms_factor(x)
-    base = x * factor
-    gb = gn * gain
-    gx = ghst + factor * (gb - base * jnp.mean(gb * base, axis=-1, keepdims=True))
-    return gx, gx.astype(jnp.bfloat16), jnp.sum(gn * base, axis=0, keepdims=True)
+    return ghst, jnp.stack(go), jnp.concatenate(gwo, axis=0), jnp.concatenate(sums + [grad_router], axis=0), glog
 
 
 def turn_tables(seq):
@@ -1125,117 +1499,96 @@
     groups = ctx_size // 2
     blk = count // 2
     seq = blk * ctx_size
-    own, pack = lax.axis_index("ctx"), lax.axis_index("fsdp")
-    sequence, group = own // groups, own % groups
+    pack = lax.axis_index("fsdp")
+    z, xx, y, k = place()
+    sequence = z // 2
     inner = GROUP_HEADS * HEAD_DIM
     lanes = -(-inner // 128) * 128
     shard = width // packs
     f32, bf = jnp.float32, jnp.bfloat16
+    everyone = ("ctx", "fsdp")
 
     cosine, sine = turn_tables(seq)
-    order = lax.dynamic_index_in_dim(block_order[0].reshape(ctx_size, 2), sequence, 1, keepdims=False) - ctx_size * sequence
+    routes_t = jnp.swapaxes(routes[:, 0], 1, 2)
+    ints = jnp.concatenate([routes_t.reshape(-1), block_order[0]])
+    ints = jnp.pad(ints, (0, -ints.size % 1024)).reshape(-1, 128)
+    ints = lax.all_gather(ints, "fsdp", axis=0, tiled=False).reshape(packs, -1)
+    near = jnp.stack([pack, 2 * y + 1 - k, 2 * (1 - y) + k, 2 * (1 - y) + 1 - k])
+    routes_f = ints[near][:, : routes_t.size].reshape((packs,) + routes_t.shape)
+    order = lax.dynamic_index_in_dim(ints, 2 * y + xx, 0, keepdims=False)[routes_t.size : routes_t.size + 2 * ctx_size].reshape(ctx_size, 2)
+    order = lax.dynamic_index_in_dim(order, sequence, 1, keepdims=False) - ctx_size * sequence
     ids = jnp.arange(ctx_size, dtype=jnp.int32)
     inv = jnp.sum(jnp.where(order[None, :] == ids[:, None], ids[None, :], 0), axis=1)
 
     smalls = jnp.concatenate([gains, const_values, jnp.swapaxes(router, 1, 2)], axis=1)
-    smalls = lax.all_gather(smalls, "fsdp", axis=2, tiled=True)
-    qkv_cols = lax.dynamic_slice_in_dim(qkv_weights, group * inner, inner, axis=3)
-    qkv_cols = jnp.pad(qkv_cols, ((0, 0), (0, 0), (0, 0), (0, lanes - inner)))
-    qkv_cols = jnp.swapaxes(qkv_cols, 1, 2).reshape(LAYERS, shard, 3 * lanes)
-    w_attn = [lax.all_gather(qkv_cols[l], "fsdp", axis=0, tiled=True) for l in range(LAYERS)]
-    w_out = [lax.all_gather(out_weight[l], "fsdp", axis=0, tiled=False) for l in range(LAYERS)]
-    routes_t = jnp.swapaxes(routes[:, 0], 1, 2)
-    routes_f = lax.all_gather(routes_t, "fsdp", axis=1, tiled=False)
-
-    def gain_of(l, which):
-        return smalls[l, which : which + 1].astype(f32)
-
+    per_layer = smalls.shape[1]
+    smalls = lax.all_gather(smalls.reshape(LAYERS * per_layer, shard), "fsdp", axis=1, tiled=True)
+    smalls = [smalls[l * per_layer : (l + 1) * per_layer] for l in range(LAYERS)]
+    pairs = lax.dynamic_slice_in_dim(qkv_weights, 2 * inner * (z % 2), 2 * inner, axis=3)
+    pairs = pairs.reshape(LAYERS, 3, shard, 2, inner)
+    pairs = jnp.pad(pairs, ((0, 0),) * 4 + ((0, lanes - inner),))
+    pairs = jnp.transpose(pairs, (0, 3, 2, 1, 4)).reshape(LAYERS, 2, shard, 3 * lanes)
+    w_attn, w_out = [], []
+    for l in range(LAYERS):
+        send = jnp.concatenate([pairs[l], pairs[l]], axis=0)
+        w_attn.append(lax.all_to_all(send, "fsdp", 0, 0).reshape(width, 3 * lanes))
+        w_out.append(lax.all_gather(out_weight[l], "fsdp", axis=0, tiled=False))
+
+    gm_all = [None, lax.all_gather(cotangent[0], everyone, axis=0, tiled=False)]
     x = tokens[0].astype(f32)
-    gm_low = cotangent[0]
-    gm_all = [None, lax.all_gather(gm_low, ("ctx", "fsdp"), axis=0, tiled=False)]
     before = jnp.zeros((packs, 16, count), f32)
-    (n1,) = block_call(lambda a, b: (norm_low(a, b),), [shape_of((count, width), bf)], (x, gain_of(0, 0)), "norm")
-    kept = []
+    kept, ext_all = [], [None] * LAYERS
     for l in range(LAYERS):
-        consts, router_t = smalls[l, 2 : 2 + NC], smalls[l, 2 + NC :]
-        send = jnp.broadcast_to(n1.reshape(2, 1, blk, width), (2, groups, blk, width)).reshape(ctx_size, blk, width)
-        n1_all = lax.all_to_all(send, "ctx", 0, 0)
-        qkv, o, lse, ob = attn_forward(inv, n1_all, w_attn[l], cosine, sine)
-        ob = lax.all_to_all(ob, "ctx", 0, 0)
-        hst, ub = block_call(
-            post_attention,
-            [shape_of((count, width), f32), shape_of((count, width), bf)],
-            (ob, x, w_out[l], gain_of(l, 1)),
-            "post_attention",
-        )
-        ub_f = lax.all_gather(ub, "fsdp", axis=0, tiled=False)
-        ub_all = lax.all_gather(ub, ("ctx", "fsdp"), axis=0, tiled=False)
-        parts, table_f = ffn_forward(l, ub_f, routes_f[l], before, router_t, w_gate_up, w_down)
-        before = table_f[:, LOGI : LOGI + 16]
-        table = lax.dynamic_index_in_dim(table_f, pack, 0, keepdims=False)
-        small_all = lax.all_gather(
-            jnp.concatenate([table[COEF : COEF + NF], table[SLOT : SLOT + NF]], axis=0), ("ctx", "fsdp"), axis=0, tiled=False
-        )
-        parts = lax.all_to_all(parts, "fsdp", 0, 0)
-        x_next, n1 = block_call(
-            combine,
-            [shape_of((count, width), f32), shape_of((count, width), bf)],
-            (hst, parts, table, gain_of(l, 1), consts, gain_of(min(l + 1, LAYERS - 1), 0)),
-            "combine",
-        )
-        kept.append((x, n1_all, qkv, o, lse, ob, hst, ub, ub_f, ub_all, table_f, table, small_all, consts, router_t))
+        if l == 1:
+            x, gm_all[1] = lax.optimization_barrier((x, gm_all[1]))
+        n1s, qkv, o, lse, ob, hst, ub = attn_forward(order, inv, x, smalls[l], w_attn[l], cosine, sine, w_out[l], 2 * l)
+        ubf, table, ext, x_next = ffn_forward(
+            l, ub, hst, smalls[l], routes_f[:, l], before, w_gate_up, w_down, 2 * l + 1
+        )
+        before = table[:, LOGI : LOGI + 16]
+        ext_all[l] = lax.all_gather(ext, everyone, axis=0, tiled=False)
+        kept.append((x, n1s, qkv, o, lse, ob, hst, ubf, table))
         x = x_next
     output = x
-    gx = cotangent[0].astype(f32)
+    gm = cotangent[0]
+    gx = gm.astype(f32)
     gprev = jnp.zeros((16, count), f32)
     small_grads, qkv_grads, out_grads = [None] * LAYERS, [None] * LAYERS, [None] * LAYERS
+    for l in reversed(range(LAYERS)):
+        x, n1s, qkv, o, lse, ob, hst, ubf, table = kept[l]
+        number = 2 * LAYERS + 2 * l
+        gm, ext_all[l - 1 if l else 1] = lax.optimization_barrier((gm, ext_all[l - 1 if l else 1]))
+        ghst, go, gwo, small, gprev = ffn_backward(
+            l, gm, gx, ubf, table, hst, smalls[l], routes_t[l], gprev, w_out[l], ob, w_gate_up, w_down, number
+        )
+        out_grads[l] = lax.psum_scatter(gwo, "fsdp", scatter_dimension=0, tiled=True)
+        gx, gm, gain_grad, gw = attn_backward(
+            order, inv, n1s, w_attn[l], cosine, sine, qkv, o, lse, go, ghst, x, smalls[l], number + 1
+        )
+        if l > 0:
+            gm_all[l - 1] = lax.all_gather(gm, everyone, axis=0, tiled=False)
+        small_grads[l] = jnp.concatenate([gain_grad, small], axis=0)
+        gw = gw.reshape(width, 3, lanes)[:, :, :inner].reshape(width, 1, 3 * inner)
+        gw = lax.dynamic_update_slice_in_dim(
+            jnp.zeros((width, groups, 3 * inner), bf), gw, 2 * (z % 2) + k, axis=1
+        ).reshape(width, 3 * width)
+        qkv_grads[l] = lax.psum_scatter(gw, "fsdp", scatter_dimension=0, tiled=True)
     done = ()
     for l in reversed(range(LAYERS)):
-        x, n1_all, qkv, o, lse, ob, hst, ub, ub_f, ub_all, table_f, table, small_all, consts, router_t = kept[l]
-        gm_f = lax.all_gather(gm_low, "fsdp", axis=0, tiled=False)
-        if gm_all[l] is None:
-            gm_all[l] = lax.all_gather(gm_low, ("ctx", "fsdp"), axis=0, tiled=False)
-        parts, gcoef = ffn_backward(l, ub_f, gm_f, table_f, w_gate_up, w_down)
-        parts = lax.all_to_all(parts, "fsdp", 0, 0)
-        gcoef = jnp.sum(lax.all_to_all(gcoef, "fsdp", 0, 0), axis=0)
-        ghst, go, gwo, small, gprev = block_call(
-            middle,
-            [
-                shape_of((count, width), f32),
-                shape_of((ctx_size, blk, lanes), bf),
-                shape_of((width, width), bf),
-                shape_of((1 + NC + 16, width), f32),
-                shape_of((16, count), f32),
-            ],
-            (gx, parts, gcoef, table, routes_t[l], gprev, hst, ub, gain_of(l, 1), consts, router_t, w_out[l], ob),
-            "middle",
-        )
-        out_grads[l] = lax.psum(lax.psum_scatter(gwo, "fsdp", scatter_dimension=0, tiled=True), "ctx")
-        go = lax.all_to_all(go, "ctx", 0, 0)
-        gn, gw = attn_backward(inv, n1_all, w_attn[l], cosine, sine, qkv, o, lse, go)
-        gw = lax.psum_scatter(gw, "fsdp", scatter_dimension=0, tiled=True)
-        gw = lax.all_gather(gw, "ctx", axis=0, tiled=False).reshape(2, groups, shard, 3, lanes)[..., :inner]
-        gw = jnp.sum(gw.astype(f32), axis=0)
-        qkv_grads[l] = jnp.transpose(gw, (2, 1, 0, 3)).reshape(3, shard, width)
-        gn = lax.all_to_all(gn, "ctx", 0, 0)
-        gx, gm_low, gain_grad = block_call(
-            finish,
-            [shape_of((count, width), f32), shape_of((count, width), bf), shape_of((1, width), f32)],
-            (gn, ghst, x, gain_of(l, 0)),
-            "finish",
-        )
-        small_grads[l] = jnp.concatenate([gain_grad, small], axis=0)
-        x_all, g_all = dispatch(small_all, ub_all, gm_all[l])
+        x_all, g_all = dispatch(ext_all[l], gm_all[l])
         rows = x_all.shape[1] * x_all.shape[2]
         done = weight_grads(l, x_all.reshape(NF, rows, width), g_all.reshape(NF, rows, width), w_gate_up, w_down, done)
-    small = lax.psum(jnp.stack(small_grads).astype(bf), ("ctx", "fsdp"))
+    small = lax.psum(jnp.stack(small_grads).astype(bf), everyone)
     small = lax.dynamic_slice_in_dim(small, pack * shard, shard, axis=2).astype(f32)
+    dense = jnp.concatenate([jnp.stack(qkv_grads), jnp.stack(out_grads)], axis=2)
+    dense = lax.psum(dense, "ctx").astype(f32)
+    qkv_sum = dense[:, :, : 3 * width].reshape(LAYERS, shard, groups, 3, inner)
     return (
         output[None],
         gx[None],
         small[:, :2],
-        jnp.stack(qkv_grads),
-        jnp.stack(out_grads).astype(f32),
+        jnp.transpose(qkv_sum, (0, 3, 1, 2, 4)).reshape(LAYERS, 3, shard, width),
+        dense[:, :, 3 * width :],
         jnp.swapaxes(small[:, 2 + NC :], 1, 2),
         small[:, 2 : 2 + NC],
         done[0],

time: 1330 us -> 985 us (0.74)
  waiting for transfers between devices: 439 us -> 58.9 us
  Pallas kernels: 451 us -> 752 us
  blocking collectives: 294 us -> 64.8 us
  starting transfers between devices: 37.3 us -> 9.08 us
  other arithmetic: 25.8 us -> 9.62 us
  local copies, waits for them, and re-layouts: 52.9 us -> 67 us
    pallas_call x17 -> x8, Pallas kernels: 154 us -> 456 us  [the longest x2 137 us: attn_forward(): pl.pallas_call(attn_fwd_kernel, out_shape=[shape_of((seq, width), bf), sh...]
    all_gather x14 -> x6, waiting for transfers between devices: 299 us -> 0.03 us  [the longest x2 0.02 us: by_heads(): ext_all[l] = lax.all_gather(ext, everyone, axis=0, tiled=False)]
    all_to_all x6 -> x0, blocking collectives: 118 us -> none  [the longest x1 40.4 us: by_heads(): gn = lax.all_to_all(gn, 'ctx', 0, 0)]
    all_gather x4 -> x2, blocking collectives: 137 us -> 24.1 us  [the longest x1 18.5 us: by_heads(): ints = lax.all_gather(ints, 'fsdp', axis=0, tiled=False).reshape(packs, -1)]
    all_to_all x8 -> x2, waiting for transfers between devices: 112 us -> 14.4 us  [by_heads(): w_attn.append(lax.all_to_all(send, 'fsdp', 0, 0).reshape(width, 3 * lanes))]
    unnamed x19 -> x13, waiting for transfers between devices: 5.43 us -> 44.4 us
    all_to_all x8 -> x2, starting transfers between devices: 35.7 us -> 8.08 us  [by_heads(): w_attn.append(lax.all_to_all(send, 'fsdp', 0, 0).reshape(width, 3 * lanes))]
    reduce_scatter x2 -> x0, waiting for transfers between devices: 22.9 us -> none  [by_heads(): gw = lax.psum_scatter(gw, 'fsdp', scatter_dimension=0, tiled=True)]
  transfers between devices with their start and end apart: 27 -> 13, of which waited for: 17 -> 2; matrix products, arithmetic and copies ran while one was open for 4% -> 5% of each run, Pallas kernels for 18% -> 77%
where the time goes in v2:
time: 985 us; the launch traced here: 976 us
  Pallas kernels  752 us (76%)
  local copies, waits for them, and re-layouts  67 us (7%)
  blocking collectives  64.8 us (7%)
  waiting for transfers between devices  58.9 us (6%)
  between operations  14.8 us (2%)
    pallas_call x2, Pallas kernels, weight_grads(): pl.pallas_call(kernel, grid=(NF,), out_shape=[shape_of(wgu.shape, jnp.flo...  217 us
    pallas_call x2, Pallas kernels, attn_forward(): pl.pallas_call(attn_fwd_kernel, out_shape=[shape_of((seq, width), bf), sh...  137 us
    pallas_call x2, Pallas kernels, attn_backward(): pl.pallas_call(attn_bwd_kernel, out_shape=[shape_of((count, width), jnp.f...  120 us
    pallas_call x2, Pallas kernels, ffn_backward(): pl.pallas_call(ffn_bwd_kernel, grid=(NF,), out_shape=outs, in_specs=[whol...  107 us
    pallas_call x2, Pallas kernels, ffn_forward(): pl.pallas_call(ffn_fwd_kernel, grid=(NF,), out_shape=outs, in_specs=[whol...  92.3 us
    pallas_call x2, Pallas kernels, dispatch(): pl.pallas_call(dispatch_kernel, grid=(devices,), out_shape=[outs, outs],...  78.6 us
    unnamed x13, waiting for transfers between devices  44.4 us
    psum x1, blocking collectives, by_heads(): small = lax.psum(jnp.stack(small_grads).astype(bf), everyone)  40.7 us
  transfers between devices with their start and end apart: 13, of which 2 were waited for; matrix products, arithmetic and copies ran while one was open for 5% of the time, Pallas kernels for 77%

profile of v2, /device:TPU:0, one launch (start us, length us, event | category | flops | bytes accessed | tf_op | source)
XLA Modules:
  0.0 976.0 jit_solution(12569703252094345560)
XLA Ops:
  7.2 2.0 fusion.2
  9.3 0.7 all-gather.13.cloned.1.call-update
  10.1 0.7 all-gather.15.cloned.1.call-update
  10.8 1.0 constant_dynamic-slice_fusion
  11.8 3.3 reshape.259
  15.2 1.1 pad_bitcast_fusion
  16.3 0.8 fusion.1
  17.7 0.7 squeeze.36
  18.4 1.1 pad_maximum_fusion.1
  19.5 4.2 all-to-all-start
  24.0 18.5 %all_gather.33 = s32[4,16,128]{2,1,0:T(8,128)S(1)} all-gather(s32[1,16,128]{2,1,0:T(8,128)S(1)} %pad_bitcast_fusion.1), channel_id=1, replica_groups=mesh['ctx'=8,'fsdp'=4] {'fsdp'}, dimensions={0}, use_global_device_ids=true | all-gather | bytes 40960 | tf_op jit(solution)/shard_map/all_gather | solution.py:1515
  43.4 5.6 all-gather.3
  49.3 0.7 select_reduce_fusion.inv
  50.0 0.6 slice_bitcast_fusion.1
  50.6 0.6 fusion.3
  51.2 0.9 bitcast_convert_fusion.x
  52.2 1.0 copy-done.2
  53.2 60.4 %attn_fwd.2 = (bf16[1024,768]{1,0:T(8,128)(2,1)}, bf16[1024,768]{1,0:T(8,128)(2,1)}, f32[1024,256]{1,0:T(8,128)}, f32[1024,128]{1,0:T(8,128)}, bf16[8,128,256]{2...) custom-call(s32[8]{0:T(128)} %copy-done.12, s32[8]{0:T(128)} %select_reduce_fusion.inv, ...), custom_call_target="tpu_custom_call" | custom-call | tf_op jit(solution)/shard_map/attn_fwd/pallas_call | solution.py:747
  113.6 0.6 broadcast_in_dim.30.before
  114.2 46.4 %ffn_fwd.2 = (bf16[4,256,768]{2,1,0:T(8,128)(2,1)}, f32[4,56,256]{2,1,0:T(8,128)}, bf16[272,768]{1,0:T(8,128)(2,1)}, f32[256,768]{1,0:T(8,128)}) custom-call(bf16[256,768]{1,0:T(8,128)(2,1)} %get-tuple-element.61.ub, f32[256,768]{1,0:T(8,128)} %get-tuple-element.62.hst, bf16[20,768]{1,0:T(8,128)(2,1)} %get-tuple-element.154.small, ...), custom_call_target="tpu_custom_call" | custom-call | tf_op jit(solution)/shard_map/ffn_fwd/pallas_call | solution.py:1114
  161.1 0.7 squeeze.38
  161.9 1.1 pad_maximum_fusion.2
  163.0 3.8 all-to-all-start.1
  166.8 1.5 slice.75.before
  168.3 14.4 %all-to-all-done.1 = bf16[4,192,768]{2,1,0:T(8,128)(2,1)S(1)} async-done(((bf16[4,192,768]{2,1,0:T(8,128)(2,1)}), bf16[4,192,768]{2,1,0:T(8,128)(2,1)S(1)}, u32[]{:S(2)}, u32[]{:S(2)}) %all-to-all-start.1) | async-done | bytes 1179680 | tf_op jit(solution)/shard_map/all_to_all | solution.py:1534
  182.7 1.0 copy-done.3
  183.7 76.7 %attn_fwd.3 = (bf16[1024,768]{1,0:T(8,128)(2,1)}, bf16[1024,768]{1,0:T(8,128)(2,1)}, f32[1024,256]{1,0:T(8,128)}, f32[1024,128]{1,0:T(8,128)}, bf16[8,128,256]{2...) custom-call(s32[8]{0:T(128)} %copy-done.12, s32[8]{0:T(128)} %select_reduce_fusion.inv, ...), custom_call_target="tpu_custom_call" | custom-call | tf_op jit(solution)/shard_map/attn_fwd/pallas_call | solution.py:747
  260.4 45.9 %ffn_fwd.3 = (bf16[4,256,768]{2,1,0:T(8,128)(2,1)}, f32[4,56,256]{2,1,0:T(8,128)}, bf16[272,768]{1,0:T(8,128)(2,1)}, f32[256,768]{1,0:T(8,128)}) custom-call(bf16[256,768]{1,0:T(8,128)(2,1)} %get-tuple-element.65.ub, f32[256,768]{1,0:T(8,128)} %get-tuple-element.66.hst, bf16[20,768]{1,0:T(8,128)(2,1)} %get-tuple-element.153.small, ...), custom_call_target="tpu_custom_call" | custom-call | tf_op jit(solution)/shard_map/ffn_fwd/pallas_call | solution.py:1114
  307.2 0.9 bitcast_convert_fusion.1.gx
  308.1 0.6 broadcast_in_dim.32.gprev
  308.7 52.3 %ffn_bwd.2 = (f32[256,768]{1,0:T(8,128)}, bf16[8,128,256]{2,1,0:T(8,128)(2,1)}, bf16[768,768]{1,0:T(8,128)(2,1)}, f32[19,768]{1,0:T(8,128)}, f32[16,256]{1,0:T(8,128)}) custom-call(bf16[256,768]{1,0:T(8,128)(2,1)} %bitcast.98, f32[256,768]{1,0:T(8,128)} %bitcast_convert_fusion.1.gx, bf16[4,256,768]{2,1,0:T(8,128)(2,1)} %get-tuple-element.79.ubf, ...), custom_call_target="tpu_custom_call" | custom-call | tf_op jit(solution)/shard_map/ffn_bwd/pallas_call | solution.py:1266
  361.1 68.2 %attn_bwd.2 = (f32[256,768]{1,0:T(8,128)}, bf16[256,768]{1,0:T(8,128)(2,1)}, f32[1,768]{1,0:T(1,128)}, bf16[768,768]{1,0:T(8,128)(2,1)}) custom-call(s32[8]{0:T(128)} %copy-done.12, s32[8]{0:T(128)} %select_reduce_fusion.inv, bf16[1024,768]{1,0:T(8,128)(2,1)} %get-tuple-element.73.n1s, bf16[768,768]{1,0:T(8,128)(2,1)} %bitcast.93, ...), custom_call_target="tpu_custom_call" | custom-call | tf_op jit(solution)/shard_map/attn_bwd/pallas_call | solution.py:919
  429.3 1.6 copy.62
  431.0 2.0 broadcast.41.clone
  433.0 1.0 bitcast_dynamic-update-slice_fusion
  434.0 5.8 copy.68
  439.8 0.7 reduce-scatter.11.cloned.1.call-update
  440.8 54.5 %ffn_bwd.3 = (f32[256,768]{1,0:T(8,128)}, bf16[8,128,256]{2,1,0:T(8,128)(2,1)}, bf16[768,768]{1,0:T(8,128)(2,1)}, f32[19,768]{1,0:T(8,128)}, f32[16,256]{1,0:T(8,128)}) custom-call(bf16[256,768]{1,0:T(8,128)(2,1)} %get-tuple-element.86.gm, f32[256,768]{1,0:T(8,128)} %get-tuple-element.87.gx, bf16[4,256,768]{2,1,0:T(8,128)(2,1)} %get-tuple-element.88.ubf, ...), custom_call_target="tpu_custom_call" | custom-call | tf_op jit(solution)/shard_map/ffn_bwd/pallas_call | solution.py:1266
  495.4 51.9 %attn_bwd.3 = (f32[256,768]{1,0:T(8,128)}, bf16[256,768]{1,0:T(8,128)(2,1)}, f32[1,768]{1,0:T(1,128)}, bf16[768,768]{1,0:T(8,128)(2,1)}) custom-call(s32[8]{0:T(128)} %copy-done.12, s32[8]{0:T(128)} %select_reduce_fusion.inv, bf16[1024,768]{1,0:T(8,128)(2,1)} %get-tuple-element.69.n1s, bf16[768,768]{1,0:T(8,128)(2,1)} %bitcast.91, ...), custom_call_target="tpu_custom_call" | custom-call | tf_op jit(solution)/shard_map/attn_bwd/pallas_call | solution.py:919
  547.3 1.6 copy.61
  548.9 2.0 broadcast.41.clone.1
  551.0 1.0 bitcast_dynamic-update-slice_fusion.1
  551.9 5.7 copy.66
  558.6 1.5 copy.69
  560.2 1.1 pad_maximum_fusion.3
  561.3 1.2 copy.63
  562.5 41.7 %reduce-scatter.13.cloned.1.call-done = bf16[192,2304]{1,0:T(8,128)(2,1)} async-done(((bf16[768,2304]{1,0:T(8,128)(2,1)}), bf16[192,2304]{1,0:T(8,128)(2,1)}) %reduce-scatter.13.cloned.1.call-update) | async-done | bytes 884752
  604.2 1.5 copy.67
  605.7 3.3 pad_maximum_fusion
  609.0 0.6 copy-done.13
  609.9 39.3 %dispatch.3 = (bf16[8,32,64,768]{3,2,1,0:T(8,128)(2,1)}, bf16[8,32,64,768]{3,2,1,0:T(8,128)(2,1)}) custom-call(bf16[32,272,768]{2,1,0:T(8,128)(2,1)} %bitcast.88, bf16[32,256,768]{2,1,0:T(8,128)(2,1)} %all-gather.13.cloned.1.call-done.gm), custom_call_target="tpu_custom_call" | custom-call | tf_op jit(solution)/shard_map/dispatch/pallas_call | solution.py:1310
  649.2 108.5 %weight_grads.2 = (f32[2,8,2,768,512]{4,3,2,1,0:T(8,128)}, f32[2,8,512,768]{3,2,1,0:T(8,128)}) custom-call(bf16[8,2048,768]{2,1,0:T(8,128)(2,1)} %bitcast.84, bf16[8,2048,768]{2,1,0:T(8,128)(2,1)} %bitcast.85, bf16[2,8,2,768,512]{4,3,2,1,0:T(8,128)(2,1)} %refs_2_.3, bf16[2,8,512,768]{3,2,1,0:T(8,128)(2,1)} %refs_3_.3), custom_call_target="tpu_custom_call" | custom-call | tf_op jit(solution)/shard_map/weight_grads/pallas_call | solution.py:1364
  757.7 40.7 %psum.14 = bf16[2,20,768]{2,1,0:T(8,128)(2,1)S(1)} all-reduce(bf16[2,20,768]{2,1,0:T(8,128)(2,1)S(1)} %pad_maximum_fusion.4), channel_id=1, replica_groups=mesh['ctx'=8,'fsdp'=4] {'ctx','fsdp'}, use_global_device_ids=true, to_apply=%region_1.2 | all-reduce | flops 30720 | bytes 122880 | tf_op jit(solution)/shard_map/psum | solution.py:1581
  798.5 0.6 fusion.4
  799.1 0.6 slice_bitcast_fusion
  799.7 39.3 %dispatch.2 = (bf16[8,32,64,768]{3,2,1,0:T(8,128)(2,1)}, bf16[8,32,64,768]{3,2,1,0:T(8,128)(2,1)}) custom-call(bf16[32,272,768]{2,1,0:T(8,128)(2,1)} %bitcast.87, bf16[32,256,768]{2,1,0:T(8,128)(2,1)} %bitcast.89), custom_call_target="tpu_custom_call" | custom-call | tf_op jit(solution)/shard_map/dispatch/pallas_call | solution.py:1310
  839.0 108.4 %weight_grads.3 = (f32[2,8,2,768,512]{4,3,2,1,0:T(8,128)}, f32[2,8,512,768]{3,2,1,0:T(8,128)}) custom-call(bf16[8,2048,768]{2,1,0:T(8,128)(2,1)} %bitcast.82, bf16[8,2048,768]{2,1,0:T(8,128)(2,1)} %bitcast.83, bf16[2,8,2,768,512]{4,3,2,1,0:T(8,128)(2,1)} %refs_2_.3, bf16[2,8,512,768]{3,2,1,0:T(8,128)(2,1)} %refs_3_.3, ...), custom_call_target="tpu_custom_call", output_to_operand_aliasing={{0}: (4, {}), {1}: (5, {})} | custom-call | tf_op jit(solution)/shard_map/weight_grads/pallas_call | solution.py:1364
  947.4 1.2 slice.100
  948.7 1.5 copy.65
  950.2 4.2 slice.99
  954.3 6.8 copy.64
  961.1 6.2 reshape.270
  967.3 0.9 copy.83
  968.2 0.9 copy.84
  (91 shorter events, 5.2 us)
Async XLA Ops:
  7.2 3.6 copy-start
  7.2 45.0 %all-gather.11.cloned.1.call-start = ((), (), s32[]{:S(2)}) async-start(), calls=%async_computation.6 | async-start | bytes 1474560 | tf_op jit(solution)/shard_map/all_gather | solution.py:1535
  9.3 159.0 %all-gather.13.cloned.1.call-start = ((), (), s32[]{:S(2)}) async-start(), calls=%async_computation.7 | async-start | bytes 12976128 | tf_op jit(solution)/shard_map/all_gather | solution.py:1537
  10.0 172.7 %all-gather.15.cloned.1.call-start = ((), (), s32[]{:S(2)}) async-start(), calls=%async_computation.8 | async-start | bytes 1474560 | tf_op jit(solution)/shard_map/all_gather | solution.py:1535
  17.1 6.7 copy-start.10
  17.1 6.7 copy-start.17
  17.7 6.2 copy-start.11
  17.7 6.2 copy-start.15
  17.7 6.2 copy-start.16
  17.7 33.5 %copy-start.7 = (bf16[1,256,768]{2,1,0:T(8,128)(2,1)S(1)}, bf16[1,256,768]{2,1,0:T(8,128)(2,1)}, u32[]{:S(2)}) copy-start(bf16[1,256,768]{2,1,0:T(8,128)(2,1)} %param.14) | copy-start | bytes 1179652
  19.5 32.6 %all-to-all-start = ((bf16[4,192,768]{2,1,0:T(8,128)(2,1)}), bf16[4,192,768]{2,1,0:T(8,128)(2,1)S(1)}, u32[]{:S(2)}, u32[]{:S(2)}) async-start(bf16[4,192,768]{2,1,0:T(8,128)(2,1)} %pad_maximum_fusion.1), calls=%async_computation | async-start | bytes 2359296 | tf_op jit(solution)/shard_map/all_to_all | solution.py:1534
  23.8 284.3 %all-gather.17.cloned.1.call-start = ((), (), s32[]{:S(2)}) async-start(), calls=%async_computation.12 | async-start | bytes 13787136 | tf_op jit(solution)/shard_map/all_gather | solution.py:1549
  49.3 2.8 copy-start.12
  52.2 1.0 copy-start.2
  163.0 19.7 %all-to-all-start.1 = ((bf16[4,192,768]{2,1,0:T(8,128)(2,1)}), bf16[4,192,768]{2,1,0:T(8,128)(2,1)S(1)}, u32[]{:S(2)}, u32[]{:S(2)}) async-start(bf16[4,192,768]{2,1,0:T(8,128)(2,1)} %pad_maximum_fusion.2), calls=%async_computation.1 | async-start | bytes 2359296 | tf_op jit(solution)/shard_map/all_to_all | solution.py:1534
  166.8 273.9 %all-gather.19.cloned.1.call-start = ((), (), s32[]{:S(2)}) async-start(), calls=%async_computation.13 | async-start | bytes 13787136 | tf_op jit(solution)/shard_map/all_gather | solution.py:1549
  182.7 1.0 copy-start.3
  260.4 46.8 %copy-start.4 = (bf16[1,256,768]{2,1,0:T(8,128)(2,1)S(1)}, bf16[1,256,768]{2,1,0:T(8,128)(2,1)}, u32[]{:S(2)}) copy-start(bf16[1,256,768]{2,1,0:T(8,128)(2,1)} %param.15) | copy-start | bytes 1179652
  306.3 252.3 %reduce-scatter.15.cloned.1.call-start = ((), (), s32[]{:S(2)}) async-start(), calls=%async_computation.16 | async-start | bytes 4423680
  439.8 120.4 %reduce-scatter.11.cloned.1.call-start = ((), (), s32[]{:S(2)}) async-start(), calls=%async_computation.10 | async-start | bytes 1474560 | tf_op jit(solution)/shard_map/reduce_scatter | solution.py:1564
  440.5 119.7 %reduce-scatter.9.cloned.1.call-start = ((), (), s32[]{:S(2)}) async-start(), calls=%async_computation.9 | async-start | bytes 1474560 | tf_op jit(solution)/shard_map/reduce_scatter | solution.py:1564
  495.3 108.9 %reduce-scatter.13.cloned.1.call-start = ((), (), s32[]{:S(2)}) async-start(), calls=%async_computation.15 | async-start | bytes 4423680
  557.7 242.0 %all-gather.21.cloned.1.call-start = ((), (), s32[]{:S(2)}) async-start(), calls=%async_computation.14 | async-start | bytes 12976128 | tf_op jit(solution)/shard_map/all_gather | solution.py:1569
  558.3 389.1 %all-reduce.4.cloned.1.call-start = ((), (), s32[]{:S(2)}) async-start(), calls=%async_computation.11 | async-start | bytes 6291456 | tf_op jit(solution)/shard_map/psum | solution.py:1584
  609.0 0.7 copy-start.13
  609.0 0.9 copy-start.8
  609.0 0.9 copy-start.14
  609.0 0.9 copy-start.9
  961.1 6.2 copy-start.5
  961.1 7.1 copy-start.6
  961.1 7.9 copy-start.1
Sparse Core Ops, SparseCore 0:
  10.2 21.9 all-gather.10
  35.1 109.1 all-gather.12
  146.5 18.1 all-gather.14
  167.4 124.9 all-gather.16
  306.5 134.0 all-gather.18
  443.6 55.3 reduce-scatter.14
  501.7 24.8 reduce-scatter.10
  529.2 25.7 reduce-scatter.8
  558.2 45.8 reduce-scatter.12
  606.9 95.9 all-gather.20
  707.0 127.0 all-reduce.3

commit v3 on v2

--- a/solution.py
+++ b/solution.py
@@ -581,10 +581,14 @@
     )
 
 
-def greet_plane(contexts):
+def greet_plane(contexts, across=False):
     own = lax.axis_index("ctx")
     _, _, y, k = place()
     barrier = pltpu.get_barrier_semaphore()
+    if across:
+        for core in (k, 1 - k):
+            device = (own, 2 * (1 - y) + core)
+            pl.semaphore_signal(barrier, inc=1, device_id=device, device_id_type=pl.DeviceIdType.MESH)
     for ctx in range(contexts):
         for core in range(2):
 
@@ -592,7 +596,7 @@
             def _():
                 pl.semaphore_signal(barrier, inc=1, device_id=(ctx, 2 * y + core), device_id_type=pl.DeviceIdType.MESH)
 
-    return barrier, 2 * contexts - 1
+    return barrier, 2 * contexts - 1 + (2 if across else 0)
 
 
 def greet_packs():
@@ -605,10 +609,10 @@
 
 
 def attn_fwd_kernel(
-    order, inv, x, small, w, cosine, sine, wo,
-    n1s, qkv, o, lse, ob, hst, ub,
-    n1own, n1r, osort, osend, orecv,
-    n_send, n_recv, f_send, f_recv, o_send, o_recv,
+    order, inv, x, small, wq, cosine, sine, wo_own,
+    n1s, qkv, o, lse, ob, hst, ub, w, wo,
+    n1own, n1r, osort, osend, orecv, cols, w_s, wo_s,
+    n_send, n_recv, f_send, f_recv, o_send, o_recv, w_send, w_recv, v_send, v_recv,
 ):
     blocks, blk, _ = n1r.shape
     lanes = o.shape[1]
@@ -618,8 +622,11 @@
     z, xx, y, k = place()
     depth = blocks // 2
     same = xx == k
-
-    barrier, others = greet_plane(blocks)
+    pack = lax.axis_index("fsdp")
+    inner = wo_own.shape[1]
+    beside, over, corner = 2 * y + 1 - k, 2 * (1 - y) + k, 2 * (1 - y) + 1 - k
+
+    barrier, others = greet_plane(blocks, across=True)
     n1 = norm_low(x[...], small[0:1, :].astype(jnp.float32))
     n1own[0] = n1[:blk]
     n1own[1] = n1[blk:]
@@ -639,6 +646,37 @@
         def _():
             n1r[own] = n1own[zz // 2]
 
+    for half in range(2):
+
+        @pl.when(z % 2 == half)
+        def _():
+            for core in range(2):
+                first = (2 * half + core) * inner
+                for c in range(3):
+                    cols[core, :, c * lanes : c * lanes + inner] = wq[0, c, :, first : first + inner]
+                    cols[core, :, c * lanes + inner : (c + 1) * lanes] = jnp.zeros((inner, lanes - inner), jnp.bfloat16)
+
+    def rows_of(device):
+        return pl.ds(pl.multiple_of(device * inner, inner), inner)
+
+    def w_copy(index):
+        device, core = ((beside, 1 - k), (over, k), (corner, 1 - k))[index]
+        return remote(cols.at[core], w_s.at[rows_of(pack), :], w_send.at[index], w_recv.at[index], own, device)
+
+    def w_wait(index):
+        rows = w_s.at[rows_of((beside, over, corner)[index]), :]
+        remote(cols.at[0], rows, w_send.at[index], w_recv.at[index], own, beside).wait_recv()
+
+    w_s[rows_of(pack), :] = cols[k]
+    wo_s[pack] = wo_own[0]
+    for index in (1, 2, 0):
+        w_copy(index).start()
+    v_far = remote(wo_s.at[pack], wo_s.at[pack], v_send.at[0], v_recv.at[0], own, over)
+    v_near = remote(wo_s.at[pack], wo_s.at[pack], v_send.at[1], v_recv.at[1], own, beside)
+    v_on = remote(wo_s.at[over], wo_s.at[over], v_send.at[2], v_recv.at[2], own, beside)
+    v_far.start()
+    v_near.start()
+
     def forward_copy(zz):
         slot = n1r.at[2 * zz + k]
         return remote(slot, slot, f_send.at[zz], f_recv.at[zz], own, 2 * y + 1 - k)
@@ -654,11 +692,14 @@
         slot = n1r.at[2 * zz + 1 - k]
         remote(slot, slot, f_send.at[zz], f_recv.at[zz], own, 2 * y + 1 - k).wait_recv()
 
+    for index in range(3):
+        w_wait(index)
+    w[...] = w_s[...]
     for b in range(blocks):
         n1s[b * blk : (b + 1) * blk, :] = n1r[inv[b]]
     for i in range(seq // step):
         part = slice(i * step, (i + 1) * step)
-        out = nn(n1s[part, :], w[...])
+        out = nn(n1s[part, :], w_s[...])
         cos2 = jnp.concatenate([cosine[part, :]] * (lanes // 128), axis=1)
         sin2 = jnp.concatenate([sine[part, :]] * (lanes // 128), axis=1)
         q = spin(out[:, :lanes], cos2, sin2).astype(jnp.bfloat16)
@@ -695,6 +736,8 @@
         osort[2 * i + 1] = o[part, :][blk:].astype(jnp.bfloat16)
 
     mine_at = 2 * z + k
+    remote(wo_s.at[over], wo_s.at[over], v_send.at[0], v_recv.at[0], own, over).wait_recv()
+    v_on.start()
 
     def o_copy(ctx):
         return remote(osend.at[ctx], orecv.at[mine_at], o_send.at[ctx], o_recv.at[mine_at], ctx, 2 * y + xx)
@@ -718,7 +761,10 @@
             remote(osend.at[0], orecv.at[src], o_send.at[0], o_recv.at[src], 2 * (src // 2) + k, 2 * y + src % 2).wait_recv()
 
     ob[...] = orecv[...]
-    total, low = post_attention(orecv[...], x[...], wo[...], small[1:2, :].astype(jnp.float32))
+    remote(wo_s.at[beside], wo_s.at[beside], v_send.at[1], v_recv.at[1], own, beside).wait_recv()
+    remote(wo_s.at[corner], wo_s.at[corner], v_send.at[2], v_recv.at[2], own, beside).wait_recv()
+    wo[...] = wo_s[...]
+    total, low = post_attention(orecv[...], x[...], wo_s[...], small[1:2, :].astype(jnp.float32))
     hst[...] = total
     ub[...] = low
     for zz in range(depth):
@@ -728,6 +774,11 @@
             n1_copy(zz).wait_send()
 
         forward_copy(zz).wait_send()
+    for index in range(3):
+        w_copy(index).wait_send()
+    v_far.wait_send()
+    v_near.wait_send()
+    v_on.wait_send()
     for ctx in range(blocks):
 
         @pl.when(jnp.logical_not(jnp.logical_and(same, ctx == own)))
@@ -735,10 +786,11 @@
             o_copy(ctx).wait_send()
 
 
-def attn_forward(order, inv, x, small, w, cosine, sine, wo, number):
+def attn_forward(layer, order, inv, x, small, wq, cosine, sine, wo, number):
     count, width = x.shape
     blocks, blk = order.shape[0], count // 2
-    lanes = w.shape[1] // 3
+    packs, inner = width // wo.shape[1], wo.shape[1]
+    lanes = -(-inner // 128) * 128
     seq = blocks * blk
     vm = pl.BlockSpec(memory_space=pltpu.VMEM)
     sm = pl.BlockSpec(memory_space=pltpu.SMEM)
@@ -746,6 +798,7 @@
     dma = pltpu.SemaphoreType.DMA
     return pl.pallas_call(
         attn_fwd_kernel,
+        grid=(1,),
         out_shape=[
             shape_of((seq, width), bf),
             shape_of((seq, 3 * lanes), bf),
@@ -754,26 +807,34 @@
             shape_of((blocks, blk, lanes), bf),
             shape_of((count, width), jnp.float32),
             shape_of((count, width), bf),
+            shape_of((width, 3 * lanes), bf),
+            shape_of((packs, inner, width), bf),
         ],
-        in_specs=[sm] * 2 + [vm] * 6,
-        out_specs=[vm] * 7,
+        in_specs=[sm, sm, vm, vm]
+        + [pl.BlockSpec((1, 3, inner, width), lambda _: (layer, 0, 0, 0)), vm, vm]
+        + [pl.BlockSpec((1, inner, width), lambda _: (layer, 0, 0))],
+        out_specs=[vm] * 9,
         scratch_shapes=[
             pltpu.VMEM((2, blk, width), bf),
             pltpu.VMEM((blocks, blk, width), bf),
             pltpu.VMEM((blocks, blk, lanes), bf),
             pltpu.VMEM((blocks, blk, lanes), bf),
             pltpu.VMEM((blocks, blk, lanes), bf),
+            pltpu.VMEM((2, inner, 3 * lanes), bf),
+            pltpu.VMEM((width, 3 * lanes), bf),
+            pltpu.VMEM((packs, inner, width), bf),
         ]
         + [dma((blocks // 2,))] * 4
-        + [dma((blocks,))] * 2,
+        + [dma((blocks,))] * 2
+        + [dma((3,))] * 4,
         compiler_params=params_of(collective_id=number, has_side_effects=True),
         name="attn_fwd",
-    )(order, inv, x, small, w, cosine, sine, wo)
+    )(order, inv, x, small, wq, cosine, sine, wo)
 
 
 def attn_bwd_kernel(
-    order, inv, n1s, w, cosine, sine, qkv, o, lse, go, ghst, x, small,
-    gx, gm, ggain, gw,
+    order, inv, n1s, w, cosine, sine, qkv, o, lse, go, ghst, x, small, gsmall,
+    gx, gm, gw,
     gor, gos, grads, acc, keep, sib_out, sib_in, gn_out, gnr,
     o_send, o_recv, s_send, s_recv, g_send, g_recv,
 ):
@@ -868,10 +929,20 @@
         def _():
             gnr[z] = gn_out[zz]
 
+    groups = depth
+    inner = GROUP_HEADS * HEAD_DIM
+    gw[:, : 3 * width] = jnp.zeros((width, 3 * width), jnp.bfloat16)
     for i in range(width // 256):
         part = slice(i * 256, (i + 1) * 256)
-        total = jnp.zeros((256, 3 * lanes), jnp.float32)
-        gw[part, :] = tn(n1s[:, part], grads[...].reshape(seq, 3 * lanes)).astype(jnp.bfloat16)
+        piece = tn(n1s[:, part], grads[...].reshape(seq, 3 * lanes)).astype(jnp.bfloat16)
+        for group in range(groups):
+
+            @pl.when(2 * (z % 2) + k == group)
+            def _():
+                for c in range(3):
+                    first = c * width + group * inner
+                    gw[part, first : first + inner] = piece[:, c * lanes : c * lanes + inner]
+
     for zz in range(depth):
 
         @pl.when(jnp.logical_not(jnp.logical_and(same, zz == z)))
@@ -892,7 +963,9 @@
     grad = ghst[...] + factor * (gb - base * jnp.mean(gb * base, axis=-1, keepdims=True))
     gx[...] = grad
     gm[...] = grad.astype(jnp.bfloat16)
-    ggain[...] = jnp.sum(gn * base, axis=0, keepdims=True)
+    sums = jnp.concatenate([jnp.sum(gn * base, axis=0, keepdims=True), gsmall[...]], axis=0)
+    sums = jnp.concatenate([sums, jnp.zeros((128 - sums.shape[0], width), jnp.float32)], axis=0)
+    gw[:, 3 * width :] = jnp.transpose(sums).astype(jnp.bfloat16)
     for unit in range(blocks):
 
         @pl.when(jnp.logical_not(jnp.logical_and(same, unit == 2 * z + k)))
@@ -907,7 +980,7 @@
             gn_copy(zz).wait_send()
 
 
-def attn_backward(order, inv, n1s, w, cosine, sine, qkv, o, lse, go, ghst, x, small, number):
+def attn_backward(order, inv, n1s, w, cosine, sine, qkv, o, lse, go, ghst, x, small, gsmall, number):
     blocks, blk, lanes = go.shape
     seq, width = n1s.shape
     count = x.shape[0]
@@ -921,11 +994,10 @@
         out_shape=[
             shape_of((count, width), jnp.float32),
             shape_of((count, width), bf),
-            shape_of((1, width), jnp.float32),
-            shape_of((width, 3 * lanes), bf),
+            shape_of((width, 3 * width + 128), bf),
         ],
-        in_specs=[sm] * 2 + [vm] * 11,
-        out_specs=[vm] * 4,
+        in_specs=[sm] * 2 + [vm] * 12,
+        out_specs=[vm] * 3,
         scratch_shapes=[
             pltpu.VMEM((blocks, blk, lanes), bf),
             pltpu.VMEM((seq, lanes), bf),
@@ -941,7 +1013,7 @@
         + [dma((depth,))] * 4,
         compiler_params=params_of(collective_id=number, has_side_effects=True),
         name="attn_bwd",
-    )(order, inv, n1s, w, cosine, sine, qkv, o, lse, go, ghst, x, small)
+    )(order, inv, n1s, w, cosine, sine, qkv, o, lse, go, ghst, x, small, gsmall)
 
 
 def routing(raw, before, routes):
@@ -1496,43 +1568,35 @@
 ):
     count, width = tokens.shape[1], tokens.shape[2]
     ctx_size, packs = lax.axis_size("ctx"), lax.axis_size("fsdp")
-    groups = ctx_size // 2
     blk = count // 2
     seq = blk * ctx_size
     pack = lax.axis_index("fsdp")
     z, xx, y, k = place()
     sequence = z // 2
-    inner = GROUP_HEADS * HEAD_DIM
-    lanes = -(-inner // 128) * 128
     shard = width // packs
     f32, bf = jnp.float32, jnp.bfloat16
     everyone = ("ctx", "fsdp")
 
     cosine, sine = turn_tables(seq)
     routes_t = jnp.swapaxes(routes[:, 0], 1, 2)
+    smalls = jnp.concatenate([gains, const_values, jnp.swapaxes(router, 1, 2)], axis=1)
+    per_layer = smalls.shape[1]
     ints = jnp.concatenate([routes_t.reshape(-1), block_order[0]])
-    ints = jnp.pad(ints, (0, -ints.size % 1024)).reshape(-1, 128)
-    ints = lax.all_gather(ints, "fsdp", axis=0, tiled=False).reshape(packs, -1)
+    places = ints.size
+    ints = jnp.pad(ints, (0, -places % shard)).astype(bf).reshape(-1, shard)
+    smalls = jnp.concatenate([smalls.reshape(LAYERS * per_layer, shard), ints], axis=0)
+    smalls = jnp.pad(smalls, ((0, -smalls.shape[0] % 16), (0, 0)))
+    smalls = lax.all_gather(smalls, "fsdp", axis=1, tiled=True)
+    ints = smalls[LAYERS * per_layer : LAYERS * per_layer + ints.shape[0]].reshape(-1, packs, shard)
+    ints = jnp.swapaxes(ints, 0, 1).reshape(packs, -1).astype(jnp.int32)
+    smalls = [smalls[l * per_layer : (l + 1) * per_layer] for l in range(LAYERS)]
     near = jnp.stack([pack, 2 * y + 1 - k, 2 * (1 - y) + k, 2 * (1 - y) + 1 - k])
     routes_f = ints[near][:, : routes_t.size].reshape((packs,) + routes_t.shape)
-    order = lax.dynamic_index_in_dim(ints, 2 * y + xx, 0, keepdims=False)[routes_t.size : routes_t.size + 2 * ctx_size].reshape(ctx_size, 2)
+    order = lax.dynamic_index_in_dim(ints, 2 * y + xx, 0, keepdims=False)
+    order = order[routes_t.size : places].reshape(ctx_size, 2)
     order = lax.dynamic_index_in_dim(order, sequence, 1, keepdims=False) - ctx_size * sequence
     ids = jnp.arange(ctx_size, dtype=jnp.int32)
     inv = jnp.sum(jnp.where(order[None, :] == ids[:, None], ids[None, :], 0), axis=1)
-
-    smalls = jnp.concatenate([gains, const_values, jnp.swapaxes(router, 1, 2)], axis=1)
-    per_layer = smalls.shape[1]
-    smalls = lax.all_gather(smalls.reshape(LAYERS * per_layer, shard), "fsdp", axis=1, tiled=True)
-    smalls = [smalls[l * per_layer : (l + 1) * per_layer] for l in range(LAYERS)]
-    pairs = lax.dynamic_slice_in_dim(qkv_weights, 2 * inner * (z % 2), 2 * inner, axis=3)
-    pairs = pairs.reshape(LAYERS, 3, shard, 2, inner)
-    pairs = jnp.pad(pairs, ((0, 0),) * 4 + ((0, lanes - inner),))
-    pairs = jnp.transpose(pairs, (0, 3, 2, 1, 4)).reshape(LAYERS, 2, shard, 3 * lanes)
-    w_attn, w_out = [], []
-    for l in range(LAYERS):
-        send = jnp.concatenate([pairs[l], pairs[l]], axis=0)
-        w_attn.append(lax.all_to_all(send, "fsdp", 0, 0).reshape(width, 3 * lanes))
-        w_out.append(lax.all_gather(out_weight[l], "fsdp", axis=0, tiled=False))
 
     gm_all = [None, lax.all_gather(cotangent[0], everyone, axis=0, tiled=False)]
     x = tokens[0].astype(f32)
@@ -1541,13 +1605,15 @@
     for l in range(LAYERS):
         if l == 1:
             x, gm_all[1] = lax.optimization_barrier((x, gm_all[1]))
-        n1s, qkv, o, lse, ob, hst, ub = attn_forward(order, inv, x, smalls[l], w_attn[l], cosine, sine, w_out[l], 2 * l)
+        n1s, qkv, o, lse, ob, hst, ub, w, wo = attn_forward(
+            l, order, inv, x, smalls[l], qkv_weights, cosine, sine, out_weight, 2 * l
+        )
         ubf, table, ext, x_next = ffn_forward(
             l, ub, hst, smalls[l], routes_f[:, l], before, w_gate_up, w_down, 2 * l + 1
         )
         before = table[:, LOGI : LOGI + 16]
         ext_all[l] = lax.all_gather(ext, everyone, axis=0, tiled=False)
-        kept.append((x, n1s, qkv, o, lse, ob, hst, ubf, table))
+        kept.append((x, n1s, qkv, o, lse, ob, hst, w, wo, ubf, table))
         x = x_next
     output = x
     gm = cotangent[0]
@@ -1555,41 +1621,38 @@
     gprev = jnp.zeros((16, count), f32)
     small_grads, qkv_grads, out_grads = [None] * LAYERS, [None] * LAYERS, [None] * LAYERS
     for l in reversed(range(LAYERS)):
-        x, n1s, qkv, o, lse, ob, hst, ubf, table = kept[l]
+        x, n1s, qkv, o, lse, ob, hst, w, wo, ubf, table = kept[l]
         number = 2 * LAYERS + 2 * l
         gm, ext_all[l - 1 if l else 1] = lax.optimization_barrier((gm, ext_all[l - 1 if l else 1]))
         ghst, go, gwo, small, gprev = ffn_backward(
-            l, gm, gx, ubf, table, hst, smalls[l], routes_t[l], gprev, w_out[l], ob, w_gate_up, w_down, number
-        )
-        out_grads[l] = lax.psum_scatter(gwo, "fsdp", scatter_dimension=0, tiled=True)
-        gx, gm, gain_grad, gw = attn_backward(
-            order, inv, n1s, w_attn[l], cosine, sine, qkv, o, lse, go, ghst, x, smalls[l], number + 1
+            l, gm, gx, ubf, table, hst, smalls[l], routes_t[l], gprev, wo, ob, w_gate_up, w_down, number
+        )
+        gx, gm, gw = attn_backward(
+            order, inv, n1s, w, cosine, sine, qkv, o, lse, go, ghst, x, smalls[l], small, number + 1
         )
         if l > 0:
             gm_all[l - 1] = lax.all_gather(gm, everyone, axis=0, tiled=False)
-        small_grads[l] = jnp.concatenate([gain_grad, small], axis=0)
-        gw = gw.reshape(width, 3, lanes)[:, :, :inner].reshape(width, 1, 3 * inner)
-        gw = lax.dynamic_update_slice_in_dim(
-            jnp.zeros((width, groups, 3 * inner), bf), gw, 2 * (z % 2) + k, axis=1
-        ).reshape(width, 3 * width)
+            gw, gwo, gm_all[l - 1] = lax.optimization_barrier((gw, gwo, gm_all[l - 1]))
+        out_grads[l] = lax.psum_scatter(gwo, "fsdp", scatter_dimension=0, tiled=True)
         qkv_grads[l] = lax.psum_scatter(gw, "fsdp", scatter_dimension=0, tiled=True)
     done = ()
     for l in reversed(range(LAYERS)):
         x_all, g_all = dispatch(ext_all[l], gm_all[l])
         rows = x_all.shape[1] * x_all.shape[2]
         done = weight_grads(l, x_all.reshape(NF, rows, width), g_all.reshape(NF, rows, width), w_gate_up, w_down, done)
-    small = lax.psum(jnp.stack(small_grads).astype(bf), everyone)
-    small = lax.dynamic_slice_in_dim(small, pack * shard, shard, axis=2).astype(f32)
+        if l > 0:
+            qkv_grads, out_grads, done = lax.optimization_barrier((qkv_grads, out_grads, done))
     dense = jnp.concatenate([jnp.stack(qkv_grads), jnp.stack(out_grads)], axis=2)
     dense = lax.psum(dense, "ctx").astype(f32)
-    qkv_sum = dense[:, :, : 3 * width].reshape(LAYERS, shard, groups, 3, inner)
+    qkv_sum = jnp.stack([dense[:, :, c * width : (c + 1) * width] for c in range(3)], axis=1)
+    small = jnp.swapaxes(dense[:, :, 3 * width : 3 * width + 128], 1, 2)
     return (
         output[None],
         gx[None],
         small[:, :2],
-        jnp.transpose(qkv_sum, (0, 3, 1, 2, 4)).reshape(LAYERS, 3, shard, width),
-        dense[:, :, 3 * width :],
-        jnp.swapaxes(small[:, 2 + NC :], 1, 2),
+        qkv_sum,
+        dense[:, :, 3 * width + 128 :],
+        dense[:, :, 3 * width + 2 + NC : 3 * width + 2 + NC + 16],
         small[:, 2 : 2 + NC],
         done[0],
         done[1],

time: 985 us -> 986 us (level)
  waiting for transfers between devices: 58.9 us -> 235 us
  Pallas kernels: 752 us -> 692 us
  blocking collectives: 64.8 us -> 6.33 us
  local copies, waits for them, and re-layouts: 67 us -> 14.9 us
    all_gather x2, waiting for transfers between devices: 0.02 us -> 121 us  [by_heads(): ext_all[l] = lax.all_gather(ext, everyone, axis=0, tiled=False)]
    all_gather x1, waiting for transfers between devices: 0.01 us -> 102 us  [by_heads(): gm_all[l - 1] = lax.all_gather(gm, everyone, axis=0, tiled=False)]
    unnamed x13 -> x9, waiting for transfers between devices: 44.4 us -> 2 us
    psum x1 -> x0, blocking collectives: 40.7 us -> none  [by_heads(): small = lax.psum(jnp.stack(small_grads).astype(bf), everyone)]
    pallas_call x2, Pallas kernels: 120 us -> 93.9 us  [attn_backward(): pl.pallas_call(attn_bwd_kernel, out_shape=[shape_of((count, width), jnp.f...]
    pallas_call x2, Pallas kernels: 137 us -> 115 us  [attn_forward(): pl.pallas_call(attn_fwd_kernel, grid=(1,), out_shape=[shape_of((seq, widt...]
    all_gather x2 -> x1, blocking collectives: 24.1 us -> 6.33 us  [by_heads(): smalls = lax.all_gather(smalls, 'fsdp', axis=1, tiled=True)]
    pallas_call x2, Pallas kernels: 107 us -> 91 us  [ffn_backward(): pl.pallas_call(ffn_bwd_kernel, grid=(NF,), out_shape=outs, in_specs=[whol...]
  transfers between devices with their start and end apart: 13 -> 9, of which waited for: 2 -> 4; matrix products, arithmetic and copies ran while one was open for 5% -> 1% of each run, Pallas kernels for 77% -> 62%
where the time goes in v3:
time: 986 us; the launch traced here: 974 us
  Pallas kernels  692 us (70%)
  waiting for transfers between devices  235 us (24%)
  local copies, waits for them, and re-layouts  14.9 us (2%)
  between operations  14.6 us (1%)
  other arithmetic  11.5 us (1%)
    pallas_call x2, Pallas kernels, weight_grads(): pl.pallas_call(kernel, grid=(NF,), out_shape=[shape_of(wgu.shape, jnp.flo...  218 us
    all_gather x2, waiting for transfers between devices, by_heads(): ext_all[l] = lax.all_gather(ext, everyone, axis=0, tiled=False)  121 us
    pallas_call x2, Pallas kernels, attn_forward(): pl.pallas_call(attn_fwd_kernel, grid=(1,), out_shape=[shape_of((seq, widt...  115 us
    all_gather x1, waiting for transfers between devices, by_heads(): gm_all[l - 1] = lax.all_gather(gm, everyone, axis=0, tiled=False)  102 us
    pallas_call x2, Pallas kernels, ffn_forward(): pl.pallas_call(ffn_fwd_kernel, grid=(NF,), out_shape=outs, in_specs=[whol...  95.7 us
    pallas_call x2, Pallas kernels, attn_backward(): pl.pallas_call(attn_bwd_kernel, out_shape=[shape_of((count, width), jnp.f...  93.9 us
    pallas_call x2, Pallas kernels, ffn_backward(): pl.pallas_call(ffn_bwd_kernel, grid=(NF,), out_shape=outs, in_specs=[whol...  91 us
    pallas_call x2, Pallas kernels, dispatch(): pl.pallas_call(dispatch_kernel, grid=(devices,), out_shape=[outs, outs],...  78.9 us
  transfers between devices with their start and end apart: 9, of which 4 were waited for; matrix products, arithmetic and copies ran while one was open for 1% of the time, Pallas kernels for 62%

profile of v3, /device:TPU:0, one launch (start us, length us, event | category | flops | bytes accessed | tf_op | source)
XLA Modules:
  0.0 974.4 jit_solution(884397472678386552)
XLA Ops:
  7.2 0.0 all-gather.9.cloned.1.call-start
  7.2 0.7 all-gather.9.cloned.1.call-update
  7.9 0.0 all-gather.11.cloned.1.call-start
  8.0 0.7 pad_maximum_fusion.1
  8.8 0.7 convert_bitcast_fusion
  9.5 0.7 convert_bitcast_fusion.1
  10.2 0.1 reshape.226
  10.3 6.3 all-gather.3
  16.6 0.1 copy.45
  16.6 0.1 reshape.248
  16.8 0.1 reshape.235
  16.9 0.1 reshape.233
  17.0 0.1 dynamic-slice_reduce_fusion
  17.1 0.1 reshape.227
  17.1 0.1 fusion.7
  17.2 0.6 gather_fusion
  17.8 0.2 subtract_reduce_fusion.order
  18.0 0.6 select_reduce_fusion.inv
  18.6 0.6 fusion.9
  19.3 1.9 bitcast_convert_fusion.x
  21.2 55.4 %attn_fwd.2 = (bf16[1024,768]{1,0:T(8,128)(2,1)}, bf16[1024,768]{1,0:T(8,128)(2,1)}, f32[1024,256]{1,0:T(8,128)}, f32[1024,128]{1,0:T(8,128)}, bf16[8,128,256]{2...) custom-call(s32[8]{0:T(128)} %copy-done.5, ...), custom_call_target="tpu_custom_call" | custom-call | tf_op jit(solution)/shard_map/attn_fwd/pallas_call | solution.py:799
  76.6 0.6 slice_bitcast_fusion.4
  77.2 0.6 broadcast_in_dim.30.before
  77.9 46.4 %ffn_fwd.2 = (bf16[4,256,768]{2,1,0:T(8,128)(2,1)}, f32[4,56,256]{2,1,0:T(8,128)}, bf16[272,768]{1,0:T(8,128)(2,1)}, f32[256,768]{1,0:T(8,128)}) custom-call(bf16[256,768]{1,0:T(8,128)(2,1)} %get-tuple-element.72.ub, f32[256,768]{1,0:T(8,128)} %get-tuple-element.73.hst, bf16[20,768]{1,0:T(8,128)(2,1)} %get-tuple-element.177.small, ...), custom_call_target="tpu_custom_call" | custom-call | tf_op jit(solution)/shard_map/ffn_fwd/pallas_call | solution.py:1186
  124.3 0.0 all-gather.15.cloned.1.call-start
  124.4 1.5 slice.62.before
  125.9 0.6 slice_bitcast_fusion.6
  126.5 0.9 bitcast_convert_fusion.1.gx
  127.4 10.0 %all-gather.9.cloned.1.call-done.gm = bf16[32,256,768]{2,1,0:T(8,128)(2,1)} async-done(((bf16[1,256,768]{2,1,0:T(8,128)(2,1)}), bf16[32,256,768]{2,1,0:T(8,128)(2,1)}) %all-gather.9.cloned.1.call-update) | async-done | bytes 12582928 | tf_op jit(solution)/shard_map/all_gather | solution.py:1601
  137.4 59.2 %attn_fwd.3 = (bf16[1024,768]{1,0:T(8,128)(2,1)}, bf16[1024,768]{1,0:T(8,128)(2,1)}, f32[1024,256]{1,0:T(8,128)}, f32[1024,128]{1,0:T(8,128)}, bf16[8,128,256]{2...) custom-call(s32[8]{0:T(128)} %copy-done.5, ...), custom_call_target="tpu_custom_call" | custom-call | tf_op jit(solution)/shard_map/attn_fwd/pallas_call | solution.py:799
  196.6 49.2 %ffn_fwd.3 = (bf16[4,256,768]{2,1,0:T(8,128)(2,1)}, f32[4,56,256]{2,1,0:T(8,128)}, bf16[272,768]{1,0:T(8,128)(2,1)}, f32[256,768]{1,0:T(8,128)}) custom-call(bf16[256,768]{1,0:T(8,128)(2,1)} %get-tuple-element.76.ub, f32[256,768]{1,0:T(8,128)} %get-tuple-element.77.hst, bf16[20,768]{1,0:T(8,128)(2,1)} %get-tuple-element.176.small, ...), custom_call_target="tpu_custom_call" | custom-call | tf_op jit(solution)/shard_map/ffn_fwd/pallas_call | solution.py:1186
  245.9 20.7 %all-gather.11.cloned.1.call-done = bf16[8704,768]{1,0:T(8,128)(2,1)} async-done(((bf16[272,768]{1,0:T(8,128)(2,1)}), bf16[8704,768]{1,0:T(8,128)(2,1)}) %all-gather.11.cloned.1.call-update) | async-done | bytes 13369360 | tf_op jit(solution)/shard_map/all_gather | solution.py:1615
  266.6 0.6 broadcast_in_dim.32.gprev
  267.2 44.9 %ffn_bwd.2 = (f32[256,768]{1,0:T(8,128)}, bf16[8,128,256]{2,1,0:T(8,128)(2,1)}, bf16[768,768]{1,0:T(8,128)(2,1)}, f32[19,768]{1,0:T(8,128)}, f32[16,256]{1,0:T(8,128)}) custom-call(bf16[256,768]{1,0:T(8,128)(2,1)} %bitcast.71, f32[256,768]{1,0:T(8,128)} %bitcast_convert_fusion.1.gx, bf16[4,256,768]{2,1,0:T(8,128)(2,1)} %get-tuple-element.92.ubf, ...), custom_call_target="tpu_custom_call" | custom-call | tf_op jit(solution)/shard_map/ffn_bwd/pallas_call | solution.py:1338
  312.1 47.1 %attn_bwd.2 = (f32[256,768]{1,0:T(8,128)}, bf16[256,768]{1,0:T(8,128)(2,1)}, bf16[768,2432]{1,0:T(8,128)(2,1)}) custom-call(s32[8]{0:T(128)} %copy-done.5, s32[8]{0:T(128)} %select_reduce_fusion.inv, bf16[1024,768]{1,0:T(8,128)(2,1)} %get-tuple-element.85.n1s, bf16[768,768]{1,0:T(8,128)(2,1)} %get-tuple-element.86.w, f32[1024,128]{1,0:T(8,128)} %constant.76.clone.cosine, ...), custom_call_target="tpu_custom_call" | custom-call | tf_op jit(solution)/shard_map/attn_bwd/pallas_call | solution.py:992
  359.2 0.0 all-gather.13.cloned.1.call-start
  359.3 0.5 all-gather.13.cloned.1.call-update
  359.8 0.0 reduce-scatter.11.cloned.1.call-start
  359.8 101.8 %all-gather.15.cloned.1.call-done = bf16[8192,768]{1,0:T(8,128)(2,1)} async-done(((bf16[256,768]{1,0:T(8,128)(2,1)}), bf16[8192,768]{1,0:T(8,128)(2,1)}) %all-gather.15.cloned.1.call-update) | async-done | bytes 12582928 | tf_op jit(solution)/shard_map/all_gather | solution.py:1634
  461.7 0.0 reduce-scatter.9.cloned.1.call-start
  461.8 100.5 %all-gather.13.cloned.1.call-done = bf16[8704,768]{1,0:T(8,128)(2,1)} async-done(((bf16[272,768]{1,0:T(8,128)(2,1)}), bf16[8704,768]{1,0:T(8,128)(2,1)}) %all-gather.13.cloned.1.call-update) | async-done | bytes 13369360 | tf_op jit(solution)/shard_map/all_gather | solution.py:1615
  562.3 46.1 %ffn_bwd.3 = (f32[256,768]{1,0:T(8,128)}, bf16[8,128,256]{2,1,0:T(8,128)(2,1)}, bf16[768,768]{1,0:T(8,128)(2,1)}, f32[19,768]{1,0:T(8,128)}, f32[16,256]{1,0:T(8,128)}) custom-call(bf16[256,768]{1,0:T(8,128)(2,1)} %get-tuple-element.101.gm, f32[256,768]{1,0:T(8,128)} %get-tuple-element.102.gx, bf16[4,256,768]{2,1,0:T(8,128)(2,1)} %get-tuple-element.103.ubf, ...), custom_call_target="tpu_custom_call" | custom-call | tf_op jit(solution)/shard_map/ffn_bwd/pallas_call | solution.py:1338
  608.4 0.0 reduce-scatter.7.cloned.1.call-start
  608.4 0.7 reduce-scatter.7.cloned.1.call-update
  609.1 0.0 reduce-scatter.5.cloned.1.call-start
  609.2 46.8 %attn_bwd.3 = (f32[256,768]{1,0:T(8,128)}, bf16[256,768]{1,0:T(8,128)(2,1)}, bf16[768,2432]{1,0:T(8,128)(2,1)}) custom-call(s32[8]{0:T(128)} %copy-done.5, s32[8]{0:T(128)} %select_reduce_fusion.inv, bf16[1024,768]{1,0:T(8,128)(2,1)} %get-tuple-element.80.n1s, bf16[768,768]{1,0:T(8,128)(2,1)} %get-tuple-element.81.w, f32[1024,128]{1,0:T(8,128)} %constant.76.clone.cosine, ...), custom_call_target="tpu_custom_call" | custom-call | tf_op jit(solution)/shard_map/attn_bwd/pallas_call | solution.py:992
  656.0 0.0 all-reduce.4.cloned.1.call-start
  656.1 39.7 %dispatch.2 = (bf16[8,32,64,768]{3,2,1,0:T(8,128)(2,1)}, bf16[8,32,64,768]{3,2,1,0:T(8,128)(2,1)}) custom-call(bf16[32,272,768]{2,1,0:T(8,128)(2,1)} %bitcast.69, bf16[32,256,768]{2,1,0:T(8,128)(2,1)} %all-gather.9.cloned.1.call-done.gm), custom_call_target="tpu_custom_call" | custom-call | tf_op jit(solution)/shard_map/dispatch/pallas_call | solution.py:1382
  695.8 109.1 %weight_grads.2 = (f32[2,8,2,768,512]{4,3,2,1,0:T(8,128)}, f32[2,8,512,768]{3,2,1,0:T(8,128)}) custom-call(bf16[8,2048,768]{2,1,0:T(8,128)(2,1)} %bitcast.66, bf16[8,2048,768]{2,1,0:T(8,128)(2,1)} %bitcast.67, bf16[2,8,2,768,512]{4,3,2,1,0:T(8,128)(2,1)} %refs_2_.3, bf16[2,8,512,768]{3,2,1,0:T(8,128)(2,1)} %refs_3_.3), custom_call_target="tpu_custom_call" | custom-call | tf_op jit(solution)/shard_map/weight_grads/pallas_call | solution.py:1436
  804.9 3.3 maximum_maximum_fusion
  808.2 39.2 %dispatch.3 = (bf16[8,32,64,768]{3,2,1,0:T(8,128)(2,1)}, bf16[8,32,64,768]{3,2,1,0:T(8,128)(2,1)}) custom-call(bf16[32,272,768]{2,1,0:T(8,128)(2,1)} %bitcast.68, bf16[32,256,768]{2,1,0:T(8,128)(2,1)} %bitcast.70), custom_call_target="tpu_custom_call" | custom-call | tf_op jit(solution)/shard_map/dispatch/pallas_call | solution.py:1382
  847.4 108.5 %weight_grads.3 = (f32[2,8,2,768,512]{4,3,2,1,0:T(8,128)}, f32[2,8,512,768]{3,2,1,0:T(8,128)}) custom-call(bf16[8,2048,768]{2,1,0:T(8,128)(2,1)} %bitcast.64, bf16[8,2048,768]{2,1,0:T(8,128)(2,1)} %bitcast.65, bf16[2,8,2,768,512]{4,3,2,1,0:T(8,128)(2,1)} %refs_2_.3, bf16[2,8,512,768]{3,2,1,0:T(8,128)(2,1)} %refs_3_.3, ...), custom_call_target="tpu_custom_call", output_to_operand_aliasing={{0}: (4, {}), {1}: (5, {})} | custom-call | tf_op jit(solution)/shard_map/weight_grads/pallas_call | solution.py:1436
  955.9 2.0 convert_element_type.33
  957.9 0.3 slice_bitcast_fusion.2
  958.3 0.4 pad_maximum_fusion
  958.7 2.0 copy.50
  960.7 0.7 fusion.8
  961.4 1.6 copy.49
  963.1 0.7 copy.52
  963.8 0.1 slice.89
  963.9 0.7 copy.51
  964.6 1.1 slice.88
  965.7 0.9 copy.63
  966.6 0.9 copy.64
  (33 shorter events, 0.3 us)
Async XLA Ops:
  7.2 130.2 %all-gather.9.cloned.1.call-start = ((), (), s32[]{:S(2)}) async-start(), calls=%async_computation.4 | async-start | bytes 12976128 | tf_op jit(solution)/shard_map/all_gather | solution.py:1601
  7.9 258.7 %all-gather.11.cloned.1.call-start = ((), (), s32[]{:S(2)}) async-start(), calls=%async_computation.10 | async-start | bytes 13787136 | tf_op jit(solution)/shard_map/all_gather | solution.py:1615
  18.0 3.2 copy-start.5
  77.9 48.0 %copy-start.4 = (s32[2,1,256,2]{2,3,1,0:T(2,128)S(1)}, s32[2,1,256,2]{2,3,1,0:T(2,128)}, u32[]{:S(2)}) copy-start(s32[2,1,256,2]{2,3,1,0:T(2,128)} %param.17) | copy-start | bytes 12292
  77.9 48.6 %copy-start.1 = (bf16[1,256,768]{2,1,0:T(8,128)(2,1)S(1)}, bf16[1,256,768]{2,1,0:T(8,128)(2,1)}, u32[]{:S(2)}) copy-start(bf16[1,256,768]{2,1,0:T(8,128)(2,1)} %param.15) | copy-start | bytes 1179652
  124.3 337.3 %all-gather.15.cloned.1.call-start = ((), (), s32[]{:S(2)}) async-start(), calls=%async_computation.12 | async-start | bytes 12976128 | tf_op jit(solution)/shard_map/all_gather | solution.py:1634
  359.2 203.1 %all-gather.13.cloned.1.call-start = ((), (), s32[]{:S(2)}) async-start(), calls=%async_computation.11 | async-start | bytes 13787136 | tf_op jit(solution)/shard_map/all_gather | solution.py:1615
  359.8 445.0 %reduce-scatter.11.cloned.1.call-start = ((), (), s32[]{:S(2)}) async-start(), calls=%async_computation.8 | async-start | bytes 1474560 | tf_op jit(solution)/shard_map/reduce_scatter | solution.py:1636
  461.7 343.1 %reduce-scatter.9.cloned.1.call-start = ((), (), s32[]{:S(2)}) async-start(), calls=%async_computation.7 | async-start | bytes 1474560 | tf_op jit(solution)/shard_map/reduce_scatter | solution.py:1636
  608.4 196.5 %reduce-scatter.7.cloned.1.call-start = ((), (), s32[]{:S(2)}) async-start(), calls=%async_computation.6 | async-start | bytes 4669440 | tf_op jit(solution)/shard_map/reduce_scatter | solution.py:1637
  609.1 195.8 %reduce-scatter.5.cloned.1.call-start = ((), (), s32[]{:S(2)}) async-start(), calls=%async_computation.5 | async-start | bytes 4669440 | tf_op jit(solution)/shard_map/reduce_scatter | solution.py:1637
  656.0 299.9 %all-reduce.4.cloned.1.call-start = ((), (), s32[]{:S(2)}) async-start(), calls=%async_computation.9 | async-start | bytes 4915200 | tf_op jit(solution)/shard_map/psum | solution.py:1646
  958.7 5.1 copy-start
  960.7 5.0 copy-start.2
  964.6 2.0 copy-start.3
Sparse Core Ops, SparseCore 0:
  10.9 126.4 all-gather.8
  140.3 126.2 all-gather.10
  359.3 102.2 all-gather.14
  464.4 97.8 all-gather.12
  564.7 23.8 reduce-scatter.10
  608.5 23.9 reduce-scatter.8
  635.0 41.6 reduce-scatter.6
  679.4 41.6 reduce-scatter.4
  808.3 115.9 all-reduce.3

commit v4 on v3

--- a/solution.py
+++ b/solution.py
@@ -1,3 +1,5 @@
+import functools
+
 import jax
 import jax.numpy as jnp
 import numpy as np
@@ -506,9 +508,11 @@
 
 
 MINLEN = 1024
+GRAD_LANES = 768
 ROUT = 56
 RAW, COEF, SLOT, LOGI = 0, 16, 32, 40
 VMEM_MB = 60
+BRIEF = pl.CostEstimate(flops=1, bytes_accessed=1, transcendentals=0)
 
 
 def nt(a, b):
@@ -828,6 +832,7 @@
         + [dma((blocks,))] * 2
         + [dma((3,))] * 4,
         compiler_params=params_of(collective_id=number, has_side_effects=True),
+        cost_estimate=BRIEF,
         name="attn_fwd",
     )(order, inv, x, small, wq, cosine, sine, wo)
 
@@ -929,20 +934,13 @@
         def _():
             gnr[z] = gn_out[zz]
 
-    groups = depth
     inner = GROUP_HEADS * HEAD_DIM
-    gw[:, : 3 * width] = jnp.zeros((width, 3 * width), jnp.bfloat16)
+    gw[:, 128 + 3 * inner :] = jnp.zeros((width, gw.shape[1] - 128 - 3 * inner), jnp.bfloat16)
     for i in range(width // 256):
         part = slice(i * 256, (i + 1) * 256)
         piece = tn(n1s[:, part], grads[...].reshape(seq, 3 * lanes)).astype(jnp.bfloat16)
-        for group in range(groups):
-
-            @pl.when(2 * (z % 2) + k == group)
-            def _():
-                for c in range(3):
-                    first = c * width + group * inner
-                    gw[part, first : first + inner] = piece[:, c * lanes : c * lanes + inner]
-
+        for c in range(3):
+            gw[part, 128 + c * inner : 128 + (c + 1) * inner] = piece[:, c * lanes : c * lanes + inner]
     for zz in range(depth):
 
         @pl.when(jnp.logical_not(jnp.logical_and(same, zz == z)))
@@ -965,7 +963,7 @@
     gm[...] = grad.astype(jnp.bfloat16)
     sums = jnp.concatenate([jnp.sum(gn * base, axis=0, keepdims=True), gsmall[...]], axis=0)
     sums = jnp.concatenate([sums, jnp.zeros((128 - sums.shape[0], width), jnp.float32)], axis=0)
-    gw[:, 3 * width :] = jnp.transpose(sums).astype(jnp.bfloat16)
+    gw[:, :128] = jnp.transpose(sums).astype(jnp.bfloat16)
     for unit in range(blocks):
 
         @pl.when(jnp.logical_not(jnp.logical_and(same, unit == 2 * z + k)))
@@ -994,7 +992,7 @@
         out_shape=[
             shape_of((count, width), jnp.float32),
             shape_of((count, width), bf),
-            shape_of((width, 3 * width + 128), bf),
+            shape_of((width, GRAD_LANES), bf),
         ],
         in_specs=[sm] * 2 + [vm] * 12,
         out_specs=[vm] * 3,
@@ -1012,6 +1010,7 @@
         + [dma((blocks,))] * 2
         + [dma((depth,))] * 4,
         compiler_params=params_of(collective_id=number, has_side_effects=True),
+        cost_estimate=BRIEF,
         name="attn_bwd",
     )(order, inv, n1s, w, cosine, sine, qkv, o, lse, go, ghst, x, small, gsmall)
 
@@ -1203,6 +1202,7 @@
         + exchange_scratch(packs, count, width)
         + [pltpu.SemaphoreType.DMA((3,))] * 4,
         compiler_params=params_of(collective_id=number, has_side_effects=True),
+        cost_estimate=BRIEF,
         name="ffn_fwd",
     )(ub, hst, small, routes, before, wgu, wd)
 
@@ -1359,38 +1359,44 @@
         + exchange_scratch(packs, count, width)
         + [dma((3,))] * 6,
         compiler_params=params_of(collective_id=number, has_side_effects=True),
+        cost_estimate=BRIEF,
         name="ffn_bwd",
     )(*args, wgu, wd)
 
 
-def dispatch_kernel(ext, gm, x, g):
-    count = gm.shape[1]
-    rows = ext[0, count:, :].astype(jnp.float32)
+def slot_rows(ext, weighted):
+    rows = ext.astype(jnp.float32)
+    count = rows.shape[1] // 3
     coef, slot = rows[:NF, :count], rows[:NF, count : 2 * count].astype(jnp.int32)
-    ids = lax.broadcasted_iota(jnp.int32, (NF, MOST, count), 1)
-    hit = ids == slot[:, None, :]
-    hot = jnp.where(hit, 1.0, 0.0).astype(jnp.bfloat16).reshape(NF * MOST, count)
-    weighted = jnp.where(hit, coef[:, None, :], 0.0).astype(jnp.bfloat16).reshape(NF * MOST, count)
-    x[...] = nn(hot, ext[0, :count, :]).astype(jnp.bfloat16).reshape(x.shape)
-    g[...] = nn(weighted, gm[0]).astype(jnp.bfloat16).reshape(g.shape)
-
-
-def dispatch(ext, gm):
-    devices, count, width = gm.shape
-    grouped = pl.BlockSpec((NF, 1, MOST, width), lambda d: (0, d, 0, 0))
-    outs = shape_of((NF, devices, MOST, width), jnp.bfloat16)
-    return pl.pallas_call(
-        dispatch_kernel,
-        grid=(devices,),
-        out_shape=[outs, outs],
+    hit = lax.broadcasted_iota(jnp.int32, (NF, MOST, count), 1) == slot[:, None, :]
+    hot = jnp.where(hit, coef[:, None, :] if weighted else 1.0, 0.0)
+    return hot.astype(jnp.bfloat16).reshape(NF * MOST, count)
+
+
+def dispatch_kernel(rows, weighted, tail, values, out):
+    for d in range(values.shape[0]):
+        low = nn(slot_rows(tail[d], weighted), values[d, :rows, :]).astype(jnp.bfloat16)
+        out[:, d] = low.reshape(NF, MOST, low.shape[1])
+
+
+def dispatch(ext, values, weighted):
+    devices, _, width = ext.shape
+    rows = ext.shape[1] - 16
+    some = 4
+    out = pl.pallas_call(
+        functools.partial(dispatch_kernel, rows, weighted),
+        grid=(devices // some,),
+        out_shape=shape_of((NF, devices, MOST, width), jnp.bfloat16),
         in_specs=[
-            pl.BlockSpec((1,) + ext.shape[1:], lambda d: (d, 0, 0)),
-            pl.BlockSpec((1, count, width), lambda d: (d, 0, 0)),
+            pl.BlockSpec((some, 16, width), lambda d: (d, rows // 16, 0)),
+            pl.BlockSpec((some,) + values.shape[1:], lambda d: (d, 0, 0)),
         ],
-        out_specs=[grouped, grouped],
+        out_specs=pl.BlockSpec((NF, some, MOST, width), lambda d: (0, d, 0, 0)),
         compiler_params=params_of(),
+        cost_estimate=BRIEF,
         name="dispatch",
-    )(ext, gm)
+    )(ext, values)
+    return out.reshape(NF, devices * MOST, width)
 
 
 def dw_kernel(*refs):
@@ -1426,22 +1432,22 @@
     lax.fori_loop(0, hid_s.shape[1] // 256, second, 0)
 
 
-def weight_grads(layer, x, g, wgu, wd, earlier):
+def weight_grads(layer, first, last, x, g, wgu, wd, earlier):
     _, rows, width = x.shape
     hidden = wd.shape[2]
-    gu_spec = pl.BlockSpec((1, 1, 2, width, hidden), lambda e: (layer, e, 0, 0, 0))
-    d_spec = pl.BlockSpec((1, 1, hidden, width), lambda e: (layer, e, 0, 0))
-    row_spec = pl.BlockSpec((1, rows, width), lambda e: (e, 0, 0))
-    kernel = dw_kernel
+    gu_spec = pl.BlockSpec((1, 1, 2, width, hidden), lambda e: (layer, e + first, 0, 0, 0))
+    d_spec = pl.BlockSpec((1, 1, hidden, width), lambda e: (layer, e + first, 0, 0))
+    row_spec = pl.BlockSpec((1, rows, width), lambda e: (e + first, 0, 0))
     return pl.pallas_call(
-        kernel,
-        grid=(NF,),
+        dw_kernel,
+        grid=(last - first,),
         out_shape=[shape_of(wgu.shape, jnp.float32), shape_of(wd.shape, jnp.float32)],
         in_specs=[row_spec, row_spec, gu_spec, d_spec] + [pl.BlockSpec(memory_space=pl.ANY)] * len(earlier),
         out_specs=[gu_spec, d_spec],
         input_output_aliases={4 + i: i for i in range(len(earlier))},
         scratch_shapes=[pltpu.VMEM((rows, hidden), jnp.bfloat16)] * 3,
         compiler_params=params_of(),
+        cost_estimate=BRIEF,
         name="weight_grads",
     )(x, g, wgu, wd, *earlier)
 
@@ -1603,11 +1609,11 @@
     before = jnp.zeros((packs, 16, count), f32)
     kept, ext_all = [], [None] * LAYERS
     for l in range(LAYERS):
-        if l == 1:
-            x, gm_all[1] = lax.optimization_barrier((x, gm_all[1]))
         n1s, qkv, o, lse, ob, hst, ub, w, wo = attn_forward(
             l, order, inv, x, smalls[l], qkv_weights, cosine, sine, out_weight, 2 * l
         )
+        if l == 1:
+            ub, gm_all[1] = lax.optimization_barrier((ub, gm_all[1]))
         ubf, table, ext, x_next = ffn_forward(
             l, ub, hst, smalls[l], routes_f[:, l], before, w_gate_up, w_down, 2 * l + 1
         )
@@ -1619,40 +1625,78 @@
     gm = cotangent[0]
     gx = gm.astype(f32)
     gprev = jnp.zeros((16, count), f32)
-    small_grads, qkv_grads, out_grads = [None] * LAYERS, [None] * LAYERS, [None] * LAYERS
+    grads = [None] * LAYERS
     for l in reversed(range(LAYERS)):
         x, n1s, qkv, o, lse, ob, hst, w, wo, ubf, table = kept[l]
         number = 2 * LAYERS + 2 * l
-        gm, ext_all[l - 1 if l else 1] = lax.optimization_barrier((gm, ext_all[l - 1 if l else 1]))
         ghst, go, gwo, small, gprev = ffn_backward(
             l, gm, gx, ubf, table, hst, smalls[l], routes_t[l], gprev, wo, ob, w_gate_up, w_down, number
         )
+        if l == 1:
+            go, ext_all[0] = lax.optimization_barrier((go, ext_all[0]))
         gx, gm, gw = attn_backward(
             order, inv, n1s, w, cosine, sine, qkv, o, lse, go, ghst, x, smalls[l], small, number + 1
         )
         if l > 0:
             gm_all[l - 1] = lax.all_gather(gm, everyone, axis=0, tiled=False)
-            gw, gwo, gm_all[l - 1] = lax.optimization_barrier((gw, gwo, gm_all[l - 1]))
-        out_grads[l] = lax.psum_scatter(gwo, "fsdp", scatter_dimension=0, tiled=True)
-        qkv_grads[l] = lax.psum_scatter(gw, "fsdp", scatter_dimension=0, tiled=True)
-    done = ()
-    for l in reversed(range(LAYERS)):
-        x_all, g_all = dispatch(ext_all[l], gm_all[l])
-        rows = x_all.shape[1] * x_all.shape[2]
-        done = weight_grads(l, x_all.reshape(NF, rows, width), g_all.reshape(NF, rows, width), w_gate_up, w_down, done)
-        if l > 0:
-            qkv_grads, out_grads, done = lax.optimization_barrier((qkv_grads, out_grads, done))
-    dense = jnp.concatenate([jnp.stack(qkv_grads), jnp.stack(out_grads)], axis=2)
-    dense = lax.psum(dense, "ctx").astype(f32)
-    qkv_sum = jnp.stack([dense[:, :, c * width : (c + 1) * width] for c in range(3)], axis=1)
-    small = jnp.swapaxes(dense[:, :, 3 * width : 3 * width + 128], 1, 2)
+        grads[l] = jnp.concatenate([gw, gwo], axis=1)
+
+    inner = GROUP_HEADS * HEAD_DIM
+    dense = jnp.stack(grads).reshape(LAYERS, packs // 2, 2, shard, 2 * width)
+    mine = lax.dynamic_index_in_dim(dense, k, 2, keepdims=False)
+    theirs = lax.dynamic_index_in_dim(dense, 1 - k, 2, keepdims=False)
+    got = lax.ppermute(theirs, "fsdp", [(i, i ^ 1) for i in range(packs)])
+    x0 = dispatch(ext_all[0], ext_all[0], False)
+    x0, got = lax.optimization_barrier((x0, got))
+
+    def ordered(swap, first, second):
+        return jnp.concatenate([jnp.where(swap, second, first), jnp.where(swap, first, second)], axis=-1)
+
+    def added(first, second):
+        return (first.astype(f32) + second.astype(f32)).astype(bf)
+
+    def split(values):
+        return values[..., 128 : 128 + 3 * inner], jnp.concatenate([values[..., :128], values[..., width:]], axis=-1)
+
+    (qkv_mine, rest_mine), (qkv_got, rest_got) = split(mine), split(got)
+    dense = jnp.concatenate([ordered(k == 1, qkv_mine, qkv_got), added(rest_mine, rest_got)], axis=-1)
+    mine = lax.dynamic_index_in_dim(dense, y, 1, keepdims=False)
+    theirs = lax.dynamic_index_in_dim(dense, 1 - y, 1, keepdims=False)
+    theirs, ext_all[1] = lax.optimization_barrier((theirs, ext_all[1]))
+    got = lax.ppermute(theirs, "fsdp", [(i, i ^ 2) for i in range(packs)])
+    x1 = dispatch(ext_all[1], ext_all[1], False)
+    g1 = dispatch(ext_all[1], gm_all[1], True)
+    x1, g1, got = lax.optimization_barrier((x1, g1, got))
+    dense = added(mine, got)
+    dense, x1 = lax.optimization_barrier((dense, x1))
+    got = lax.ppermute(dense, "ctx", [(i, i ^ 1) for i in range(ctx_size)])
+    done = weight_grads(1, 0, NF // 2, x1, g1, w_gate_up, w_down, ())
+    done, got = lax.optimization_barrier((done, got))
+    dense = added(dense, got)
+    dense, done = lax.optimization_barrier((dense, done))
+    got = lax.ppermute(dense, "ctx", [(i, i ^ 4) for i in range(ctx_size)])
+    done = weight_grads(1, NF // 2, NF, x1, g1, w_gate_up, w_down, done)
+    done, gm_all[0] = lax.optimization_barrier((done, gm_all[0]))
+    g0 = dispatch(ext_all[0], gm_all[0], True)
+    g0, got = lax.optimization_barrier((g0, got))
+    dense = added(dense, got)
+    dense, g0 = lax.optimization_barrier((dense, g0))
+    got = lax.ppermute(dense, "ctx", [(i, i ^ 2) for i in range(ctx_size)])
+    done = weight_grads(0, 0, NF // 2, x0, g0, w_gate_up, w_down, done)
+    done, got = lax.optimization_barrier((done, got))
+    pairs = 6 * inner
+    rest = dense[..., pairs:].astype(f32) + got[..., pairs:].astype(f32)
+    qkv = ordered(z % 2 == 1, dense[..., :pairs], got[..., :pairs]).reshape(LAYERS, shard, 4, 3, inner)
+    qkv = jnp.stack([qkv[:, :, :, c, :].reshape(LAYERS, shard, width) for c in range(3)], axis=1).astype(f32)
+    small = jnp.swapaxes(rest[..., :128], 1, 2)
+    done = weight_grads(0, NF // 2, NF, x0, g0, w_gate_up, w_down, done)
     return (
         output[None],
         gx[None],
         small[:, :2],
-        qkv_sum,
-        dense[:, :, 3 * width + 128 :],
-        dense[:, :, 3 * width + 2 + NC : 3 * width + 2 + NC + 16],
+        qkv,
+        rest[..., 128:],
+        rest[..., 2 + NC : 2 + NC + 16],
         small[:, 2 : 2 + NC],
         done[0],
         done[1],

time: 986 us -> 873 us (0.89)
  waiting for transfers between devices: 235 us -> 1.57 us
  Pallas kernels: 692 us -> 771 us
  starting transfers between devices: 0.36 us -> 17.9 us
  local copies, waits for them, and re-layouts: 14.9 us -> 31.8 us
  other arithmetic: 11.5 us -> 23 us
    all_gather x2, waiting for transfers between devices: 121 us -> 0.02 us  [by_heads(): ext_all[l] = lax.all_gather(ext, everyone, axis=0, tiled=False)]
    all_gather x1, waiting for transfers between devices: 102 us -> 0.01 us  [by_heads(): gm_all[l - 1] = lax.all_gather(gm, everyone, axis=0, tiled=False)]
    pallas_call x2, Pallas kernels: 93.9 us -> 162 us  [attn_backward(): pl.pallas_call(attn_bwd_kernel, out_shape=[shape_of((count, width), jnp.f...]
    ppermute x0 -> x5, starting transfers between devices: none -> 17.6 us  [the longest x1 6.4 us: by_heads(): got = lax.ppermute(dense, 'ctx', [(i, i ^ 4) for i in range(ctx_size)])]
    all_gather x1, waiting for transfers between devices: 9.98 us -> 0.01 us  [by_heads(): gm_all = [None, lax.all_gather(cotangent[0], everyone, axis=0, tiled=False)]]
    pallas_call x4 -> x8, Pallas kernels: 296 us -> 297 us  [the longest x4 228 us: weight_grads(): pl.pallas_call(dw_kernel, grid=(last - first,), out_shape=[shape_of(wgu.s...]
  transfers between devices with their start and end apart: 9 -> 9, of which waited for: 4 -> 1; matrix products, arithmetic and copies ran while one was open for 1% -> 4% of each run, Pallas kernels for 62% -> 82%
where the time goes in v4:
time: 873 us; the launch traced here: 866 us
  Pallas kernels  771 us (88%)
  local copies, waits for them, and re-layouts  31.8 us (4%)
  other arithmetic  23 us (3%)
  starting transfers between devices  17.9 us (2%)
  between operations  14.7 us (2%)
    pallas_call x4, Pallas kernels, weight_grads(): pl.pallas_call(dw_kernel, grid=(last - first,), out_shape=[shape_of(wgu.s...  228 us
    pallas_call x2, Pallas kernels, attn_backward(): pl.pallas_call(attn_bwd_kernel, out_shape=[shape_of((count, width), jnp.f...  162 us
    pallas_call x2, Pallas kernels, attn_forward(): pl.pallas_call(attn_fwd_kernel, grid=(1,), out_shape=[shape_of((seq, widt...  124 us
    pallas_call x2, Pallas kernels, ffn_forward(): pl.pallas_call(ffn_fwd_kernel, grid=(NF,), out_shape=outs, in_specs=[whol...  95.5 us
    pallas_call x2, Pallas kernels, ffn_backward(): pl.pallas_call(ffn_bwd_kernel, grid=(NF,), out_shape=outs, in_specs=[whol...  91.9 us
    pallas_call x4, Pallas kernels, dispatch(): pl.pallas_call(functools.partial(dispatch_kernel, rows, weighted), grid=(...  68.9 us
  transfers between devices with their start and end apart: 9, of which 1 were waited for; matrix products, arithmetic and copies ran while one was open for 4% of the time, Pallas kernels for 82%

profile of v4, /device:TPU:0, one launch (start us, length us, event | category | flops | bytes accessed | tf_op | source)
XLA Modules:
  0.0 865.8 jit_solution(4250315298692414997)
XLA Ops:
  7.2 0.7 all-gather.9.cloned.1.call-update
  8.0 0.7 convert_bitcast_fusion
  8.7 0.7 convert_bitcast_fusion.1
  9.5 0.7 pad_maximum_fusion.3
  10.2 6.3 all-gather.3
  17.3 0.6 select_reduce_fusion.inv
  17.9 0.6 fusion.14
  18.6 1.9 bitcast_convert_fusion.x
  20.5 56.0 %attn_fwd.2 = (bf16[1024,768]{1,0:T(8,128)(2,1)}, bf16[1024,768]{1,0:T(8,128)(2,1)}, f32[1024,256]{1,0:T(8,128)}, f32[1024,128]{1,0:T(8,128)}, bf16[8,128,256]{2...) custom-call(s32[8]{0:T(128)} %copy-done.8, ...), custom_call_target="tpu_custom_call" | custom-call | flops 1 | bytes 1 | tf_op jit(solution)/shard_map/attn_fwd/pallas_call | solution.py:803
  76.7 0.6 gather_fusion
  77.3 0.6 slice_bitcast_fusion.1
  77.9 0.6 broadcast_in_dim.30.before
  78.5 46.3 %ffn_fwd.2 = (bf16[4,256,768]{2,1,0:T(8,128)(2,1)}, f32[4,56,256]{2,1,0:T(8,128)}, bf16[272,768]{1,0:T(8,128)(2,1)}, f32[256,768]{1,0:T(8,128)}) custom-call(bf16[256,768]{1,0:T(8,128)(2,1)} %get-tuple-element.86.ub, f32[256,768]{1,0:T(8,128)} %get-tuple-element.87.hst, bf16[20,768]{1,0:T(8,128)(2,1)} %get-tuple-element.229.small, ...), custom_call_target="tpu_custom_call" | custom-call | flops 1 | bytes 1 | tf_op jit(solution)/shard_map/ffn_fwd/pallas_call | solution.py:1185
  124.8 67.9 %attn_fwd.3 = (bf16[1024,768]{1,0:T(8,128)(2,1)}, bf16[1024,768]{1,0:T(8,128)(2,1)}, f32[1024,256]{1,0:T(8,128)}, f32[1024,128]{1,0:T(8,128)}, bf16[8,128,256]{2...) custom-call(s32[8]{0:T(128)} %copy-done.8, ...), custom_call_target="tpu_custom_call" | custom-call | flops 1 | bytes 1 | tf_op jit(solution)/shard_map/attn_fwd/pallas_call | solution.py:803
  192.8 1.5 slice.92.before
  194.2 49.2 %ffn_fwd.3 = (bf16[4,256,768]{2,1,0:T(8,128)(2,1)}, f32[4,56,256]{2,1,0:T(8,128)}, bf16[272,768]{1,0:T(8,128)(2,1)}, f32[256,768]{1,0:T(8,128)}) custom-call(bf16[256,768]{1,0:T(8,128)(2,1)} %get-tuple-element.90.ub, f32[256,768]{1,0:T(8,128)} %get-tuple-element.91.hst, bf16[20,768]{1,0:T(8,128)(2,1)} %get-tuple-element.228.small, ...), custom_call_target="tpu_custom_call" | custom-call | flops 1 | bytes 1 | tf_op jit(solution)/shard_map/ffn_fwd/pallas_call | solution.py:1185
  243.7 0.6 slice_bitcast_fusion.3
  244.3 0.9 bitcast_convert_fusion.1.gx
  245.2 0.6 broadcast_in_dim.32.gprev
  245.8 46.9 %ffn_bwd.2 = (f32[256,768]{1,0:T(8,128)}, bf16[8,128,256]{2,1,0:T(8,128)(2,1)}, bf16[768,768]{1,0:T(8,128)(2,1)}, f32[19,768]{1,0:T(8,128)}, f32[16,256]{1,0:T(8,128)}) custom-call(bf16[256,768]{1,0:T(8,128)(2,1)} %bitcast.91, f32[256,768]{1,0:T(8,128)} %bitcast_convert_fusion.1.gx, bf16[4,256,768]{2,1,0:T(8,128)(2,1)} %get-tuple-element.104.ubf, ...), custom_call_target="tpu_custom_call" | custom-call | flops 1 | bytes 1 | tf_op jit(solution)/shard_map/ffn_bwd/pallas_call | solution.py:1338
  292.8 82.7 %attn_bwd.2 = (f32[256,768]{1,0:T(8,128)}, bf16[256,768]{1,0:T(8,128)(2,1)}, bf16[768,768]{1,0:T(8,128)(2,1)}) custom-call(s32[8]{0:T(128)} %copy-done.8, s32[8]{0:T(128)} %select_reduce_fusion.inv, bf16[1024,768]{1,0:T(8,128)(2,1)} %get-tuple-element.99.n1s, bf16[768,768]{1,0:T(8,128)(2,1)} %get-tuple-element.100.w, f32[1024,128]{1,0:T(8,128)} %constant.95.clone.cosine, ...), custom_call_target="tpu_custom_call" | custom-call | flops 1 | bytes 1 | tf_op jit(solution)/shard_map/attn_bwd/pallas_call | solution.py:990
  375.6 45.0 %ffn_bwd.3 = (f32[256,768]{1,0:T(8,128)}, bf16[8,128,256]{2,1,0:T(8,128)(2,1)}, bf16[768,768]{1,0:T(8,128)(2,1)}, f32[19,768]{1,0:T(8,128)}, f32[16,256]{1,0:T(8,128)}) custom-call(bf16[256,768]{1,0:T(8,128)(2,1)} %get-tuple-element.113.gm, f32[256,768]{1,0:T(8,128)} %get-tuple-element.114.gx, bf16[4,256,768]{2,1,0:T(8,128)(2,1)} %get-tuple-element.115.ubf, ...), custom_call_target="tpu_custom_call" | custom-call | flops 1 | bytes 1 | tf_op jit(solution)/shard_map/ffn_bwd/pallas_call | solution.py:1338
  420.6 79.5 %attn_bwd.3 = (f32[256,768]{1,0:T(8,128)}, bf16[256,768]{1,0:T(8,128)(2,1)}, bf16[768,768]{1,0:T(8,128)(2,1)}) custom-call(s32[8]{0:T(128)} %copy-done.8, s32[8]{0:T(128)} %select_reduce_fusion.inv, bf16[1024,768]{1,0:T(8,128)(2,1)} %get-tuple-element.94.n1s, bf16[768,768]{1,0:T(8,128)(2,1)} %get-tuple-element.95.w, f32[1024,128]{1,0:T(8,128)} %constant.95.clone.cosine, ...), custom_call_target="tpu_custom_call" | custom-call | flops 1 | bytes 1 | tf_op jit(solution)/shard_map/attn_bwd/pallas_call | solution.py:990
  500.1 1.6 pad_maximum_fusion
  501.8 0.4 copy-done.3
  502.3 1.9 fusion.1
  504.2 0.5 collective-permute-start
  504.7 17.4 %dispatch.4 = bf16[8,32,64,768]{3,2,1,0:T(8,128)(2,1)} custom-call(bf16[32,272,768]{2,1,0:T(8,128)(2,1)} %bitcast.78, bf16[32,272,768]{2,1,0:T(8,128)(2,1)} %bitcast.79), custom_call_target="tpu_custom_call" | custom-call | flops 1 | bytes 1 | tf_op jit(solution)/shard_map/dispatch/pallas_call | solution.py:1386
  522.4 1.8 copy.93
  524.3 1.5 add_convert_fusion.2
  525.8 2.9 broadcast_select_fusion
  528.6 5.1 concatenate.55
  533.8 1.3 dynamic-slice_bitcast_fusion
  535.0 1.5 collective-permute-start.1
  536.5 17.3 %dispatch.5 = bf16[8,32,64,768]{3,2,1,0:T(8,128)(2,1)} custom-call(bf16[32,272,768]{2,1,0:T(8,128)(2,1)} %bitcast.81, bf16[32,272,768]{2,1,0:T(8,128)(2,1)} %bitcast.82), custom_call_target="tpu_custom_call" | custom-call | flops 1 | bytes 1 | tf_op jit(solution)/shard_map/dispatch/pallas_call | solution.py:1386
  553.8 17.0 %dispatch.6 = bf16[8,32,64,768]{3,2,1,0:T(8,128)(2,1)} custom-call(bf16[32,272,768]{2,1,0:T(8,128)(2,1)} %bitcast.83, bf16[32,256,768]{2,1,0:T(8,128)(2,1)} %all-gather.9.cloned.1.call-done.values), custom_call_target="tpu_custom_call" | custom-call | flops 1 | bytes 1 | tf_op jit(solution)/shard_map/dispatch/pallas_call | solution.py:1386
  570.8 0.8 collective-permute-done.1
  571.6 3.2 fusion
  574.8 3.4 collective-permute-start.2
  578.2 57.0 %weight_grads.4 = (f32[2,8,2,768,512]{4,3,2,1,0:T(8,128)}, f32[2,8,512,768]{3,2,1,0:T(8,128)}) custom-call(bf16[8,2048,768]{2,1,0:T(8,128)(2,1)} %bitcast.74, bf16[8,2048,768]{2,1,0:T(8,128)(2,1)} %bitcast.76, bf16[2,8,2,768,512]{4,3,2,1,0:T(8,128)(2,1)} %refs_2_.7, bf16[2,8,512,768]{3,2,1,0:T(8,128)(2,1)} %refs_3_.7), custom_call_target="tpu_custom_call" | custom-call | flops 1 | bytes 1 | tf_op jit(solution)/shard_map/weight_grads/pallas_call | solution.py:1441
  635.2 2.0 add_convert_fusion.1
  637.2 6.4 collective-permute-start.3
  643.6 57.0 %weight_grads.5 = (f32[2,8,2,768,512]{4,3,2,1,0:T(8,128)}, f32[2,8,512,768]{3,2,1,0:T(8,128)}) custom-call(bf16[8,2048,768]{2,1,0:T(8,128)(2,1)} %bitcast.75, bf16[8,2048,768]{2,1,0:T(8,128)(2,1)} %bitcast.77, bf16[2,8,2,768,512]{4,3,2,1,0:T(8,128)(2,1)} %refs_2_.7, bf16[2,8,512,768]{3,2,1,0:T(8,128)(2,1)} %refs_3_.7, ...), custom_call_target="tpu_custom_call", output_to_operand_aliasing={{0}: (4, {}), {1}: (5, {})} | custom-call | flops 1 | bytes 1 | tf_op jit(solution)/shard_map/weight_grads/pallas_call | solution.py:1441
  700.6 17.2 %dispatch.7 = bf16[8,32,64,768]{3,2,1,0:T(8,128)(2,1)} custom-call(bf16[32,272,768]{2,1,0:T(8,128)(2,1)} %bitcast.80, bf16[32,256,768]{2,1,0:T(8,128)(2,1)} %bitcast.84), custom_call_target="tpu_custom_call" | custom-call | flops 1 | bytes 1 | tf_op jit(solution)/shard_map/dispatch/pallas_call | solution.py:1386
  717.9 1.1 copy-done.1
  719.0 2.0 add_convert_fusion
  721.0 5.7 collective-permute-start.4
  726.7 57.0 %weight_grads.6 = (f32[2,8,2,768,512]{4,3,2,1,0:T(8,128)}, f32[2,8,512,768]{3,2,1,0:T(8,128)}) custom-call(bf16[8,2048,768]{2,1,0:T(8,128)(2,1)} %bitcast.70, bf16[8,2048,768]{2,1,0:T(8,128)(2,1)} %bitcast.72, bf16[2,8,2,768,512]{4,3,2,1,0:T(8,128)(2,1)} %refs_2_.7, bf16[2,8,512,768]{3,2,1,0:T(8,128)(2,1)} %refs_3_.7, ...), custom_call_target="tpu_custom_call", output_to_operand_aliasing={{0}: (4, {}), {1}: (5, {})} | custom-call | flops 1 | bytes 1 | tf_op jit(solution)/shard_map/weight_grads/pallas_call | solution.py:1441
  784.0 1.1 slice.134
  785.2 0.7 fusion.13
  786.0 1.6 copy.101
  787.8 1.3 pad_maximum_fusion.2
  789.1 2.7 copy.97
  791.8 1.3 fusion.12
  793.1 1.4 copy.107
  794.5 1.4 copy.106
  795.9 0.3 copy.105
  796.2 0.3 maximum_convert_fusion
  796.5 2.0 copy.102
  798.5 0.7 copy.103
  799.2 0.7 copy.104
  799.9 57.1 %weight_grads.7 = (f32[2,8,2,768,512]{4,3,2,1,0:T(8,128)}, f32[2,8,512,768]{3,2,1,0:T(8,128)}) custom-call(bf16[8,2048,768]{2,1,0:T(8,128)(2,1)} %bitcast.71, bf16[8,2048,768]{2,1,0:T(8,128)(2,1)} %bitcast.73, bf16[2,8,2,768,512]{4,3,2,1,0:T(8,128)(2,1)} %refs_2_.7, bf16[2,8,512,768]{3,2,1,0:T(8,128)(2,1)} %refs_3_.7, ...), custom_call_target="tpu_custom_call", output_to_operand_aliasing={{0}: (4, {}), {1}: (5, {})} | custom-call | flops 1 | bytes 1 | tf_op jit(solution)/shard_map/weight_grads/pallas_call | solution.py:1441
  857.0 0.9 copy.125
  857.9 0.9 copy.126
  (59 shorter events, 2.5 us)
Async XLA Ops:
  7.2 187.1 %all-gather.9.cloned.1.call-start = ((), (), s32[]{:S(2)}) async-start(), calls=%async_computation | async-start | bytes 12976128 | tf_op jit(solution)/shard_map/all_gather | solution.py:1607
  7.9 284.9 %all-gather.11.cloned.1.call-start = ((), (), s32[]{:S(2)}) async-start(), calls=%async_computation.1 | async-start | bytes 13787136 | tf_op jit(solution)/shard_map/all_gather | solution.py:1621
  17.3 3.2 copy-start.8
  124.8 410.2 %all-gather.13.cloned.1.call-start = ((), (), s32[]{:S(2)}) async-start(), calls=%async_computation.2 | async-start | bytes 13787136 | tf_op jit(solution)/shard_map/all_gather | solution.py:1621
  194.2 49.5 %copy-start.7 = (s32[2,1,256,2]{2,3,1,0:T(2,128)S(1)}, s32[2,1,256,2]{2,3,1,0:T(2,128)}, u32[]{:S(2)}) copy-start(s32[2,1,256,2]{2,3,1,0:T(2,128)} %param.17) | copy-start | bytes 12292
  194.2 50.1 %copy-start = (bf16[1,256,768]{2,1,0:T(8,128)(2,1)S(1)}, bf16[1,256,768]{2,1,0:T(8,128)(2,1)}, u32[]{:S(2)}) copy-start(bf16[1,256,768]{2,1,0:T(8,128)(2,1)} %param.15) | copy-start | bytes 1179652
  243.5 457.1 %all-gather.15.cloned.1.call-start = ((), (), s32[]{:S(2)}) async-start(), calls=%async_computation.3 | async-start | bytes 12976128 | tf_op jit(solution)/shard_map/all_gather | solution.py:1641
  420.6 79.5 %copy-start.4 = (bf16[768,768]{1,0:T(8,128)(2,1)S(1)}, bf16[768,768]{1,0:T(8,128)(2,1)}, u32[]{:S(2)}) copy-start(bf16[768,768]{1,0:T(8,128)(2,1)} %get-tuple-element.125) | copy-start | bytes 3538948
  500.1 1.7 copy-start.2
  500.1 2.0 copy-start.3
  504.2 18.2 %collective-permute-start = (bf16[2,2,192,1536]{3,2,1,0:T(8,128)(2,1)}, bf16[2,2,192,1536]{3,2,1,0:T(8,128)(2,1)}, u32[]{:S(2)}, u32[]{:S(2)}) collective-permute-start(bf16[2,2,192,1536]{3,2,1,0:T(8,128)(2,1)} %get-tuple-element.220), channel_id=1, source_target_pairs={{0,1},{1,0},{2,3},{3,2},{4,5},{5,4},{6,7},{7,6},{8,9},{9,8},{10,11... | collective-permute-start | bytes 7077896 | tf_op jit(solution)/shard_map/ppermute | solution.py:1648
  535.0 36.6 %collective-permute-start.1 = (bf16[2,192,2048]{2,1,0:T(8,128)(2,1)}, bf16[2,192,2048]{2,1,0:T(8,128)(2,1)}, u32[]{:S(2)}, u32[]{:S(2)}) collective-permute-start(bf16[2,192,2048]{2,1,0:T(8,128)(2,1)} %dynamic-slice_bitcast_fusion), channel_id=1, source_target_pairs={{0,2},{1,3},{2,0},{3,1},{4,6},{5,7},{6,4},{7,5},{8,10},{9,11},{10,... | collective-permute-start | bytes 4718600 | tf_op jit(solution)/shard_map/ppermute | solution.py:1666
  574.8 60.4 %collective-permute-start.2 = (bf16[2,192,2048]{2,1,0:T(8,128)(2,1)}, bf16[2,192,2048]{2,1,0:T(8,128)(2,1)S(1)}, u32[]{:S(2)}, u32[]{:S(2)}) collective-permute-start(bf16[2,192,2048]{2,1,0:T(8,128)(2,1)} %fusion), channel_id=1, source_target_pairs={{0,4},{4,0},{8,12},{12,8},{16,20},{20,16},{24,28},{28,24},{1,5},{5... | collective-permute-start | bytes 4718600 | tf_op jit(solution)/shard_map/ppermute | solution.py:1672
  637.2 80.6 %collective-permute-start.3 = (bf16[2,192,2048]{2,1,0:T(8,128)(2,1)S(1)}, bf16[2,192,2048]{2,1,0:T(8,128)(2,1)S(1)}, u32[]{:S(2)}, u32[]{:S(2)}) collective-permute-start(bf16[2,192,2048]{2,1,0:T(8,128)(2,1)S(1)} %add_convert_fusion.1), channel_id=1, source_target_pairs={{0,16},{4,20},{8,24},{12,28},{16,0},{20,4},{24,8},{28,12},{1,17},{... | collective-permute-start | bytes 4718600 | tf_op jit(solution)/shard_map/ppermute | solution.py:1677
  717.9 1.1 copy-start.1
  721.0 62.7 %collective-permute-start.4 = (bf16[2,192,2048]{2,1,0:T(8,128)(2,1)S(1)}, bf16[2,192,2048]{2,1,0:T(8,128)(2,1)S(1)}, u32[]{:S(2)}, u32[]{:S(2)}) collective-permute-start(bf16[2,192,2048]{2,1,0:T(8,128)(2,1)S(1)} %add_convert_fusion), channel_id=1, source_target_pairs={{0,8},{4,12},{8,0},{12,4},{16,24},{20,28},{24,16},{28,20},{1,9},{5... | collective-permute-start | bytes 4718600 | tf_op jit(solution)/shard_map/ppermute | solution.py:1684
  799.9 57.1 %copy-start.5 = (f32[256,768]{1,0:T(8,128)S(1)}, f32[256,768]{1,0:T(8,128)}, u32[]{:S(2)}) copy-start(f32[256,768]{1,0:T(8,128)} %get-tuple-element.93) | copy-start | bytes 2359300
  799.9 58.0 %copy-start.6 = (f32[256,768]{1,0:T(8,128)S(1)}, f32[256,768]{1,0:T(8,128)}, u32[]{:S(2)}) copy-start(f32[256,768]{1,0:T(8,128)} %get-tuple-element.122) | copy-start | bytes 2359300
Sparse Core Ops, SparseCore 0:
  10.9 126.7 all-gather.8
  140.6 123.0 all-gather.10
  266.7 121.4 all-gather.12
  390.9 120.9 all-gather.14

commit v5 on v4

--- a/solution.py
+++ b/solution.py
@@ -508,7 +508,6 @@
 
 
 MINLEN = 1024
-GRAD_LANES = 768
 ROUT = 56
 RAW, COEF, SLOT, LOGI = 0, 16, 32, 40
 VMEM_MB = 60
@@ -838,10 +837,10 @@
 
 
 def attn_bwd_kernel(
-    order, inv, n1s, w, cosine, sine, qkv, o, lse, go, ghst, x, small, gsmall,
-    gx, gm, gw,
-    gor, gos, grads, acc, keep, sib_out, sib_in, gn_out, gnr,
-    o_send, o_recv, s_send, s_recv, g_send, g_recv,
+    order, inv, n1s, w, cosine, sine, qkv, o, lse, go, ghst, x, small, gsmall, gwo,
+    gx, gm, dense,
+    gor, gos, grads, acc, gns, sib_out, sib_in, gn_out, gnr, gw, gw_in, go_in, both, both_in,
+    o_send, o_recv, s_send, s_recv, g_send, g_recv, r_send, r_recv,
 ):
     blocks, blk, width = grads.shape
     lanes = o.shape[1]
@@ -853,7 +852,7 @@
     depth = blocks // 2
     same = xx == k
 
-    barrier, others = greet_plane(blocks)
+    barrier, others = greet_plane(blocks, across=True)
     acc[...] = jnp.zeros_like(acc)
     pl.semaphore_wait(barrier, others)
 
@@ -916,15 +915,18 @@
     def gn_copy(zz):
         return remote(gn_out.at[zz], gnr.at[z], g_send.at[zz], g_recv.at[z], 2 * zz + k, 2 * y + xx)
 
+    gain = small[0:1, :].astype(jnp.float32)
+    ggain = jnp.zeros((1, width), jnp.float32)
+    for b in range(blocks):
+        gns[b] = nt(grads[b], w[...])
+        ggain = ggain + jnp.sum(gns[b] * n1s[b * blk : (b + 1) * blk, :].astype(jnp.float32), axis=0, keepdims=True)
     for zz in range(depth):
-        sib_out[zz] = nt(grads[order[2 * zz + 1 - k]], w[...]).astype(jnp.bfloat16)
+        sib_out[zz] = gns[order[2 * zz + 1 - k]].astype(jnp.bfloat16)
         sib_copy(zz).start()
-    for zz in range(depth):
-        keep[zz] = nt(grads[order[2 * zz + k]], w[...])
     for zz in range(depth):
         sib_copy(zz).wait_recv()
         alone = jnp.logical_and(same, zz == z)
-        gn_out[zz] = (keep[zz] + sib_in[zz].astype(jnp.float32)).astype(jnp.bfloat16)
+        gn_out[zz] = (gns[order[2 * zz + k]] + sib_in[zz].astype(jnp.float32)).astype(jnp.bfloat16)
 
         @pl.when(jnp.logical_not(alone))
         def _():
@@ -934,13 +936,44 @@
         def _():
             gnr[z] = gn_out[zz]
 
-    inner = GROUP_HEADS * HEAD_DIM
-    gw[:, 128 + 3 * inner :] = jnp.zeros((width, gw.shape[1] - 128 - 3 * inner), jnp.bfloat16)
-    for i in range(width // 256):
-        part = slice(i * 256, (i + 1) * 256)
-        piece = tn(n1s[:, part], grads[...].reshape(seq, 3 * lanes)).astype(jnp.bfloat16)
+    packs, inner = gwo.shape[0], gwo.shape[1]
+    sums = jnp.concatenate([ggain / gain, gsmall[...]], axis=0)
+    sums = jnp.concatenate([sums, jnp.zeros((128 - sums.shape[0], width), jnp.float32)], axis=0)
+    sums = jnp.transpose(sums).astype(jnp.bfloat16)
+    for f in range(packs):
+        rows = slice(f * inner, (f + 1) * inner)
+        piece = tn(n1s[:, rows], grads[...].reshape(seq, 3 * lanes)).astype(jnp.bfloat16)
+        gw[f, :, :128] = sums[rows]
         for c in range(3):
-            gw[part, 128 + c * inner : 128 + (c + 1) * inner] = piece[:, c * lanes : c * lanes + inner]
+            gw[f, :, 128 + c * inner : 128 + (c + 1) * inner] = piece[:, c * lanes : c * lanes + inner]
+        gw[f, :, 128 + 3 * inner :] = jnp.zeros((inner, gw.shape[2] - 128 - 3 * inner), jnp.bfloat16)
+
+    def home_copy(index):
+        source, target = ((gw, gw_in), (gwo, go_in))[index % 2]
+        half = index // 2
+        return remote(
+            source.at[2 * half + 1 - k], target.at[half], r_send.at[index], r_recv.at[index], own, 2 * y + 1 - k
+        )
+
+    for index in range(4):
+        home_copy(index).start()
+    for half in range(2):
+        home_copy(2 * half).wait_recv()
+        home_copy(2 * half + 1).wait_recv()
+        kept, came = gw[2 * half + k], gw_in[half]
+        both[half, :, :128] = (kept[:, :128].astype(jnp.float32) + came[:, :128].astype(jnp.float32)).astype(jnp.bfloat16)
+        heads = slice(128, 128 + 3 * inner)
+        for core in range(2):
+
+            @pl.when(k == core)
+            def _():
+                both[half, :, 128 + core * 3 * inner : 128 + (core + 1) * 3 * inner] = kept[:, heads]
+                both[half, :, 128 + (1 - core) * 3 * inner : 128 + (2 - core) * 3 * inner] = came[:, heads]
+
+        outs = gwo[2 * half + k].astype(jnp.float32) + go_in[half].astype(jnp.float32)
+        both[half, :, 128 + 6 * inner :] = outs.astype(jnp.bfloat16)
+    over = remote(both.at[1 - y], both_in, r_send.at[4], r_recv.at[4], own, 2 * (1 - y) + k)
+    over.start()
     for zz in range(depth):
 
         @pl.when(jnp.logical_not(jnp.logical_and(same, zz == z)))
@@ -957,13 +990,15 @@
     values = x[...]
     factor = rms_factor(values)
     base = values * factor
-    gb = gn * small[0:1, :].astype(jnp.float32)
+    gb = gn * gain
     grad = ghst[...] + factor * (gb - base * jnp.mean(gb * base, axis=-1, keepdims=True))
     gx[...] = grad
     gm[...] = grad.astype(jnp.bfloat16)
-    sums = jnp.concatenate([jnp.sum(gn * base, axis=0, keepdims=True), gsmall[...]], axis=0)
-    sums = jnp.concatenate([sums, jnp.zeros((128 - sums.shape[0], width), jnp.float32)], axis=0)
-    gw[:, :128] = jnp.transpose(sums).astype(jnp.bfloat16)
+    over.wait_recv()
+    dense[...] = (both[y].astype(jnp.float32) + both_in[...].astype(jnp.float32)).astype(jnp.bfloat16)
+    for index in range(4):
+        home_copy(index).wait_send()
+    over.wait_send()
     for unit in range(blocks):
 
         @pl.when(jnp.logical_not(jnp.logical_and(same, unit == 2 * z + k)))
@@ -978,10 +1013,11 @@
             gn_copy(zz).wait_send()
 
 
-def attn_backward(order, inv, n1s, w, cosine, sine, qkv, o, lse, go, ghst, x, small, gsmall, number):
+def attn_backward(order, inv, n1s, w, cosine, sine, qkv, o, lse, go, ghst, x, small, gsmall, gwo, number):
     blocks, blk, lanes = go.shape
     seq, width = n1s.shape
     count = x.shape[0]
+    packs, inner = gwo.shape[0], gwo.shape[1]
     depth = blocks // 2
     vm = pl.BlockSpec(memory_space=pltpu.VMEM)
     sm = pl.BlockSpec(memory_space=pltpu.SMEM)
@@ -992,27 +1028,33 @@
         out_shape=[
             shape_of((count, width), jnp.float32),
             shape_of((count, width), bf),
-            shape_of((width, GRAD_LANES), bf),
+            shape_of((inner, 128 + 6 * inner + width), bf),
         ],
-        in_specs=[sm] * 2 + [vm] * 12,
+        in_specs=[sm] * 2 + [vm] * 13,
         out_specs=[vm] * 3,
         scratch_shapes=[
             pltpu.VMEM((blocks, blk, lanes), bf),
             pltpu.VMEM((seq, lanes), bf),
             pltpu.VMEM((blocks, blk, 3 * lanes), bf),
             pltpu.VMEM((seq, 3 * lanes), jnp.float32),
-            pltpu.VMEM((depth, blk, width), jnp.float32),
+            pltpu.VMEM((blocks, blk, width), jnp.float32),
             pltpu.VMEM((depth, blk, width), bf),
             pltpu.VMEM((depth, blk, width), bf),
             pltpu.VMEM((depth, blk, width), bf),
             pltpu.VMEM((depth, blk, width), bf),
+            pltpu.VMEM((packs, inner, 3 * lanes), bf),
+            pltpu.VMEM((2, inner, 3 * lanes), bf),
+            pltpu.VMEM((2, inner, width), bf),
+            pltpu.VMEM((2, inner, 128 + 6 * inner + width), bf),
+            pltpu.VMEM((inner, 128 + 6 * inner + width), bf),
         ]
         + [dma((blocks,))] * 2
-        + [dma((depth,))] * 4,
+        + [dma((depth,))] * 4
+        + [dma((5,))] * 2,
         compiler_params=params_of(collective_id=number, has_side_effects=True),
         cost_estimate=BRIEF,
         name="attn_bwd",
-    )(order, inv, n1s, w, cosine, sine, qkv, o, lse, go, ghst, x, small, gsmall)
+    )(order, inv, n1s, w, cosine, sine, qkv, o, lse, go, ghst, x, small, gsmall, gwo)
 
 
 def routing(raw, before, routes):
@@ -1329,7 +1371,7 @@
     outs = [
         shape_of((count, width), f32),
         shape_of(ob.shape, bf),
-        shape_of((width, width), bf),
+        shape_of(wo.shape, bf),
         shape_of((1 + NC + 16, width), f32),
         shape_of((16, count), f32),
     ]
@@ -1545,7 +1587,44 @@
             go[h * groups + g] = value[h * blk : (h + 1) * blk]
         mixed = jnp.concatenate([ob[g], ob[groups + g]], axis=0)
         gwo.append(tn(mixed, gy)[:inner].astype(jnp.bfloat16))
-    return ghst, jnp.stack(go), jnp.concatenate(gwo, axis=0), jnp.concatenate(sums + [grad_router], axis=0), glog
+    return ghst, jnp.stack(go), jnp.stack(gwo), jnp.concatenate(sums + [grad_router], axis=0), glog
+
+
+def assemble_kernel(ours, theirs, qkv, out, small):
+    z, _, _, _ = place()
+    layers, shard = ours.shape[0], ours.shape[1]
+    inner = GROUP_HEADS * HEAD_DIM
+    for l in range(layers):
+        small[l] = ours[l, :, :128].astype(jnp.float32) + theirs[l, :, :128].astype(jnp.float32)
+        first = 128 + 6 * inner
+        out[l] = ours[l, :, first:].astype(jnp.float32) + theirs[l, :, first:].astype(jnp.float32)
+        for group in range(4):
+            for odd in range(2):
+
+                @pl.when(z % 2 == odd)
+                def _():
+                    source = ours if group // 2 == odd else theirs
+                    for c in range(3):
+                        at = 128 + (group % 2) * 3 * inner + c * inner
+                        qkv[l, c, :, group * inner : (group + 1) * inner] = source[l, :, at : at + inner].astype(jnp.float32)
+
+
+def assemble(ours, theirs, width):
+    layers, shard, _ = ours.shape
+    vm = pl.BlockSpec(memory_space=pltpu.VMEM)
+    return pl.pallas_call(
+        assemble_kernel,
+        out_shape=[
+            shape_of((layers, 3, shard, width), jnp.float32),
+            shape_of((layers, shard, width), jnp.float32),
+            shape_of((layers, shard, 128), jnp.float32),
+        ],
+        in_specs=[vm] * 2,
+        out_specs=[vm] * 3,
+        compiler_params=params_of(),
+        cost_estimate=BRIEF,
+        name="assemble",
+    )(ours, theirs)
 
 
 def turn_tables(seq):
@@ -1634,70 +1713,51 @@
         )
         if l == 1:
             go, ext_all[0] = lax.optimization_barrier((go, ext_all[0]))
-        gx, gm, gw = attn_backward(
-            order, inv, n1s, w, cosine, sine, qkv, o, lse, go, ghst, x, smalls[l], small, number + 1
+        gx, gm, grads[l] = attn_backward(
+            order, inv, n1s, w, cosine, sine, qkv, o, lse, go, ghst, x, smalls[l], small, gwo, number + 1
         )
         if l > 0:
-            gm_all[l - 1] = lax.all_gather(gm, everyone, axis=0, tiled=False)
-        grads[l] = jnp.concatenate([gw, gwo], axis=1)
-
-    inner = GROUP_HEADS * HEAD_DIM
-    dense = jnp.stack(grads).reshape(LAYERS, packs // 2, 2, shard, 2 * width)
-    mine = lax.dynamic_index_in_dim(dense, k, 2, keepdims=False)
-    theirs = lax.dynamic_index_in_dim(dense, 1 - k, 2, keepdims=False)
-    got = lax.ppermute(theirs, "fsdp", [(i, i ^ 1) for i in range(packs)])
-    x0 = dispatch(ext_all[0], ext_all[0], False)
-    x0, got = lax.optimization_barrier((x0, got))
-
-    def ordered(swap, first, second):
-        return jnp.concatenate([jnp.where(swap, second, first), jnp.where(swap, first, second)], axis=-1)
+            gm_all[l - 1] = gm
+
+    dense = jnp.stack(grads)
+    dense, gm = lax.optimization_barrier((dense, gm_all[0]))
+    gm_all[0] = lax.all_gather(gm, everyone, axis=0, tiled=False)
+
+    def partner(values, distance):
+        return lax.ppermute(values, "ctx", [(i, i ^ distance) for i in range(ctx_size)])
 
     def added(first, second):
         return (first.astype(f32) + second.astype(f32)).astype(bf)
 
-    def split(values):
-        return values[..., 128 : 128 + 3 * inner], jnp.concatenate([values[..., :128], values[..., width:]], axis=-1)
-
-    (qkv_mine, rest_mine), (qkv_got, rest_got) = split(mine), split(got)
-    dense = jnp.concatenate([ordered(k == 1, qkv_mine, qkv_got), added(rest_mine, rest_got)], axis=-1)
-    mine = lax.dynamic_index_in_dim(dense, y, 1, keepdims=False)
-    theirs = lax.dynamic_index_in_dim(dense, 1 - y, 1, keepdims=False)
-    theirs, ext_all[1] = lax.optimization_barrier((theirs, ext_all[1]))
-    got = lax.ppermute(theirs, "fsdp", [(i, i ^ 2) for i in range(packs)])
+    got = partner(dense, 1)
     x1 = dispatch(ext_all[1], ext_all[1], False)
     g1 = dispatch(ext_all[1], gm_all[1], True)
     x1, g1, got = lax.optimization_barrier((x1, g1, got))
-    dense = added(mine, got)
+    dense = added(dense, got)
     dense, x1 = lax.optimization_barrier((dense, x1))
-    got = lax.ppermute(dense, "ctx", [(i, i ^ 1) for i in range(ctx_size)])
-    done = weight_grads(1, 0, NF // 2, x1, g1, w_gate_up, w_down, ())
+    got = partner(dense, 4)
+    done = weight_grads(1, 0, NF, x1, g1, w_gate_up, w_down, ())
     done, got = lax.optimization_barrier((done, got))
     dense = added(dense, got)
-    dense, done = lax.optimization_barrier((dense, done))
-    got = lax.ppermute(dense, "ctx", [(i, i ^ 4) for i in range(ctx_size)])
-    done = weight_grads(1, NF // 2, NF, x1, g1, w_gate_up, w_down, done)
-    done, gm_all[0] = lax.optimization_barrier((done, gm_all[0]))
-    g0 = dispatch(ext_all[0], gm_all[0], True)
-    g0, got = lax.optimization_barrier((g0, got))
-    dense = added(dense, got)
-    dense, g0 = lax.optimization_barrier((dense, g0))
-    got = lax.ppermute(dense, "ctx", [(i, i ^ 2) for i in range(ctx_size)])
+    dense, ext = lax.optimization_barrier((dense, ext_all[0]))
+    got = partner(dense, 2)
+    x0 = dispatch(ext, ext, False)
+    gm, x0 = lax.optimization_barrier((gm_all[0], x0))
+    g0 = dispatch(ext, gm, True)
     done = weight_grads(0, 0, NF // 2, x0, g0, w_gate_up, w_down, done)
     done, got = lax.optimization_barrier((done, got))
-    pairs = 6 * inner
-    rest = dense[..., pairs:].astype(f32) + got[..., pairs:].astype(f32)
-    qkv = ordered(z % 2 == 1, dense[..., :pairs], got[..., :pairs]).reshape(LAYERS, shard, 4, 3, inner)
-    qkv = jnp.stack([qkv[:, :, :, c, :].reshape(LAYERS, shard, width) for c in range(3)], axis=1).astype(f32)
-    small = jnp.swapaxes(rest[..., :128], 1, 2)
+    qkv, out, small = assemble(dense, got, width)
+    done, qkv, out, small = lax.optimization_barrier((done, qkv, out, small))
     done = weight_grads(0, NF // 2, NF, x0, g0, w_gate_up, w_down, done)
+    rows = jnp.swapaxes(small[..., : 2 + NC], 1, 2)
     return (
         output[None],
         gx[None],
-        small[:, :2],
+        rows[:, :2],
         qkv,
-        rest[..., 128:],
-        rest[..., 2 + NC : 2 + NC + 16],
-        small[:, 2 : 2 + NC],
+        out,
+        small[..., 2 + NC : 2 + NC + 16],
+        rows[:, 2:],
         done[0],
         done[1],
     )

time: 873 us -> 833 us (0.954)
  local copies, waits for them, and re-layouts: 31.8 us -> 13.5 us
  other arithmetic: 23 us -> 10.2 us
  waiting for transfers between devices: 1.57 us -> 13 us
  Pallas kernels: 771 us -> 760 us
  starting transfers between devices: 17.9 us -> 8.32 us
    pallas_call x2, Pallas kernels: 162 us -> 149 us  [attn_backward(): pl.pallas_call(attn_bwd_kernel, out_shape=[shape_of((count, width), jnp.f...]
    ppermute x5 -> x3, waiting for transfers between devices: 0.81 us -> 12.2 us  [partner(): lax.ppermute(values, 'ctx', [(i, i ^ distance) for i in range(ctx_size)])]
    ppermute x5 -> x3, starting transfers between devices: 17.6 us -> 7.7 us  [partner(): lax.ppermute(values, 'ctx', [(i, i ^ distance) for i in range(ctx_size)])]
    pallas_call x4 -> x3, Pallas kernels: 228 us -> 223 us  [weight_grads(): pl.pallas_call(dw_kernel, grid=(last - first,), out_shape=[shape_of(wgu.s...]
  transfers between devices with their start and end apart: 9 -> 7, of which waited for: 1 -> 2; matrix products, arithmetic and copies ran while one was open for 4% -> 2% of each run, Pallas kernels for 82% -> 85%
where the time goes in v5:
time: 833 us; the launch traced here: 826 us
  Pallas kernels  760 us (91%)
  between operations  14.3 us (2%)
  local copies, waits for them, and re-layouts  13.5 us (2%)
  waiting for transfers between devices  13 us (2%)
  other arithmetic  10.2 us (1%)
    pallas_call x3, Pallas kernels, weight_grads(): pl.pallas_call(dw_kernel, grid=(last - first,), out_shape=[shape_of(wgu.s...  223 us
    pallas_call x2, Pallas kernels, attn_backward(): pl.pallas_call(attn_bwd_kernel, out_shape=[shape_of((count, width), jnp.f...  149 us
    pallas_call x2, Pallas kernels, attn_forward(): pl.pallas_call(attn_fwd_kernel, grid=(1,), out_shape=[shape_of((seq, widt...  127 us
    pallas_call x2, Pallas kernels, ffn_forward(): pl.pallas_call(ffn_fwd_kernel, grid=(NF,), out_shape=outs, in_specs=[whol...  95 us
    pallas_call x2, Pallas kernels, ffn_backward(): pl.pallas_call(ffn_bwd_kernel, grid=(NF,), out_shape=outs, in_specs=[whol...  92.6 us
    pallas_call x4, Pallas kernels, dispatch(): pl.pallas_call(functools.partial(dispatch_kernel, rows, weighted), grid=(...  68.7 us
  transfers between devices with their start and end apart: 7, of which 2 were waited for; matrix products, arithmetic and copies ran while one was open for 2% of the time, Pallas kernels for 85%

profile of v5, /device:TPU:0, one launch (start us, length us, event | category | flops | bytes accessed | tf_op | source)
XLA Modules:
  0.0 825.6 jit_solution(2430047295899539301)
XLA Ops:
  7.2 0.0 all-gather.9.cloned.1.call-start
  7.2 0.7 all-gather.9.cloned.1.call-update
  7.9 0.0 all-gather.11.cloned.1.call-start
  8.0 0.7 convert_bitcast_fusion
  8.7 0.7 convert_bitcast_fusion.1
  9.4 0.1 reshape.226
  9.5 0.7 pad_maximum_fusion.1
  10.3 6.3 all-gather.3
  16.6 0.1 copy.44
  16.6 0.1 reshape.248
  16.8 0.1 reshape.235
  16.9 0.1 reshape.233
  17.0 0.1 dynamic-slice_reduce_fusion
  17.1 0.1 reshape.227
  17.1 0.2 subtract_reduce_fusion.order
  17.3 0.6 select_reduce_fusion.inv
  18.0 0.6 fusion.9
  18.6 0.9 bitcast_convert_fusion.x
  19.5 57.1 %attn_fwd.2 = (bf16[1024,768]{1,0:T(8,128)(2,1)}, bf16[1024,768]{1,0:T(8,128)(2,1)}, f32[1024,256]{1,0:T(8,128)}, f32[1024,128]{1,0:T(8,128)}, bf16[8,128,256]{2...) custom-call(s32[8]{0:T(128)} %copy-done.8, ...), custom_call_target="tpu_custom_call" | custom-call | flops 1 | bytes 1 | tf_op jit(solution)/shard_map/attn_fwd/pallas_call | solution.py:802
  76.7 0.1 fusion.7
  76.8 0.6 gather_fusion
  77.4 0.6 slice_bitcast_fusion.1
  78.0 0.6 broadcast_in_dim.30.before
  78.6 46.2 %ffn_fwd.2 = (bf16[4,256,768]{2,1,0:T(8,128)(2,1)}, f32[4,56,256]{2,1,0:T(8,128)}, bf16[272,768]{1,0:T(8,128)(2,1)}, f32[256,768]{1,0:T(8,128)}) custom-call(bf16[256,768]{1,0:T(8,128)(2,1)} %get-tuple-element.84.ub, f32[256,768]{1,0:T(8,128)} %get-tuple-element.85.hst, bf16[20,768]{1,0:T(8,128)(2,1)} %get-tuple-element.198.small, ...), custom_call_target="tpu_custom_call" | custom-call | flops 1 | bytes 1 | tf_op jit(solution)/shard_map/ffn_fwd/pallas_call | solution.py:1227
  124.9 0.0 all-gather.11.cloned.1.call-update
  124.9 0.0 all-gather.15.cloned.1.call-start
  125.0 69.8 %attn_fwd.3 = (bf16[1024,768]{1,0:T(8,128)(2,1)}, bf16[1024,768]{1,0:T(8,128)(2,1)}, f32[1024,256]{1,0:T(8,128)}, f32[1024,128]{1,0:T(8,128)}, bf16[8,128,256]{2...) custom-call(s32[8]{0:T(128)} %copy-done.8, ...), custom_call_target="tpu_custom_call" | custom-call | flops 1 | bytes 1 | tf_op jit(solution)/shard_map/attn_fwd/pallas_call | solution.py:802
  194.8 1.5 slice.50.before
  196.2 48.8 %ffn_fwd.3 = (bf16[4,256,768]{2,1,0:T(8,128)(2,1)}, f32[4,56,256]{2,1,0:T(8,128)}, bf16[272,768]{1,0:T(8,128)(2,1)}, f32[256,768]{1,0:T(8,128)}) custom-call(bf16[256,768]{1,0:T(8,128)(2,1)} %get-tuple-element.88.ub, f32[256,768]{1,0:T(8,128)} %get-tuple-element.89.hst, bf16[20,768]{1,0:T(8,128)(2,1)} %get-tuple-element.197.small, ...), custom_call_target="tpu_custom_call" | custom-call | flops 1 | bytes 1 | tf_op jit(solution)/shard_map/ffn_fwd/pallas_call | solution.py:1227
  245.1 0.5 all-gather.13.cloned.1.call-start
  245.6 0.6 slice_bitcast_fusion.3
  246.2 0.9 bitcast_convert_fusion.1.gx
  247.1 0.6 broadcast_in_dim.32.gprev
  247.7 46.6 %ffn_bwd.2 = (f32[256,768]{1,0:T(8,128)}, bf16[8,128,256]{2,1,0:T(8,128)(2,1)}, bf16[4,192,768]{2,1,0:T(8,128)(2,1)}, f32[19,768]{1,0:T(8,128)}, f32[16,256]{1,0:T(8,128)}) custom-call(bf16[256,768]{1,0:T(8,128)(2,1)} %bitcast.69, f32[256,768]{1,0:T(8,128)} %bitcast_convert_fusion.1.gx, bf16[4,256,768]{2,1,0:T(8,128)(2,1)} %get-tuple-element.102.ubf, ...), custom_call_target="tpu_custom_call" | custom-call | flops 1 | bytes 1 | tf_op jit(solution)/shard_map/ffn_bwd/pallas_call | solution.py:1380
  294.3 0.0 all-gather.11.cloned.1.call-done
  294.3 83.7 %attn_bwd.2 = (f32[256,768]{1,0:T(8,128)}, bf16[256,768]{1,0:T(8,128)(2,1)}, bf16[192,2048]{1,0:T(8,128)(2,1)}) custom-call(s32[8]{0:T(128)} %copy-done.8, s32[8]{0:T(128)} %select_reduce_fusion.inv, bf16[1024,768]{1,0:T(8,128)(2,1)} %get-tuple-element.97.n1s, bf16[768,768]{1,0:T(8,128)(2,1)} %get-tuple-element.98.w, f32[1024,128]{1,0:T(8,128)} %constant.76.clone.cosine, ...), custom_call_target="tpu_custom_call" | custom-call | flops 1 | bytes 1 | tf_op jit(solution)/shard_map/attn_bwd/pallas_call | solution.py:1026
  378.0 46.0 %ffn_bwd.3 = (f32[256,768]{1,0:T(8,128)}, bf16[8,128,256]{2,1,0:T(8,128)(2,1)}, bf16[4,192,768]{2,1,0:T(8,128)(2,1)}, f32[19,768]{1,0:T(8,128)}, f32[16,256]{1,0:T(8,128)}) custom-call(bf16[256,768]{1,0:T(8,128)(2,1)} %get-tuple-element.125.gm, f32[256,768]{1,0:T(8,128)} %get-tuple-element.113.gx, bf16[4,256,768]{2,1,0:T(8,128)(2,1)} %get-tuple-element.114.ubf, ...), custom_call_target="tpu_custom_call" | custom-call | flops 1 | bytes 1 | tf_op jit(solution)/shard_map/ffn_bwd/pallas_call | solution.py:1380
  424.0 65.3 %attn_bwd.3 = (f32[256,768]{1,0:T(8,128)}, bf16[256,768]{1,0:T(8,128)(2,1)}, bf16[192,2048]{1,0:T(8,128)(2,1)}) custom-call(s32[8]{0:T(128)} %copy-done.8, s32[8]{0:T(128)} %select_reduce_fusion.inv, bf16[1024,768]{1,0:T(8,128)(2,1)} %get-tuple-element.92.n1s, bf16[768,768]{1,0:T(8,128)(2,1)} %get-tuple-element.93.w, f32[1024,128]{1,0:T(8,128)} %constant.76.clone.cosine, ...), custom_call_target="tpu_custom_call" | custom-call | flops 1 | bytes 1 | tf_op jit(solution)/shard_map/attn_bwd/pallas_call | solution.py:1026
  489.3 1.3 pad_maximum_fusion
  490.6 1.1 collective-permute-start
  491.8 17.4 %dispatch.4 = bf16[8,32,64,768]{3,2,1,0:T(8,128)(2,1)} custom-call(bf16[32,272,768]{2,1,0:T(8,128)(2,1)} %bitcast.63, bf16[32,272,768]{2,1,0:T(8,128)(2,1)} %bitcast.64), custom_call_target="tpu_custom_call" | custom-call | flops 1 | bytes 1 | tf_op jit(solution)/shard_map/dispatch/pallas_call | solution.py:1428
  509.1 17.0 %dispatch.5 = bf16[8,32,64,768]{3,2,1,0:T(8,128)(2,1)} custom-call(bf16[32,272,768]{2,1,0:T(8,128)(2,1)} %bitcast.65, bf16[32,256,768]{2,1,0:T(8,128)(2,1)} %all-gather.9.cloned.1.call-done.values), custom_call_target="tpu_custom_call" | custom-call | flops 1 | bytes 1 | tf_op jit(solution)/shard_map/dispatch/pallas_call | solution.py:1428
  526.2 9.9 %collective-permute-done = bf16[2,192,2048]{2,1,0:T(8,128)(2,1)} collective-permute-done((bf16[2,192,2048]{2,1,0:T(8,128)(2,1)S(1)}, bf16[2,192,2048]{2,1,0:T(8,128)(2,1)}, u32[]{:S(2)}, u32[]{:S(2)}) %collective-permute-start) | collective-permute-done | bytes 1572896 | tf_op jit(solution)/shard_map/ppermute | solution.py:1727
  536.1 2.0 add_convert_fusion.1
  538.1 0.3 collective-permute-start.1
  538.4 108.4 %weight_grads.3 = (f32[2,8,2,768,512]{4,3,2,1,0:T(8,128)}, f32[2,8,512,768]{3,2,1,0:T(8,128)}) custom-call(bf16[8,2048,768]{2,1,0:T(8,128)(2,1)} %bitcast.66, bf16[8,2048,768]{2,1,0:T(8,128)(2,1)} %bitcast.67, bf16[2,8,2,768,512]{4,3,2,1,0:T(8,128)(2,1)} %refs_2_.5, bf16[2,8,512,768]{3,2,1,0:T(8,128)(2,1)} %refs_3_.5), custom_call_target="tpu_custom_call" | custom-call | flops 1 | bytes 1 | tf_op jit(solution)/shard_map/weight_grads/pallas_call | solution.py:1483
  646.9 2.3 collective-permute-done.1
  649.2 2.0 add_convert_fusion.ours
  651.2 6.3 collective-permute-start.2
  657.5 17.3 %dispatch.6 = bf16[8,32,64,768]{3,2,1,0:T(8,128)(2,1)} custom-call(bf16[32,272,768]{2,1,0:T(8,128)(2,1)} %bitcast.60, bf16[32,272,768]{2,1,0:T(8,128)(2,1)} %bitcast.61), custom_call_target="tpu_custom_call" | custom-call | flops 1 | bytes 1 | tf_op jit(solution)/shard_map/dispatch/pallas_call | solution.py:1428
  674.8 17.0 %dispatch.7 = bf16[8,32,64,768]{3,2,1,0:T(8,128)(2,1)} custom-call(bf16[32,272,768]{2,1,0:T(8,128)(2,1)} %bitcast.62, bf16[32,256,768]{2,1,0:T(8,128)(2,1)} %bitcast.68), custom_call_target="tpu_custom_call" | custom-call | flops 1 | bytes 1 | tf_op jit(solution)/shard_map/dispatch/pallas_call | solution.py:1428
  691.8 57.0 %weight_grads.4 = (f32[2,8,2,768,512]{4,3,2,1,0:T(8,128)}, f32[2,8,512,768]{3,2,1,0:T(8,128)}) custom-call(bf16[8,2048,768]{2,1,0:T(8,128)(2,1)} %bitcast.56, bf16[8,2048,768]{2,1,0:T(8,128)(2,1)} %bitcast.58, bf16[2,8,2,768,512]{4,3,2,1,0:T(8,128)(2,1)} %refs_2_.5, bf16[2,8,512,768]{3,2,1,0:T(8,128)(2,1)} %refs_3_.5, ...), custom_call_target="tpu_custom_call", output_to_operand_aliasing={{0}: (4, {}), {1}: (5, {})} | custom-call | flops 1 | bytes 1 | tf_op jit(solution)/shard_map/weight_grads/pallas_call | solution.py:1483
  748.8 1.1 copy-done.2
  749.9 5.3 assemble.1
  755.2 1.0 slice.55
  756.3 0.9 slice_bitcast_fusion
  757.2 0.7 copy.49
  757.9 0.1 fusion.8
  758.1 0.7 copy.50
  758.8 0.7 copy.48
  759.5 57.1 %weight_grads.5 = (f32[2,8,2,768,512]{4,3,2,1,0:T(8,128)}, f32[2,8,512,768]{3,2,1,0:T(8,128)}) custom-call(bf16[8,2048,768]{2,1,0:T(8,128)(2,1)} %bitcast.57, bf16[8,2048,768]{2,1,0:T(8,128)(2,1)} %bitcast.59, bf16[2,8,2,768,512]{4,3,2,1,0:T(8,128)(2,1)} %refs_2_.5, bf16[2,8,512,768]{3,2,1,0:T(8,128)(2,1)} %refs_3_.5, ...), custom_call_target="tpu_custom_call", output_to_operand_aliasing={{0}: (4, {}), {1}: (5, {})} | custom-call | flops 1 | bytes 1 | tf_op jit(solution)/shard_map/weight_grads/pallas_call | solution.py:1483
  816.6 0.9 copy.62
  817.5 0.5 copy-done.4
  818.0 0.9 copy.63
  (31 shorter events, 0.2 us)
Async XLA Ops:
  7.2 11.4 %copy-start.6 = (bf16[1,256,768]{2,1,0:T(8,128)(2,1)S(1)}, bf16[1,256,768]{2,1,0:T(8,128)(2,1)}, u32[]{:S(2)}) copy-start(bf16[1,256,768]{2,1,0:T(8,128)(2,1)} %param.14) | copy-start | bytes 1179652
  7.2 189.1 %all-gather.9.cloned.1.call-start = ((), (), s32[]{:S(2)}) async-start(), calls=%async_computation | async-start | bytes 12976128 | tf_op jit(solution)/shard_map/all_gather | solution.py:1686
  7.9 286.4 %all-gather.11.cloned.1.call-start = ((), (), s32[]{:S(2)}) async-start(), calls=%async_computation.1 | async-start | bytes 13787136 | tf_op jit(solution)/shard_map/all_gather | solution.py:1700
  17.3 2.2 copy-start.8
  124.9 366.9 %all-gather.15.cloned.1.call-start = ((), (), s32[]{:S(2)}) async-start(), calls=%async_computation.3 | async-start | bytes 13787136 | tf_op jit(solution)/shard_map/all_gather | solution.py:1700
  196.2 49.3 %copy-start.7 = (s32[2,1,256,2]{2,3,1,0:T(2,128)S(1)}, s32[2,1,256,2]{2,3,1,0:T(2,128)}, u32[]{:S(2)}) copy-start(s32[2,1,256,2]{2,3,1,0:T(2,128)} %param.17) | copy-start | bytes 12292
  196.2 49.9 %copy-start.1 = (bf16[1,256,768]{2,1,0:T(8,128)(2,1)S(1)}, bf16[1,256,768]{2,1,0:T(8,128)(2,1)}, u32[]{:S(2)}) copy-start(bf16[1,256,768]{2,1,0:T(8,128)(2,1)} %param.15) | copy-start | bytes 1179652
  245.1 429.7 %all-gather.13.cloned.1.call-start = ((), (), s32[]{:S(2)}) async-start(), calls=%async_computation.2 | async-start | bytes 12976128 | tf_op jit(solution)/shard_map/all_gather | solution.py:1724
  424.0 65.3 %copy-start.5 = (bf16[192,2048]{1,0:T(8,128)(2,1)S(1)}, bf16[192,2048]{1,0:T(8,128)(2,1)}, u32[]{:S(2)}) copy-start(bf16[192,2048]{1,0:T(8,128)(2,1)} %get-tuple-element.124) | copy-start | bytes 2359300
  490.6 45.5 %collective-permute-start = (bf16[2,192,2048]{2,1,0:T(8,128)(2,1)S(1)}, bf16[2,192,2048]{2,1,0:T(8,128)(2,1)}, u32[]{:S(2)}, u32[]{:S(2)}) collective-permute-start(bf16[2,192,2048]{2,1,0:T(8,128)(2,1)S(1)} %pad_maximum_fusion), channel_id=1, source_target_pairs={{0,4},{4,0},{8,12},{12,8},{16,20},{20,16},{24,28},{28,24},{1,5},{5... | collective-permute-start | bytes 4718600 | tf_op jit(solution)/shard_map/ppermute | solution.py:1727
  538.1 111.0 %collective-permute-start.1 = (bf16[2,192,2048]{2,1,0:T(8,128)(2,1)S(1)}, bf16[2,192,2048]{2,1,0:T(8,128)(2,1)}, u32[]{:S(2)}, u32[]{:S(2)}) collective-permute-start(bf16[2,192,2048]{2,1,0:T(8,128)(2,1)S(1)} %add_convert_fusion.1), channel_id=1, source_target_pairs={{0,16},{4,20},{8,24},{12,28},{16,0},{20,4},{24,8},{28,12},{1,17},{... | collective-permute-start | bytes 4718600 | tf_op jit(solution)/shard_map/ppermute | solution.py:1727
  651.2 23.6 %copy-start = (bf16[2,192,2048]{2,1,0:T(8,128)(2,1)}, bf16[2,192,2048]{2,1,0:T(8,128)(2,1)S(1)}, u32[]{:S(2)}) copy-start(bf16[2,192,2048]{2,1,0:T(8,128)(2,1)S(1)} %add_convert_fusion.ours) | copy-start | bytes 4718596
  651.2 97.6 %collective-permute-start.2 = (bf16[2,192,2048]{2,1,0:T(8,128)(2,1)S(1)}, bf16[2,192,2048]{2,1,0:T(8,128)(2,1)S(1)}, u32[]{:S(2)}, u32[]{:S(2)}) collective-permute-start(bf16[2,192,2048]{2,1,0:T(8,128)(2,1)S(1)} %add_convert_fusion.ours), channel_id=1, source_target_pairs={{0,8},{4,12},{8,0},{12,4},{16,24},{20,28},{24,16},{28,20},{1,9},{5... | collective-permute-start | bytes 4718600 | tf_op jit(solution)/shard_map/ppermute | solution.py:1727
  748.8 1.2 copy-start.2
  759.5 57.1 %copy-start.3 = (f32[256,768]{1,0:T(8,128)S(1)}, f32[256,768]{1,0:T(8,128)}, u32[]{:S(2)}) copy-start(f32[256,768]{1,0:T(8,128)} %get-tuple-element.91) | copy-start | bytes 2359300
  816.6 1.4 copy-start.4
Sparse Core Ops, SparseCore 0:
  10.9 126.8 all-gather.8
  140.7 124.6 all-gather.10
  268.3 121.2 all-gather.14
  490.7 155.4 all-gather.12

commit v6 on v5

--- a/solution.py
+++ b/solution.py
@@ -839,8 +839,8 @@
 def attn_bwd_kernel(
     order, inv, n1s, w, cosine, sine, qkv, o, lse, go, ghst, x, small, gsmall, gwo,
     gx, gm, dense,
-    gor, gos, grads, acc, gns, sib_out, sib_in, gn_out, gnr, gw, gw_in, go_in, both, both_in,
-    o_send, o_recv, s_send, s_recv, g_send, g_recv, r_send, r_recv,
+    gor, gos, grads, acc, gns, sib_out, sib_in, gn_out, gnr, gw, gw_in, both, both_in, wo_in, wo_both, wo_over,
+    o_send, o_recv, s_send, s_recv, g_send, g_recv, r_send, r_recv, w_send, w_recv,
 ):
     blocks, blk, width = grads.shape
     lanes = o.shape[1]
@@ -870,12 +870,25 @@
         def _():
             gor[own] = go[unit]
 
+    def wo_copy(half):
+        return remote(
+            gwo.at[2 * half + 1 - k], wo_in.at[half], w_send.at[half], w_recv.at[half], own, 2 * y + 1 - k
+        )
+
+    wo_far = remote(wo_both.at[1 - y], wo_over, w_send.at[2], w_recv.at[2], own, 2 * (1 - y) + k)
+    wo_copy(0).start()
+    wo_copy(1).start()
     for ctx in range(blocks):
 
         @pl.when(jnp.logical_not(jnp.logical_and(same, ctx == own)))
         def _():
             remote(go.at[0], gor.at[ctx], o_send.at[0], o_recv.at[ctx], ctx, 2 * y + xx).wait_recv()
 
+    for half in range(2):
+        wo_copy(half).wait_recv()
+        total = gwo[2 * half + k].astype(jnp.float32) + wo_in[half].astype(jnp.float32)
+        wo_both[half] = total.astype(jnp.bfloat16)
+    wo_far.start()
     for b in range(blocks):
         gos[b * blk : (b + 1) * blk, :] = gor[inv[b]]
     lane = lax.broadcasted_iota(jnp.int32, (step, 128), 1)
@@ -939,28 +952,26 @@
     packs, inner = gwo.shape[0], gwo.shape[1]
     sums = jnp.concatenate([ggain / gain, gsmall[...]], axis=0)
     sums = jnp.concatenate([sums, jnp.zeros((128 - sums.shape[0], width), jnp.float32)], axis=0)
-    sums = jnp.transpose(sums).astype(jnp.bfloat16)
-    for f in range(packs):
-        rows = slice(f * inner, (f + 1) * inner)
-        piece = tn(n1s[:, rows], grads[...].reshape(seq, 3 * lanes)).astype(jnp.bfloat16)
-        gw[f, :, :128] = sums[rows]
+    gw[:, :128] = jnp.transpose(sums).astype(jnp.bfloat16)
+    gw[:, 128 + 3 * inner :] = jnp.zeros((width, gw.shape[1] - 128 - 3 * inner), jnp.bfloat16)
+    for i in range(width // 256):
+        part = slice(i * 256, (i + 1) * 256)
+        piece = tn(n1s[:, part], grads[...].reshape(seq, 3 * lanes)).astype(jnp.bfloat16)
         for c in range(3):
-            gw[f, :, 128 + c * inner : 128 + (c + 1) * inner] = piece[:, c * lanes : c * lanes + inner]
-        gw[f, :, 128 + 3 * inner :] = jnp.zeros((inner, gw.shape[2] - 128 - 3 * inner), jnp.bfloat16)
-
-    def home_copy(index):
-        source, target = ((gw, gw_in), (gwo, go_in))[index % 2]
-        half = index // 2
-        return remote(
-            source.at[2 * half + 1 - k], target.at[half], r_send.at[index], r_recv.at[index], own, 2 * y + 1 - k
-        )
-
-    for index in range(4):
-        home_copy(index).start()
+            gw[part, 128 + c * inner : 128 + (c + 1) * inner] = piece[:, c * lanes : c * lanes + inner]
+
+    def rows_of(f):
+        return pl.ds(pl.multiple_of(f * inner, inner), inner)
+
+    def home_copy(half):
+        rows = gw.at[rows_of(2 * half + 1 - k), :]
+        return remote(rows, gw_in.at[half], r_send.at[half], r_recv.at[half], own, 2 * y + 1 - k)
+
     for half in range(2):
-        home_copy(2 * half).wait_recv()
-        home_copy(2 * half + 1).wait_recv()
-        kept, came = gw[2 * half + k], gw_in[half]
+        home_copy(half).start()
+    for half in range(2):
+        home_copy(half).wait_recv()
+        kept, came = gw[rows_of(2 * half + k), :], gw_in[half]
         both[half, :, :128] = (kept[:, :128].astype(jnp.float32) + came[:, :128].astype(jnp.float32)).astype(jnp.bfloat16)
         heads = slice(128, 128 + 3 * inner)
         for core in range(2):
@@ -970,9 +981,7 @@
                 both[half, :, 128 + core * 3 * inner : 128 + (core + 1) * 3 * inner] = kept[:, heads]
                 both[half, :, 128 + (1 - core) * 3 * inner : 128 + (2 - core) * 3 * inner] = came[:, heads]
 
-        outs = gwo[2 * half + k].astype(jnp.float32) + go_in[half].astype(jnp.float32)
-        both[half, :, 128 + 6 * inner :] = outs.astype(jnp.bfloat16)
-    over = remote(both.at[1 - y], both_in, r_send.at[4], r_recv.at[4], own, 2 * (1 - y) + k)
+    over = remote(both.at[1 - y], both_in, r_send.at[2], r_recv.at[2], own, 2 * (1 - y) + k)
     over.start()
     for zz in range(depth):
 
@@ -994,10 +1003,15 @@
     grad = ghst[...] + factor * (gb - base * jnp.mean(gb * base, axis=-1, keepdims=True))
     gx[...] = grad
     gm[...] = grad.astype(jnp.bfloat16)
+    wo_far.wait_recv()
+    edge = both.shape[2]
+    dense[:, edge:] = (wo_both[y].astype(jnp.float32) + wo_over[...].astype(jnp.float32)).astype(jnp.bfloat16)
     over.wait_recv()
-    dense[...] = (both[y].astype(jnp.float32) + both_in[...].astype(jnp.float32)).astype(jnp.bfloat16)
-    for index in range(4):
-        home_copy(index).wait_send()
+    dense[:, :edge] = (both[y].astype(jnp.float32) + both_in[...].astype(jnp.float32)).astype(jnp.bfloat16)
+    for half in range(2):
+        home_copy(half).wait_send()
+        wo_copy(half).wait_send()
+    wo_far.wait_send()
     over.wait_send()
     for unit in range(blocks):
 
@@ -1042,15 +1056,17 @@
             pltpu.VMEM((depth, blk, width), bf),
             pltpu.VMEM((depth, blk, width), bf),
             pltpu.VMEM((depth, blk, width), bf),
-            pltpu.VMEM((packs, inner, 3 * lanes), bf),
+            pltpu.VMEM((packs * inner, 3 * lanes), bf),
             pltpu.VMEM((2, inner, 3 * lanes), bf),
+            pltpu.VMEM((2, inner, 128 + 6 * inner), bf),
+            pltpu.VMEM((inner, 128 + 6 * inner), bf),
             pltpu.VMEM((2, inner, width), bf),
-            pltpu.VMEM((2, inner, 128 + 6 * inner + width), bf),
-            pltpu.VMEM((inner, 128 + 6 * inner + width), bf),
+            pltpu.VMEM((2, inner, width), bf),
+            pltpu.VMEM((inner, width), bf),
         ]
         + [dma((blocks,))] * 2
         + [dma((depth,))] * 4
-        + [dma((5,))] * 2,
+        + [dma((3,))] * 4,
         compiler_params=params_of(collective_id=number, has_side_effects=True),
         cost_estimate=BRIEF,
         name="attn_bwd",
@@ -1406,92 +1422,190 @@
     )(*args, wgu, wd)
 
 
-def slot_rows(ext, weighted):
-    rows = ext.astype(jnp.float32)
-    count = rows.shape[1] // 3
-    coef, slot = rows[:NF, :count], rows[:NF, count : 2 * count].astype(jnp.int32)
-    hit = lax.broadcasted_iota(jnp.int32, (NF, MOST, count), 1) == slot[:, None, :]
-    hot = jnp.where(hit, coef[:, None, :] if weighted else 1.0, 0.0)
-    return hot.astype(jnp.bfloat16).reshape(NF * MOST, count)
-
-
-def dispatch_kernel(rows, weighted, tail, values, out):
-    for d in range(values.shape[0]):
-        low = nn(slot_rows(tail[d], weighted), values[d, :rows, :]).astype(jnp.bfloat16)
-        out[:, d] = low.reshape(NF, MOST, low.shape[1])
-
-
-def dispatch(ext, values, weighted):
-    devices, _, width = ext.shape
-    rows = ext.shape[1] - 16
-    some = 4
-    out = pl.pallas_call(
-        functools.partial(dispatch_kernel, rows, weighted),
-        grid=(devices // some,),
-        out_shape=shape_of((NF, devices, MOST, width), jnp.bfloat16),
-        in_specs=[
-            pl.BlockSpec((some, 16, width), lambda d: (d, rows // 16, 0)),
-            pl.BlockSpec((some,) + values.shape[1:], lambda d: (d, 0, 0)),
-        ],
-        out_specs=pl.BlockSpec((NF, some, MOST, width), lambda d: (0, d, 0, 0)),
+PACK = 80
+
+
+def pack_kernel(counts, bases, totals, tail, ext, gm, out, buf, carry, blank, sems):
+    step = pl.program_id(0)
+    some, count, width = gm.shape
+
+    @pl.when(step == 0)
+    def _():
+        carry[...] = jnp.zeros_like(carry)
+        blank[...] = jnp.zeros_like(blank)
+
+    def whole_groups(d, e):
+        at = d * NF + e
+        return (bases[at] % 16 + counts[at]) // 16
+
+    def each_copy(block, what):
+        for i in range(some):
+            for e in range(NF):
+                groups = whole_groups(block * some + i, e)
+                start = pl.multiple_of(bases[(block * some + i) * NF + e] // 16 * 16, 16)
+                for n in range(1, PACK // 16):
+
+                    @pl.when(groups == n)
+                    def _():
+                        source = buf.at[block % 2, i, e, pl.ds(0, 16 * n), :]
+                        what(pltpu.make_async_copy(source, out.at[e, pl.ds(start, 16 * n), :], sems.at[block % 2, i, e]))
+
+    def begin(copy):
+        copy.start()
+
+    def end(copy):
+        copy.wait()
+
+    @pl.when(step >= 2)
+    def _():
+        each_copy(step - 2, end)
+
+    ids = lax.broadcasted_iota(jnp.int32, (PACK, count), 0)
+    side = step % 2
+    for i in range(some):
+        d = step * some + i
+        rows = tail[i].astype(jnp.float32)
+        slot = rows[:NF, count : 2 * count].astype(jnp.int32)
+        slot = jnp.where(slot < 0, -PACK, slot)
+        hot, weighted = [], []
+        for e in range(NF):
+            hit = ids == slot[e : e + 1] + bases[d * NF + e] % 16
+            hot.append(jnp.where(hit, 1.0, 0.0).astype(jnp.bfloat16))
+            weighted.append(jnp.where(hit, rows[e : e + 1, :count], 0.0).astype(jnp.bfloat16))
+        low = nn(jnp.concatenate(hot, axis=0), ext[i, :count, :]).astype(jnp.bfloat16)
+        low_g = nn(jnp.concatenate(weighted, axis=0), gm[i]).astype(jnp.bfloat16)
+        for lanes, values in ((slice(0, width), low), (slice(width, 2 * width), low_g)):
+            for e in range(NF):
+                buf[side, i, e, :, lanes] = values[e * PACK : (e + 1) * PACK]
+    for i in range(some):
+        for e in range(NF):
+            buf[side, i, e, :16, :] += carry[e]
+            group = pl.multiple_of(whole_groups(step * some + i, e) * 16, 16)
+            carry[e] = buf[side, i, e, pl.ds(group, 16), :]
+    each_copy(step, begin)
+
+    @pl.when(step == pl.num_programs(0) - 1)
+    def _():
+        last = pl.num_programs(0)
+        each_copy(last - 2, end)
+        each_copy(last - 1, end)
+        copies = []
+        for e in range(NF):
+            start = pl.multiple_of(totals[e] // 16 * 16, 16)
+            copies.append(pltpu.make_async_copy(carry.at[e], out.at[e, pl.ds(start, 16), :], sems.at[0, 0, e]))
+            rest = out.at[e, pl.ds(start + 16, blank.shape[0]), :]
+            copies.append(pltpu.make_async_copy(blank, rest, sems.at[1, 0, e]))
+        for copy in copies:
+            copy.start()
+        for copy in copies:
+            copy.wait()
+
+
+def expert_counts(ext):
+    count = ext.shape[2] // 3
+    slot = ext[:, ext.shape[1] - 16 : ext.shape[1] - 16 + NF, count : 2 * count].astype(jnp.float32)
+    counts = (jnp.max(slot, axis=2) + 1.0).astype(jnp.int32)
+    upto = jnp.cumsum(counts, axis=0)
+    return counts.reshape(-1), (upto - counts).reshape(-1), upto[-1]
+
+
+def pack_rows(numbers, ext, gm):
+    devices, count, width = gm.shape
+    some, blank = 4, 256
+    bf = jnp.bfloat16
+    return pl.pallas_call(
+        pack_kernel,
+        grid_spec=pltpu.PrefetchScalarGridSpec(
+            num_scalar_prefetch=3,
+            grid=(devices // some,),
+            in_specs=[
+                pl.BlockSpec((some, 16, width), lambda d, *_: (d, count // 16, 0)),
+                pl.BlockSpec((some,) + ext.shape[1:], lambda d, *_: (d, 0, 0)),
+                pl.BlockSpec((some, count, width), lambda d, *_: (d, 0, 0)),
+            ],
+            out_specs=pl.BlockSpec(memory_space=pl.ANY),
+            scratch_shapes=[
+                pltpu.VMEM((2, some, NF, PACK, 2 * width), bf),
+                pltpu.VMEM((NF, 16, 2 * width), bf),
+                pltpu.VMEM((blank, 2 * width), bf),
+                pltpu.SemaphoreType.DMA((2, some, NF)),
+            ],
+        ),
+        out_shape=shape_of((NF, devices * MOST + 16 + blank, 2 * width), bf),
         compiler_params=params_of(),
         cost_estimate=BRIEF,
-        name="dispatch",
-    )(ext, values)
-    return out.reshape(NF, devices * MOST, width)
-
-
-def dw_kernel(*refs):
-    x, g, wgu, wd, dgu, dd, dg_s, du_s, hid_s = refs[:4] + refs[-5:]
-    rows = x.shape[1]
-    chunk = 256
-
-    def pieces(i, _):
-        part = pl.ds(pl.multiple_of(i * chunk, chunk), chunk)
-        xs = x[0, part, :]
-        hid, dg, du = silu_parts(nn(xs, wgu[0, 0, 0]), nn(xs, wgu[0, 0, 1]), nt(g[0, part, :], wd[0, 0]))
+        name="pack_rows",
+    )(*numbers, ext, ext, gm)
+
+
+def dw_kernel(first, totals, packed, wgu, wd, *refs):
+    dgu, dd, dg_s, du_s, hid_s = refs[-5:]
+    total = totals[first + pl.program_id(0)]
+    width = packed.shape[2] // 2
+    chunk = 512
+
+    def pieces(part):
+        xs, gs = packed[0, part, :width], packed[0, part, width:]
+        hid, dg, du = silu_parts(nn(xs, wgu[0, 0, 0]), nn(xs, wgu[0, 0, 1]), nt(gs, wd[0, 0]))
         hid_s[part, :] = hid.astype(jnp.bfloat16)
         dg_s[part, :] = dg
         du_s[part, :] = du
+
+    def chunk_of(i, _):
+        pieces(pl.ds(pl.multiple_of(i * chunk, chunk), chunk))
         return 0
 
-    lax.fori_loop(0, rows // chunk, pieces, 0)
-
-    def first(i, _):
-        part = pl.ds(pl.multiple_of(i * 256, 256), 256)
-        xs = x[0, :, part]
-        dgu[0, 0, 0, part, :] = tn(xs, dg_s[...])
-        dgu[0, 0, 1, part, :] = tn(xs, du_s[...])
-        return 0
-
-    lax.fori_loop(0, x.shape[2] // 256, first, 0)
-
-    def second(i, _):
-        part = pl.ds(pl.multiple_of(i * 256, 256), 256)
-        dd[0, 0, part, :] = tn(hid_s[:, part], g[0])
-        return 0
-
-    lax.fori_loop(0, hid_s.shape[1] // 256, second, 0)
-
-
-def weight_grads(layer, first, last, x, g, wgu, wd, earlier):
-    _, rows, width = x.shape
-    hidden = wd.shape[2]
-    gu_spec = pl.BlockSpec((1, 1, 2, width, hidden), lambda e: (layer, e + first, 0, 0, 0))
-    d_spec = pl.BlockSpec((1, 1, hidden, width), lambda e: (layer, e + first, 0, 0))
-    row_spec = pl.BlockSpec((1, rows, width), lambda e: (e + first, 0, 0))
+    needed = jnp.maximum((total + 255) // 256, 1)
+    lax.fori_loop(0, needed // 2, chunk_of, 0)
+
+    @pl.when(needed % 2 == 1)
+    def _():
+        pieces(pl.ds(pl.multiple_of((needed - 1) * 256, 256), 256))
+
+    for size in range(1, hid_s.shape[0] // 256 + 1):
+
+        @pl.when(needed == size)
+        def _():
+            rows = 256 * size
+
+            def inputs(i, _):
+                part = pl.ds(pl.multiple_of(i * 256, 256), 256)
+                xs = packed[0, :rows, part]
+                dgu[0, 0, 0, part, :] = tn(xs, dg_s[:rows, :])
+                dgu[0, 0, 1, part, :] = tn(xs, du_s[:rows, :])
+                return 0
+
+            lax.fori_loop(0, width // 256, inputs, 0)
+
+            def outputs(i, _):
+                part = pl.ds(pl.multiple_of(i * 256, 256), 256)
+                dd[0, 0, part, :] = tn(hid_s[:rows, part], packed[0, :rows, width:])
+                return 0
+
+            lax.fori_loop(0, hid_s.shape[1] // 256, outputs, 0)
+
+
+def weight_grads(layer, first, last, totals, packed, wgu, wd, earlier):
+    _, rows, both = packed.shape
+    hidden, width = wd.shape[2], wd.shape[3]
+    gu_spec = pl.BlockSpec((1, 1, 2, width, hidden), lambda e, *_: (layer, e + first, 0, 0, 0))
+    d_spec = pl.BlockSpec((1, 1, hidden, width), lambda e, *_: (layer, e + first, 0, 0))
+    row_spec = pl.BlockSpec((1, rows, both), lambda e, *_: (e + first, 0, 0))
     return pl.pallas_call(
-        dw_kernel,
-        grid=(last - first,),
+        functools.partial(dw_kernel, first),
+        grid_spec=pltpu.PrefetchScalarGridSpec(
+            num_scalar_prefetch=1,
+            grid=(last - first,),
+            in_specs=[row_spec, gu_spec, d_spec] + [pl.BlockSpec(memory_space=pl.ANY)] * len(earlier),
+            out_specs=[gu_spec, d_spec],
+            scratch_shapes=[pltpu.VMEM((rows // 256 * 256 - 256, hidden), jnp.bfloat16)] * 3,
+        ),
         out_shape=[shape_of(wgu.shape, jnp.float32), shape_of(wd.shape, jnp.float32)],
-        in_specs=[row_spec, row_spec, gu_spec, d_spec] + [pl.BlockSpec(memory_space=pl.ANY)] * len(earlier),
-        out_specs=[gu_spec, d_spec],
         input_output_aliases={4 + i: i for i in range(len(earlier))},
-        scratch_shapes=[pltpu.VMEM((rows, hidden), jnp.bfloat16)] * 3,
         compiler_params=params_of(),
         cost_estimate=BRIEF,
         name="weight_grads",
-    )(x, g, wgu, wd, *earlier)
+    )(totals, packed, wgu, wd, *earlier)
 
 
 def norm_low(x, gain):
@@ -1729,26 +1843,27 @@
     def added(first, second):
         return (first.astype(f32) + second.astype(f32)).astype(bf)
 
+    half = NF // 2
+    numbers = expert_counts(ext_all[1])
+    packed = pack_rows(numbers, ext_all[1], gm_all[1])
+    done = weight_grads(1, 0, half, numbers[2], packed, w_gate_up, w_down, ())
+    dense, done = lax.optimization_barrier((dense, done))
     got = partner(dense, 1)
-    x1 = dispatch(ext_all[1], ext_all[1], False)
-    g1 = dispatch(ext_all[1], gm_all[1], True)
-    x1, g1, got = lax.optimization_barrier((x1, g1, got))
-    dense = added(dense, got)
-    dense, x1 = lax.optimization_barrier((dense, x1))
-    got = partner(dense, 4)
-    done = weight_grads(1, 0, NF, x1, g1, w_gate_up, w_down, ())
+    done = weight_grads(1, half, NF, numbers[2], packed, w_gate_up, w_down, done)
     done, got = lax.optimization_barrier((done, got))
     dense = added(dense, got)
-    dense, ext = lax.optimization_barrier((dense, ext_all[0]))
+    dense, ext, gm = lax.optimization_barrier((dense, ext_all[0], gm_all[0]))
+    got = partner(dense, 4)
+    numbers = expert_counts(ext)
+    packed = pack_rows(numbers, ext, gm)
+    done = weight_grads(0, 0, half, numbers[2], packed, w_gate_up, w_down, done)
+    done, got = lax.optimization_barrier((done, got))
+    dense = added(dense, got)
+    dense, done = lax.optimization_barrier((dense, done))
     got = partner(dense, 2)
-    x0 = dispatch(ext, ext, False)
-    gm, x0 = lax.optimization_barrier((gm_all[0], x0))
-    g0 = dispatch(ext, gm, True)
-    done = weight_grads(0, 0, NF // 2, x0, g0, w_gate_up, w_down, done)
+    done = weight_grads(0, half, NF, numbers[2], packed, w_gate_up, w_down, done)
     done, got = lax.optimization_barrier((done, got))
     qkv, out, small = assemble(dense, got, width)
-    done, qkv, out, small = lax.optimization_barrier((done, qkv, out, small))
-    done = weight_grads(0, NF // 2, NF, x0, g0, w_gate_up, w_down, done)
     rows = jnp.swapaxes(small[..., : 2 + NC], 1, 2)
     return (
         output[None],

time: 833 us -> 775 us (0.930)
  Pallas kernels: 760 us -> 709 us
  waiting for transfers between devices: 13 us -> 0.8 us
    pallas_call x7 -> x6, Pallas kernels: 291 us -> 248 us  [the longest x4 180 us: weight_grads(): pl.pallas_call(functools.partial(dw_kernel, first), grid_spec=pltpu.Prefe...]
    ppermute x3, waiting for transfers between devices: 12.2 us -> 0.01 us  [partner(): lax.ppermute(values, 'ctx', [(i, i ^ distance) for i in range(ctx_size)])]
  transfers between devices with their start and end apart: 7 -> 7, of which waited for: 2 -> 0; matrix products, arithmetic and copies ran while one was open for 2% -> 2% of each run, Pallas kernels for 85% -> 92%
where the time goes in v6:
time: 775 us; the launch traced here: 768 us
  Pallas kernels  709 us (91%)
  local copies, waits for them, and re-layouts  14.4 us (2%)
  between operations  14.4 us (2%)
  other arithmetic  13.5 us (2%)
  starting transfers between devices  9.75 us (1%)
    pallas_call x4, Pallas kernels, weight_grads(): pl.pallas_call(functools.partial(dw_kernel, first), grid_spec=pltpu.Prefe...  180 us
    pallas_call x2, Pallas kernels, attn_backward(): pl.pallas_call(attn_bwd_kernel, out_shape=[shape_of((count, width), jnp.f...  142 us
    pallas_call x2, Pallas kernels, attn_forward(): pl.pallas_call(attn_fwd_kernel, grid=(1,), out_shape=[shape_of((seq, widt...  126 us
    pallas_call x2, Pallas kernels, ffn_forward(): pl.pallas_call(ffn_fwd_kernel, grid=(NF,), out_shape=outs, in_specs=[whol...  95 us
    pallas_call x2, Pallas kernels, ffn_backward(): pl.pallas_call(ffn_bwd_kernel, grid=(NF,), out_shape=outs, in_specs=[whol...  92.4 us
    pallas_call x2, Pallas kernels, pack_rows(): pl.pallas_call(pack_kernel, grid_spec=pltpu.PrefetchScalarGridSpec(num_sc...  67.5 us
  transfers between devices with their start and end apart: 7, of which 0 were waited for; matrix products, arithmetic and copies ran while one was open for 2% of the time, Pallas kernels for 92%

profile of v6, /device:TPU:0, one launch (start us, length us, event | category | flops | bytes accessed | tf_op | source)
XLA Modules:
  0.0 767.8 jit_solution(12256695240249436259)
XLA Ops:
  7.2 0.7 all-gather.9.cloned.1.call-update
  8.0 0.7 convert_bitcast_fusion
  8.7 0.7 convert_bitcast_fusion.1
  9.4 0.1 reshape.232
  9.5 0.7 pad_maximum_fusion.1
  10.2 6.3 all-gather.3
  16.6 0.1 reshape.250
  16.8 0.1 reshape.237
  16.9 0.1 reshape.235
  17.0 0.1 dynamic-slice_reduce_fusion
  17.0 0.1 reshape.233
  17.1 0.2 subtract_reduce_fusion.order
  17.3 0.7 select_reduce_fusion.inv
  18.0 0.6 fusion.9
  18.7 0.9 bitcast_convert_fusion.x
  19.6 57.0 %attn_fwd.2 = (bf16[1024,768]{1,0:T(8,128)(2,1)}, bf16[1024,768]{1,0:T(8,128)(2,1)}, f32[1024,256]{1,0:T(8,128)}, f32[1024,128]{1,0:T(8,128)}, bf16[8,128,256]{2...) custom-call(s32[8]{0:T(128)} %copy-done.8, ...), custom_call_target="tpu_custom_call" | custom-call | flops 1 | bytes 1 | tf_op jit(solution)/shard_map/attn_fwd/pallas_call | solution.py:802
  76.6 0.1 fusion.7
  76.7 0.6 gather_fusion
  77.3 0.6 slice_bitcast_fusion.1
  77.9 0.6 broadcast_in_dim.30.before
  78.5 46.2 %ffn_fwd.2 = (bf16[4,256,768]{2,1,0:T(8,128)(2,1)}, f32[4,56,256]{2,1,0:T(8,128)}, bf16[272,768]{1,0:T(8,128)(2,1)}, f32[256,768]{1,0:T(8,128)}) custom-call(bf16[256,768]{1,0:T(8,128)(2,1)} %get-tuple-element.84.ub, f32[256,768]{1,0:T(8,128)} %get-tuple-element.85.hst, bf16[20,768]{1,0:T(8,128)(2,1)} %get-tuple-element.198.small, ...), custom_call_target="tpu_custom_call" | custom-call | flops 1 | bytes 1 | tf_op jit(solution)/shard_map/ffn_fwd/pallas_call | solution.py:1243
  124.8 69.3 %attn_fwd.3 = (bf16[1024,768]{1,0:T(8,128)(2,1)}, bf16[1024,768]{1,0:T(8,128)(2,1)}, f32[1024,256]{1,0:T(8,128)}, f32[1024,128]{1,0:T(8,128)}, bf16[8,128,256]{2...) custom-call(s32[8]{0:T(128)} %copy-done.8, ...), custom_call_target="tpu_custom_call" | custom-call | flops 1 | bytes 1 | tf_op jit(solution)/shard_map/attn_fwd/pallas_call | solution.py:802
  194.1 1.5 slice.62.before
  195.6 48.9 %ffn_fwd.3 = (bf16[4,256,768]{2,1,0:T(8,128)(2,1)}, f32[4,56,256]{2,1,0:T(8,128)}, bf16[272,768]{1,0:T(8,128)(2,1)}, f32[256,768]{1,0:T(8,128)}) custom-call(bf16[256,768]{1,0:T(8,128)(2,1)} %get-tuple-element.88.ub, f32[256,768]{1,0:T(8,128)} %get-tuple-element.89.hst, bf16[20,768]{1,0:T(8,128)(2,1)} %get-tuple-element.197.small, ...), custom_call_target="tpu_custom_call" | custom-call | flops 1 | bytes 1 | tf_op jit(solution)/shard_map/ffn_fwd/pallas_call | solution.py:1243
  244.5 0.4 all-gather.15.cloned.1.call-start
  244.9 0.6 slice_bitcast_fusion.3
  245.5 0.9 bitcast_convert_fusion.1.gx
  246.4 0.6 broadcast_in_dim.32.gprev
  247.0 46.5 %ffn_bwd.2 = (f32[256,768]{1,0:T(8,128)}, bf16[8,128,256]{2,1,0:T(8,128)(2,1)}, bf16[4,192,768]{2,1,0:T(8,128)(2,1)}, f32[19,768]{1,0:T(8,128)}, f32[16,256]{1,0:T(8,128)}) custom-call(bf16[256,768]{1,0:T(8,128)(2,1)} %bitcast.63, f32[256,768]{1,0:T(8,128)} %bitcast_convert_fusion.1.gx, bf16[4,256,768]{2,1,0:T(8,128)(2,1)} %get-tuple-element.102.ubf, ...), custom_call_target="tpu_custom_call" | custom-call | flops 1 | bytes 1 | tf_op jit(solution)/shard_map/ffn_bwd/pallas_call | solution.py:1396
  293.6 83.9 %attn_bwd.2 = (f32[256,768]{1,0:T(8,128)}, bf16[256,768]{1,0:T(8,128)(2,1)}, bf16[192,2048]{1,0:T(8,128)(2,1)}) custom-call(s32[8]{0:T(128)} %copy-done.8, s32[8]{0:T(128)} %select_reduce_fusion.inv, bf16[1024,768]{1,0:T(8,128)(2,1)} %get-tuple-element.97.n1s, bf16[768,768]{1,0:T(8,128)(2,1)} %get-tuple-element.98.w, f32[1024,128]{1,0:T(8,128)} %constant.86.clone.cosine, ...), custom_call_target="tpu_custom_call" | custom-call | flops 1 | bytes 1 | tf_op jit(solution)/shard_map/attn_bwd/pallas_call | solution.py:1040
  377.5 45.9 %ffn_bwd.3 = (f32[256,768]{1,0:T(8,128)}, bf16[8,128,256]{2,1,0:T(8,128)(2,1)}, bf16[4,192,768]{2,1,0:T(8,128)(2,1)}, f32[19,768]{1,0:T(8,128)}, f32[16,256]{1,0:T(8,128)}) custom-call(bf16[256,768]{1,0:T(8,128)(2,1)} %get-tuple-element.137.gm, f32[256,768]{1,0:T(8,128)} %get-tuple-element.113.gx, bf16[4,256,768]{2,1,0:T(8,128)(2,1)} %get-tuple-element.114.ubf, ...), custom_call_target="tpu_custom_call" | custom-call | flops 1 | bytes 1 | tf_op jit(solution)/shard_map/ffn_bwd/pallas_call | solution.py:1396
  423.4 58.3 %attn_bwd.3 = (f32[256,768]{1,0:T(8,128)}, bf16[256,768]{1,0:T(8,128)(2,1)}, bf16[192,2048]{1,0:T(8,128)(2,1)}) custom-call(s32[8]{0:T(128)} %copy-done.8, s32[8]{0:T(128)} %select_reduce_fusion.inv, bf16[1024,768]{1,0:T(8,128)(2,1)} %get-tuple-element.92.n1s, bf16[768,768]{1,0:T(8,128)(2,1)} %get-tuple-element.93.w, f32[1024,128]{1,0:T(8,128)} %constant.86.clone.cosine, ...), custom_call_target="tpu_custom_call" | custom-call | flops 1 | bytes 1 | tf_op jit(solution)/shard_map/attn_bwd/pallas_call | solution.py:1040
  481.8 1.3 pad_maximum_fusion
  483.1 1.0 slice_reduce_fusion
  484.2 0.1 convert_element_type.67.counts
  484.3 0.1 reduce_window_sum.22
  484.4 0.6 sub.45.bases
  485.0 0.5 slice_bitcast_fusion.6.totals
  485.5 33.7 %pack_rows.2.packed = bf16[8,2320,1536]{2,1,0:T(8,128)(2,1)} custom-call(s32[256]{0:T(256)} %copy-done.9, s32[256]{0:T(256)} %sub.45.bases, s32[8]{0:T(128)} %slice_bitcast_fusion.6.totals, bf16[32,272,768]{2,1,0:T(8,128)(2,1)} %bitcast.60, bf16[32,272,768]{2,1,0:T(8,128)(2,1)} %bitcast.61, bf16[32,256,768]{2,1,0:T(8,128)(2,1)} %all-gather.9.cloned.1.call-done.gm), custom_call_target="tpu_custom_call" | custom-call | flops 1 | bytes 1 | tf_op jit(solution)/shard_map/pack_rows/pallas_call | solution.py:1516
  519.2 50.4 %weight_grads.4 = (f32[2,8,2,768,512]{4,3,2,1,0:T(8,128)}, f32[2,8,512,768]{3,2,1,0:T(8,128)}) custom-call(s32[8]{0:T(128)} %slice_bitcast_fusion.6.totals, bf16[8,2320,1536]{2,1,0:T(8,128)(2,1)} %pack_rows.2.packed, bf16[2,8,2,768,512]{4,3,2,1,0:T(8,128)(2,1)} %wgu.15, bf16[2,8,512,768]{3,2,1,0:T(8,128)(2,1)} %wd.15), custom_call_target="tpu_custom_call" | custom-call | flops 1 | bytes 1 | tf_op jit(solution)/shard_map/weight_grads/pallas_call | solution.py:1594
  569.6 1.0 collective-permute-start
  570.6 39.8 %weight_grads.5 = (f32[2,8,2,768,512]{4,3,2,1,0:T(8,128)}, f32[2,8,512,768]{3,2,1,0:T(8,128)}) custom-call(s32[8]{0:T(128)} %slice_bitcast_fusion.6.totals, bf16[8,2320,1536]{2,1,0:T(8,128)(2,1)} %pack_rows.2.packed, bf16[2,8,2,768,512]{4,3,2,1,0:T(8,128)(2,1)} %wgu.15, bf16[2,8,512,768]{3,2,1,0:T(8,128)(2,1)} %wd.15, ...), custom_call_target="tpu_custom_call", output_to_operand_aliasing={{0}: (4, {}), {1}: (5, {})} | custom-call | flops 1 | bytes 1 | tf_op jit(solution)/shard_map/weight_grads/pallas_call | solution.py:1594
  610.4 2.0 add_convert_fusion.1
  612.5 2.4 collective-permute-start.1
  614.8 1.0 slice_reduce_fusion.1
  615.9 0.1 convert_element_type.73.counts
  616.0 0.1 reduce_window_sum.24
  616.1 0.6 sub.46.bases
  616.7 0.5 slice_bitcast_fusion.5.totals
  617.2 33.8 %pack_rows.3.packed = bf16[8,2320,1536]{2,1,0:T(8,128)(2,1)} custom-call(s32[256]{0:T(256)} %copy-done.10, s32[256]{0:T(256)} %sub.46.bases, s32[8]{0:T(128)} %slice_bitcast_fusion.5.totals, bf16[32,272,768]{2,1,0:T(8,128)(2,1)} %bitcast.57, bf16[32,272,768]{2,1,0:T(8,128)(2,1)} %bitcast.58, bf16[32,256,768]{2,1,0:T(8,128)(2,1)} %bitcast.62), custom_call_target="tpu_custom_call" | custom-call | flops 1 | bytes 1 | tf_op jit(solution)/shard_map/pack_rows/pallas_call | solution.py:1516
  651.0 50.5 %weight_grads.6 = (f32[2,8,2,768,512]{4,3,2,1,0:T(8,128)}, f32[2,8,512,768]{3,2,1,0:T(8,128)}) custom-call(s32[8]{0:T(128)} %slice_bitcast_fusion.5.totals, bf16[8,2320,1536]{2,1,0:T(8,128)(2,1)} %pack_rows.3.packed, bf16[2,8,2,768,512]{4,3,2,1,0:T(8,128)(2,1)} %wgu.15, bf16[2,8,512,768]{3,2,1,0:T(8,128)(2,1)} %wd.15, ...), custom_call_target="tpu_custom_call", output_to_operand_aliasing={{0}: (4, {}), {1}: (5, {})} | custom-call | flops 1 | bytes 1 | tf_op jit(solution)/shard_map/weight_grads/pallas_call | solution.py:1594
  701.5 2.0 add_convert_fusion.ours
  703.5 5.8 collective-permute-start.2
  709.3 39.4 %weight_grads.7 = (f32[2,8,2,768,512]{4,3,2,1,0:T(8,128)}, f32[2,8,512,768]{3,2,1,0:T(8,128)}) custom-call(s32[8]{0:T(128)} %slice_bitcast_fusion.5.totals, bf16[8,2320,1536]{2,1,0:T(8,128)(2,1)} %pack_rows.3.packed, bf16[2,8,2,768,512]{4,3,2,1,0:T(8,128)(2,1)} %wgu.15, bf16[2,8,512,768]{3,2,1,0:T(8,128)(2,1)} %wd.15, ...), custom_call_target="tpu_custom_call", output_to_operand_aliasing={{0}: (4, {}), {1}: (5, {})} | custom-call | flops 1 | bytes 1 | tf_op jit(solution)/shard_map/weight_grads/pallas_call | solution.py:1594
  748.7 1.2 copy-done.2
  749.9 5.1 assemble.1
  755.0 1.0 slice_bitcast_fusion
  756.0 1.0 slice.71
  757.0 0.1 fusion.8
  757.2 0.7 copy.50
  757.9 0.7 copy.51
  758.6 0.7 copy.52
  759.3 0.9 copy.66
  760.2 0.9 copy.67
  (48 shorter events, 0.6 us)
Async XLA Ops:
  7.2 11.5 %copy-start.6 = (bf16[1,256,768]{2,1,0:T(8,128)(2,1)S(1)}, bf16[1,256,768]{2,1,0:T(8,128)(2,1)}, u32[]{:S(2)}) copy-start(bf16[1,256,768]{2,1,0:T(8,128)(2,1)} %param.14) | copy-start | bytes 1179652
  7.2 188.4 %all-gather.9.cloned.1.call-start = ((), (), s32[]{:S(2)}) async-start(), calls=%async_computation | async-start | bytes 12976128 | tf_op jit(solution)/shard_map/all_gather | solution.py:1800
  7.9 285.7 %all-gather.11.cloned.1.call-start = ((), (), s32[]{:S(2)}) async-start(), calls=%async_computation.1 | async-start | bytes 13787136 | tf_op jit(solution)/shard_map/all_gather | solution.py:1814
  17.3 2.3 copy-start.8
  124.7 358.4 %all-gather.13.cloned.1.call-start = ((), (), s32[]{:S(2)}) async-start(), calls=%async_computation.2 | async-start | bytes 13787136 | tf_op jit(solution)/shard_map/all_gather | solution.py:1814
  195.5 49.4 %copy-start.7 = (s32[2,1,256,2]{2,3,1,0:T(2,128)S(1)}, s32[2,1,256,2]{2,3,1,0:T(2,128)}, u32[]{:S(2)}) copy-start(s32[2,1,256,2]{2,3,1,0:T(2,128)} %param.17) | copy-start | bytes 12292
  195.5 50.0 %copy-start.1 = (bf16[1,256,768]{2,1,0:T(8,128)(2,1)S(1)}, bf16[1,256,768]{2,1,0:T(8,128)(2,1)}, u32[]{:S(2)}) copy-start(bf16[1,256,768]{2,1,0:T(8,128)(2,1)} %param.15) | copy-start | bytes 1179652
  244.5 368.0 %all-gather.15.cloned.1.call-start = ((), (), s32[]{:S(2)}) async-start(), calls=%async_computation.3 | async-start | bytes 12976128 | tf_op jit(solution)/shard_map/all_gather | solution.py:1838
  423.4 58.3 %copy-start.5 = (bf16[192,2048]{1,0:T(8,128)(2,1)S(1)}, bf16[192,2048]{1,0:T(8,128)(2,1)}, u32[]{:S(2)}) copy-start(bf16[192,2048]{1,0:T(8,128)(2,1)} %get-tuple-element.124) | copy-start | bytes 2359300
  484.3 1.2 copy-start.9
  569.6 40.8 %collective-permute-start = (bf16[2,192,2048]{2,1,0:T(8,128)(2,1)S(1)}, bf16[2,192,2048]{2,1,0:T(8,128)(2,1)}, u32[]{:S(2)}, u32[]{:S(2)}) collective-permute-start(bf16[2,192,2048]{2,1,0:T(8,128)(2,1)S(1)} %pad_maximum_fusion), channel_id=1, source_target_pairs={{0,4},{4,0},{8,12},{12,8},{16,20},{20,16},{24,28},{28,24},{1,5},{5... | collective-permute-start | bytes 4718600 | tf_op jit(solution)/shard_map/ppermute | solution.py:1841
  612.5 89.0 %collective-permute-start.1 = (bf16[2,192,2048]{2,1,0:T(8,128)(2,1)S(1)}, bf16[2,192,2048]{2,1,0:T(8,128)(2,1)}, u32[]{:S(2)}, u32[]{:S(2)}) collective-permute-start(bf16[2,192,2048]{2,1,0:T(8,128)(2,1)S(1)} %add_convert_fusion.1), channel_id=1, source_target_pairs={{0,16},{4,20},{8,24},{12,28},{16,0},{20,4},{24,8},{28,12},{1,17},{... | collective-permute-start | bytes 4718600 | tf_op jit(solution)/shard_map/ppermute | solution.py:1841
  616.0 1.2 copy-start.10
  703.5 45.2 %copy-start = (bf16[2,192,2048]{2,1,0:T(8,128)(2,1)}, bf16[2,192,2048]{2,1,0:T(8,128)(2,1)S(1)}, u32[]{:S(2)}) copy-start(bf16[2,192,2048]{2,1,0:T(8,128)(2,1)S(1)} %add_convert_fusion.ours) | copy-start | bytes 4718596
  703.5 45.2 %collective-permute-start.2 = (bf16[2,192,2048]{2,1,0:T(8,128)(2,1)S(1)}, bf16[2,192,2048]{2,1,0:T(8,128)(2,1)S(1)}, u32[]{:S(2)}, u32[]{:S(2)}) collective-permute-start(bf16[2,192,2048]{2,1,0:T(8,128)(2,1)S(1)} %add_convert_fusion.ours), channel_id=1, source_target_pairs={{0,8},{4,12},{8,0},{12,4},{16,24},{20,28},{24,16},{28,20},{1,9},{5... | collective-permute-start | bytes 4718600 | tf_op jit(solution)/shard_map/ppermute | solution.py:1841
  748.7 1.2 copy-start.2
  755.0 4.3 copy-start.3
  757.0 3.1 copy-start.4
Sparse Core Ops, SparseCore 0:
  10.9 126.7 all-gather.8
  140.6 124.1 all-gather.10
  267.7 121.2 all-gather.12
  483.2 99.7 all-gather.14

commit v7 on v6

--- a/solution.py
+++ b/solution.py
@@ -615,7 +615,7 @@
     order, inv, x, small, wq, cosine, sine, wo_own,
     n1s, qkv, o, lse, ob, hst, ub, w, wo,
     n1own, n1r, osort, osend, orecv, cols, w_s, wo_s,
-    n_send, n_recv, f_send, f_recv, o_send, o_recv, w_send, w_recv, v_send, v_recv,
+    n_send, n_recv, f_send, f_recv, p_send, o_send, o_recv, w_send, w_recv, v_send, v_recv,
 ):
     blocks, blk, _ = n1r.shape
     lanes = o.shape[1]
@@ -638,14 +638,25 @@
     def n1_copy(zz):
         return remote(n1own.at[zz // 2], n1r.at[own], n_send.at[zz], n_recv.at[z], 2 * zz + k, 2 * y + xx)
 
+    def sent(zz):
+        there = jnp.logical_not(jnp.logical_and(same, zz == z))
+        return there if zz in (1, 2) else jnp.logical_and(there, z // 2 == zz // 2)
+
+    def passed(zz):
+        return jnp.logical_and(z // 2 != zz // 2, jnp.logical_or(z == 1, z == 2))
+
+    def pass_copy(zz):
+        slot = n1r.at[2 * zz + k]
+        other = z // 2 * 2 + 1 - z % 2
+        return remote(slot, slot, p_send.at[zz], n_recv.at[zz], 2 * other + xx, 2 * y + k)
+
     for zz in range(depth):
-        alone = jnp.logical_and(same, zz == z)
-
-        @pl.when(jnp.logical_not(alone))
+
+        @pl.when(sent(zz))
         def _():
             n1_copy(zz).start()
 
-        @pl.when(alone)
+        @pl.when(jnp.logical_and(same, zz == z))
         def _():
             n1r[own] = n1own[zz // 2]
 
@@ -689,6 +700,10 @@
         @pl.when(jnp.logical_not(jnp.logical_and(same, zz == z)))
         def _():
             remote(n1own.at[0], n1r.at[2 * zz + k], n_send.at[zz], n_recv.at[zz], 2 * zz + k, 2 * y + xx).wait_recv()
+
+        @pl.when(passed(zz))
+        def _():
+            pass_copy(zz).start()
 
         forward_copy(zz).start()
     for zz in range(depth):
@@ -772,9 +787,13 @@
     ub[...] = low
     for zz in range(depth):
 
-        @pl.when(jnp.logical_not(jnp.logical_and(same, zz == z)))
+        @pl.when(sent(zz))
         def _():
             n1_copy(zz).wait_send()
+
+        @pl.when(passed(zz))
+        def _():
+            pass_copy(zz).wait_send()
 
         forward_copy(zz).wait_send()
     for index in range(3):
@@ -827,7 +846,7 @@
             pltpu.VMEM((width, 3 * lanes), bf),
             pltpu.VMEM((packs, inner, width), bf),
         ]
-        + [dma((blocks // 2,))] * 4
+        + [dma((blocks // 2,))] * 5
         + [dma((blocks,))] * 2
         + [dma((3,))] * 4,
         compiler_params=params_of(collective_id=number, has_side_effects=True),
@@ -839,7 +858,7 @@
 def attn_bwd_kernel(
     order, inv, n1s, w, cosine, sine, qkv, o, lse, go, ghst, x, small, gsmall, gwo,
     gx, gm, dense,
-    gor, gos, grads, acc, gns, sib_out, sib_in, gn_out, gnr, gw, gw_in, both, both_in, wo_in, wo_both, wo_over,
+    gor, gos, grads, acc, gns, sib_out, sib_in, gn_out, gnr, gw, gw_in, both, both_in, wo_in, wo_both, wo_over, probs,
     o_send, o_recv, s_send, s_recv, g_send, g_recv, r_send, r_recv, w_send, w_recv,
 ):
     blocks, blk, width = grads.shape
@@ -878,6 +897,19 @@
     wo_far = remote(wo_both.at[1 - y], wo_over, w_send.at[2], w_recv.at[2], own, 2 * (1 - y) + k)
     wo_copy(0).start()
     wo_copy(1).start()
+    lane = lax.broadcasted_iota(jnp.int32, (step, 128), 1)
+    for i in range(seq // step):
+        part = slice(i * step, (i + 1) * step)
+        span = (i + 1) * step
+        seen = lax.broadcasted_iota(jnp.int32, (step, span), 1) <= (
+            lax.broadcasted_iota(jnp.int32, (step, span), 0) + i * step
+        )
+        for head in range(GROUP_HEADS):
+            at = head // 2 * 128
+            q = jnp.where(lane // 64 == head % 2, qkv[part, at : at + 128], zero)
+            s = nt(q, qkv[:span, lanes + at : lanes + at + 128])
+            p = jnp.exp(jnp.where(seen, s, -1e30) - lse[part, head : head + 1])
+            probs[head, part, :span] = jnp.where(seen, p, 0.0)
     for ctx in range(blocks):
 
         @pl.when(jnp.logical_not(jnp.logical_and(same, ctx == own)))
@@ -891,13 +923,9 @@
     wo_far.start()
     for b in range(blocks):
         gos[b * blk : (b + 1) * blk, :] = gor[inv[b]]
-    lane = lax.broadcasted_iota(jnp.int32, (step, 128), 1)
     for i in range(seq // step):
         part = slice(i * step, (i + 1) * step)
         span = (i + 1) * step
-        seen = lax.broadcasted_iota(jnp.int32, (step, span), 1) <= (
-            lax.broadcasted_iota(jnp.int32, (step, span), 0) + i * step
-        )
         key_lane = lax.broadcasted_iota(jnp.int32, (span, 128), 1)
         for head in range(GROUP_HEADS):
             tile, side = head // 2, head % 2
@@ -908,8 +936,7 @@
             keys = qkv[:span, lanes + at : lanes + at + 128]
             values = qkv[:span, 2 * lanes + at : 2 * lanes + at + 128]
             delta = jnp.sum(g.astype(jnp.float32) * o[part, at : at + 128], axis=1, keepdims=True)
-            s = nt(q, keys)
-            p = jnp.where(seen, jnp.exp(jnp.where(seen, s, -1e30) - lse[part, head : head + 1]), 0.0)
+            p = probs[head, part, :span]
             ds = (p * (nt(g, values) - delta)).astype(jnp.bfloat16)
             acc[:span, 2 * lanes + at : 2 * lanes + at + 128] += tn(p.astype(jnp.bfloat16), g)
             acc[:span, lanes + at : lanes + at + 128] += tn(ds, q)
@@ -1063,6 +1090,7 @@
             pltpu.VMEM((2, inner, width), bf),
             pltpu.VMEM((2, inner, width), bf),
             pltpu.VMEM((inner, width), bf),
+            pltpu.VMEM((GROUP_HEADS, seq, seq), jnp.float32),
         ]
         + [dma((blocks,))] * 2
         + [dma((depth,))] * 4
@@ -1539,24 +1567,29 @@
 
 
 def dw_kernel(first, totals, packed, wgu, wd, *refs):
-    dgu, dd, dg_s, du_s, hid_s = refs[-5:]
+    dgu, dd, pair_s, hid_s = refs[-4:]
+    hidden = hid_s.shape[1]
     total = totals[first + pl.program_id(0)]
     width = packed.shape[2] // 2
-    chunk = 512
+    chunk = 1024
 
     def pieces(part):
         xs, gs = packed[0, part, :width], packed[0, part, width:]
         hid, dg, du = silu_parts(nn(xs, wgu[0, 0, 0]), nn(xs, wgu[0, 0, 1]), nt(gs, wd[0, 0]))
         hid_s[part, :] = hid.astype(jnp.bfloat16)
-        dg_s[part, :] = dg
-        du_s[part, :] = du
+        pair_s[part, :hidden] = dg
+        pair_s[part, hidden:] = du
 
     def chunk_of(i, _):
         pieces(pl.ds(pl.multiple_of(i * chunk, chunk), chunk))
         return 0
 
     needed = jnp.maximum((total + 255) // 256, 1)
-    lax.fori_loop(0, needed // 2, chunk_of, 0)
+    lax.fori_loop(0, needed // 4, chunk_of, 0)
+
+    @pl.when(needed % 4 >= 2)
+    def _():
+        pieces(pl.ds(pl.multiple_of(needed // 4 * chunk, 512), 512))
 
     @pl.when(needed % 2 == 1)
     def _():
@@ -1569,20 +1602,21 @@
             rows = 256 * size
 
             def inputs(i, _):
-                part = pl.ds(pl.multiple_of(i * 256, 256), 256)
+                part = pl.ds(pl.multiple_of(i * 384, 384), 384)
                 xs = packed[0, :rows, part]
-                dgu[0, 0, 0, part, :] = tn(xs, dg_s[:rows, :])
-                dgu[0, 0, 1, part, :] = tn(xs, du_s[:rows, :])
+                both = tn(xs, pair_s[:rows, :])
+                dgu[0, 0, 0, part, :] = both[:, :hidden]
+                dgu[0, 0, 1, part, :] = both[:, hidden:]
                 return 0
 
-            lax.fori_loop(0, width // 256, inputs, 0)
+            lax.fori_loop(0, width // 384, inputs, 0)
 
             def outputs(i, _):
-                part = pl.ds(pl.multiple_of(i * 256, 256), 256)
+                part = pl.ds(pl.multiple_of(i * 512, 512), 512)
                 dd[0, 0, part, :] = tn(hid_s[:rows, part], packed[0, :rows, width:])
                 return 0
 
-            lax.fori_loop(0, hid_s.shape[1] // 256, outputs, 0)
+            lax.fori_loop(0, hid_s.shape[1] // 512, outputs, 0)
 
 
 def weight_grads(layer, first, last, totals, packed, wgu, wd, earlier):
@@ -1598,7 +1632,10 @@
             grid=(last - first,),
             in_specs=[row_spec, gu_spec, d_spec] + [pl.BlockSpec(memory_space=pl.ANY)] * len(earlier),
             out_specs=[gu_spec, d_spec],
-            scratch_shapes=[pltpu.VMEM((rows // 256 * 256 - 256, hidden), jnp.bfloat16)] * 3,
+            scratch_shapes=[
+                pltpu.VMEM((rows // 256 * 256 - 256, 2 * hidden), jnp.bfloat16),
+                pltpu.VMEM((rows // 256 * 256 - 256, hidden), jnp.bfloat16),
+            ],
         ),
         out_shape=[shape_of(wgu.shape, jnp.float32), shape_of(wd.shape, jnp.float32)],
         input_output_aliases={4 + i: i for i in range(len(earlier))},
@@ -1704,12 +1741,16 @@
     return ghst, jnp.stack(go), jnp.stack(gwo), jnp.concatenate(sums + [grad_router], axis=0), glog
 
 
-def assemble_kernel(ours, theirs, qkv, out, small):
+def assemble_kernel(ours, theirs, qkv, out, gains, router, consts):
     z, _, _, _ = place()
-    layers, shard = ours.shape[0], ours.shape[1]
+    layers = ours.shape[0]
     inner = GROUP_HEADS * HEAD_DIM
     for l in range(layers):
-        small[l] = ours[l, :, :128].astype(jnp.float32) + theirs[l, :, :128].astype(jnp.float32)
+        small = ours[l, :, :128].astype(jnp.float32) + theirs[l, :, :128].astype(jnp.float32)
+        router[l] = small[:, 2 + NC : 2 + NC + 16]
+        rows = jnp.transpose(small)
+        gains[l] = rows[:2]
+        consts[l] = rows[2 : 2 + NC]
         first = 128 + 6 * inner
         out[l] = ours[l, :, first:].astype(jnp.float32) + theirs[l, :, first:].astype(jnp.float32)
         for group in range(4):
@@ -1726,15 +1767,18 @@
 def assemble(ours, theirs, width):
     layers, shard, _ = ours.shape
     vm = pl.BlockSpec(memory_space=pltpu.VMEM)
+    f32 = jnp.float32
     return pl.pallas_call(
         assemble_kernel,
         out_shape=[
-            shape_of((layers, 3, shard, width), jnp.float32),
-            shape_of((layers, shard, width), jnp.float32),
-            shape_of((layers, shard, 128), jnp.float32),
+            shape_of((layers, 3, shard, width), f32),
+            shape_of((layers, shard, width), f32),
+            shape_of((layers, 2, shard), f32),
+            shape_of((layers, shard, 16), f32),
+            shape_of((layers, NC, shard), f32),
         ],
         in_specs=[vm] * 2,
-        out_specs=[vm] * 3,
+        out_specs=[vm] * 5,
         compiler_params=params_of(),
         cost_estimate=BRIEF,
         name="assemble",
@@ -1807,11 +1851,13 @@
         )
         if l == 1:
             ub, gm_all[1] = lax.optimization_barrier((ub, gm_all[1]))
+            hst, first_ext = lax.optimization_barrier((hst, ext_all[0]))
+            ext_all[0] = lax.all_gather(first_ext, everyone, axis=0, tiled=False)
         ubf, table, ext, x_next = ffn_forward(
             l, ub, hst, smalls[l], routes_f[:, l], before, w_gate_up, w_down, 2 * l + 1
         )
         before = table[:, LOGI : LOGI + 16]
-        ext_all[l] = lax.all_gather(ext, everyone, axis=0, tiled=False)
+        ext_all[l] = ext if l == 0 else lax.all_gather(ext, everyone, axis=0, tiled=False)
         kept.append((x, n1s, qkv, o, lse, ob, hst, w, wo, ubf, table))
         x = x_next
     output = x
@@ -1846,10 +1892,9 @@
     half = NF // 2
     numbers = expert_counts(ext_all[1])
     packed = pack_rows(numbers, ext_all[1], gm_all[1])
-    done = weight_grads(1, 0, half, numbers[2], packed, w_gate_up, w_down, ())
-    dense, done = lax.optimization_barrier((dense, done))
+    dense, packed = lax.optimization_barrier((dense, packed))
     got = partner(dense, 1)
-    done = weight_grads(1, half, NF, numbers[2], packed, w_gate_up, w_down, done)
+    done = weight_grads(1, 0, NF, numbers[2], packed, w_gate_up, w_down, ())
     done, got = lax.optimization_barrier((done, got))
     dense = added(dense, got)
     dense, ext, gm = lax.optimization_barrier((dense, ext_all[0], gm_all[0]))
@@ -1863,16 +1908,15 @@
     got = partner(dense, 2)
     done = weight_grads(0, half, NF, numbers[2], packed, w_gate_up, w_down, done)
     done, got = lax.optimization_barrier((done, got))
-    qkv, out, small = assemble(dense, got, width)
-    rows = jnp.swapaxes(small[..., : 2 + NC], 1, 2)
+    qkv, out, gain_grad, router_grad, const_grad = assemble(dense, got, width)
     return (
         output[None],
         gx[None],
-        rows[:, :2],
+        gain_grad,
         qkv,
         out,
-        small[..., 2 + NC : 2 + NC + 16],
-        rows[:, 2:],
+        router_grad,
+        const_grad,
         done[0],
         done[1],
     )

time: 775 us -> 748 us (0.965)
  Pallas kernels: 709 us -> 671 us
  waiting for transfers between devices: 0.8 us -> 10.7 us
    pallas_call x2, Pallas kernels: 142 us -> 117 us  [attn_backward(): pl.pallas_call(attn_bwd_kernel, out_shape=[shape_of((count, width), jnp.f...]
    pallas_call x4 -> x3, Pallas kernels: 180 us -> 163 us  [weight_grads(): pl.pallas_call(functools.partial(dw_kernel, first), grid_spec=pltpu.Prefe...]
    pallas_call x2, Pallas kernels: 92.4 us -> 106 us  [ffn_backward(): pl.pallas_call(ffn_bwd_kernel, grid=(NF,), out_shape=outs, in_specs=[whol...]
    pallas_call x2, Pallas kernels: 126 us -> 116 us  [attn_forward(): pl.pallas_call(attn_fwd_kernel, grid=(1,), out_shape=[shape_of((seq, widt...]
    all_gather x2, waiting for transfers between devices: 0.04 us -> 8.1 us  [the longest x1 8.08 us: by_heads(): ext_all[0] = lax.all_gather(first_ext, everyone, axis=0, tiled=False)]
  transfers between devices with their start and end apart: 7 -> 7, of which waited for: 0 -> 2; matrix products, arithmetic and copies ran while one was open for 2% -> 3% of each run, Pallas kernels for 92% -> 91%
where the time goes in v7:
time: 748 us; the launch traced here: 735 us
  Pallas kernels  671 us (90%)
  between operations  14.3 us (2%)
  other arithmetic  13.5 us (2%)
  local copies, waits for them, and re-layouts  11.8 us (2%)
  waiting for transfers between devices  10.7 us (1%)
  starting transfers between devices  7.74 us (1%)
    pallas_call x3, Pallas kernels, weight_grads(): pl.pallas_call(functools.partial(dw_kernel, first), grid_spec=pltpu.Prefe...  163 us
    pallas_call x2, Pallas kernels, attn_backward(): pl.pallas_call(attn_bwd_kernel, out_shape=[shape_of((count, width), jnp.f...  117 us
    pallas_call x2, Pallas kernels, attn_forward(): pl.pallas_call(attn_fwd_kernel, grid=(1,), out_shape=[shape_of((seq, widt...  116 us
    pallas_call x2, Pallas kernels, ffn_backward(): pl.pallas_call(ffn_bwd_kernel, grid=(NF,), out_shape=outs, in_specs=[whol...  106 us
    pallas_call x2, Pallas kernels, ffn_forward(): pl.pallas_call(ffn_fwd_kernel, grid=(NF,), out_shape=outs, in_specs=[whol...  96.1 us
    pallas_call x2, Pallas kernels, pack_rows(): pl.pallas_call(pack_kernel, grid_spec=pltpu.PrefetchScalarGridSpec(num_sc...  67.3 us
  transfers between devices with their start and end apart: 7, of which 2 were waited for; matrix products, arithmetic and copies ran while one was open for 3% of the time, Pallas kernels for 91%

profile of v7, /device:TPU:0, one launch (start us, length us, event | category | flops | bytes accessed | tf_op | source)
XLA Modules:
  0.0 735.2 jit_solution(8156002565405766419)
XLA Ops:
  7.2 0.7 all-gather.9.cloned.1.call-update
  8.0 0.7 convert_bitcast_fusion
  8.7 0.7 convert_bitcast_fusion.1
  9.4 0.1 reshape.232
  9.5 0.7 pad_maximum_fusion.1
  10.2 6.3 all-gather.3
  16.6 0.1 copy.38
  16.6 0.1 reshape.250
  16.8 0.1 reshape.237
  16.9 0.1 reshape.235
  17.0 0.1 dynamic-slice_reduce_fusion
  17.0 0.1 reshape.233
  17.1 0.2 subtract_reduce_fusion.order
  17.3 0.7 select_reduce_fusion.inv
  18.0 0.6 fusion.8
  18.6 0.9 bitcast_convert_fusion.x
  19.6 68.0 %attn_fwd.2 = (bf16[1024,768]{1,0:T(8,128)(2,1)}, bf16[1024,768]{1,0:T(8,128)(2,1)}, f32[1024,256]{1,0:T(8,128)}, f32[1024,128]{1,0:T(8,128)}, bf16[8,128,256]{2...) custom-call(s32[8]{0:T(128)} %copy-done.8, ...), custom_call_target="tpu_custom_call" | custom-call | flops 1 | bytes 1 | tf_op jit(solution)/shard_map/attn_fwd/pallas_call | solution.py:821
  87.6 0.1 fusion.7
  87.7 0.6 gather_fusion
  88.3 0.6 slice_bitcast_fusion
  88.9 0.6 broadcast_in_dim.30.before
  89.5 49.5 %ffn_fwd.2 = (bf16[4,256,768]{2,1,0:T(8,128)(2,1)}, f32[4,56,256]{2,1,0:T(8,128)}, bf16[272,768]{1,0:T(8,128)(2,1)}, f32[256,768]{1,0:T(8,128)}) custom-call(bf16[256,768]{1,0:T(8,128)(2,1)} %get-tuple-element.85.ub, f32[256,768]{1,0:T(8,128)} %get-tuple-element.86.hst, bf16[20,768]{1,0:T(8,128)(2,1)} %get-tuple-element.198.small, ...), custom_call_target="tpu_custom_call" | custom-call | flops 1 | bytes 1 | tf_op jit(solution)/shard_map/ffn_fwd/pallas_call | solution.py:1271
  139.0 47.8 %attn_fwd.3 = (bf16[1024,768]{1,0:T(8,128)(2,1)}, bf16[1024,768]{1,0:T(8,128)(2,1)}, f32[1024,256]{1,0:T(8,128)}, f32[1024,128]{1,0:T(8,128)}, bf16[8,128,256]{2...) custom-call(s32[8]{0:T(128)} %copy-done.8, ...), custom_call_target="tpu_custom_call" | custom-call | flops 1 | bytes 1 | tf_op jit(solution)/shard_map/attn_fwd/pallas_call | solution.py:821
  186.8 0.0 all-gather.13.cloned.1.call-start
  186.9 1.5 slice.50.before
  188.4 46.6 %ffn_fwd.3 = (bf16[4,256,768]{2,1,0:T(8,128)(2,1)}, f32[4,56,256]{2,1,0:T(8,128)}, bf16[272,768]{1,0:T(8,128)(2,1)}, f32[256,768]{1,0:T(8,128)}) custom-call(bf16[256,768]{1,0:T(8,128)(2,1)} %get-tuple-element.89.ub, f32[256,768]{1,0:T(8,128)} %get-tuple-element.92.hst, bf16[20,768]{1,0:T(8,128)(2,1)} %get-tuple-element.197.small, ...), custom_call_target="tpu_custom_call" | custom-call | flops 1 | bytes 1 | tf_op jit(solution)/shard_map/ffn_fwd/pallas_call | solution.py:1271
  235.0 0.5 all-gather.15.cloned.1.call-start
  235.5 0.6 slice_bitcast_fusion.2
  236.1 0.9 bitcast_convert_fusion.1.gx
  237.1 0.6 broadcast_in_dim.32.gprev
  237.7 51.1 %ffn_bwd.2 = (f32[256,768]{1,0:T(8,128)}, bf16[8,128,256]{2,1,0:T(8,128)(2,1)}, bf16[4,192,768]{2,1,0:T(8,128)(2,1)}, f32[19,768]{1,0:T(8,128)}, f32[16,256]{1,0:T(8,128)}) custom-call(bf16[256,768]{1,0:T(8,128)(2,1)} %bitcast.61, f32[256,768]{1,0:T(8,128)} %bitcast_convert_fusion.1.gx, bf16[4,256,768]{2,1,0:T(8,128)(2,1)} %get-tuple-element.105.ubf, ...), custom_call_target="tpu_custom_call" | custom-call | flops 1 | bytes 1 | tf_op jit(solution)/shard_map/ffn_bwd/pallas_call | solution.py:1424
  288.8 8.1 %all-gather.11.cloned.1.call-done = bf16[8704,768]{1,0:T(8,128)(2,1)} async-done(((bf16[272,768]{1,0:T(8,128)(2,1)}), bf16[8704,768]{1,0:T(8,128)(2,1)}) %all-gather.11.cloned.1.call-update) | async-done | bytes 13369360 | tf_op jit(solution)/shard_map/all_gather | solution.py:1855
  296.9 55.3 %attn_bwd.2 = (f32[256,768]{1,0:T(8,128)}, bf16[256,768]{1,0:T(8,128)(2,1)}, bf16[192,2048]{1,0:T(8,128)(2,1)}) custom-call(s32[8]{0:T(128)} %copy-done.8, s32[8]{0:T(128)} %select_reduce_fusion.inv, bf16[1024,768]{1,0:T(8,128)(2,1)} %get-tuple-element.100.n1s, bf16[768,768]{1,0:T(8,128)(2,1)} %get-tuple-element.101.w, f32[1024,128]{1,0:T(8,128)} %constant.86.clone.cosine, ...), custom_call_target="tpu_custom_call" | custom-call | flops 1 | bytes 1 | tf_op jit(solution)/shard_map/attn_bwd/pallas_call | solution.py:1067
  352.2 55.4 %ffn_bwd.3 = (f32[256,768]{1,0:T(8,128)}, bf16[8,128,256]{2,1,0:T(8,128)(2,1)}, bf16[4,192,768]{2,1,0:T(8,128)(2,1)}, f32[19,768]{1,0:T(8,128)}, f32[16,256]{1,0:T(8,128)}) custom-call(bf16[256,768]{1,0:T(8,128)(2,1)} %get-tuple-element.137.gm, f32[256,768]{1,0:T(8,128)} %get-tuple-element.116.gx, bf16[4,256,768]{2,1,0:T(8,128)(2,1)} %get-tuple-element.117.ubf, ...), custom_call_target="tpu_custom_call" | custom-call | flops 1 | bytes 1 | tf_op jit(solution)/shard_map/ffn_bwd/pallas_call | solution.py:1424
  407.6 61.6 %attn_bwd.3 = (f32[256,768]{1,0:T(8,128)}, bf16[256,768]{1,0:T(8,128)(2,1)}, bf16[192,2048]{1,0:T(8,128)(2,1)}) custom-call(s32[8]{0:T(128)} %copy-done.8, s32[8]{0:T(128)} %select_reduce_fusion.inv, bf16[1024,768]{1,0:T(8,128)(2,1)} %get-tuple-element.95.n1s, bf16[768,768]{1,0:T(8,128)(2,1)} %get-tuple-element.96.w, f32[1024,128]{1,0:T(8,128)} %constant.86.clone.cosine, ...), custom_call_target="tpu_custom_call" | custom-call | flops 1 | bytes 1 | tf_op jit(solution)/shard_map/attn_bwd/pallas_call | solution.py:1067
  469.2 1.3 pad_maximum_fusion
  470.5 1.0 slice_reduce_fusion
  471.5 0.1 reduce_window_sum.21
  471.6 0.1 convert_element_type.67.counts
  471.7 0.1 reduce_window_sum.22
  471.8 0.6 sub.45.bases
  472.4 0.5 slice_bitcast_fusion.5.totals
  472.9 33.6 %pack_rows.2.packed = bf16[8,2320,1536]{2,1,0:T(8,128)(2,1)} custom-call(s32[256]{0:T(256)} %copy-done.9, s32[256]{0:T(256)} %sub.45.bases, s32[8]{0:T(128)} %slice_bitcast_fusion.5.totals, bf16[32,272,768]{2,1,0:T(8,128)(2,1)} %bitcast.58, bf16[32,272,768]{2,1,0:T(8,128)(2,1)} %bitcast.59, bf16[32,256,768]{2,1,0:T(8,128)(2,1)} %all-gather.9.cloned.1.call-done.gm), custom_call_target="tpu_custom_call" | custom-call | flops 1 | bytes 1 | tf_op jit(solution)/shard_map/pack_rows/pallas_call | solution.py:1544
  506.5 0.7 collective-permute-start
  507.2 78.2 %weight_grads.3 = (f32[2,8,2,768,512]{4,3,2,1,0:T(8,128)}, f32[2,8,512,768]{3,2,1,0:T(8,128)}) custom-call(s32[8]{0:T(128)} %slice_bitcast_fusion.5.totals, bf16[8,2320,1536]{2,1,0:T(8,128)(2,1)} %pack_rows.2.packed, bf16[2,8,2,768,512]{4,3,2,1,0:T(8,128)(2,1)} %wgu.13, bf16[2,8,512,768]{3,2,1,0:T(8,128)(2,1)} %wd.13), custom_call_target="tpu_custom_call" | custom-call | flops 1 | bytes 1 | tf_op jit(solution)/shard_map/weight_grads/pallas_call | solution.py:1628
  585.4 2.0 add_convert_fusion.1
  587.4 1.9 all-gather.15.cloned.1.call-done
  589.3 1.5 collective-permute-start.1
  590.8 1.0 slice_reduce_fusion.1
  591.8 0.1 reduce_window_sum.23
  591.9 0.1 convert_element_type.73.counts
  592.0 0.1 reduce_window_sum.24
  592.0 0.6 sub.46.bases
  592.6 0.5 slice_bitcast_fusion.4.totals
  593.1 33.7 %pack_rows.3.packed = bf16[8,2320,1536]{2,1,0:T(8,128)(2,1)} custom-call(s32[256]{0:T(256)} %copy-done.10, s32[256]{0:T(256)} %sub.46.bases, s32[8]{0:T(128)} %slice_bitcast_fusion.4.totals, bf16[32,272,768]{2,1,0:T(8,128)(2,1)} %bitcast.55, bf16[32,272,768]{2,1,0:T(8,128)(2,1)} %bitcast.56, bf16[32,256,768]{2,1,0:T(8,128)(2,1)} %bitcast.60), custom_call_target="tpu_custom_call" | custom-call | flops 1 | bytes 1 | tf_op jit(solution)/shard_map/pack_rows/pallas_call | solution.py:1544
  626.9 37.0 %weight_grads.4 = (f32[2,8,2,768,512]{4,3,2,1,0:T(8,128)}, f32[2,8,512,768]{3,2,1,0:T(8,128)}) custom-call(s32[8]{0:T(128)} %slice_bitcast_fusion.4.totals, bf16[8,2320,1536]{2,1,0:T(8,128)(2,1)} %pack_rows.3.packed, bf16[2,8,2,768,512]{4,3,2,1,0:T(8,128)(2,1)} %wgu.13, bf16[2,8,512,768]{3,2,1,0:T(8,128)(2,1)} %wd.13, ...), custom_call_target="tpu_custom_call", output_to_operand_aliasing={{0}: (4, {}), {1}: (5, {})} | custom-call | flops 1 | bytes 1 | tf_op jit(solution)/shard_map/weight_grads/pallas_call | solution.py:1628
  663.9 2.0 add_convert_fusion.ours
  665.9 4.9 collective-permute-start.2
  670.8 47.7 %weight_grads.5 = (f32[2,8,2,768,512]{4,3,2,1,0:T(8,128)}, f32[2,8,512,768]{3,2,1,0:T(8,128)}) custom-call(s32[8]{0:T(128)} %slice_bitcast_fusion.4.totals, bf16[8,2320,1536]{2,1,0:T(8,128)(2,1)} %pack_rows.3.packed, bf16[2,8,2,768,512]{4,3,2,1,0:T(8,128)(2,1)} %wgu.13, bf16[2,8,512,768]{3,2,1,0:T(8,128)(2,1)} %wd.13, ...), custom_call_target="tpu_custom_call", output_to_operand_aliasing={{0}: (4, {}), {1}: (5, {})} | custom-call | flops 1 | bytes 1 | tf_op jit(solution)/shard_map/weight_grads/pallas_call | solution.py:1628
  718.5 1.2 copy-done.2
  719.6 5.4 assemble.1
  725.0 1.7 copy.42
  726.7 0.9 copy.54
  727.6 0.9 copy.55
  (42 shorter events, 0.3 us)
Async XLA Ops:
  7.2 11.4 %copy-start.6 = (bf16[1,256,768]{2,1,0:T(8,128)(2,1)S(1)}, bf16[1,256,768]{2,1,0:T(8,128)(2,1)}, u32[]{:S(2)}) copy-start(bf16[1,256,768]{2,1,0:T(8,128)(2,1)} %param.14) | copy-start | bytes 1179652
  7.2 181.2 %all-gather.9.cloned.1.call-start = ((), (), s32[]{:S(2)}) async-start(), calls=%async_computation | async-start | bytes 12976128 | tf_op jit(solution)/shard_map/all_gather | solution.py:1844
  7.9 289.0 %all-gather.11.cloned.1.call-start = ((), (), s32[]{:S(2)}) async-start(), calls=%async_computation.1 | async-start | bytes 13787136 | tf_op jit(solution)/shard_map/all_gather | solution.py:1855
  17.3 2.2 copy-start.8
  186.8 283.6 %all-gather.13.cloned.1.call-start = ((), (), s32[]{:S(2)}) async-start(), calls=%async_computation.2 | async-start | bytes 13787136 | tf_op jit(solution)/shard_map/all_gather | solution.py:1860
  188.4 47.2 %copy-start.7 = (s32[2,1,256,2]{2,3,1,0:T(2,128)S(1)}, s32[2,1,256,2]{2,3,1,0:T(2,128)}, u32[]{:S(2)}) copy-start(s32[2,1,256,2]{2,3,1,0:T(2,128)} %param.17) | copy-start | bytes 12292
  188.4 47.8 %copy-start.1 = (bf16[1,256,768]{2,1,0:T(8,128)(2,1)S(1)}, bf16[1,256,768]{2,1,0:T(8,128)(2,1)}, u32[]{:S(2)}) copy-start(bf16[1,256,768]{2,1,0:T(8,128)(2,1)} %param.15) | copy-start | bytes 1179652
  235.0 354.3 %all-gather.15.cloned.1.call-start = ((), (), s32[]{:S(2)}) async-start(), calls=%async_computation.3 | async-start | bytes 12976128 | tf_op jit(solution)/shard_map/all_gather | solution.py:1884
  407.6 61.6 %copy-start.5 = (bf16[192,2048]{1,0:T(8,128)(2,1)S(1)}, bf16[192,2048]{1,0:T(8,128)(2,1)}, u32[]{:S(2)}) copy-start(bf16[192,2048]{1,0:T(8,128)(2,1)} %get-tuple-element.127) | copy-start | bytes 2359300
  471.7 1.2 copy-start.9
  506.5 78.9 %collective-permute-start = (bf16[2,192,2048]{2,1,0:T(8,128)(2,1)S(1)}, bf16[2,192,2048]{2,1,0:T(8,128)(2,1)}, u32[]{:S(2)}, u32[]{:S(2)}) collective-permute-start(bf16[2,192,2048]{2,1,0:T(8,128)(2,1)S(1)} %pad_maximum_fusion), channel_id=1, source_target_pairs={{0,4},{4,0},{8,12},{12,8},{16,20},{20,16},{24,28},{28,24},{1,5},{5... | collective-permute-start | bytes 4718600 | tf_op jit(solution)/shard_map/ppermute | solution.py:1887
  589.3 74.6 %collective-permute-start.1 = (bf16[2,192,2048]{2,1,0:T(8,128)(2,1)S(1)}, bf16[2,192,2048]{2,1,0:T(8,128)(2,1)}, u32[]{:S(2)}, u32[]{:S(2)}) collective-permute-start(bf16[2,192,2048]{2,1,0:T(8,128)(2,1)S(1)} %add_convert_fusion.1), channel_id=1, source_target_pairs={{0,16},{4,20},{8,24},{12,28},{16,0},{20,4},{24,8},{28,12},{1,17},{... | collective-permute-start | bytes 4718600 | tf_op jit(solution)/shard_map/ppermute | solution.py:1887
  591.9 1.2 copy-start.10
  665.9 52.6 %copy-start = (bf16[2,192,2048]{2,1,0:T(8,128)(2,1)}, bf16[2,192,2048]{2,1,0:T(8,128)(2,1)S(1)}, u32[]{:S(2)}) copy-start(bf16[2,192,2048]{2,1,0:T(8,128)(2,1)S(1)} %add_convert_fusion.ours) | copy-start | bytes 4718596
  665.9 52.6 %collective-permute-start.2 = (bf16[2,192,2048]{2,1,0:T(8,128)(2,1)S(1)}, bf16[2,192,2048]{2,1,0:T(8,128)(2,1)S(1)}, u32[]{:S(2)}, u32[]{:S(2)}) collective-permute-start(bf16[2,192,2048]{2,1,0:T(8,128)(2,1)S(1)} %add_convert_fusion.ours), channel_id=1, source_target_pairs={{0,8},{4,12},{8,0},{12,4},{16,24},{20,28},{24,16},{28,20},{1,9},{5... | collective-permute-start | bytes 4718600 | tf_op jit(solution)/shard_map/ppermute | solution.py:1887
  718.5 1.2 copy-start.2
  719.6 7.1 copy-start.3
  725.0 2.6 copy-start.4
Sparse Core Ops, SparseCore 0:
  10.9 122.9 all-gather.8
  187.0 109.8 all-gather.10
  299.8 121.6 all-gather.12
  470.6 118.6 all-gather.14

commit v8 on v7

--- a/solution.py
+++ b/solution.py
@@ -615,7 +615,7 @@
     order, inv, x, small, wq, cosine, sine, wo_own,
     n1s, qkv, o, lse, ob, hst, ub, w, wo,
     n1own, n1r, osort, osend, orecv, cols, w_s, wo_s,
-    n_send, n_recv, f_send, f_recv, p_send, o_send, o_recv, w_send, w_recv, v_send, v_recv,
+    n_send, n_recv, f_send, f_recv, o_send, o_recv, w_send, w_recv, v_send, v_recv,
 ):
     blocks, blk, _ = n1r.shape
     lanes = o.shape[1]
@@ -638,25 +638,14 @@
     def n1_copy(zz):
         return remote(n1own.at[zz // 2], n1r.at[own], n_send.at[zz], n_recv.at[z], 2 * zz + k, 2 * y + xx)
 
-    def sent(zz):
-        there = jnp.logical_not(jnp.logical_and(same, zz == z))
-        return there if zz in (1, 2) else jnp.logical_and(there, z // 2 == zz // 2)
-
-    def passed(zz):
-        return jnp.logical_and(z // 2 != zz // 2, jnp.logical_or(z == 1, z == 2))
-
-    def pass_copy(zz):
-        slot = n1r.at[2 * zz + k]
-        other = z // 2 * 2 + 1 - z % 2
-        return remote(slot, slot, p_send.at[zz], n_recv.at[zz], 2 * other + xx, 2 * y + k)
-
     for zz in range(depth):
-
-        @pl.when(sent(zz))
+        alone = jnp.logical_and(same, zz == z)
+
+        @pl.when(jnp.logical_not(alone))
         def _():
             n1_copy(zz).start()
 
-        @pl.when(jnp.logical_and(same, zz == z))
+        @pl.when(alone)
         def _():
             n1r[own] = n1own[zz // 2]
 
@@ -700,10 +689,6 @@
         @pl.when(jnp.logical_not(jnp.logical_and(same, zz == z)))
         def _():
             remote(n1own.at[0], n1r.at[2 * zz + k], n_send.at[zz], n_recv.at[zz], 2 * zz + k, 2 * y + xx).wait_recv()
-
-        @pl.when(passed(zz))
-        def _():
-            pass_copy(zz).start()
 
         forward_copy(zz).start()
     for zz in range(depth):
@@ -787,13 +772,9 @@
     ub[...] = low
     for zz in range(depth):
 
-        @pl.when(sent(zz))
+        @pl.when(jnp.logical_not(jnp.logical_and(same, zz == z)))
         def _():
             n1_copy(zz).wait_send()
-
-        @pl.when(passed(zz))
-        def _():
-            pass_copy(zz).wait_send()
 
         forward_copy(zz).wait_send()
     for index in range(3):
@@ -846,7 +827,7 @@
             pltpu.VMEM((width, 3 * lanes), bf),
             pltpu.VMEM((packs, inner, width), bf),
         ]
-        + [dma((blocks // 2,))] * 5
+        + [dma((blocks // 2,))] * 4
         + [dma((blocks,))] * 2
         + [dma((3,))] * 4,
         compiler_params=params_of(collective_id=number, has_side_effects=True),
@@ -1010,6 +991,9 @@
 
     over = remote(both.at[1 - y], both_in, r_send.at[2], r_recv.at[2], own, 2 * (1 - y) + k)
     over.start()
+    values = x[...]
+    factor = rms_factor(values)
+    base = values * factor
     for zz in range(depth):
 
         @pl.when(jnp.logical_not(jnp.logical_and(same, zz == z)))
@@ -1023,9 +1007,6 @@
             total = total + gnr[h * (depth // 2) + zz].astype(jnp.float32)
         halves.append(total)
     gn = jnp.concatenate(halves, axis=0)
-    values = x[...]
-    factor = rms_factor(values)
-    base = values * factor
     gb = gn * gain
     grad = ghst[...] + factor * (gb - base * jnp.mean(gb * base, axis=-1, keepdims=True))
     gx[...] = grad
@@ -1177,7 +1158,7 @@
         rows_s[0] = ub[...]
 
         def prepare(d):
-            rows = routing(nt(router, rows_s[d]), before[d], routes[d])
+            rows = routing(nt(router, rows_s[d]), before[d, LOGI : LOGI + 16, :], routes[d])
             table[d] = rows
             hot = one_hot(rows[SLOT : SLOT + NF])
             coef_s[d] = slot_values(hot, rows[COEF : COEF + NF])
@@ -1387,6 +1368,7 @@
         mid[...] = (away + beside_in[1].astype(jnp.float32)).astype(jnp.bfloat16)
         third.start()
         home = tn(hot_s[0], y_s[0])
+        ready = middle_ready(gx[...], table[0], hst[...], small[...])
         second.wait_recv()
         home = home + beside_in[0].astype(jnp.float32)
         total = gcoef[0]
@@ -1396,8 +1378,7 @@
         third.wait_recv()
         home = home + across_in[...].astype(jnp.float32)
         results = middle(
-            gx[...], home, total, table[0], routes[...], gprev[...], hst[...], ubf[0],
-            small[...], wo[...], ob[...],
+            ready, gx[...], home, total, table[0], routes[...], gprev[...], ubf[0], small[...], wo[...], ob[...]
         )
         for ref, value in zip((ghst, go, gwo, gsmall, glog), results):
             ref[...] = value
@@ -1678,13 +1659,9 @@
     return pairs, shares, scale_u, [shares[c] * pairs[c][1] for c in range(NC)]
 
 
-def middle(gx, parts, gcoef, table, routes, gprev, hst, ub, small, wo, ob):
-    groups = wo.shape[0]
-    inner = wo.shape[1]
-    blk = ob.shape[1]
+def middle_ready(gx, table, hst, small):
     gain = small[1:2].astype(jnp.float32)
     consts = small[2 : 2 + NC].astype(jnp.float32)
-    router = small[2 + NC :]
     pairs, shares, scale_u, scale_c = mixing_rows(table)
     columns = to_columns([scale_u] + scale_c)
     factor = rms_factor(hst)
@@ -1693,6 +1670,16 @@
     dots = [jnp.sum(gx * u, axis=1, keepdims=True)]
     dots += [jnp.sum(gx * consts[c : c + 1], axis=1, keepdims=True) for c in range(NC)]
     dots = to_rows(dots, 8)
+    const_sums = [jnp.sum(gx * columns[1 + c], axis=0, keepdims=True) for c in range(NC)]
+    return pairs, shares, gain, factor, base, dots, const_sums, gx * columns[0]
+
+
+def middle(ready, gx, parts, gcoef, table, routes, gprev, ub, small, wo, ob):
+    pairs, shares, gain, factor, base, dots, const_sums, grad_in = ready
+    groups = wo.shape[0]
+    inner = wo.shape[1]
+    blk = ob.shape[1]
+    router = small[2 + NC :]
     dot_u = dots[0:1]
     dot_c = [dots[1 + c : 2 + c] for c in range(NC)]
     ids = lax.broadcasted_iota(jnp.int32, (16, gx.shape[0]), 0)
@@ -1723,9 +1710,9 @@
         graw = jnp.where(ids == NE + index, row, graw)
     graw = graw.astype(jnp.bfloat16)
     grad_router = nn(graw, ub)
-    gu = gx * columns[0] + tn(graw, router) + parts
+    gu = grad_in + tn(graw, router) + parts
     sums = [jnp.sum(gu * base, axis=0, keepdims=True)]
-    sums += [jnp.sum(gx * columns[1 + c], axis=0, keepdims=True) for c in range(NC)]
+    sums += const_sums
     gb = gu * gain
     ghst = gx + factor * (gb - base * jnp.mean(gb * base, axis=-1, keepdims=True))
     gy = ghst.astype(jnp.bfloat16)
@@ -1843,7 +1830,7 @@
 
     gm_all = [None, lax.all_gather(cotangent[0], everyone, axis=0, tiled=False)]
     x = tokens[0].astype(f32)
-    before = jnp.zeros((packs, 16, count), f32)
+    before = jnp.zeros((packs, ROUT, count), f32)
     kept, ext_all = [], [None] * LAYERS
     for l in range(LAYERS):
         n1s, qkv, o, lse, ob, hst, ub, w, wo = attn_forward(
@@ -1856,7 +1843,7 @@
         ubf, table, ext, x_next = ffn_forward(
             l, ub, hst, smalls[l], routes_f[:, l], before, w_gate_up, w_down, 2 * l + 1
         )
-        before = table[:, LOGI : LOGI + 16]
+        before = table
         ext_all[l] = ext if l == 0 else lax.all_gather(ext, everyone, axis=0, tiled=False)
         kept.append((x, n1s, qkv, o, lse, ob, hst, w, wo, ubf, table))
         x = x_next
@@ -1871,7 +1858,7 @@
         ghst, go, gwo, small, gprev = ffn_backward(
             l, gm, gx, ubf, table, hst, smalls[l], routes_t[l], gprev, wo, ob, w_gate_up, w_down, number
         )
-        if l == 1:
+        if l == 0:
             go, ext_all[0] = lax.optimization_barrier((go, ext_all[0]))
         gx, gm, grads[l] = attn_backward(
             order, inv, n1s, w, cosine, sine, qkv, o, lse, go, ghst, x, smalls[l], small, gwo, number + 1

time: 748 us -> 722 us (0.965); the launches traced: 735 us -> 719 us
  waiting for transfers between devices: 10.7 us -> 2.49 us
    pallas_call x2, Pallas kernels: 96.1 us -> 87.3 us  [ffn_forward(): pl.pallas_call(ffn_fwd_kernel, grid=(NF,), out_shape=outs, in_specs=[whol...]
    all_gather x1, waiting for transfers between devices: 8.08 us -> 0.02 us  [by_heads(): ext_all[0] = lax.all_gather(first_ext, everyone, axis=0, tiled=False)]
  transfers between devices with their start and end apart: 7 -> 7, of which waited for: 2 -> 1; matrix products, arithmetic and copies ran while one was open for 3% -> 2% of each run, Pallas kernels for 91% -> 92%
where the time goes in v8:
time: 722 us; the launch traced here: 719 us
  Pallas kernels  664 us (92%)
  between operations  14.3 us (2%)
  other arithmetic  13.5 us (2%)
  local copies, waits for them, and re-layouts  10.4 us (1%)
  starting transfers between devices  7.74 us (1%)
    pallas_call x3, Pallas kernels, weight_grads(): pl.pallas_call(functools.partial(dw_kernel, first), grid_spec=pltpu.Prefe...  163 us
    pallas_call x2, Pallas kernels, attn_backward(): pl.pallas_call(attn_bwd_kernel, out_shape=[shape_of((count, width), jnp.f...  115 us
    pallas_call x2, Pallas kernels, attn_forward(): pl.pallas_call(attn_fwd_kernel, grid=(1,), out_shape=[shape_of((seq, widt...  114 us
    pallas_call x2, Pallas kernels, ffn_backward(): pl.pallas_call(ffn_bwd_kernel, grid=(NF,), out_shape=outs, in_specs=[whol...  111 us
    pallas_call x2, Pallas kernels, ffn_forward(): pl.pallas_call(ffn_fwd_kernel, grid=(NF,), out_shape=outs, in_specs=[whol...  87.3 us
    pallas_call x2, Pallas kernels, pack_rows(): pl.pallas_call(pack_kernel, grid_spec=pltpu.PrefetchScalarGridSpec(num_sc...  67.5 us
  transfers between devices with their start and end apart: 7, of which 1 were waited for; matrix products, arithmetic and copies ran while one was open for 2% of the time, Pallas kernels for 92%

profile of v8, /device:TPU:0, one launch (start us, length us, event | category | flops | bytes accessed | tf_op | source)
XLA Modules:
  0.0 718.6 jit_solution(18211386202657759319)
XLA Ops:
  7.2 0.0 all-gather.9.cloned.1.call-start
  7.2 0.7 all-gather.9.cloned.1.call-update
  7.9 0.0 all-gather.11.cloned.1.call-start
  8.0 0.7 convert_bitcast_fusion
  8.7 0.7 convert_bitcast_fusion.1
  9.4 0.1 reshape.232
  9.5 0.7 pad_maximum_fusion.1
  10.2 6.3 all-gather.3
  16.6 0.1 copy.38
  16.6 0.1 reshape.250
  16.8 0.1 reshape.237
  16.9 0.1 reshape.235
  17.0 0.1 dynamic-slice_reduce_fusion
  17.0 0.1 reshape.233
  17.1 0.2 subtract_reduce_fusion.order
  17.3 0.7 select_reduce_fusion.inv
  18.0 0.6 fusion.8
  18.6 0.9 bitcast_convert_fusion.x
  19.6 57.0 %attn_fwd.2 = (bf16[1024,768]{1,0:T(8,128)(2,1)}, bf16[1024,768]{1,0:T(8,128)(2,1)}, f32[1024,256]{1,0:T(8,128)}, f32[1024,128]{1,0:T(8,128)}, bf16[8,128,256]{2...) custom-call(s32[8]{0:T(128)} %copy-done.8, ...), custom_call_target="tpu_custom_call" | custom-call | flops 1 | bytes 1 | tf_op jit(solution)/shard_map/attn_fwd/pallas_call | solution.py:802
  76.6 0.1 fusion.7
  76.7 0.6 gather_fusion
  77.3 0.6 slice_bitcast_fusion
  77.9 0.7 broadcast_in_dim.30.before
  78.6 46.2 %ffn_fwd.2 = (bf16[4,256,768]{2,1,0:T(8,128)(2,1)}, f32[4,56,256]{2,1,0:T(8,128)}, bf16[272,768]{1,0:T(8,128)(2,1)}, f32[256,768]{1,0:T(8,128)}) custom-call(bf16[256,768]{1,0:T(8,128)(2,1)} %get-tuple-element.85.ub, f32[256,768]{1,0:T(8,128)} %get-tuple-element.86.hst, bf16[20,768]{1,0:T(8,128)(2,1)} %get-tuple-element.198.small, ...), custom_call_target="tpu_custom_call" | custom-call | flops 1 | bytes 1 | tf_op jit(solution)/shard_map/ffn_fwd/pallas_call | solution.py:1252
  124.8 57.4 %attn_fwd.3 = (bf16[1024,768]{1,0:T(8,128)(2,1)}, bf16[1024,768]{1,0:T(8,128)(2,1)}, f32[1024,256]{1,0:T(8,128)}, f32[1024,128]{1,0:T(8,128)}, bf16[8,128,256]{2...) custom-call(s32[8]{0:T(128)} %copy-done.8, ...), custom_call_target="tpu_custom_call" | custom-call | flops 1 | bytes 1 | tf_op jit(solution)/shard_map/attn_fwd/pallas_call | solution.py:802
  182.2 0.0 all-gather.13.cloned.1.call-start
  182.3 41.1 %ffn_fwd.3 = (bf16[4,256,768]{2,1,0:T(8,128)(2,1)}, f32[4,56,256]{2,1,0:T(8,128)}, bf16[272,768]{1,0:T(8,128)(2,1)}, f32[256,768]{1,0:T(8,128)}) custom-call(bf16[256,768]{1,0:T(8,128)(2,1)} %get-tuple-element.89.ub, f32[256,768]{1,0:T(8,128)} %get-tuple-element.92.hst, bf16[20,768]{1,0:T(8,128)(2,1)} %get-tuple-element.197.small, ...), custom_call_target="tpu_custom_call" | custom-call | flops 1 | bytes 1 | tf_op jit(solution)/shard_map/ffn_fwd/pallas_call | solution.py:1252
  223.5 0.5 all-gather.15.cloned.1.call-start
  224.0 0.6 slice_bitcast_fusion.2
  224.6 0.9 bitcast_convert_fusion.1.gx
  225.5 0.6 broadcast_in_dim.32.gprev
  226.1 56.2 %ffn_bwd.2 = (f32[256,768]{1,0:T(8,128)}, bf16[8,128,256]{2,1,0:T(8,128)(2,1)}, bf16[4,192,768]{2,1,0:T(8,128)(2,1)}, f32[19,768]{1,0:T(8,128)}, f32[16,256]{1,0:T(8,128)}) custom-call(bf16[256,768]{1,0:T(8,128)(2,1)} %bitcast.61, f32[256,768]{1,0:T(8,128)} %bitcast_convert_fusion.1.gx, bf16[4,256,768]{2,1,0:T(8,128)(2,1)} %get-tuple-element.105.ubf, ...), custom_call_target="tpu_custom_call" | custom-call | flops 1 | bytes 1 | tf_op jit(solution)/shard_map/ffn_bwd/pallas_call | solution.py:1405
  282.3 56.4 %attn_bwd.2 = (f32[256,768]{1,0:T(8,128)}, bf16[256,768]{1,0:T(8,128)(2,1)}, bf16[192,2048]{1,0:T(8,128)(2,1)}) custom-call(s32[8]{0:T(128)} %copy-done.8, s32[8]{0:T(128)} %select_reduce_fusion.inv, bf16[1024,768]{1,0:T(8,128)(2,1)} %get-tuple-element.100.n1s, bf16[768,768]{1,0:T(8,128)(2,1)} %get-tuple-element.101.w, f32[1024,128]{1,0:T(8,128)} %constant.86.clone.cosine, ...), custom_call_target="tpu_custom_call" | custom-call | flops 1 | bytes 1 | tf_op jit(solution)/shard_map/attn_bwd/pallas_call | solution.py:1048
  338.7 55.2 %ffn_bwd.3 = (f32[256,768]{1,0:T(8,128)}, bf16[8,128,256]{2,1,0:T(8,128)(2,1)}, bf16[4,192,768]{2,1,0:T(8,128)(2,1)}, f32[19,768]{1,0:T(8,128)}, f32[16,256]{1,0:T(8,128)}) custom-call(bf16[256,768]{1,0:T(8,128)(2,1)} %get-tuple-element.137.gm, f32[256,768]{1,0:T(8,128)} %get-tuple-element.114.gx, bf16[4,256,768]{2,1,0:T(8,128)(2,1)} %get-tuple-element.115.ubf, ...), custom_call_target="tpu_custom_call" | custom-call | flops 1 | bytes 1 | tf_op jit(solution)/shard_map/ffn_bwd/pallas_call | solution.py:1405
  394.0 58.5 %attn_bwd.3 = (f32[256,768]{1,0:T(8,128)}, bf16[256,768]{1,0:T(8,128)(2,1)}, bf16[192,2048]{1,0:T(8,128)(2,1)}) custom-call(s32[8]{0:T(128)} %copy-done.8, s32[8]{0:T(128)} %select_reduce_fusion.inv, bf16[1024,768]{1,0:T(8,128)(2,1)} %get-tuple-element.95.n1s, bf16[768,768]{1,0:T(8,128)(2,1)} %get-tuple-element.96.w, f32[1024,128]{1,0:T(8,128)} %constant.86.clone.cosine, ...), custom_call_target="tpu_custom_call" | custom-call | flops 1 | bytes 1 | tf_op jit(solution)/shard_map/attn_bwd/pallas_call | solution.py:1048
  452.5 1.3 pad_maximum_fusion
  453.8 1.0 slice_reduce_fusion
  454.8 0.1 reduce_window_sum.21
  454.9 0.1 convert_element_type.67.counts
  455.0 0.1 reduce_window_sum.22
  455.1 0.6 sub.45.bases
  455.7 0.5 slice_bitcast_fusion.5.totals
  456.2 33.7 %pack_rows.2.packed = bf16[8,2320,1536]{2,1,0:T(8,128)(2,1)} custom-call(s32[256]{0:T(256)} %copy-done.9, s32[256]{0:T(256)} %sub.45.bases, s32[8]{0:T(128)} %slice_bitcast_fusion.5.totals, bf16[32,272,768]{2,1,0:T(8,128)(2,1)} %bitcast.58, bf16[32,272,768]{2,1,0:T(8,128)(2,1)} %bitcast.59, bf16[32,256,768]{2,1,0:T(8,128)(2,1)} %all-gather.9.cloned.1.call-done.gm), custom_call_target="tpu_custom_call" | custom-call | flops 1 | bytes 1 | tf_op jit(solution)/shard_map/pack_rows/pallas_call | solution.py:1525
  489.9 0.1 collective-permute-start
  490.0 78.3 %weight_grads.3 = (f32[2,8,2,768,512]{4,3,2,1,0:T(8,128)}, f32[2,8,512,768]{3,2,1,0:T(8,128)}) custom-call(s32[8]{0:T(128)} %slice_bitcast_fusion.5.totals, bf16[8,2320,1536]{2,1,0:T(8,128)(2,1)} %pack_rows.2.packed, bf16[2,8,2,768,512]{4,3,2,1,0:T(8,128)(2,1)} %wgu.13, bf16[2,8,512,768]{3,2,1,0:T(8,128)(2,1)} %wd.13), custom_call_target="tpu_custom_call" | custom-call | flops 1 | bytes 1 | tf_op jit(solution)/shard_map/weight_grads/pallas_call | solution.py:1609
  568.3 2.0 add_convert_fusion.1
  570.3 1.7 all-gather.15.cloned.1.call-done
  572.0 1.5 collective-permute-start.1
  573.5 1.0 slice_reduce_fusion.1
  574.6 0.1 reduce_window_sum.23
  574.6 0.1 convert_element_type.73.counts
  574.7 0.1 reduce_window_sum.24
  574.8 0.6 sub.46.bases
  575.4 0.5 slice_bitcast_fusion.4.totals
  575.9 33.8 %pack_rows.3.packed = bf16[8,2320,1536]{2,1,0:T(8,128)(2,1)} custom-call(s32[256]{0:T(256)} %copy-done.10, s32[256]{0:T(256)} %sub.46.bases, s32[8]{0:T(128)} %slice_bitcast_fusion.4.totals, bf16[32,272,768]{2,1,0:T(8,128)(2,1)} %bitcast.55, bf16[32,272,768]{2,1,0:T(8,128)(2,1)} %bitcast.56, bf16[32,256,768]{2,1,0:T(8,128)(2,1)} %bitcast.60), custom_call_target="tpu_custom_call" | custom-call | flops 1 | bytes 1 | tf_op jit(solution)/shard_map/pack_rows/pallas_call | solution.py:1525
  609.7 42.4 %weight_grads.4 = (f32[2,8,2,768,512]{4,3,2,1,0:T(8,128)}, f32[2,8,512,768]{3,2,1,0:T(8,128)}) custom-call(s32[8]{0:T(128)} %slice_bitcast_fusion.4.totals, bf16[8,2320,1536]{2,1,0:T(8,128)(2,1)} %pack_rows.3.packed, bf16[2,8,2,768,512]{4,3,2,1,0:T(8,128)(2,1)} %wgu.13, bf16[2,8,512,768]{3,2,1,0:T(8,128)(2,1)} %wd.13, ...), custom_call_target="tpu_custom_call", output_to_operand_aliasing={{0}: (4, {}), {1}: (5, {})} | custom-call | flops 1 | bytes 1 | tf_op jit(solution)/shard_map/weight_grads/pallas_call | solution.py:1609
  652.1 2.0 add_convert_fusion.ours
  654.1 5.5 collective-permute-start.2
  659.7 42.2 %weight_grads.5 = (f32[2,8,2,768,512]{4,3,2,1,0:T(8,128)}, f32[2,8,512,768]{3,2,1,0:T(8,128)}) custom-call(s32[8]{0:T(128)} %slice_bitcast_fusion.4.totals, bf16[8,2320,1536]{2,1,0:T(8,128)(2,1)} %pack_rows.3.packed, bf16[2,8,2,768,512]{4,3,2,1,0:T(8,128)(2,1)} %wgu.13, bf16[2,8,512,768]{3,2,1,0:T(8,128)(2,1)} %wd.13, ...), custom_call_target="tpu_custom_call", output_to_operand_aliasing={{0}: (4, {}), {1}: (5, {})} | custom-call | flops 1 | bytes 1 | tf_op jit(solution)/shard_map/weight_grads/pallas_call | solution.py:1609
  701.9 1.2 copy-done.2
  703.1 5.4 assemble.1
  708.4 1.7 copy.42
  710.2 0.9 copy.54
  711.0 0.9 copy.55
  (41 shorter events, 0.3 us)
Async XLA Ops:
  7.2 11.4 %copy-start.6 = (bf16[1,256,768]{2,1,0:T(8,128)(2,1)S(1)}, bf16[1,256,768]{2,1,0:T(8,128)(2,1)}, u32[]{:S(2)}) copy-start(bf16[1,256,768]{2,1,0:T(8,128)(2,1)} %param.14) | copy-start | bytes 1179652
  7.2 175.1 %all-gather.9.cloned.1.call-start = ((), (), s32[]{:S(2)}) async-start(), calls=%async_computation | async-start | bytes 12976128 | tf_op jit(solution)/shard_map/all_gather | solution.py:1831
  7.9 386.1 %all-gather.11.cloned.1.call-start = ((), (), s32[]{:S(2)}) async-start(), calls=%async_computation.1 | async-start | bytes 13787136 | tf_op jit(solution)/shard_map/all_gather | solution.py:1842
  17.3 2.2 copy-start.8
  182.2 271.6 %all-gather.13.cloned.1.call-start = ((), (), s32[]{:S(2)}) async-start(), calls=%async_computation.2 | async-start | bytes 13787136 | tf_op jit(solution)/shard_map/all_gather | solution.py:1847
  182.3 41.7 %copy-start.7 = (s32[2,1,256,2]{2,3,1,0:T(2,128)S(1)}, s32[2,1,256,2]{2,3,1,0:T(2,128)}, u32[]{:S(2)}) copy-start(s32[2,1,256,2]{2,3,1,0:T(2,128)} %param.17) | copy-start | bytes 12292
  182.3 42.3 %copy-start.1 = (bf16[1,256,768]{2,1,0:T(8,128)(2,1)S(1)}, bf16[1,256,768]{2,1,0:T(8,128)(2,1)}, u32[]{:S(2)}) copy-start(bf16[1,256,768]{2,1,0:T(8,128)(2,1)} %param.15) | copy-start | bytes 1179652
  223.5 348.6 %all-gather.15.cloned.1.call-start = ((), (), s32[]{:S(2)}) async-start(), calls=%async_computation.3 | async-start | bytes 12976128 | tf_op jit(solution)/shard_map/all_gather | solution.py:1871
  394.0 58.5 %copy-start.5 = (bf16[192,2048]{1,0:T(8,128)(2,1)S(1)}, bf16[192,2048]{1,0:T(8,128)(2,1)}, u32[]{:S(2)}) copy-start(bf16[192,2048]{1,0:T(8,128)(2,1)} %get-tuple-element.127) | copy-start | bytes 2359300
  455.0 1.2 copy-start.9
  489.9 78.4 %collective-permute-start = (bf16[2,192,2048]{2,1,0:T(8,128)(2,1)S(1)}, bf16[2,192,2048]{2,1,0:T(8,128)(2,1)}, u32[]{:S(2)}, u32[]{:S(2)}) collective-permute-start(bf16[2,192,2048]{2,1,0:T(8,128)(2,1)S(1)} %pad_maximum_fusion), channel_id=1, source_target_pairs={{0,4},{4,0},{8,12},{12,8},{16,20},{20,16},{24,28},{28,24},{1,5},{5... | collective-permute-start | bytes 4718600 | tf_op jit(solution)/shard_map/ppermute | solution.py:1874
  572.0 80.1 %collective-permute-start.1 = (bf16[2,192,2048]{2,1,0:T(8,128)(2,1)S(1)}, bf16[2,192,2048]{2,1,0:T(8,128)(2,1)}, u32[]{:S(2)}, u32[]{:S(2)}) collective-permute-start(bf16[2,192,2048]{2,1,0:T(8,128)(2,1)S(1)} %add_convert_fusion.1), channel_id=1, source_target_pairs={{0,16},{4,20},{8,24},{12,28},{16,0},{20,4},{24,8},{28,12},{1,17},{... | collective-permute-start | bytes 4718600 | tf_op jit(solution)/shard_map/ppermute | solution.py:1874
  574.7 1.2 copy-start.10
  654.1 47.8 %copy-start = (bf16[2,192,2048]{2,1,0:T(8,128)(2,1)}, bf16[2,192,2048]{2,1,0:T(8,128)(2,1)S(1)}, u32[]{:S(2)}) copy-start(bf16[2,192,2048]{2,1,0:T(8,128)(2,1)S(1)} %add_convert_fusion.ours) | copy-start | bytes 4718596
  654.1 47.8 %collective-permute-start.2 = (bf16[2,192,2048]{2,1,0:T(8,128)(2,1)S(1)}, bf16[2,192,2048]{2,1,0:T(8,128)(2,1)S(1)}, u32[]{:S(2)}, u32[]{:S(2)}) collective-permute-start(bf16[2,192,2048]{2,1,0:T(8,128)(2,1)S(1)} %add_convert_fusion.ours), channel_id=1, source_target_pairs={{0,8},{4,12},{8,0},{12,4},{16,24},{20,28},{24,16},{28,20},{1,9},{5... | collective-permute-start | bytes 4718600 | tf_op jit(solution)/shard_map/ppermute | solution.py:1874
  701.9 1.2 copy-start.2
  703.1 7.1 copy-start.3
  708.4 2.6 copy-start.4
Sparse Core Ops, SparseCore 0:
  10.9 126.8 all-gather.8
  182.3 113.5 all-gather.10
  298.9 129.1 all-gather.12
  453.9 118.0 all-gather.14

commit v9 on v8

--- a/solution.py
+++ b/solution.py
@@ -830,7 +830,7 @@
         + [dma((blocks // 2,))] * 4
         + [dma((blocks,))] * 2
         + [dma((3,))] * 4,
-        compiler_params=params_of(collective_id=number, has_side_effects=True),
+        compiler_params=params_of(44, collective_id=number, has_side_effects=True),
         cost_estimate=BRIEF,
         name="attn_fwd",
     )(order, inv, x, small, wq, cosine, sine, wo)
@@ -1076,7 +1076,7 @@
         + [dma((blocks,))] * 2
         + [dma((depth,))] * 4
         + [dma((3,))] * 4,
-        compiler_params=params_of(collective_id=number, has_side_effects=True),
+        compiler_params=params_of(54, collective_id=number, has_side_effects=True),
         cost_estimate=BRIEF,
         name="attn_bwd",
     )(order, inv, n1s, w, cosine, sine, qkv, o, lse, go, ghst, x, small, gsmall, gwo)
@@ -1268,7 +1268,7 @@
         ]
         + exchange_scratch(packs, count, width)
         + [pltpu.SemaphoreType.DMA((3,))] * 4,
-        compiler_params=params_of(collective_id=number, has_side_effects=True),
+        compiler_params=params_of(40, collective_id=number, has_side_effects=True),
         cost_estimate=BRIEF,
         name="ffn_fwd",
     )(ub, hst, small, routes, before, wgu, wd)
@@ -1425,7 +1425,7 @@
         ]
         + exchange_scratch(packs, count, width)
         + [dma((3,))] * 6,
-        compiler_params=params_of(collective_id=number, has_side_effects=True),
+        compiler_params=params_of(50, collective_id=number, has_side_effects=True),
         cost_estimate=BRIEF,
         name="ffn_bwd",
     )(*args, wgu, wd)

time: 722 us -> 737 us (1.021)
  local copies, waits for them, and re-layouts: 10.4 us -> 32.7 us
  Pallas kernels: 664 us -> 655 us
    unnamed x27 -> x103, local copies, waits for them, and re-layouts: 4.82 us -> 30.2 us
  transfers between devices with their start and end apart: 7 -> 7, of which waited for: 1 -> 0; matrix products, arithmetic and copies ran while one was open for 2% -> 2% of each run, Pallas kernels for 92% -> 89%
where the time goes in v9:
time: 737 us; the launch traced here: 732 us
  Pallas kernels  655 us (89%)
  local copies, waits for them, and re-layouts  32.7 us (4%)
  between operations  14.6 us (2%)
  other arithmetic  12.8 us (2%)
  starting transfers between devices  9.68 us (1%)
    pallas_call x3, Pallas kernels, weight_grads(): pl.pallas_call(functools.partial(dw_kernel, first), grid_spec=pltpu.Prefe...  167 us
    pallas_call x2, Pallas kernels, attn_backward(): pl.pallas_call(attn_bwd_kernel, out_shape=[shape_of((count, width), jnp.f...  114 us
    pallas_call x2, Pallas kernels, attn_forward(): pl.pallas_call(attn_fwd_kernel, grid=(1,), out_shape=[shape_of((seq, widt...  110 us
    pallas_call x2, Pallas kernels, ffn_backward(): pl.pallas_call(ffn_bwd_kernel, grid=(NF,), out_shape=outs, in_specs=[whol...  109 us
    pallas_call x2, Pallas kernels, ffn_forward(): pl.pallas_call(ffn_fwd_kernel, grid=(NF,), out_shape=outs, in_specs=[whol...  83.2 us
    pallas_call x2, Pallas kernels, pack_rows(): pl.pallas_call(pack_kernel, grid_spec=pltpu.PrefetchScalarGridSpec(num_sc...  67.6 us
    unnamed x103, local copies, waits for them, and re-layouts  30.2 us
  transfers between devices with their start and end apart: 7, of which 0 were waited for; matrix products, arithmetic and copies ran while one was open for 2% of the time, Pallas kernels for 89%

profile of v9, /device:TPU:0, one launch (start us, length us, event | category | flops | bytes accessed | tf_op | source)
XLA Modules:
  0.0 732.3 jit_solution(14771721679072325530)
XLA Ops:
  7.3 0.7 all-gather.9.cloned.1.call-update
  8.0 0.7 convert_bitcast_fusion
  8.7 0.7 convert_bitcast_fusion.1
  9.5 0.7 pad_maximum_fusion.1
  10.3 6.3 all-gather.3
  17.6 55.9 %attn_fwd.2 = (bf16[1024,768]{1,0:T(8,128)(2,1)S(1)}, bf16[1024,768]{1,0:T(8,128)(2,1)}, f32[1024,256]{1,0:T(8,128)S(1)}, f32[1024,128]{1,0:T(8,128)S(1)}, bf16[...) custom-call(s32[8]{0:T(128)S(1)} %subtract_reduce_fusion.order, ...), custom_call_target="tpu_custom_call" | custom-call | flops 1 | bytes 1 | tf_op jit(solution)/shard_map/attn_fwd/pallas_call | solution.py:802
  73.5 1.1 copy-done.9
  74.7 1.0 copy-done.13
  75.7 1.0 copy-done.15
  76.7 1.0 copy-done.17
  77.7 0.8 copy-done.24
  78.5 0.8 copy-done.28
  79.3 0.7 copy-done.33
  80.1 0.6 gather_fusion
  80.8 1.0 copy-done.34
  81.8 44.2 %ffn_fwd.2 = (bf16[4,256,768]{2,1,0:T(8,128)(2,1)S(1)}, f32[4,56,256]{2,1,0:T(8,128)S(1)}, bf16[272,768]{1,0:T(8,128)(2,1)S(1)}, f32[256,768]{1,0:T(8,128)S(1)}) custom-call(bf16[256,768]{1,0:T(8,128)(2,1)S(1)} %copy-done.34, f32[256,768]{1,0:T(8,128)S(1)} %get-tuple-element.86.hst, bf16[20,768]{1,0:T(8,128)(2,1)S(1)} %get-tuple-element.198.small, ...), custom_call_target="tpu_custom_call" | custom-call | flops 1 | bytes 1 | tf_op jit(solution)/shard_map/ffn_fwd/pallas_call | solution.py:1252
  126.0 1.1 copy-done.11
  127.1 0.8 copy-done.32
  127.9 53.7 %attn_fwd.3 = (bf16[1024,768]{1,0:T(8,128)(2,1)S(1)}, bf16[1024,768]{1,0:T(8,128)(2,1)}, f32[1024,256]{1,0:T(8,128)S(1)}, f32[1024,128]{1,0:T(8,128)S(1)}, bf16[...) custom-call(s32[8]{0:T(128)S(1)} %subtract_reduce_fusion.order, ...), custom_call_target="tpu_custom_call" | custom-call | flops 1 | bytes 1 | tf_op jit(solution)/shard_map/attn_fwd/pallas_call | solution.py:802
  181.6 1.1 copy-done.10
  182.8 1.0 copy-done.14
  183.8 1.0 copy-done.16
  184.8 1.0 copy-done.18
  185.8 0.8 copy-done.26
  186.6 0.8 copy-done.29
  187.3 0.7 copy-done.35
  188.2 1.2 copy-done.36
  189.4 39.0 %ffn_fwd.3 = (bf16[4,256,768]{2,1,0:T(8,128)(2,1)S(1)}, f32[4,56,256]{2,1,0:T(8,128)S(1)}, bf16[272,768]{1,0:T(8,128)(2,1)}, f32[256,768]{1,0:T(8,128)S(1)}) custom-call(bf16[256,768]{1,0:T(8,128)(2,1)S(1)} %copy-done.36, f32[256,768]{1,0:T(8,128)S(1)} %get-tuple-element.92.hst, bf16[20,768]{1,0:T(8,128)(2,1)S(1)} %get-tuple-element.197.small, ...), custom_call_target="tpu_custom_call" | custom-call | flops 1 | bytes 1 | tf_op jit(solution)/shard_map/ffn_fwd/pallas_call | solution.py:1252
  228.4 1.1 copy-done.12
  229.6 0.5 all-gather.15.cloned.1.call-start
  230.2 0.4 copy-done.27
  230.6 55.2 %ffn_bwd.2 = (f32[256,768]{1,0:T(8,128)S(1)}, bf16[8,128,256]{2,1,0:T(8,128)(2,1)S(1)}, bf16[4,192,768]{2,1,0:T(8,128)(2,1)}, f32[19,768]{1,0:T(8,128)S(1)}, f32[16,256]{1,0:T(8,128)S(1)}) custom-call(bf16[256,768]{1,0:T(8,128)(2,1)S(1)} %bitcast.54, f32[256,768]{1,0:T(8,128)S(1)} %bitcast_convert_fusion.1.gx, bf16[4,256,768]{2,1,0:T(8,128)(2,1)} %copy-done.12, ...), custom_call_target="tpu_custom_call" | custom-call | flops 1 | bytes 1 | tf_op jit(solution)/shard_map/ffn_bwd/pallas_call | solution.py:1405
  285.8 0.9 copy-done.22
  286.7 0.8 copy-done.31
  287.4 0.6 copy-done.38
  288.1 58.5 %attn_bwd.2 = (f32[256,768]{1,0:T(8,128)}, bf16[256,768]{1,0:T(8,128)(2,1)}, bf16[192,2048]{1,0:T(8,128)(2,1)}) custom-call(s32[8]{0:T(128)} %copy-done.39, s32[8]{0:T(128)} %copy-done.40, bf16[1024,768]{1,0:T(8,128)(2,1)} %copy-done.10, bf16[768,768]{1,0:T(8,128)(2,1)} %copy-done.16, f32[1024,128]{1,0:T(8,128)} %constant.86.clone.cosine, ...), custom_call_target="tpu_custom_call" | custom-call | flops 1 | bytes 1 | tf_op jit(solution)/shard_map/attn_bwd/pallas_call | solution.py:1048
  346.6 1.0 copy-done.8
  347.6 1.1 copy-done.23
  348.7 53.5 %ffn_bwd.3 = (f32[256,768]{1,0:T(8,128)S(1)}, bf16[8,128,256]{2,1,0:T(8,128)(2,1)S(1)}, bf16[4,192,768]{2,1,0:T(8,128)(2,1)}, f32[19,768]{1,0:T(8,128)S(1)}, f32[16,256]{1,0:T(8,128)}) custom-call(bf16[256,768]{1,0:T(8,128)(2,1)S(1)} %copy-done.8, f32[256,768]{1,0:T(8,128)S(1)} %copy-done.23, bf16[4,256,768]{2,1,0:T(8,128)(2,1)} %copy-done.11, ...), custom_call_target="tpu_custom_call" | custom-call | flops 1 | bytes 1 | tf_op jit(solution)/shard_map/ffn_bwd/pallas_call | solution.py:1405
  402.2 0.9 copy-done.21
  403.1 0.8 copy-done.30
  403.8 0.6 copy-done.37
  404.5 55.9 %attn_bwd.3 = (f32[256,768]{1,0:T(8,128)}, bf16[256,768]{1,0:T(8,128)(2,1)}, bf16[192,2048]{1,0:T(8,128)(2,1)}) custom-call(s32[8]{0:T(128)} %copy-done.39, s32[8]{0:T(128)} %copy-done.40, bf16[1024,768]{1,0:T(8,128)(2,1)} %copy-done.9, bf16[768,768]{1,0:T(8,128)(2,1)} %copy-done.15, f32[1024,128]{1,0:T(8,128)} %constant.86.clone.cosine, ...), custom_call_target="tpu_custom_call" | custom-call | flops 1 | bytes 1 | tf_op jit(solution)/shard_map/attn_bwd/pallas_call | solution.py:1048
  460.4 1.3 pad_maximum_fusion
  461.7 1.0 slice_reduce_fusion
  463.0 0.6 sub.45.bases
  463.6 0.5 slice_bitcast_fusion.5.totals
  464.1 33.8 %pack_rows.2.packed = bf16[8,2320,1536]{2,1,0:T(8,128)(2,1)} custom-call(s32[256]{0:T(256)} %copy-done.47, s32[256]{0:T(256)} %sub.45.bases, s32[8]{0:T(128)} %slice_bitcast_fusion.5.totals, bf16[32,272,768]{2,1,0:T(8,128)(2,1)} %bitcast.60, bf16[32,272,768]{2,1,0:T(8,128)(2,1)} %bitcast.61, bf16[32,256,768]{2,1,0:T(8,128)(2,1)} %all-gather.9.cloned.1.call-done.gm), custom_call_target="tpu_custom_call" | custom-call | flops 1 | bytes 1 | tf_op jit(solution)/shard_map/pack_rows/pallas_call | solution.py:1525
  497.9 79.5 %weight_grads.3 = (f32[2,8,2,768,512]{4,3,2,1,0:T(8,128)}, f32[2,8,512,768]{3,2,1,0:T(8,128)}) custom-call(s32[8]{0:T(128)} %slice_bitcast_fusion.5.totals, bf16[8,2320,1536]{2,1,0:T(8,128)(2,1)} %pack_rows.2.packed, bf16[2,8,2,768,512]{4,3,2,1,0:T(8,128)(2,1)} %wgu.13, bf16[2,8,512,768]{3,2,1,0:T(8,128)(2,1)} %wd.13), custom_call_target="tpu_custom_call" | custom-call | flops 1 | bytes 1 | tf_op jit(solution)/shard_map/weight_grads/pallas_call | solution.py:1609
  577.4 3.2 add_convert_fusion.1
  580.6 3.2 collective-permute-start.1
  583.8 1.0 slice_reduce_fusion.1
  585.1 0.6 sub.46.bases
  585.6 0.5 slice_bitcast_fusion.4.totals
  586.1 33.8 %pack_rows.3.packed = bf16[8,2320,1536]{2,1,0:T(8,128)(2,1)} custom-call(s32[256]{0:T(256)} %copy-done.48, s32[256]{0:T(256)} %sub.46.bases, s32[8]{0:T(128)} %slice_bitcast_fusion.4.totals, bf16[32,272,768]{2,1,0:T(8,128)(2,1)} %bitcast.57, bf16[32,272,768]{2,1,0:T(8,128)(2,1)} %bitcast.58, bf16[32,256,768]{2,1,0:T(8,128)(2,1)} %bitcast.62), custom_call_target="tpu_custom_call" | custom-call | flops 1 | bytes 1 | tf_op jit(solution)/shard_map/pack_rows/pallas_call | solution.py:1525
  620.0 42.4 %weight_grads.4 = (f32[2,8,2,768,512]{4,3,2,1,0:T(8,128)}, f32[2,8,512,768]{3,2,1,0:T(8,128)}) custom-call(s32[8]{0:T(128)} %slice_bitcast_fusion.4.totals, bf16[8,2320,1536]{2,1,0:T(8,128)(2,1)} %pack_rows.3.packed, bf16[2,8,2,768,512]{4,3,2,1,0:T(8,128)(2,1)} %wgu.13, bf16[2,8,512,768]{3,2,1,0:T(8,128)(2,1)} %wd.13, ...), custom_call_target="tpu_custom_call", output_to_operand_aliasing={{0}: (4, {}), {1}: (5, {})} | custom-call | flops 1 | bytes 1 | tf_op jit(solution)/shard_map/weight_grads/pallas_call | solution.py:1609
  662.4 1.2 copy-done.42
  663.6 2.5 add_convert_fusion.ours
  666.1 5.8 collective-permute-start.2
  671.9 44.9 %weight_grads.5 = (f32[2,8,2,768,512]{4,3,2,1,0:T(8,128)}, f32[2,8,512,768]{3,2,1,0:T(8,128)}) custom-call(s32[8]{0:T(128)} %slice_bitcast_fusion.4.totals, bf16[8,2320,1536]{2,1,0:T(8,128)(2,1)} %pack_rows.3.packed, bf16[2,8,2,768,512]{4,3,2,1,0:T(8,128)(2,1)} %wgu.13, bf16[2,8,512,768]{3,2,1,0:T(8,128)(2,1)} %wd.13, ...), custom_call_target="tpu_custom_call", output_to_operand_aliasing={{0}: (4, {}), {1}: (5, {})} | custom-call | flops 1 | bytes 1 | tf_op jit(solution)/shard_map/weight_grads/pallas_call | solution.py:1609
  716.8 5.3 assemble.1
  722.1 1.7 copy.42
  723.8 0.9 copy.54
  724.7 0.9 copy.55
  (117 shorter events, 2.1 us)
Async XLA Ops:
  7.2 10.4 %copy-start = (f32[1024,128]{1,0:T(8,128)S(1)}, f32[1024,128]{1,0:T(8,128)}, u32[]{:S(2)}) copy-start(f32[1024,128]{1,0:T(8,128)} %constant.86.clone.cosine) | copy-start | bytes 1572868
  7.2 10.4 %copy-start.1 = (f32[1024,128]{1,0:T(8,128)S(1)}, f32[1024,128]{1,0:T(8,128)}, u32[]{:S(2)}) copy-start(f32[1024,128]{1,0:T(8,128)} %constant.87.clone.sine) | copy-start | bytes 1572868
  7.2 10.3 %copy-start.45 = (bf16[1,256,768]{2,1,0:T(8,128)(2,1)S(1)}, bf16[1,256,768]{2,1,0:T(8,128)(2,1)}, u32[]{:S(2)}) copy-start(bf16[1,256,768]{2,1,0:T(8,128)(2,1)} %param.14) | copy-start | bytes 1179652
  7.2 10.4 %copy-start.7 = (bf16[2,192,768]{2,1,0:T(8,128)(2,1)S(1)}, bf16[2,192,768]{2,1,0:T(8,128)(2,1)}, u32[]{:S(2)}) copy-start(bf16[2,192,768]{2,1,0:T(8,128)(2,1)} %wo_own.3) | copy-start | bytes 1769476
  7.2 181.0 %all-gather.9.cloned.1.call-start = ((), (), s32[]{:S(2)}) async-start(), calls=%async_computation | async-start | bytes 12976128 | tf_op jit(solution)/shard_map/all_gather | solution.py:1831
  8.0 396.5 %all-gather.11.cloned.1.call-start = ((), (), s32[]{:S(2)}) async-start(), calls=%async_computation.1 | async-start | bytes 13787136 | tf_op jit(solution)/shard_map/all_gather | solution.py:1842
  17.4 110.6 %copy-start.39 = (s32[8]{0:T(128)}, s32[8]{0:T(128)S(1)}, u32[]{:S(2)}) copy-start(s32[8]{0:T(128)S(1)} %subtract_reduce_fusion.order) | copy-start | bytes 100
  17.5 110.4 %copy-start.40 = (s32[8]{0:T(128)}, s32[8]{0:T(128)S(1)}, u32[]{:S(2)}) copy-start(s32[8]{0:T(128)S(1)} %select_reduce_fusion.inv) | copy-start | bytes 100
  17.5 212.7 %copy-start.20 = (bf16[20,768]{1,0:T(8,128)(2,1)}, bf16[20,768]{1,0:T(8,128)(2,1)S(1)}, u32[]{:S(2)}) copy-start(bf16[20,768]{1,0:T(8,128)(2,1)S(1)} %get-tuple-element.197.small) | copy-start | bytes 92164
  17.5 329.0 %copy-start.19 = (bf16[20,768]{1,0:T(8,128)(2,1)}, bf16[20,768]{1,0:T(8,128)(2,1)S(1)}, u32[]{:S(2)}) copy-start(bf16[20,768]{1,0:T(8,128)(2,1)S(1)} %get-tuple-element.198.small) | copy-start | bytes 92164
  17.6 55.9 %copy-start.2 = (f32[256,768]{1,0:T(8,128)}, f32[256,768]{1,0:T(8,128)S(1)}, u32[]{:S(2)}) copy-start(f32[256,768]{1,0:T(8,128)S(1)} %bitcast_convert_fusion.x) | copy-start | bytes 2359300
  73.5 1.1 copy-start.9
  74.7 1.0 copy-start.13
  75.7 1.0 copy-start.15
  76.7 1.0 copy-start.17
  77.7 0.8 copy-start.24
  78.5 0.8 copy-start.28
  79.3 0.7 copy-start.33
  80.1 45.9 %copy-start.5 = (f32[256,768]{1,0:T(8,128)}, f32[256,768]{1,0:T(8,128)S(1)}, u32[]{:S(2)}) copy-start(f32[256,768]{1,0:T(8,128)S(1)} %get-tuple-element.86.hst) | copy-start | bytes 2359300
  80.8 1.0 copy-start.34
  126.0 1.1 copy-start.11
  127.1 0.8 copy-start.32
  127.9 53.7 %copy-start.4 = (f32[256,768]{1,0:T(8,128)}, f32[256,768]{1,0:T(8,128)S(1)}, u32[]{:S(2)}) copy-start(f32[256,768]{1,0:T(8,128)S(1)} %get-tuple-element.87.x) | copy-start | bytes 2359300
  181.6 1.1 copy-start.10
  182.8 1.0 copy-start.14
  183.8 1.0 copy-start.16
  184.8 1.0 copy-start.18
  185.7 0.8 copy-start.26
  186.5 0.8 copy-start.29
  187.3 0.7 copy-start.35
  188.1 40.3 %copy-start.6 = (f32[256,768]{1,0:T(8,128)}, f32[256,768]{1,0:T(8,128)S(1)}, u32[]{:S(2)}) copy-start(f32[256,768]{1,0:T(8,128)S(1)} %get-tuple-element.92.hst) | copy-start | bytes 2359300
  188.1 273.6 %all-gather.13.cloned.1.call-start = ((), (), s32[]{:S(2)}) async-start(), calls=%async_computation.2 | async-start | bytes 13787136 | tf_op jit(solution)/shard_map/all_gather | solution.py:1847
  188.2 1.2 copy-start.36
  189.4 40.7 %copy-start.46 = (s32[2,1,256,2]{2,3,1,0:T(2,128)S(1)}, s32[2,1,256,2]{2,3,1,0:T(2,128)}, u32[]{:S(2)}) copy-start(s32[2,1,256,2]{2,3,1,0:T(2,128)} %param.17) | copy-start | bytes 12292
  189.4 40.7 %copy-start.3 = (bf16[1,256,768]{2,1,0:T(8,128)(2,1)S(1)}, bf16[1,256,768]{2,1,0:T(8,128)(2,1)}, u32[]{:S(2)}) copy-start(bf16[1,256,768]{2,1,0:T(8,128)(2,1)} %param.15) | copy-start | bytes 1179652
  228.4 1.1 copy-start.12
  229.5 1.0 copy-start.27
  229.6 351.0 %all-gather.15.cloned.1.call-start = ((), (), s32[]{:S(2)}) async-start(), calls=%async_computation.3 | async-start | bytes 12976128 | tf_op jit(solution)/shard_map/all_gather | solution.py:1871
  285.8 0.9 copy-start.22
  286.7 0.8 copy-start.31
  287.4 0.6 copy-start.38
  288.1 58.5 %copy-start.25 = (bf16[8,128,256]{2,1,0:T(8,128)(2,1)S(1)}, bf16[8,128,256]{2,1,0:T(8,128)(2,1)}, u32[]{:S(2)}) copy-start(bf16[8,128,256]{2,1,0:T(8,128)(2,1)} %copy-done.24) | copy-start | bytes 1572868
  346.6 1.0 copy-start.8
  347.6 1.1 copy-start.23
  402.2 0.9 copy-start.21
  403.1 0.8 copy-start.30
  403.8 0.6 copy-start.37
  404.5 55.9 %copy-start.44 = (bf16[192,2048]{1,0:T(8,128)(2,1)S(1)}, bf16[192,2048]{1,0:T(8,128)(2,1)}, u32[]{:S(2)}) copy-start(bf16[192,2048]{1,0:T(8,128)(2,1)} %get-tuple-element.127) | copy-start | bytes 2359300
  462.9 1.2 copy-start.47
  497.8 79.6 %collective-permute-start = (bf16[2,192,2048]{2,1,0:T(8,128)(2,1)S(1)}, bf16[2,192,2048]{2,1,0:T(8,128)(2,1)}, u32[]{:S(2)}, u32[]{:S(2)}) collective-permute-start(bf16[2,192,2048]{2,1,0:T(8,128)(2,1)S(1)} %pad_maximum_fusion), channel_id=1, source_target_pairs={{0,4},{4,0},{8,12},{12,8},{16,20},{20,16},{24,28},{28,24},{1,5},{5... | collective-permute-start | bytes 4718600 | tf_op jit(solution)/shard_map/ppermute | solution.py:1874
  580.6 81.8 %collective-permute-start.1 = (bf16[2,192,2048]{2,1,0:T(8,128)(2,1)}, bf16[2,192,2048]{2,1,0:T(8,128)(2,1)S(1)}, u32[]{:S(2)}, u32[]{:S(2)}) collective-permute-start(bf16[2,192,2048]{2,1,0:T(8,128)(2,1)} %add_convert_fusion.1), channel_id=1, source_target_pairs={{0,16},{4,20},{8,24},{12,28},{16,0},{20,4},{24,8},{28,12},{1,17},{... | collective-permute-start | bytes 4718600 | tf_op jit(solution)/shard_map/ppermute | solution.py:1874
  585.0 1.2 copy-start.48
  662.4 1.2 copy-start.42
  666.1 50.7 %copy-start.41 = (bf16[2,192,2048]{2,1,0:T(8,128)(2,1)}, bf16[2,192,2048]{2,1,0:T(8,128)(2,1)S(1)}, u32[]{:S(2)}) copy-start(bf16[2,192,2048]{2,1,0:T(8,128)(2,1)S(1)} %add_convert_fusion.ours) | copy-start | bytes 4718596
  666.1 50.7 %collective-permute-start.2 = (bf16[2,192,2048]{2,1,0:T(8,128)(2,1)S(1)}, bf16[2,192,2048]{2,1,0:T(8,128)(2,1)}, u32[]{:S(2)}, u32[]{:S(2)}) collective-permute-start(bf16[2,192,2048]{2,1,0:T(8,128)(2,1)S(1)} %add_convert_fusion.ours), channel_id=1, source_target_pairs={{0,8},{4,12},{8,0},{12,4},{16,24},{20,28},{24,16},{28,20},{1,9},{5... | collective-permute-start | bytes 4718600 | tf_op jit(solution)/shard_map/ppermute | solution.py:1874
  722.1 2.6 copy-start.43
Sparse Core Ops, SparseCore 0:
  10.9 127.4 all-gather.8
  188.2 116.1 all-gather.10
  307.4 127.1 all-gather.12
  461.8 118.1 all-gather.14

commit v10 on v8

--- a/solution.py
+++ b/solution.py
@@ -613,9 +613,9 @@
 
 def attn_fwd_kernel(
     order, inv, x, small, wq, cosine, sine, wo_own,
-    n1s, qkv, o, lse, ob, hst, ub, w, wo,
-    n1own, n1r, osort, osend, orecv, cols, w_s, wo_s,
-    n_send, n_recv, f_send, f_recv, o_send, o_recv, w_send, w_recv, v_send, v_recv,
+    n1s_h, qkv_h, o, lse, ob, hst, ub, w_h, wo_h,
+    n1own, n1r, osort, osend, orecv, cols, w_s, wo_s, n1s, qkv,
+    n_send, n_recv, f_send, f_recv, o_send, o_recv, w_send, w_recv, v_send, v_recv, early,
 ):
     blocks, blk, _ = n1r.shape
     lanes = o.shape[1]
@@ -697,9 +697,14 @@
 
     for index in range(3):
         w_wait(index)
-    w[...] = w_s[...]
+    stores = [
+        pltpu.make_async_copy(source, target, early.at[index])
+        for index, (source, target) in enumerate(((w_s, w_h), (n1s, n1s_h), (qkv, qkv_h), (wo_s, wo_h)))
+    ]
+    stores[0].start()
     for b in range(blocks):
         n1s[b * blk : (b + 1) * blk, :] = n1r[inv[b]]
+    stores[1].start()
     for i in range(seq // step):
         part = slice(i * step, (i + 1) * step)
         out = nn(n1s[part, :], w_s[...])
@@ -709,6 +714,7 @@
         qkv[part, :lanes] = q * jnp.asarray(HEAD_DIM**-0.5, jnp.bfloat16)
         qkv[part, lanes : 2 * lanes] = spin(out[:, lanes : 2 * lanes], cos2, sin2).astype(jnp.bfloat16)
         qkv[part, 2 * lanes :] = out[:, 2 * lanes :].astype(jnp.bfloat16)
+    stores[2].start()
     lane = lax.broadcasted_iota(jnp.int32, (step, 128), 1)
     for i in range(seq // step):
         part = slice(i * step, (i + 1) * step)
@@ -766,7 +772,7 @@
     ob[...] = orecv[...]
     remote(wo_s.at[beside], wo_s.at[beside], v_send.at[1], v_recv.at[1], own, beside).wait_recv()
     remote(wo_s.at[corner], wo_s.at[corner], v_send.at[2], v_recv.at[2], own, beside).wait_recv()
-    wo[...] = wo_s[...]
+    stores[3].start()
     total, low = post_attention(orecv[...], x[...], wo_s[...], small[1:2, :].astype(jnp.float32))
     hst[...] = total
     ub[...] = low
@@ -782,6 +788,8 @@
     v_far.wait_send()
     v_near.wait_send()
     v_on.wait_send()
+    for store in stores:
+        store.wait()
     for ctx in range(blocks):
 
         @pl.when(jnp.logical_not(jnp.logical_and(same, ctx == own)))
@@ -795,6 +803,7 @@
     packs, inner = width // wo.shape[1], wo.shape[1]
     lanes = -(-inner // 128) * 128
     seq = blocks * blk
+    hm = pl.BlockSpec(memory_space=pl.ANY)
     vm = pl.BlockSpec(memory_space=pltpu.VMEM)
     sm = pl.BlockSpec(memory_space=pltpu.SMEM)
     bf = jnp.bfloat16
@@ -816,7 +825,7 @@
         in_specs=[sm, sm, vm, vm]
         + [pl.BlockSpec((1, 3, inner, width), lambda _: (layer, 0, 0, 0)), vm, vm]
         + [pl.BlockSpec((1, inner, width), lambda _: (layer, 0, 0))],
-        out_specs=[vm] * 9,
+        out_specs=[hm, hm] + [vm] * 5 + [hm, hm],
         scratch_shapes=[
             pltpu.VMEM((2, blk, width), bf),
             pltpu.VMEM((blocks, blk, width), bf),
@@ -826,10 +835,13 @@
             pltpu.VMEM((2, inner, 3 * lanes), bf),
             pltpu.VMEM((width, 3 * lanes), bf),
             pltpu.VMEM((packs, inner, width), bf),
+            pltpu.VMEM((seq, width), bf),
+            pltpu.VMEM((seq, 3 * lanes), bf),
         ]
         + [dma((blocks // 2,))] * 4
         + [dma((blocks,))] * 2
-        + [dma((3,))] * 4,
+        + [dma((3,))] * 4
+        + [dma((4,))],
         compiler_params=params_of(collective_id=number, has_side_effects=True),
         cost_estimate=BRIEF,
         name="attn_fwd",
@@ -837,10 +849,10 @@
 
 
 def attn_bwd_kernel(
-    order, inv, n1s, w, cosine, sine, qkv, o, lse, go, ghst, x, small, gsmall, gwo,
+    order, inv, n1s_h, w_h, cosine_h, sine_h, qkv, o_h, lse, go, ghst, x, small, gsmall, gwo,
     gx, gm, dense,
-    gor, gos, grads, acc, gns, sib_out, sib_in, gn_out, gnr, gw, gw_in, both, both_in, wo_in, wo_both, wo_over, probs,
-    o_send, o_recv, s_send, s_recv, g_send, g_recv, r_send, r_recv, w_send, w_recv,
+    gor, gos, grads, acc, gns, sib_out, sib_in, gn_out, gnr, gw, gw_in, both, both_in, wo_in, wo_both, wo_over, probs, n1s, w, cosine, sine, o,
+    o_send, o_recv, s_send, s_recv, g_send, g_recv, r_send, r_recv, w_send, w_recv, late,
 ):
     blocks, blk, width = grads.shape
     lanes = o.shape[1]
@@ -852,6 +864,14 @@
     depth = blocks // 2
     same = xx == k
 
+    loads = [
+        pltpu.make_async_copy(source, target, late.at[index])
+        for index, (source, target) in enumerate(
+            ((o_h, o), (n1s_h, n1s), (w_h, w), (cosine_h, cosine), (sine_h, sine))
+        )
+    ]
+    for load in loads:
+        load.start()
     barrier, others = greet_plane(blocks, across=True)
     acc[...] = jnp.zeros_like(acc)
     pl.semaphore_wait(barrier, others)
@@ -897,6 +917,8 @@
         def _():
             remote(go.at[0], gor.at[ctx], o_send.at[0], o_recv.at[ctx], ctx, 2 * y + xx).wait_recv()
 
+    for load in loads:
+        load.wait()
     for half in range(2):
         wo_copy(half).wait_recv()
         total = gwo[2 * half + k].astype(jnp.float32) + wo_in[half].astype(jnp.float32)
@@ -1041,6 +1063,7 @@
     count = x.shape[0]
     packs, inner = gwo.shape[0], gwo.shape[1]
     depth = blocks // 2
+    hm = pl.BlockSpec(memory_space=pl.ANY)
     vm = pl.BlockSpec(memory_space=pltpu.VMEM)
     sm = pl.BlockSpec(memory_space=pltpu.SMEM)
     bf = jnp.bfloat16
@@ -1052,7 +1075,7 @@
             shape_of((count, width), bf),
             shape_of((inner, 128 + 6 * inner + width), bf),
         ],
-        in_specs=[sm] * 2 + [vm] * 13,
+        in_specs=[sm] * 2 + [hm] * 4 + [vm, hm] + [vm] * 7,
         out_specs=[vm] * 3,
         scratch_shapes=[
             pltpu.VMEM((blocks, blk, lanes), bf),
@@ -1072,10 +1095,16 @@
             pltpu.VMEM((2, inner, width), bf),
             pltpu.VMEM((inner, width), bf),
             pltpu.VMEM((GROUP_HEADS, seq, seq), jnp.float32),
+            pltpu.VMEM(n1s.shape, bf),
+            pltpu.VMEM(w.shape, bf),
+            pltpu.VMEM(cosine.shape, jnp.float32),
+            pltpu.VMEM(sine.shape, jnp.float32),
+            pltpu.VMEM(o.shape, jnp.float32),
         ]
         + [dma((blocks,))] * 2
         + [dma((depth,))] * 4
-        + [dma((3,))] * 4,
+        + [dma((3,))] * 4
+        + [dma((5,))],
         compiler_params=params_of(collective_id=number, has_side_effects=True),
         cost_estimate=BRIEF,
         name="attn_bwd",

time: 722 us -> 710 us (0.983)
  Pallas kernels: 664 us -> 650 us
  transfers between devices with their start and end apart: 7 -> 7, of which waited for: 1 -> 1; matrix products, arithmetic and copies ran while one was open for 2% -> 2% of each run, Pallas kernels for 92% -> 91%
where the time goes in v10:
time: 710 us; the launch traced here: 705 us
  Pallas kernels  650 us (92%)
  between operations  14.3 us (2%)
  other arithmetic  13.7 us (2%)
  local copies, waits for them, and re-layouts  10.4 us (1%)
    pallas_call x3, Pallas kernels, weight_grads(): pl.pallas_call(functools.partial(dw_kernel, first), grid_spec=pltpu.Prefe...  157 us
    pallas_call x2, Pallas kernels, attn_backward(): pl.pallas_call(attn_bwd_kernel, out_shape=[shape_of((count, width), jnp.f...  112 us
    pallas_call x2, Pallas kernels, ffn_backward(): pl.pallas_call(ffn_bwd_kernel, grid=(NF,), out_shape=outs, in_specs=[whol...  112 us
    pallas_call x2, Pallas kernels, attn_forward(): pl.pallas_call(attn_fwd_kernel, grid=(1,), out_shape=[shape_of((seq, widt...  109 us
    pallas_call x2, Pallas kernels, ffn_forward(): pl.pallas_call(ffn_fwd_kernel, grid=(NF,), out_shape=outs, in_specs=[whol...  88.4 us
    pallas_call x2, Pallas kernels, pack_rows(): pl.pallas_call(pack_kernel, grid_spec=pltpu.PrefetchScalarGridSpec(num_sc...  67 us
  transfers between devices with their start and end apart: 7, of which 1 were waited for; matrix products, arithmetic and copies ran while one was open for 2% of the time, Pallas kernels for 91%

profile of v10, /device:TPU:0, one launch (start us, length us, event | category | flops | bytes accessed | tf_op | source)
XLA Modules:
  0.0 705.0 jit_solution(15303087174343132764)
XLA Ops:
  7.2 0.0 all-gather.9.cloned.1.call-start
  7.2 0.7 all-gather.9.cloned.1.call-update
  7.9 0.0 all-gather.11.cloned.1.call-start
  8.0 0.7 convert_bitcast_fusion
  8.7 0.7 convert_bitcast_fusion.1
  9.4 0.1 reshape.232
  9.5 0.7 pad_maximum_fusion.1
  10.2 6.3 all-gather.3
  16.6 0.1 copy.38
  16.6 0.1 reshape.250
  16.8 0.1 reshape.237
  16.9 0.1 reshape.235
  17.0 0.1 dynamic-slice_reduce_fusion
  17.0 0.1 reshape.233
  17.1 0.2 subtract_reduce_fusion.order
  17.3 0.7 select_reduce_fusion.inv
  18.0 0.6 fusion.8
  18.6 0.9 bitcast_convert_fusion.x
  19.6 55.5 %attn_fwd.2 = (bf16[1024,768]{1,0:T(8,128)(2,1)}, bf16[1024,768]{1,0:T(8,128)(2,1)}, f32[1024,256]{1,0:T(8,128)}, f32[1024,128]{1,0:T(8,128)}, bf16[8,128,256]{2...) custom-call(s32[8]{0:T(128)} %copy-done.8, ...), custom_call_target="tpu_custom_call" | custom-call | flops 1 | bytes 1 | tf_op jit(solution)/shard_map/attn_fwd/pallas_call | solution.py:811
  75.0 0.1 fusion.7
  75.1 0.6 gather_fusion
  75.7 0.6 slice_bitcast_fusion
  76.4 0.7 broadcast_in_dim.30.before
  77.1 47.4 %ffn_fwd.2 = (bf16[4,256,768]{2,1,0:T(8,128)(2,1)}, f32[4,56,256]{2,1,0:T(8,128)}, bf16[272,768]{1,0:T(8,128)(2,1)}, f32[256,768]{1,0:T(8,128)}) custom-call(bf16[256,768]{1,0:T(8,128)(2,1)} %get-tuple-element.85.ub, f32[256,768]{1,0:T(8,128)} %get-tuple-element.86.hst, bf16[20,768]{1,0:T(8,128)(2,1)} %get-tuple-element.198.small, ...), custom_call_target="tpu_custom_call" | custom-call | flops 1 | bytes 1 | tf_op jit(solution)/shard_map/ffn_fwd/pallas_call | solution.py:1281
  124.4 53.7 %attn_fwd.3 = (bf16[1024,768]{1,0:T(8,128)(2,1)}, bf16[1024,768]{1,0:T(8,128)(2,1)}, f32[1024,256]{1,0:T(8,128)}, f32[1024,128]{1,0:T(8,128)}, bf16[8,128,256]{2...) custom-call(s32[8]{0:T(128)} %copy-done.8, ...), custom_call_target="tpu_custom_call" | custom-call | flops 1 | bytes 1 | tf_op jit(solution)/shard_map/attn_fwd/pallas_call | solution.py:811
  178.1 0.0 all-gather.13.cloned.1.call-start
  178.2 41.1 %ffn_fwd.3 = (bf16[4,256,768]{2,1,0:T(8,128)(2,1)}, f32[4,56,256]{2,1,0:T(8,128)}, bf16[272,768]{1,0:T(8,128)(2,1)}, f32[256,768]{1,0:T(8,128)}) custom-call(bf16[256,768]{1,0:T(8,128)(2,1)} %get-tuple-element.89.ub, f32[256,768]{1,0:T(8,128)} %get-tuple-element.92.hst, bf16[20,768]{1,0:T(8,128)(2,1)} %get-tuple-element.197.small, ...), custom_call_target="tpu_custom_call" | custom-call | flops 1 | bytes 1 | tf_op jit(solution)/shard_map/ffn_fwd/pallas_call | solution.py:1281
  219.3 0.0 all-gather.15.cloned.1.call-start
  219.4 0.6 slice_bitcast_fusion.2
  220.0 0.9 bitcast_convert_fusion.1.gx
  220.9 0.6 broadcast_in_dim.32.gprev
  221.5 56.3 %ffn_bwd.2 = (f32[256,768]{1,0:T(8,128)}, bf16[8,128,256]{2,1,0:T(8,128)(2,1)}, bf16[4,192,768]{2,1,0:T(8,128)(2,1)}, f32[19,768]{1,0:T(8,128)}, f32[16,256]{1,0:T(8,128)}) custom-call(bf16[256,768]{1,0:T(8,128)(2,1)} %bitcast.61, f32[256,768]{1,0:T(8,128)} %bitcast_convert_fusion.1.gx, bf16[4,256,768]{2,1,0:T(8,128)(2,1)} %get-tuple-element.105.ubf, ...), custom_call_target="tpu_custom_call" | custom-call | flops 1 | bytes 1 | tf_op jit(solution)/shard_map/ffn_bwd/pallas_call | solution.py:1434
  277.8 55.9 %attn_bwd.2 = (f32[256,768]{1,0:T(8,128)}, bf16[256,768]{1,0:T(8,128)(2,1)}, bf16[192,2048]{1,0:T(8,128)(2,1)}) custom-call(s32[8]{0:T(128)} %copy-done.8, s32[8]{0:T(128)} %select_reduce_fusion.inv, bf16[1024,768]{1,0:T(8,128)(2,1)} %get-tuple-element.100.n1s_h, bf16[768,768]{1,0:T(8,128)(2,1)} %get-tuple-element.101.w_h, ...), custom_call_target="tpu_custom_call" | custom-call | flops 1 | bytes 1 | tf_op jit(solution)/shard_map/attn_bwd/pallas_call | solution.py:1071
  333.7 55.5 %ffn_bwd.3 = (f32[256,768]{1,0:T(8,128)}, bf16[8,128,256]{2,1,0:T(8,128)(2,1)}, bf16[4,192,768]{2,1,0:T(8,128)(2,1)}, f32[19,768]{1,0:T(8,128)}, f32[16,256]{1,0:T(8,128)}) custom-call(bf16[256,768]{1,0:T(8,128)(2,1)} %get-tuple-element.137.gm, f32[256,768]{1,0:T(8,128)} %get-tuple-element.114.gx, bf16[4,256,768]{2,1,0:T(8,128)(2,1)} %get-tuple-element.115.ubf, ...), custom_call_target="tpu_custom_call" | custom-call | flops 1 | bytes 1 | tf_op jit(solution)/shard_map/ffn_bwd/pallas_call | solution.py:1434
  389.3 56.2 %attn_bwd.3 = (f32[256,768]{1,0:T(8,128)}, bf16[256,768]{1,0:T(8,128)(2,1)}, bf16[192,2048]{1,0:T(8,128)(2,1)}) custom-call(s32[8]{0:T(128)} %copy-done.8, s32[8]{0:T(128)} %select_reduce_fusion.inv, bf16[1024,768]{1,0:T(8,128)(2,1)} %get-tuple-element.95.n1s_h, bf16[768,768]{1,0:T(8,128)(2,1)} %get-tuple-element.96.w_h, ...), custom_call_target="tpu_custom_call" | custom-call | flops 1 | bytes 1 | tf_op jit(solution)/shard_map/attn_bwd/pallas_call | solution.py:1071
  445.5 1.3 pad_maximum_fusion
  446.8 1.0 slice_reduce_fusion
  447.9 0.1 reduce_window_sum.21
  447.9 0.1 convert_element_type.67.counts
  448.0 0.1 reduce_window_sum.22
  448.1 0.6 sub.45.bases
  448.7 0.5 slice_bitcast_fusion.5.totals
  449.2 33.5 %pack_rows.2.packed = bf16[8,2320,1536]{2,1,0:T(8,128)(2,1)} custom-call(s32[256]{0:T(256)} %copy-done.9, s32[256]{0:T(256)} %sub.45.bases, s32[8]{0:T(128)} %slice_bitcast_fusion.5.totals, bf16[32,272,768]{2,1,0:T(8,128)(2,1)} %bitcast.58, bf16[32,272,768]{2,1,0:T(8,128)(2,1)} %bitcast.59, bf16[32,256,768]{2,1,0:T(8,128)(2,1)} %all-gather.9.cloned.1.call-done.gm), custom_call_target="tpu_custom_call" | custom-call | flops 1 | bytes 1 | tf_op jit(solution)/shard_map/pack_rows/pallas_call | solution.py:1554
  482.7 0.1 collective-permute-start
  482.8 76.0 %weight_grads.3 = (f32[2,8,2,768,512]{4,3,2,1,0:T(8,128)}, f32[2,8,512,768]{3,2,1,0:T(8,128)}) custom-call(s32[8]{0:T(128)} %slice_bitcast_fusion.5.totals, bf16[8,2320,1536]{2,1,0:T(8,128)(2,1)} %pack_rows.2.packed, bf16[2,8,2,768,512]{4,3,2,1,0:T(8,128)(2,1)} %wgu.13, bf16[2,8,512,768]{3,2,1,0:T(8,128)(2,1)} %wd.13), custom_call_target="tpu_custom_call" | custom-call | flops 1 | bytes 1 | tf_op jit(solution)/shard_map/weight_grads/pallas_call | solution.py:1638
  558.9 2.2 add_convert_fusion.1
  561.0 5.2 all-gather.15.cloned.1.call-done
  566.2 1.5 collective-permute-start.1
  567.7 1.0 slice_reduce_fusion.1
  568.8 0.1 reduce_window_sum.23
  568.8 0.1 convert_element_type.73.counts
  568.9 0.1 reduce_window_sum.24
  569.0 0.6 sub.46.bases
  569.6 0.5 slice_bitcast_fusion.4.totals
  570.1 33.5 %pack_rows.3.packed = bf16[8,2320,1536]{2,1,0:T(8,128)(2,1)} custom-call(s32[256]{0:T(256)} %copy-done.10, s32[256]{0:T(256)} %sub.46.bases, s32[8]{0:T(128)} %slice_bitcast_fusion.4.totals, bf16[32,272,768]{2,1,0:T(8,128)(2,1)} %bitcast.55, bf16[32,272,768]{2,1,0:T(8,128)(2,1)} %bitcast.56, bf16[32,256,768]{2,1,0:T(8,128)(2,1)} %bitcast.60), custom_call_target="tpu_custom_call" | custom-call | flops 1 | bytes 1 | tf_op jit(solution)/shard_map/pack_rows/pallas_call | solution.py:1554
  603.6 34.2 %weight_grads.4 = (f32[2,8,2,768,512]{4,3,2,1,0:T(8,128)}, f32[2,8,512,768]{3,2,1,0:T(8,128)}) custom-call(s32[8]{0:T(128)} %slice_bitcast_fusion.4.totals, bf16[8,2320,1536]{2,1,0:T(8,128)(2,1)} %pack_rows.3.packed, bf16[2,8,2,768,512]{4,3,2,1,0:T(8,128)(2,1)} %wgu.13, bf16[2,8,512,768]{3,2,1,0:T(8,128)(2,1)} %wd.13, ...), custom_call_target="tpu_custom_call", output_to_operand_aliasing={{0}: (4, {}), {1}: (5, {})} | custom-call | flops 1 | bytes 1 | tf_op jit(solution)/shard_map/weight_grads/pallas_call | solution.py:1638
  637.8 2.0 add_convert_fusion.ours
  639.8 2.1 collective-permute-start.2
  641.9 46.3 %weight_grads.5 = (f32[2,8,2,768,512]{4,3,2,1,0:T(8,128)}, f32[2,8,512,768]{3,2,1,0:T(8,128)}) custom-call(s32[8]{0:T(128)} %slice_bitcast_fusion.4.totals, bf16[8,2320,1536]{2,1,0:T(8,128)(2,1)} %pack_rows.3.packed, bf16[2,8,2,768,512]{4,3,2,1,0:T(8,128)(2,1)} %wgu.13, bf16[2,8,512,768]{3,2,1,0:T(8,128)(2,1)} %wd.13, ...), custom_call_target="tpu_custom_call", output_to_operand_aliasing={{0}: (4, {}), {1}: (5, {})} | custom-call | flops 1 | bytes 1 | tf_op jit(solution)/shard_map/weight_grads/pallas_call | solution.py:1638
  688.2 1.2 copy-done.2
  689.4 5.4 assemble.1
  694.8 1.7 copy.42
  696.5 0.9 copy.54
  697.4 0.9 copy.55
  (41 shorter events, 0.3 us)
Async XLA Ops:
  7.2 11.4 %copy-start.6 = (bf16[1,256,768]{2,1,0:T(8,128)(2,1)S(1)}, bf16[1,256,768]{2,1,0:T(8,128)(2,1)}, u32[]{:S(2)}) copy-start(bf16[1,256,768]{2,1,0:T(8,128)(2,1)} %param.14) | copy-start | bytes 1179652
  7.2 171.0 %all-gather.9.cloned.1.call-start = ((), (), s32[]{:S(2)}) async-start(), calls=%async_computation | async-start | bytes 12976128 | tf_op jit(solution)/shard_map/all_gather | solution.py:1860
  7.9 381.3 %all-gather.11.cloned.1.call-start = ((), (), s32[]{:S(2)}) async-start(), calls=%async_computation.1 | async-start | bytes 13787136 | tf_op jit(solution)/shard_map/all_gather | solution.py:1871
  17.3 2.2 copy-start.8
  178.1 268.7 %all-gather.13.cloned.1.call-start = ((), (), s32[]{:S(2)}) async-start(), calls=%async_computation.2 | async-start | bytes 13787136 | tf_op jit(solution)/shard_map/all_gather | solution.py:1876
  178.2 41.2 %copy-start.7 = (s32[2,1,256,2]{2,3,1,0:T(2,128)S(1)}, s32[2,1,256,2]{2,3,1,0:T(2,128)}, u32[]{:S(2)}) copy-start(s32[2,1,256,2]{2,3,1,0:T(2,128)} %param.17) | copy-start | bytes 12292
  178.2 41.8 %copy-start.1 = (bf16[1,256,768]{2,1,0:T(8,128)(2,1)S(1)}, bf16[1,256,768]{2,1,0:T(8,128)(2,1)}, u32[]{:S(2)}) copy-start(bf16[1,256,768]{2,1,0:T(8,128)(2,1)} %param.15) | copy-start | bytes 1179652
  219.3 346.9 %all-gather.15.cloned.1.call-start = ((), (), s32[]{:S(2)}) async-start(), calls=%async_computation.3 | async-start | bytes 12976128 | tf_op jit(solution)/shard_map/all_gather | solution.py:1900
  389.2 56.2 %copy-start.5 = (bf16[192,2048]{1,0:T(8,128)(2,1)S(1)}, bf16[192,2048]{1,0:T(8,128)(2,1)}, u32[]{:S(2)}) copy-start(bf16[192,2048]{1,0:T(8,128)(2,1)} %get-tuple-element.127) | copy-start | bytes 2359300
  448.0 1.2 copy-start.9
  482.7 76.1 %collective-permute-start = (bf16[2,192,2048]{2,1,0:T(8,128)(2,1)S(1)}, bf16[2,192,2048]{2,1,0:T(8,128)(2,1)}, u32[]{:S(2)}, u32[]{:S(2)}) collective-permute-start(bf16[2,192,2048]{2,1,0:T(8,128)(2,1)S(1)} %pad_maximum_fusion), channel_id=1, source_target_pairs={{0,4},{4,0},{8,12},{12,8},{16,20},{20,16},{24,28},{28,24},{1,5},{5... | collective-permute-start | bytes 4718600 | tf_op jit(solution)/shard_map/ppermute | solution.py:1903
  566.2 71.6 %collective-permute-start.1 = (bf16[2,192,2048]{2,1,0:T(8,128)(2,1)S(1)}, bf16[2,192,2048]{2,1,0:T(8,128)(2,1)}, u32[]{:S(2)}, u32[]{:S(2)}) collective-permute-start(bf16[2,192,2048]{2,1,0:T(8,128)(2,1)S(1)} %add_convert_fusion.1), channel_id=1, source_target_pairs={{0,16},{4,20},{8,24},{12,28},{16,0},{20,4},{24,8},{28,12},{1,17},{... | collective-permute-start | bytes 4718600 | tf_op jit(solution)/shard_map/ppermute | solution.py:1903
  568.9 1.2 copy-start.10
  639.8 48.4 %copy-start = (bf16[2,192,2048]{2,1,0:T(8,128)(2,1)}, bf16[2,192,2048]{2,1,0:T(8,128)(2,1)S(1)}, u32[]{:S(2)}) copy-start(bf16[2,192,2048]{2,1,0:T(8,128)(2,1)S(1)} %add_convert_fusion.ours) | copy-start | bytes 4718596
  639.8 48.4 %collective-permute-start.2 = (bf16[2,192,2048]{2,1,0:T(8,128)(2,1)S(1)}, bf16[2,192,2048]{2,1,0:T(8,128)(2,1)S(1)}, u32[]{:S(2)}, u32[]{:S(2)}) collective-permute-start(bf16[2,192,2048]{2,1,0:T(8,128)(2,1)S(1)} %add_convert_fusion.ours), channel_id=1, source_target_pairs={{0,8},{4,12},{8,0},{12,4},{16,24},{20,28},{24,16},{28,20},{1,9},{5... | collective-permute-start | bytes 4718600 | tf_op jit(solution)/shard_map/ppermute | solution.py:1903
  688.2 1.2 copy-start.2
  689.4 7.1 %copy-start.3 = (f32[256,768]{1,0:T(8,128)S(1)}, f32[256,768]{1,0:T(8,128)}, u32[]{:S(2)}) copy-start(f32[256,768]{1,0:T(8,128)} %get-tuple-element.94) | copy-start | bytes 2359300
  694.8 2.6 copy-start.4
Sparse Core Ops, SparseCore 0:
  10.9 125.5 all-gather.8
  178.3 113.7 all-gather.10
  295.0 129.8 all-gather.12
  446.9 119.2 all-gather.14
